TPU v7x, 768 devices: a whole 4x8x12 slice. The times are simulated.
768 devices in a mesh: seq: 48 (over y, z_hi, core), col: 16 (over x, z_lo).
Axes of the slice: x: 4, y: 8, z: 12 (z_hi: 3, z_lo: 4; z = z_hi * 4 + z_lo), core: 2. Of those that a mesh axis runs over, the one named last changes fastest.
Arguments:
- outer_gate: bfloat16 [3072, 12288], P('col', 'seq'), may hold values from -6 to 6
- inner_gate: bfloat16 [3072, 12288], P('col', 'seq'), may hold values from -6 to 6
- value_proj: bfloat16 [3072, 12288], P('col', 'seq'), may hold values from -6 to 6
- residues: float32 [3072, 16], P('col'), may hold values from -1.5 to 1.5
- decays: float32 [3072, 16], P('col'), may hold values from 2.4414062e-05 to 0.04
- out_weight: bfloat16 [3072, 4096], P(None, 'col'), may hold values from -0.15625 to 0.15625
- out_grad: bfloat16 [12288, 4096], P('seq', 'col'), may hold values from -6 to 6
Outputs:
- mixed: bfloat16 [12288, 4096], P('seq', 'col')
- grad_outer: bfloat16 [3072, 12288], P('col', 'seq')
- grad_inner: bfloat16 [3072, 12288], P('col', 'seq')
- grad_value: bfloat16 [3072, 12288], P('col', 'seq')
- grad_weight: float32 [3072, 4096], P('seq', 'col')
All inputs are finite; a program needn't handle non-finite values.
Results may differ from a plain program's by a relative error of at most 0.0064.
Values may be sent and summed in bfloat16 or wider, within the bound.
No kernel may reach another device: no remote copies, remote signals or barrier semaphores. Data moves between devices by JAX's collectives and lax.ppermute only.
A program may use at most 64 MiB of HBM per device.

v0:
```python
import math

import jax
import jax.numpy as jnp
from jax import lax
from jax.sharding import PartitionSpec as P

block_cells = 256
highest = lax.Precision.HIGHEST


def block_width(count, length):
    width = math.gcd(length, block_cells)
    while count * width * width > 2**21 and width > 8:
        width = width // 2
    return width


def modal_filter(signal, decays, coef):
    count, length = signal.shape
    width = block_width(count, length)
    blocks = length // width
    pieces = signal.reshape(count, blocks, width)
    lag = jnp.arange(width, dtype=jnp.float32)
    falling = coef[:, :, None] * jnp.exp(-decays[:, :, None] * lag[None, None, :])
    rising = jnp.exp(decays[:, :, None] * lag[None, None, :])
    causal = (lag[:, None] >= lag[None, :]).astype(jnp.float32)
    toeplitz = jnp.einsum("cki,ckj->cij", falling, rising, precision=highest) * causal[None]
    inner = jnp.einsum("cij,cnj->cni", toeplitz, pieces, precision=highest)
    tails = jnp.exp(-decays[:, :, None] * (width - 1.0 - lag)[None, None, :])
    sums = jnp.einsum("ckj,cnj->cnk", tails, pieces, precision=highest)
    order = jnp.arange(blocks)
    gap = order[:, None] - 1 - order[None, :]
    carried = jnp.where(
        gap[None, None] >= 0,
        jnp.exp(
            -decays[:, :, None, None]
            * (width * jnp.maximum(gap, 0)).astype(jnp.float32)[None, None]
        ),
        0.0,
    )
    states = jnp.einsum("cknm,cmk->cnk", carried, sums, precision=highest)
    heads = coef[:, :, None] * jnp.exp(-decays[:, :, None] * (lag + 1.0)[None, None, :])
    outer = jnp.einsum("ckj,cnk->cnj", heads, states, precision=highest)
    return (inner + outer).reshape(count, length)


def filtered_branch(signal, decays, coef, backward):
    spread = lax.all_to_all(signal, "seq", split_axis=0, concat_axis=1, tiled=True)
    rows = spread.shape[0]
    begin = lax.axis_index("seq") * rows
    own_decays = lax.dynamic_slice_in_dim(decays, begin, rows, 0)
    own_coef = lax.dynamic_slice_in_dim(coef, begin, rows, 0)
    work = spread.astype(jnp.float32)
    if backward:
        work = jnp.flip(work, 1)
    result = modal_filter(work, own_decays, own_coef)
    if backward:
        result = jnp.flip(result, 1)
    return lax.all_to_all(
        result.astype(jnp.bfloat16), "seq", split_axis=1, concat_axis=0, tiled=True
    )


def shards(outer_gate, inner_gate, value_proj, residues, decays, out_weight, out_grad):
    chan_rows, tok_rows = outer_gate.shape
    coef = residues * jnp.sqrt(-jnp.expm1(-2.0 * decays))
    gated = (inner_gate.astype(jnp.float32) * value_proj.astype(jnp.float32)).astype(jnp.bfloat16)
    filtered = filtered_branch(gated, decays, coef, False)
    product = (outer_gate.astype(jnp.float32) * filtered.astype(jnp.float32)).astype(jnp.bfloat16)
    piece = lax.all_gather(product, "col", axis=0, tiled=True)
    weight_piece = out_weight
    out_total = lax.dot_general(
        piece, weight_piece, (((0,), (0,)), ((), ())), preferred_element_type=jnp.float32
    )
    grad_piece = jnp.dot(piece, out_grad, preferred_element_type=jnp.float32)
    grad_total = grad_piece
    out_total, grad_total = (out_total, grad_total)
    mixed = out_total.astype(jnp.bfloat16)
    scale = 1.0 / math.sqrt(tok_rows * lax.axis_size("seq"))
    grad_weight = lax.psum_scatter(grad_total, "seq", scatter_dimension=0, tiled=True) * scale
    weight_piece = out_weight
    back_sum = lax.psum_scatter(
        lax.dot_general(
            weight_piece, out_grad, (((1,), (1,)), ((), ())), preferred_element_type=jnp.float32
        ),
        "col",
        scatter_dimension=0,
        tiled=True,
    )
    grad_outer = (back_sum * filtered.astype(jnp.float32)).astype(jnp.bfloat16)
    back_filtered = (back_sum * outer_gate.astype(jnp.float32)).astype(jnp.bfloat16)
    back_gated = filtered_branch(back_filtered, decays, coef, True).astype(jnp.float32)
    grad_inner = (back_gated * value_proj.astype(jnp.float32)).astype(jnp.bfloat16)
    grad_value = (back_gated * inner_gate.astype(jnp.float32)).astype(jnp.bfloat16)
    return (mixed, grad_outer, grad_inner, grad_value, grad_weight)


def solution(mesh):
    return jax.shard_map(
        shards,
        mesh=mesh,
        in_specs=(
            P("col", "seq"),
            P("col", "seq"),
            P("col", "seq"),
            P("col", None),
            P("col", None),
            P(None, "col"),
            P("seq", "col"),
        ),
        out_specs=(
            P("seq", "col"),
            P("col", "seq"),
            P("col", "seq"),
            P("col", "seq"),
            P("seq", "col"),
        ),
        check_vma=False,
    )
```

profile of v0, /device:TPU:1, one launch (start us, length us, event | category | flops | bytes accessed | tf_op | source)
XLA Modules:
  0.0 525.6 jit_solution(3503730012508230102)
XLA Ops:
  7.2 0.0 copy-start
  7.2 0.0 reduce-scatter.3.cloned.1.call-start
  7.2 1.4 copy-done
  8.6 3.2 fusion.53
  11.7 0.0 copy-start.7
  11.7 0.0 copy-start.8
  11.7 0.0 copy-start.4
  11.7 0.0 reduce-scatter.3.cloned.1.call-update
  11.8 0.7 copy-done.7
  12.5 0.0 copy-done.8
  12.5 0.1 dynamic-slice_multiply_fusion
  12.6 0.1 fusion.12
  12.6 0.1 fusion.50
  12.7 0.1 multiply_convert_fusion.1
  12.8 97.9 %reduce-scatter.3.cloned.1.call-done = f32[192,256]{1,0:T(8,128)} async-done(((f32[3072,256]{1,0:T(8,128)}), f32[192,256]{1,0:T(8,128)}) %reduce-scatter.3.cloned.1.call-update) | async-done | bytes 196624 | tf_op jit(solution)/shard_map/reduce_scatter | solution.py:83
  110.7 0.0 copy-done.4
  110.7 0.9 fusion.14
  111.7 0.7 all_to_all.44
  112.3 23.8 %all-to-all-start.2 = ((bf16[48,4,256]{2,1,0:T(4,128)(2,1)}), bf16[48,4,256]{2,1,0:T(4,128)(2,1)S(1)}, u32[]{:S(2)}, u32[]{:S(2)}) async-start(bf16[48,4,256]{2,1,0:T(4,128)(2,1)} %all_to_all.44), calls=%async_computation.3 | async-start | bytes 196608 | tf_op jit(solution)/shard_map/all_to_all | solution.py:49
  136.2 0.0 all-gather.2.cloned.1.call-start
  136.2 0.1 copy.40
  136.3 0.1 copy.32
  136.4 1.2 convolution_multiply_fusion
  137.6 10.6 %all-to-all-done.2 = bf16[48,4,256]{2,1,0:T(4,128)(2,1)S(1)} async-done(((bf16[48,4,256]{2,1,0:T(4,128)(2,1)}), bf16[48,4,256]{2,1,0:T(4,128)(2,1)S(1)}, u32[]{:S(2)}, u32[]{:S(2)}) %all-to-all-start.2) | async-done | bytes 98336 | tf_op jit(solution)/shard_map/all_to_all | solution.py:49
  148.2 8.4 %rev.7 = f32[4,12288]{1,0:T(4,128)S(1)} reverse(f32[4,12288]{1,0:T(4,128)S(1)} %bitcast.46), dimensions={1} | reverse | bytes 393216 | tf_op jit(solution)/shard_map/jit(_flip)/rev | solution.py:56
  156.6 0.3 fusion.18
  156.9 1.1 fusion.20
  158.0 0.0 copy-start.5
  158.0 0.0 copy-start.6
  158.1 2.6 fusion
  160.7 0.4 fusion.2
  161.1 0.1 copy.42
  161.2 8.6 %rev.8 = bf16[4,12288]{1,0:T(4,128)(2,1)S(1)} reverse(bf16[4,12288]{1,0:T(4,128)(2,1)S(1)} %bitcast.47), dimensions={1} | reverse | bytes 196608 | tf_op jit(solution)/shard_map/jit(_flip)/rev | solution.py:59
  169.8 17.1 %all_to_all.52 = bf16[4,48,256]{2,0,1:T(4,128)(2,1)S(1)} all-to-all(bf16[4,48,256]{2,0,1:T(4,128)(2,1)S(1)} %bitcast.48), channel_id=1, replica_groups=mesh['seq'=48,'col'=16] {'seq'}, dimensions={1} | all-to-all | bytes 196608 | tf_op jit(solution)/shard_map/all_to_all | solution.py:60
  187.0 0.1 reshape.114
  187.0 0.0 copy-done.5
  187.0 0.0 copy-done.6
  187.1 0.7 fusion.15
  187.8 17.1 %all_to_all.53 = bf16[48,4,256]{2,1,0:T(4,128)(2,1)S(1)} all-to-all(bf16[48,4,256]{2,1,0:T(4,128)(2,1)S(1)} %all_to_all.40), channel_id=1, replica_groups=mesh['seq'=48,'col'=16] {'seq'}, dimensions={0} | all-to-all | bytes 196608 | tf_op jit(solution)/shard_map/all_to_all | solution.py:49
  204.9 0.3 fusion.24
  205.2 2.6 fusion.1
  207.8 0.0 copy-start.2
  207.9 0.0 copy-start.3
  207.9 0.6 fusion.26
  208.5 0.4 fusion.3
  208.9 0.1 copy.34
  209.0 17.1 %all_to_all.54 = bf16[4,48,256]{2,0,1:T(4,128)(2,1)S(1)} all-to-all(bf16[4,48,256]{2,0,1:T(4,128)(2,1)S(1)} %copy.34), channel_id=1, replica_groups=mesh['seq'=48,'col'=16] {'seq'}, dimensions={1} | all-to-all | bytes 196608 | tf_op jit(solution)/shard_map/all_to_all | solution.py:60
  226.2 0.1 reshape.112
  226.2 0.0 copy-done.2
  226.2 0.7 multiply_convert_fusion
  227.0 0.0 all-gather.2.cloned.1.call-update
  227.0 0.0 reduce-scatter.5.cloned.1.call-start
  227.0 72.0 %all-gather.2.cloned.1.call-done = bf16[3072,256]{1,0:T(8,128)(2,1)} async-done(((bf16[192,256]{1,0:T(8,128)(2,1)}), bf16[3072,256]{1,0:T(8,128)(2,1)}) %all-gather.2.cloned.1.call-update) | async-done | bytes 1572880 | tf_op jit(solution)/shard_map/all_gather | solution.py:71
  299.0 0.0 copy-done.3
  299.0 3.6 fusion.54
  302.7 0.0 copy-start.1
  302.7 0.0 reduce-scatter.5.cloned.1.call-update
  302.7 1.4 copy-done.1
  304.1 1.3 convolution_convert_fusion
  305.4 212.3 %reduce-scatter.5.cloned.1.call-done = f32[64,256]{1,0:T(8,128)} async-done(((f32[3072,256]{1,0:T(8,128)}), f32[64,256]{1,0:T(8,128)}) %reduce-scatter.5.cloned.1.call-update) | async-done | bytes 65552 | tf_op jit(solution)/shard_map/reduce_scatter | solution.py:81
  517.6 1.5 broadcast_multiply_fusion
  (8 shorter events, 0.1 us)
Async XLA Ops:
  7.2 1.4 copy-start
  7.2 103.5 %reduce-scatter.3.cloned.1.call-start = ((), (), s32[]{:S(2)}) async-start(), calls=%async_computation.7 | async-start | bytes 3342336 | tf_op jit(solution)/shard_map/reduce_scatter | solution.py:83
  11.7 0.7 copy-start.7
  11.7 0.7 copy-start.8
  11.7 99.0 %copy-start.4 = (bf16[192,256]{1,0:T(8,128)(2,1)S(1)}, bf16[192,256]{1,0:T(8,128)(2,1)}, u32[]{:S(2)}) copy-start(bf16[192,256]{1,0:T(8,128)(2,1)} %param.7) | copy-start | bytes 294916
  112.3 35.9 %all-to-all-start.2 = ((bf16[48,4,256]{2,1,0:T(4,128)(2,1)}), bf16[48,4,256]{2,1,0:T(4,128)(2,1)S(1)}, u32[]{:S(2)}, u32[]{:S(2)}) async-start(bf16[48,4,256]{2,1,0:T(4,128)(2,1)} %all_to_all.44), calls=%async_computation.3 | async-start | bytes 196608 | tf_op jit(solution)/shard_map/all_to_all | solution.py:49
  136.2 162.9 %all-gather.2.cloned.1.call-start = ((), (), s32[]{:S(2)}) async-start(), calls=%async_computation.6 | async-start | bytes 1671168 | tf_op jit(solution)/shard_map/all_gather | solution.py:71
  158.0 29.0 %copy-start.5 = (bf16[192,256]{1,0:T(8,128)(2,1)S(1)}, bf16[192,256]{1,0:T(8,128)(2,1)}, u32[]{:S(2)}) copy-start(bf16[192,256]{1,0:T(8,128)(2,1)} %param.8) | copy-start | bytes 294916
  158.0 29.0 %copy-start.6 = (bf16[192,256]{1,0:T(8,128)(2,1)S(1)}, bf16[192,256]{1,0:T(8,128)(2,1)}, u32[]{:S(2)}) copy-start(bf16[192,256]{1,0:T(8,128)(2,1)} %param.9) | copy-start | bytes 294916
  207.8 18.4 %copy-start.2 = (f32[192,256]{1,0:T(8,128)S(1)}, f32[192,256]{1,0:T(8,128)}, u32[]{:S(2)}) copy-start(f32[192,256]{1,0:T(8,128)} %reduce-scatter.3.cloned.1.call-done) | copy-start | bytes 589828
  207.9 91.2 %copy-start.3 = (bf16[256,256]{1,0:T(8,128)(2,1)S(1)}, bf16[256,256]{1,0:T(8,128)(2,1)}, u32[]{:S(2)}) copy-start(bf16[256,256]{1,0:T(8,128)(2,1)} %param.13) | copy-start | bytes 393220
  227.0 290.6 %reduce-scatter.5.cloned.1.call-start = ((), (), s32[]{:S(2)}) async-start(), calls=%async_computation.8 | async-start | bytes 3211264 | tf_op jit(solution)/shard_map/reduce_scatter | solution.py:81
  302.7 1.4 copy-start.1
Sparse Core Ops, SparseCore 0:
  11.9 98.7 reduce-scatter.2
  227.1 71.9 all-gather.1
  304.6 212.9 reduce-scatter.4
where the time goes:
time: 526 us
  waiting for transfers between devices  393 us (75%)
  blocking collectives  51.4 us (10%)
  starting transfers between devices  24 us (5%)
  local copies, waits for them, and re-layouts  21.5 us (4%)
  matrix products  17.7 us (3%)
  between operations  14 us (3%)
    reduce_scatter x1, waiting for transfers between devices, shards(): lax.psum_scatter(grad_total, 'seq', scatter_dimension=0, tiled=True) * scale  212 us
    reduce_scatter x1, waiting for transfers between devices, shards(): lax.psum_scatter(lax.dot_general(weight_piece, out_grad, (((1,), (1,)), (...  97.9 us
    all_gather x1, waiting for transfers between devices, shards(): piece = lax.all_gather(product, 'col', axis=0, tiled=True)  72 us
    all_to_all x2, blocking collectives, filtered_branch(): lax.all_to_all(result.astype(jnp.bfloat16), 'seq', split_axis=1, concat_a...  34.3 us
    all_to_all x1, starting transfers between devices, filtered_branch(): lax.all_to_all(signal, 'seq', split_axis=0, concat_axis=1, tiled=True)  23.8 us
    all_to_all x1, blocking collectives, filtered_branch(): lax.all_to_all(signal, 'seq', split_axis=0, concat_axis=1, tiled=True)  17.1 us
    all_to_all x1, waiting for transfers between devices, filtered_branch(): lax.all_to_all(signal, 'seq', split_axis=0, concat_axis=1, tiled=True)  10.6 us
  transfers between devices with their start and end apart: 4, of which 4 were waited for; matrix products, arithmetic and copies ran while one was open for 1% of the time, Pallas kernels for 0%

commit v1 on v0

v1 whole, which is shorter than its diff:
```python
import math

import jax
import jax.numpy as jnp
from jax import lax
from jax.experimental import pallas as pl
from jax.experimental.pallas import tpu as pltpu
from jax.sharding import Mesh
from jax.sharding import PartitionSpec as P

f32 = jnp.float32
bf16 = jnp.bfloat16
SUB = 32
LANES = 128


def to_columns(tile):
    rows, width = tile.shape
    pad = jnp.zeros((LANES - rows, width), f32)
    return jnp.concatenate([tile, pad], axis=0).T


def scan_kernel(g_ref, r_ref, o_ref, d_ref, c_ref, yf_ref, yb_ref, bs_ref, sf_ref, sb_ref, gt, bt):
    width = g_ref.shape[2]
    for half in range(2):
        at = pl.ds(half * width, width)
        gt[at, :] = to_columns(g_ref[half].astype(f32))
        total = r_ref[0, :, at].astype(f32)
        for i in range(1, r_ref.shape[0]):
            total = total + r_ref[i, :, at].astype(f32)
        bs_ref[half] = total
        bt[at, :] = to_columns((total * o_ref[half].astype(f32)).astype(bf16).astype(f32))
    rate = jnp.exp(-d_ref[...])
    coef = c_ref[...]
    length = gt.shape[0]

    def step(i, carry):
        sf, sb = carry
        lo = pl.multiple_of(i * 8, 8)
        hi = pl.multiple_of(length - 8 - i * 8, 8)
        gs, bs = gt[pl.ds(lo, 8), :], bt[pl.ds(hi, 8), :]
        fs, rs = [], [None] * 8
        for t in range(8):
            sf = sf * rate + gs[t : t + 1, :]
            sb = sb * rate + bs[7 - t : 8 - t, :]
            fs.append(jnp.sum(sf * coef, axis=0, keepdims=True))
            rs[7 - t] = jnp.sum(sb * coef, axis=0, keepdims=True)
        yf_ref[pl.ds(lo, 8), :] = jnp.concatenate(fs, axis=0)
        yb_ref[pl.ds(hi, 8), :] = jnp.concatenate(rs, axis=0)
        return sf, sb

    zero = jnp.zeros_like(coef)
    sf, sb = lax.fori_loop(0, length // 8, step, (zero, zero))
    sf_ref[...] = sf
    sb_ref[...] = sb


def heads_kernel(me_ref, s_ref, d_ref, c_ref, yf_ref, yb_ref, o_ref, bs_ref, p_ref, go_ref, bg_ref, ft, bt):
    me = me_ref[0]
    decay = d_ref[...]
    rate = jnp.exp(-decay)
    coef = c_ref[...]
    length = ft.shape[0]
    chips = s_ref.shape[0]
    width = o_ref.shape[2]
    jump = jnp.exp(-decay * float(length))
    pf = jnp.zeros_like(coef)
    pb = jnp.zeros_like(coef)
    for m in range(chips):
        pf = jnp.where(m < me, pf * jump + s_ref[m], pf)
        back = chips - 1 - m
        pb = jnp.where(back > me, pb * jump + s_ref[back], pb)
    pf = pf * coef
    pb = pb * coef

    def step(i, carry):
        pf, pb = carry
        lo = pl.multiple_of(i * 8, 8)
        hi = pl.multiple_of(length - 8 - i * 8, 8)
        fs, rs = [], [None] * 8
        for t in range(8):
            pf = pf * rate
            pb = pb * rate
            fs.append(jnp.sum(pf, axis=0, keepdims=True))
            rs[7 - t] = jnp.sum(pb, axis=0, keepdims=True)
        ft[pl.ds(lo, 8), :] = yf_ref[pl.ds(lo, 8), :] + jnp.concatenate(fs, axis=0)
        bt[pl.ds(hi, 8), :] = yb_ref[pl.ds(hi, 8), :] + jnp.concatenate(rs, axis=0)
        return pf, pb

    lax.fori_loop(0, length // 8, step, (pf, pb))
    rows = o_ref.shape[1]
    for half in range(2):
        at = pl.ds(half * width, width)
        filtered = ft[at, :].T[:rows].astype(bf16).astype(f32)
        p_ref[:, at] = (o_ref[half].astype(f32) * filtered).astype(bf16)
        go_ref[half] = (bs_ref[half] * filtered).astype(bf16)
        bg_ref[half] = bt[at, :].T[:rows].astype(bf16)


def vmem(count):
    return [pl.BlockSpec(memory_space=pltpu.VMEM)] * count


params = pltpu.CompilerParams(vmem_limit_bytes=32 * 2**20)


def scan_call(gated, parts, outer, decay, coef):
    _, rows, width = gated.shape
    length = 2 * width
    modes = decay.shape[0]
    return pl.pallas_call(
        scan_kernel,
        out_shape=(
            jax.ShapeDtypeStruct((length, LANES), f32),
            jax.ShapeDtypeStruct((length, LANES), f32),
            jax.ShapeDtypeStruct((2, rows, width), f32),
            jax.ShapeDtypeStruct((modes, LANES), f32),
            jax.ShapeDtypeStruct((modes, LANES), f32),
        ),
        in_specs=vmem(5),
        out_specs=tuple(vmem(5)),
        scratch_shapes=[pltpu.VMEM((length, LANES), f32)] * 2,
        compiler_params=params,
        name="scan",
    )(gated, parts, outer, decay, coef)


def heads_call(me, states, decay, coef, yf, yb, outer, back_sum):
    _, rows, width = outer.shape
    length = 2 * width
    return pl.pallas_call(
        heads_kernel,
        out_shape=(
            jax.ShapeDtypeStruct((rows, length), bf16),
            jax.ShapeDtypeStruct((2, rows, width), bf16),
            jax.ShapeDtypeStruct((2, rows, width), bf16),
        ),
        in_specs=[pl.BlockSpec(memory_space=pltpu.SMEM)] + vmem(7),
        out_specs=tuple(vmem(3)),
        scratch_shapes=[pltpu.VMEM((length, LANES), f32)] * 2,
        compiler_params=params,
        name="heads",
    )(me, states, decay, coef, yf, yb, outer, back_sum)


def swap(x, axes):
    return lax.all_to_all(x, axes, 0, 0, tiled=True)


def by_core(x):
    rows, n = x.shape
    return x.reshape(rows // (2 * SUB), 2, SUB, n).swapaxes(0, 1).reshape(2, rows // 2, n)


def from_cores(x):
    _, rows, n = x.shape
    return x.reshape(2, rows // SUB, SUB, n).swapaxes(0, 1).reshape(2 * rows, n)


def shards(outer_gate, inner_gate, value_proj, residues, decays, out_weight, out_grad):
    chan_rows, tok = outer_gate.shape
    half = chan_rows // 2
    cols = out_weight.shape[1]
    core = lax.axis_index("core")
    chip = lax.axis_index(("y", "zh"))
    chips = lax.axis_size(("y", "zh"))
    nx, nz = lax.axis_size("x"), lax.axis_size("zl")
    inner = inner_gate.astype(f32)
    value = value_proj.astype(f32)
    gated = (inner * value).astype(bf16)

    coef = residues * jnp.sqrt(-jnp.expm1(-2.0 * decays))

    def own_modes(x):
        x = lax.dynamic_index_in_dim(by_core(x), core, 0, keepdims=False)
        return jnp.pad(x.T, ((0, 0), (0, LANES - half)))

    decay, coef = own_modes(decays), own_modes(coef)

    sent = jnp.concatenate(
        [jnp.broadcast_to(out_grad[None], (2, tok, cols)), by_core(gated), by_core(outer_gate)], axis=1
    )
    got = swap(sent, "core")
    grads = got[:, :tok].reshape(2 * tok, cols)
    gated = got[:, tok : tok + half]
    outer = got[:, tok + half :]
    weight = lax.dynamic_index_in_dim(
        out_weight.reshape(-1, 2, SUB, cols), core, 1, keepdims=False
    ).reshape(-1, cols)

    back = lax.dot_general(weight, grads, (((1,), (1,)), ((), ())), preferred_element_type=f32)
    back = swap(back.astype(bf16), "x")
    back = jnp.sum(back.reshape(nx, -1, 2 * tok).astype(f32), axis=0).astype(bf16)
    back = swap(back, "zl").reshape(nz, half, 2 * tok)

    yf, yb, back_sum, sf, sb = scan_call(gated, back, outer, decay, coef)
    order = jnp.arange(chips)[:, None, None]
    states = swap(jnp.where(order > chip, sf[None], sb[None]), ("y", "zh"))
    me = jnp.full((1,), chip, jnp.int32)
    product, grad_outer, back_gated = heads_call(me, states, decay, coef, yf, yb, outer, back_sum)

    product = lax.all_gather(product, "zl", axis=0, tiled=True)
    product = swap(jnp.broadcast_to(product[None], (nx,) + product.shape).reshape(-1, 2 * tok), "x")
    mixed = lax.dot_general(product, weight, (((0,), (0,)), ((), ())), preferred_element_type=f32)
    grad_weight = jnp.dot(product, grads, preferred_element_type=f32).astype(bf16)
    grad_weight = swap(grad_weight, ("y", "zh")).reshape(chips, 2 * SUB, cols)
    scale = 1.0 / math.sqrt(2 * tok * chips)
    grad_weight = jnp.sum(grad_weight.astype(f32), axis=0) * scale

    sent = jnp.concatenate(
        [
            mixed.reshape(2, tok, cols),
            back_gated.astype(f32),
            grad_outer.astype(f32),
            grad_weight.reshape(2, SUB, cols),
        ],
        axis=1,
    )
    got = swap(sent, "core")
    mixed = (got[0, :tok] + got[1, :tok]).astype(bf16)
    back_gated = from_cores(got[:, tok : tok + half])
    grad_outer = from_cores(got[:, tok + half : tok + 2 * half]).astype(bf16)
    grad_weight = got[:, tok + 2 * half :].reshape(2 * SUB, cols)
    grad_inner = (back_gated * value).astype(bf16)
    grad_value = (back_gated * inner).astype(bf16)
    return (mixed, grad_outer, grad_inner, grad_value, grad_weight)


def solution(mesh):
    fine = Mesh(mesh.devices.reshape(8, 3, 2, 4, 4), ("y", "zh", "core", "x", "zl"))
    seq, col = ("y", "zh", "core"), ("x", "zl")
    return jax.shard_map(
        shards,
        mesh=fine,
        in_specs=(
            P(col, seq),
            P(col, seq),
            P(col, seq),
            P(col, None),
            P(col, None),
            P(None, col),
            P(seq, col),
        ),
        out_specs=(P(seq, col), P(col, seq), P(col, seq), P(col, seq), P(seq, col)),
        check_vma=False,
    )
```

time: 526 us -> 169 us (0.32)
  waiting for transfers between devices: 393 us -> 23.2 us
  blocking collectives: 51.4 us -> 95.9 us
  between operations: 14 us -> 0.94 us
  local copies, waits for them, and re-layouts: 21.5 us -> 8.66 us
  matrix products: 17.7 us -> 5.23 us
    reduce_scatter x2 -> x0, waiting for transfers between devices: 310 us -> none  [the longest x1 212 us: shards(): lax.psum_scatter(grad_total, 'seq', scatter_dimension=0, tiled=True) * scale]
    all_gather x1 -> x0, waiting for transfers between devices: 72 us -> none  [shards(): piece = lax.all_gather(product, 'col', axis=0, tiled=True)]
    all_to_all x3 -> x4, blocking collectives: 51.4 us -> 83.7 us  [swap(): return lax.all_to_all(x, axes, 0, 0, tiled=True)]
    rev x2 -> x0, local copies, waits for them, and re-layouts: 17 us -> none  [the longest x1 8.62 us: filtered_branch(): result = jnp.flip(result, 1)]
    all_to_all x1 -> x3, waiting for transfers between devices: 10.6 us -> 23.2 us  [swap(): return lax.all_to_all(x, axes, 0, 0, tiled=True)]
    dot_general x12 -> x3, matrix products: 17.7 us -> 5.23 us  [the longest x1 2.41 us: shards(): jnp.dot(product, grads, preferred_element_type=f32).astype(bf16)]
    all_gather x0 -> x1, blocking collectives: none -> 12.2 us  [shards(): product = lax.all_gather(product, 'zl', axis=0, tiled=True)]
    all_to_all x1 -> x3, starting transfers between devices: 23.8 us -> 22.6 us  [swap(): return lax.all_to_all(x, axes, 0, 0, tiled=True)]
  transfers between devices with their start and end apart: 4 -> 3, of which waited for: 4 -> 3; matrix products, arithmetic and copies ran while one was open for 1% -> 4% of each run, Pallas kernels for 0% -> 0%
where the time goes in v1:
time: 169 us; the launch traced here: 168 us
  blocking collectives  95.9 us (57%)
  waiting for transfers between devices  23.2 us (14%)
  starting transfers between devices  22.6 us (13%)
  local copies, waits for them, and re-layouts  8.66 us (5%)
  other arithmetic  6.39 us (4%)
  matrix products  5.23 us (3%)
  Pallas kernels  4.94 us (3%)
    all_to_all x4, blocking collectives, swap(): return lax.all_to_all(x, axes, 0, 0, tiled=True)  83.7 us
    all_to_all x3, waiting for transfers between devices, swap(): return lax.all_to_all(x, axes, 0, 0, tiled=True)  23.2 us
    all_to_all x3, starting transfers between devices, swap(): return lax.all_to_all(x, axes, 0, 0, tiled=True)  22.6 us
    all_gather x1, blocking collectives, shards(): product = lax.all_gather(product, 'zl', axis=0, tiled=True)  12.2 us
  transfers between devices with their start and end apart: 3, of which 3 were waited for; matrix products, arithmetic and copies ran while one was open for 4% of the time, Pallas kernels for 0%

profile of v1, /device:TPU:1, one launch (start us, length us, event | category | flops | bytes accessed | tf_op | source)
XLA Modules:
  0.0 167.8 jit_solution(9059001287873808981)
XLA Ops:
  0.6 0.0 copy-start
  0.6 1.0 copy.37
  1.7 1.0 fusion.2
  2.6 0.9 broadcast_in_dim.44
  3.6 0.8 pad_maximum_fusion.1
  4.4 14.0 %all-to-all-start = ((bf16[2,448,256]{2,1,0:T(8,128)(2,1)}), bf16[2,448,256]{2,1,0:T(8,128)(2,1)S(1)}, u32[]{:S(2)}, u32[]{:S(2)}) async-start(bf16[2,448,256]{2,1,0:T(8,128)(2,1)} %pad_maximum_fusion.1), calls=%async_computation | async-start | bytes 917504 | tf_op jit(solution)/shard_map/all_to_all | solution.py:147
  18.4 0.0 copy-done
  18.4 0.1 constant_dynamic-slice_fusion
  18.4 0.0 copy-start.1
  18.4 1.2 all-to-all-done
  19.7 0.0 copy-start.3
  19.7 0.0 copy-start.2
  19.7 0.6 convolution_convert_fusion
  20.3 0.0 copy-done.1
  20.3 0.1 copy-done.3
  20.5 0.1 copy-done.2
  20.6 22.9 %all_to_all.51 = bf16[4,384,512]{2,1,0:T(8,128)(2,1)S(1)} all-to-all(bf16[4,384,512]{2,1,0:T(8,128)(2,1)S(1)} %bitcast.71), channel_id=1, replica_groups=mesh['y'=8,'zh'=3,'core'=2,'x'=4,'zl'=4] {'x'}, dimensions={0} | all-to-all | bytes 3145728 | tf_op jit(solution)/shard_map/all_to_all | solution.py:147
  43.5 0.0 copy-start.7
  43.5 0.0 copy-start.8
  43.5 1.1 reduce_sum.21
  44.5 3.5 %all-to-all-start.2 = ((bf16[4,96,512]{2,1,0:T(8,128)(2,1)}), bf16[4,96,512]{2,1,0:T(8,128)(2,1)S(1)}, u32[]{:S(2)}, u32[]{:S(2)}) async-start(bf16[4,96,512]{2,1,0:T(8,128)(2,1)} %bitcast.11), calls=%async_computation.2 | async-start | bytes 786432 | tf_op jit(solution)/shard_map/all_to_all | solution.py:147
  48.0 0.0 copy-done.7
  48.0 0.1 reshape.97
  48.1 0.0 copy-done.8
  48.2 0.1 reshape.99
  48.3 0.1 reshape.100
  48.4 0.1 reshape.98
  48.5 1.0 fusion.5
  49.5 8.3 %all-to-all-done.2.r_ref = bf16[4,96,512]{2,1,0:T(8,128)(2,1)S(1)} async-done(((bf16[4,96,512]{2,1,0:T(8,128)(2,1)}), bf16[4,96,512]{2,1,0:T(8,128)(2,1)S(1)}, u32[]{:S(2)}, u32[]{:S(2)}) %all-to-all-start.2) | async-done | bytes 393248 | tf_op jit(solution)/shard_map/all_to_all | solution.py:147
  57.8 2.8 %scan.1 = (f32[512,128]{1,0:T(8,128)S(1)}, f32[512,128]{1,0:T(8,128)S(1)}, f32[2,96,256]{2,1,0:T(8,128)S(1)}, f32[16,128]{1,0:T(8,128)S(1)}, f32[16,128]{1,0:T(8,128)S(1)}) custom-call(bf16[2,96,256]{2,1,0:T(8,128)(2,1)S(1)} %get-tuple-element.22.g_ref, bf16[4,96,512]{2,1,0:T(8,128)(2,1)S(1)} %all-to-all-done.2.r_ref, ...), custom_call_target="tpu_custom_call" | custom-call | tf_op jit(solution)/shard_map/scan/pallas_call | solution.py:111
  60.6 0.1 broadcast_select_fusion
  60.7 23.6 %all_to_all.52.s_ref = f32[24,16,128]{2,1,0:T(8,128)S(1)} all-to-all(f32[24,16,128]{2,1,0:T(8,128)S(1)} %broadcast_select_fusion), channel_id=1, replica_groups=mesh['y'=8,'zh'=3,'core'=2,'x'=4,'zl'=4] {'y','zh'}, dimensions={0} | all-to-all | bytes 393216 | tf_op jit(solution)/shard_map/all_to_all | solution.py:147
  84.3 2.1 %heads.1 = (bf16[96,512]{1,0:T(8,128)(2,1)S(1)}, bf16[2,96,256]{2,1,0:T(8,128)(2,1)S(1)}, bf16[2,96,256]{2,1,0:T(8,128)(2,1)S(1)}) custom-call(s32[1]{0:T(128)} %bitcast.me_ref, f32[24,16,128]{2,1,0:T(8,128)S(1)} %all_to_all.52.s_ref, f32[16,128]{1,0:T(8,128)S(1)} %pad.7.d_ref, f32[16,128]{1,0:T(8,128)S(1)} %pad.8.c_ref, ...), custom_call_target="tpu_custom_call" | custom-call | tf_op jit(solution)/shard_map/heads/pallas_call | solution.py:131
  86.5 12.2 %all_gather.3 = bf16[384,512]{1,0:T(8,128)(2,1)S(1)} all-gather(bf16[96,512]{1,0:T(8,128)(2,1)S(1)} %get-tuple-element.18), channel_id=1, replica_groups=mesh['y'=8,'zh'=3,'core'=2,'x'=4,'zl'=4] {'zl'}, dimensions={0}, use_global_device_ids=true | all-gather | bytes 491520 | tf_op jit(solution)/shard_map/all_gather | solution.py:202
  98.7 0.2 copy.41
  98.9 0.1 broadcast_in_dim.47
  99.1 15.7 %all_to_all.53 = bf16[4,384,512]{1,2,0:T(8,128)(2,1)} all-to-all(bf16[4,384,512]{1,2,0:T(8,128)(2,1)S(1)} %broadcast_in_dim.47), channel_id=1, replica_groups=mesh['y'=8,'zh'=3,'core'=2,'x'=4,'zl'=4] {'x'}, dimensions={0} | all-to-all | bytes 3145728 | tf_op jit(solution)/shard_map/all_to_all | solution.py:147
  114.8 1.7 %copy.42 = bf16[4,384,512]{2,1,0:T(8,128)(2,1)S(1)} copy(bf16[4,384,512]{1,2,0:T(8,128)(2,1)} %all_to_all.53) | data formatting | bytes 3145728 | tf_op jit(solution)/shard_map/all_to_all | solution.py:147
  116.5 2.4 %convolution_convert_fusion.1 = bf16[1536,256]{1,0:T(8,128)(2,1)} fusion(bf16[1536,512]{1,0:T(8,128)(2,1)S(1)} %bitcast.67, bf16[512,256]{1,0:T(8,128)(2,1)} %bitcast.75), kind=kOutput, calls=%fused_computation.1 | convolution fusion | flops 403046400 | bytes 2621440 | tf_op jit(solution)/shard_map/dot_general | solution.py:205
  118.9 5.1 %all-to-all-start.5 = ((bf16[24,64,256]{2,1,0:T(8,128)(2,1)}), bf16[24,64,256]{2,1,0:T(8,128)(2,1)}, u32[]{:S(2)}, u32[]{:S(2)}) async-start(bf16[24,64,256]{2,1,0:T(8,128)(2,1)} %bitcast.73), calls=%async_computation.5 | async-start | bytes 1572864 | tf_op jit(solution)/shard_map/all_to_all | solution.py:147
  124.1 0.7 convert_element_type.55
  124.8 1.6 copy.43
  126.4 0.0 copy-start.4
  126.4 2.2 %fusion.6 = f32[2,256,256]{2,1,0:T(8,128)S(1)} fusion(bf16[2,256,1536]{2,1,0:T(8,128)(2,1)} %bitcast.72, bf16[1536,256,1]{1,0,2:T(8,128)(2,1)} %bitcast.70), kind=kOutput, calls=%fused_computation.25 | convolution fusion | flops 402653184 | bytes 2883584 | tf_op jit(solution)/shard_map/dot_general | solution.py:204
  128.6 13.7 %all-to-all-done.5 = bf16[24,64,256]{2,1,0:T(8,128)(2,1)} async-done(((bf16[24,64,256]{2,1,0:T(8,128)(2,1)}), bf16[24,64,256]{2,1,0:T(8,128)(2,1)}, u32[]{:S(2)}, u32[]{:S(2)}) %all-to-all-start.5) | async-done | bytes 786464 | tf_op jit(solution)/shard_map/all_to_all | solution.py:147
  142.3 1.3 convert_reduce_fusion
  143.6 0.0 copy-done.4
  143.6 0.1 pad_maximum_fusion
  143.7 0.0 copy-start.5
  143.7 0.0 copy-start.6
  143.7 21.4 %all_to_all.54 = f32[2,480,256]{2,1,0:T(8,128)S(1)} all-to-all(f32[2,480,256]{2,1,0:T(8,128)S(1)} %pad_maximum_fusion), channel_id=1, replica_groups=mesh['y'=8,'zh'=3,'core'=2,'x'=4,'zl'=4] {'core'}, dimensions={0} | all-to-all | bytes 1966080 | tf_op jit(solution)/shard_map/all_to_all | solution.py:147
  165.1 0.6 copy.44
  165.8 0.0 copy-done.5
  165.8 0.0 copy-done.6
  165.8 0.7 fusion.1
  166.5 0.7 fusion.4
  167.2 0.6 slice.40
  (14 shorter events, 0.2 us)
Async XLA Ops:
  0.6 17.7 %copy-start = (bf16[3072,256]{1,0:T(8,128)(2,1)S(1)}, bf16[3072,256]{1,0:T(8,128)(2,1)}, u32[]{:S(2)}) copy-start(bf16[3072,256]{1,0:T(8,128)(2,1)} %param.12) | copy-start | bytes 4718596
  4.4 15.3 %all-to-all-start = ((bf16[2,448,256]{2,1,0:T(8,128)(2,1)}), bf16[2,448,256]{2,1,0:T(8,128)(2,1)S(1)}, u32[]{:S(2)}, u32[]{:S(2)}) async-start(bf16[2,448,256]{2,1,0:T(8,128)(2,1)} %pad_maximum_fusion.1), calls=%async_computation | async-start | bytes 917504 | tf_op jit(solution)/shard_map/all_to_all | solution.py:147
  18.4 1.9 %copy-start.1 = (bf16[48,1,32,256]{3,2,1,0:T(8,128)(2,1)}, bf16[48,1,32,256]{3,2,1,0:T(8,128)(2,1)S(1)}, u32[]{:S(2)}) copy-start(bf16[48,1,32,256]{3,2,1,0:T(8,128)(2,1)S(1)} %constant_dynamic-slice_fusion) | copy-start | bytes 2359300
  19.7 0.8 copy-start.3
  19.7 0.8 copy-start.2
  43.5 4.6 %copy-start.7 = (f32[192,16]{0,1:T(8,128)S(1)}, f32[192,16]{0,1:T(8,128)}, u32[]{:S(2)}) copy-start(f32[192,16]{0,1:T(8,128)} %param.11) | copy-start | bytes 36868
  43.5 4.7 %copy-start.8 = (f32[192,16]{0,1:T(8,128)S(1)}, f32[192,16]{0,1:T(8,128)}, u32[]{:S(2)}) copy-start(f32[192,16]{0,1:T(8,128)} %param.10) | copy-start | bytes 36868
  44.5 13.3 %all-to-all-start.2 = ((bf16[4,96,512]{2,1,0:T(8,128)(2,1)}), bf16[4,96,512]{2,1,0:T(8,128)(2,1)S(1)}, u32[]{:S(2)}, u32[]{:S(2)}) async-start(bf16[4,96,512]{2,1,0:T(8,128)(2,1)} %bitcast.11), calls=%async_computation.2 | async-start | bytes 786432 | tf_op jit(solution)/shard_map/all_to_all | solution.py:147
  118.9 23.4 %all-to-all-start.5 = ((bf16[24,64,256]{2,1,0:T(8,128)(2,1)}), bf16[24,64,256]{2,1,0:T(8,128)(2,1)}, u32[]{:S(2)}, u32[]{:S(2)}) async-start(bf16[24,64,256]{2,1,0:T(8,128)(2,1)} %bitcast.73), calls=%async_computation.5 | async-start | bytes 1572864 | tf_op jit(solution)/shard_map/all_to_all | solution.py:147
  126.4 17.1 %copy-start.4 = (f32[2,96,256]{2,1,0:T(8,128)S(1)}, f32[2,96,256]{2,1,0:T(8,128)}, u32[]{:S(2)}) copy-start(f32[2,96,256]{2,1,0:T(8,128)} %convert_element_type.55) | copy-start | bytes 589828
  143.7 22.1 %copy-start.5 = (bf16[192,256]{1,0:T(8,128)(2,1)S(1)}, bf16[192,256]{1,0:T(8,128)(2,1)}, u32[]{:S(2)}) copy-start(bf16[192,256]{1,0:T(8,128)(2,1)} %param.9) | copy-start | bytes 294916
  143.7 22.1 %copy-start.6 = (bf16[192,256]{1,0:T(8,128)(2,1)S(1)}, bf16[192,256]{1,0:T(8,128)(2,1)}, u32[]{:S(2)}) copy-start(bf16[192,256]{1,0:T(8,128)(2,1)} %param.8) | copy-start | bytes 294916

commit v2 on v0

v2 whole, which is shorter than its diff:
```python
import math

import jax
import jax.numpy as jnp
from jax import lax
from jax.experimental import pallas as pl
from jax.experimental.pallas import tpu as pltpu
from jax.sharding import Mesh
from jax.sharding import PartitionSpec as P

f32 = jnp.float32
bf16 = jnp.bfloat16
SUB = 32
LANES = 128
CORE, X, CHIP = 0, 1, 2


def to_columns(tile):
    rows, width = tile.shape
    pad = jnp.zeros((LANES - rows, width), f32)
    return jnp.concatenate([tile, pad], axis=0).T


def pack_kernel(i_ref, v_ref, o_ref, g_ref, sent_ref):
    tok = g_ref.shape[0]
    rows = i_ref.shape[0]
    for h in range(2):
        sent_ref[h, :tok] = g_ref[...]
        for b in range(rows // (2 * SUB)):
            src = pl.ds(2 * SUB * b + SUB * h, SUB)
            gated = (i_ref[src, :].astype(f32) * v_ref[src, :].astype(f32)).astype(bf16)
            sent_ref[h, pl.ds(tok + SUB * b, SUB)] = gated
            sent_ref[h, pl.ds(tok + rows // 2 + SUB * b, SUB)] = o_ref[src, :]


def modes_kernel(at_ref, d_ref, c_ref, od_ref, oc_ref):
    chan = lax.broadcasted_iota(jnp.int32, (d_ref.shape[1], LANES), 0)
    lane = lax.broadcasted_iota(jnp.int32, (d_ref.shape[1], LANES), 1)
    wanted = lane + SUB * (lane // SUB) + SUB * at_ref[CORE]
    pick = jnp.where((chan == wanted) & (lane < d_ref.shape[1] // 2), 1.0, 0.0).astype(f32)
    for src, dst in ((d_ref, od_ref), (c_ref, oc_ref)):
        dst[...] = jnp.dot(
            src[...], pick, precision=lax.Precision.HIGHEST, preferred_element_type=f32
        )


def back_kernel(at_ref, w_ref, got_ref, own_ref, *sent_refs):
    tok = got_ref.shape[2]
    n = 1 + len(sent_refs)
    rows = w_ref.shape[0] // n
    for k, ref in enumerate((own_ref,) + sent_refs):
        block = lax.rem(at_ref[X] + k, n)
        w = w_ref[pl.ds(pl.multiple_of(block * rows, rows), rows), :]
        for h in range(2):
            part = lax.dot_general(
                w, got_ref[h, :tok], (((1,), (1,)), ((), ())), preferred_element_type=f32
            )
            ref[:, pl.ds(h * tok, tok)] = part.astype(ref.dtype)


def scan(src, y_ref, rate, coef, reverse):
    length = src.shape[0]

    def step(i, state):
        lo = length - 8 - i * 8 if reverse else i * 8
        at = pl.ds(pl.multiple_of(lo, 8), 8)
        block = src[at, :]
        rows = [None] * 8
        for t in range(8):
            u = 7 - t if reverse else t
            state = state * rate + block[u : u + 1, :]
            rows[u] = jnp.sum(state * coef, axis=0, keepdims=True)
        y_ref[at, :] = jnp.concatenate(rows, axis=0)
        return state

    return lax.fori_loop(0, length // 8, step, jnp.zeros_like(coef))


def heads(y_ref, out, state, rate, reverse):
    length = y_ref.shape[0]

    def step(i, state):
        lo = length - 8 - i * 8 if reverse else i * 8
        at = pl.ds(pl.multiple_of(lo, 8), 8)
        rows = [None] * 8
        for t in range(8):
            u = 7 - t if reverse else t
            state = state * rate
            rows[u] = jnp.sum(state, axis=0, keepdims=True)
        out[at, :] = y_ref[at, :] + jnp.concatenate(rows, axis=0)
        return state

    lax.fori_loop(0, length // 8, step, state)


def scan_forward_kernel(got_ref, d_ref, c_ref, y_ref, s_ref, gt):
    tok = got_ref.shape[2]
    half = (got_ref.shape[1] - tok) // 2
    for h in range(2):
        gt[pl.ds(h * tok, tok), :] = to_columns(got_ref[h, tok : tok + half].astype(f32))
    state = scan(gt, y_ref, jnp.exp(-d_ref[...]), c_ref[...], False)
    for m in range(s_ref.shape[0]):
        s_ref[m] = state


def meet_kernel(at_ref, s_ref, d_ref, c_ref, y_ref, got_ref, own_ref, r1, r2, r3, sent_ref, f_ref, ft):
    tok = got_ref.shape[2]
    nz, twice, length = sent_ref.shape
    half = twice // 2
    decay = d_ref[...]
    jump = jnp.exp(-decay * float(length))
    state = jnp.zeros_like(decay)
    for m in range(s_ref.shape[0]):
        state = jnp.where(m < at_ref[CHIP], state * jump + s_ref[m], state)
    heads(y_ref, ft, state * c_ref[...], jnp.exp(-decay), False)
    for h in range(2):
        at = pl.ds(h * tok, tok)
        filtered = ft[at, :].T[:half].astype(bf16)
        f_ref[h] = filtered
        product = (got_ref[h, tok + half :].astype(f32) * filtered.astype(f32)).astype(bf16)
        for q in range(nz):
            sent_ref[q, half:, at] = product
    for q in range(nz):
        rows = pl.ds(q * half, half)
        total = own_ref[rows, :]
        for ref in (r1, r2, r3):
            total = total + ref[rows, :].astype(f32)
        sent_ref[q, :half, :] = total.astype(bf16)


def scan_backward_kernel(z_ref, got_ref, d_ref, c_ref, y_ref, s_ref, b_ref, bt):
    tok = got_ref.shape[2]
    half = z_ref.shape[1] // 2
    for h in range(2):
        at = pl.ds(h * tok, tok)
        total = z_ref[0, :half, at].astype(f32)
        for q in range(1, z_ref.shape[0]):
            total = total + z_ref[q, :half, at].astype(f32)
        b_ref[h] = total
        outer = got_ref[h, tok + half :].astype(f32)
        bt[at, :] = to_columns((total * outer).astype(bf16).astype(f32))
    state = scan(bt, y_ref, jnp.exp(-d_ref[...]), c_ref[...], True)
    for m in range(s_ref.shape[0]):
        s_ref[m] = state


def weight_kernel(at_ref, p0, p1, p2, p3, got_ref, out_ref):
    tok = got_ref.shape[2]
    rows = p0.shape[0]
    grads = got_ref[:, :tok, :].reshape(2 * tok, -1)
    for k, piece in enumerate((p0, p1, p2, p3)):
        block = lax.rem(at_ref[X] + 4 - k, 4)
        at = pl.ds(pl.multiple_of(block * rows, rows), rows)
        out_ref[at, :] = jnp.dot(piece[...], grads, preferred_element_type=f32).astype(bf16)


def mixed_kernel(at_ref, p0, p1, p2, p3, w_ref, own_ref, other_ref, total):
    rows = p0.shape[0]
    tok = own_ref.shape[1]
    for k, piece in enumerate((p0, p1, p2, p3)):
        block = lax.rem(at_ref[X] + 4 - k, 4)
        w = w_ref[pl.ds(pl.multiple_of(block * rows, rows), rows), :]
        part = lax.dot_general(w, piece[...], (((0,), (0,)), ((), ())), preferred_element_type=f32)
        if k == 0:
            total[...] = part
        else:
            total[...] += part
    core = at_ref[CORE]
    own_ref[...] = total[:, pl.ds(pl.multiple_of(core * tok, tok), tok)]
    other_ref[...] = total[:, pl.ds(pl.multiple_of((1 - core) * tok, tok), tok)]


def heads_backward_kernel(at_ref, s_ref, d_ref, c_ref, y_ref, f_ref, b_ref, own_ref, other_ref, bt):
    half, tok = f_ref.shape[1:]
    decay = d_ref[...]
    jump = jnp.exp(-decay * float(2 * tok))
    state = jnp.zeros_like(decay)
    for m in range(s_ref.shape[0] - 1, -1, -1):
        state = jnp.where(m > at_ref[CHIP], state * jump + s_ref[m], state)
    heads(y_ref, bt, state * c_ref[...], jnp.exp(-decay), True)
    core = at_ref[CORE]
    for h, ref in ((core, own_ref), (1 - core, other_ref)):
        at = pl.ds(pl.multiple_of(h * tok, tok), tok)
        ref[:half] = bt[at, :].T[:half].astype(bf16)
        ref[half:] = (b_ref[h] * f_ref[h].astype(f32)).astype(bf16)


def finish_kernel(at_ref, m_ref, mr_ref, g_ref, gr_ref, i_ref, v_ref, mixed_ref, go_ref, gi_ref, gv_ref):
    mixed_ref[...] = (m_ref[...] + mr_ref[...]).T.astype(bf16)
    half = g_ref.shape[0] // 2
    core = at_ref[CORE]
    for h, ref in ((core, g_ref), (1 - core, gr_ref)):
        for b in range(half // SUB):
            at = pl.ds(pl.multiple_of(2 * SUB * b + SUB * h, SUB), SUB)
            back = ref[pl.ds(SUB * b, SUB), :].astype(f32)
            go_ref[at, :] = ref[pl.ds(half + SUB * b, SUB), :]
            gi_ref[at, :] = (back * v_ref[at, :].astype(f32)).astype(bf16)
            gv_ref[at, :] = (back * i_ref[at, :].astype(f32)).astype(bf16)


def total_kernel(scale, at_ref, p_ref, own_ref, other_ref):
    core = at_ref[CORE]
    for h, ref in ((core, own_ref), (1 - core, other_ref)):
        at = pl.ds(pl.multiple_of(h * SUB, SUB), SUB)
        total = p_ref[0, at, :].astype(f32)
        for m in range(1, p_ref.shape[0]):
            total = total + p_ref[m, at, :].astype(f32)
        ref[...] = total * scale


def join_kernel(at_ref, own_ref, other_ref, out_ref):
    core = at_ref[CORE]
    for h, ref in ((core, own_ref), (1 - core, other_ref)):
        out_ref[pl.ds(pl.multiple_of(h * SUB, SUB), SUB), :] = ref[...]


def whole(shape):
    return pl.BlockSpec(shape, lambda i: (0,) * len(shape))


def call(kernel, name, outs, args, scratch=(), indexed=True):
    specs = [whole(arg.shape) for arg in args]
    if indexed:
        specs[0] = pl.BlockSpec(memory_space=pltpu.SMEM)
    return pl.pallas_call(
        kernel,
        grid=(1,),
        out_shape=tuple(jax.ShapeDtypeStruct(s, t) for s, t in outs),
        in_specs=specs,
        out_specs=tuple(whole(s) for s, _ in outs),
        scratch_shapes=[pltpu.VMEM(s, f32) for s in scratch],
        compiler_params=pltpu.CompilerParams(vmem_limit_bytes=24 * 2**20),
        name=name,
    )(*args)


def swap(x, axes):
    return lax.all_to_all(x, axes, 0, 0, tiled=True)


def shift(x, axis, k):
    n = lax.axis_size(axis)
    return lax.ppermute(x, axis, [(i, (i + k) % n) for i in range(n)])


def shards(outer_gate, inner_gate, value_proj, residues, decays, out_weight, out_grad):
    chan, tok = outer_gate.shape
    half = chan // 2
    length = 2 * tok
    cols = out_weight.shape[1]
    modes = decays.shape[1]
    core = lax.axis_index("core")
    chips = lax.axis_size(("y", "zh"))
    nx, nz = lax.axis_size("x"), lax.axis_size("zl")
    at = jnp.stack([core, lax.axis_index("x"), lax.axis_index(("y", "zh"))]).astype(jnp.int32)

    (sent,) = call(
        pack_kernel,
        "pack",
        [((2, tok + chan, cols), bf16)],
        (inner_gate, value_proj, outer_gate, out_grad),
        indexed=False,
    )
    got = swap(sent, "core")

    coef = residues * jnp.sqrt(-jnp.expm1(-2.0 * decays))
    small = ((modes, LANES), f32)
    decay, coef = call(modes_kernel, "modes", [small, small], (at, decays.T, coef.T))
    weight = lax.dynamic_index_in_dim(
        out_weight.reshape(-1, 2, SUB, cols), core, 1, keepdims=False
    ).reshape(-1, cols)

    rows = nz * half
    own, *parts = call(
        back_kernel,
        "back",
        [((rows, length), f32)] + [((rows, length), bf16)] * (nx - 1),
        (at, weight, got),
    )
    parts = [shift(part, "x", k + 1) for k, part in enumerate(parts)]
    columns = ((length, LANES), f32)
    states = ((chips, modes, LANES), f32)
    y, s = call(
        scan_forward_kernel,
        "scan_forward",
        [columns, states],
        (got, decay, coef),
        scratch=[(length, LANES)],
        indexed=False,
    )
    s = swap(s, ("y", "zh"))
    sent, filtered = call(
        meet_kernel,
        "meet",
        [((nz, chan, length), bf16), ((2, half, tok), bf16)],
        (at, s, decay, coef, y, got, own, *parts),
        scratch=[(length, LANES)],
    )
    both = swap(sent, "zl")

    piece = both[:, half:].reshape(rows, length)
    pieces = [piece] + [shift(piece, "x", k) for k in range(1, nx)]
    y, s, back_sum = call(
        scan_backward_kernel,
        "scan_backward",
        [columns, states, ((2, half, tok), f32)],
        (both, got, decay, coef),
        scratch=[(length, LANES)],
        indexed=False,
    )
    s = swap(s, ("y", "zh"))

    (partial,) = call(
        weight_kernel, "weight", [((nx * rows, cols), bf16)], (at, *pieces, got)
    )
    partial = swap(partial, ("y", "zh")).reshape(chips, 2 * SUB, cols)

    grads, grads_other = call(
        heads_backward_kernel,
        "heads_backward",
        [((chan, tok), bf16)] * 2,
        (at, s, decay, coef, y, filtered, back_sum),
        scratch=[(length, LANES)],
    )
    mixed, mixed_other = call(
        mixed_kernel,
        "mixed",
        [((cols, tok), f32)] * 2,
        (at, *pieces, weight),
        scratch=[(cols, length)],
    )
    mixed, grad_outer, grad_inner, grad_value = call(
        finish_kernel,
        "finish",
        [((tok, cols), bf16)] + [((chan, tok), bf16)] * 3,
        (
            at,
            mixed,
            shift(mixed_other, "core", 1),
            grads,
            shift(grads_other, "core", 1),
            inner_gate,
            value_proj,
        ),
    )

    scale = 1.0 / math.sqrt(length * chips)
    own, other = call(
        lambda *refs: total_kernel(scale, *refs),
        "total",
        [((SUB, cols), f32)] * 2,
        (at, partial),
    )
    (grad_weight,) = call(
        join_kernel, "join", [((2 * SUB, cols), f32)], (at, own, shift(other, "core", 1))
    )
    return (mixed, grad_outer, grad_inner, grad_value, grad_weight)


def solution(mesh):
    fine = Mesh(mesh.devices.reshape(8, 3, 2, 4, 4), ("y", "zh", "core", "x", "zl"))
    seq, col = ("y", "zh", "core"), ("x", "zl")
    return jax.shard_map(
        shards,
        mesh=fine,
        in_specs=(
            P(col, seq),
            P(col, seq),
            P(col, seq),
            P(col, None),
            P(col, None),
            P(None, col),
            P(seq, col),
        ),
        out_specs=(P(seq, col), P(col, seq), P(col, seq), P(col, seq), P(seq, col)),
        check_vma=False,
    )
```

time: 526 us -> 193 us (0.37)
  waiting for transfers between devices: 393 us -> 51.7 us
  starting transfers between devices: 24 us -> 76.5 us
  blocking collectives: 51.4 us -> 23.3 us
  Pallas kernels: 0 us -> 19.4 us
  matrix products: 17.7 us -> 0 us
  between operations: 14 us -> 0.95 us
    reduce_scatter x2 -> x0, waiting for transfers between devices: 310 us -> none  [the longest x1 212 us: shards(): lax.psum_scatter(grad_total, 'seq', scatter_dimension=0, tiled=True) * scale]
    all_gather x1 -> x0, waiting for transfers between devices: 72 us -> none  [shards(): piece = lax.all_gather(product, 'col', axis=0, tiled=True)]
    ppermute x0 -> x9, waiting for transfers between devices: none -> 30.2 us  [shift(): return lax.ppermute(x, axis, [(i, (i + k) % n) for i in range(n)])]
    ppermute x0 -> x9, starting transfers between devices: none -> 29.3 us  [shift(): return lax.ppermute(x, axis, [(i, (i + k) % n) for i in range(n)])]
    all_to_all x3 -> x1, blocking collectives: 51.4 us -> 23.3 us  [swap(): return lax.all_to_all(x, axes, 0, 0, tiled=True)]
    all_to_all x1 -> x4, starting transfers between devices: 23.8 us -> 47.2 us  [swap(): return lax.all_to_all(x, axes, 0, 0, tiled=True)]
    pallas_call x0 -> x12, Pallas kernels: none -> 19.4 us  [call(): pl.pallas_call(kernel, grid=(1,), out_shape=tuple((jax.ShapeDtypeStruct(s...]
    dot_general x12 -> x0, matrix products: 17.7 us -> none  [the longest x2 5.28 us: modal_filter(): states = jnp.einsum('cknm,cmk->cnk', carried, sums, precision=highest)]
  transfers between devices with their start and end apart: 4 -> 13, of which waited for: 4 -> 8; matrix products, arithmetic and copies ran while one was open for 1% -> 1% of each run, Pallas kernels for 0% -> 5%
where the time goes in v2:
time: 193 us; the launch traced here: 192 us
  starting transfers between devices  76.5 us (40%)
  waiting for transfers between devices  51.7 us (27%)
  blocking collectives  23.3 us (12%)
  local copies, waits for them, and re-layouts  20.4 us (11%)
  Pallas kernels  19.4 us (10%)
    all_to_all x4, starting transfers between devices, swap(): return lax.all_to_all(x, axes, 0, 0, tiled=True)  47.2 us
    ppermute x9, waiting for transfers between devices, shift(): return lax.ppermute(x, axis, [(i, (i + k) % n) for i in range(n)])  30.2 us
    ppermute x9, starting transfers between devices, shift(): return lax.ppermute(x, axis, [(i, (i + k) % n) for i in range(n)])  29.3 us
    all_to_all x1, blocking collectives, swap(): return lax.all_to_all(x, axes, 0, 0, tiled=True)  23.3 us
    all_to_all x4, waiting for transfers between devices, swap(): return lax.all_to_all(x, axes, 0, 0, tiled=True)  21.4 us
    pallas_call x12, Pallas kernels, call(): pl.pallas_call(kernel, grid=(1,), out_shape=tuple((jax.ShapeDtypeStruct(s...  19.4 us
    unnamed x66, local copies, waits for them, and re-layouts  19.3 us
  transfers between devices with their start and end apart: 13, of which 8 were waited for; matrix products, arithmetic and copies ran while one was open for 1% of the time, Pallas kernels for 5%

profile of v2, /device:TPU:1, one launch (start us, length us, event | category | flops | bytes accessed | tf_op | source)
XLA Modules:
  0.0 192.3 jit_solution(6936094629200012779)
XLA Ops:
  0.6 0.0 copy-start
  0.6 0.0 copy-start.15
  0.7 1.0 copy-done.15
  1.7 0.9 copy-done.17
  2.6 0.9 copy-done.27
  3.5 0.9 copy-done.28
  4.4 0.8 pack.1
  5.2 14.0 %all-to-all-start = ((bf16[2,448,256]{2,1,0:T(8,128)(2,1)}), bf16[2,448,256]{2,1,0:T(8,128)(2,1)S(1)}, u32[]{:S(2)}, u32[]{:S(2)}) async-start(bf16[2,448,256]{2,1,0:T(8,128)(2,1)} %pack.1), calls=%async_computation | async-start | bytes 917504 | tf_op jit(solution)/shard_map/all_to_all | solution.py:238
  19.2 0.1 pad_add_fusion.at_ref.refs_0_
  19.3 0.8 modes.1
  20.1 0.4 all-to-all-done.got_ref
  20.5 2.7 %scan_forward.1 = (f32[512,128]{1,0:T(8,128)S(1)}, f32[24,16,128]{2,1,0:T(8,128)}) custom-call(bf16[2,448,256]{2,1,0:T(8,128)(2,1)S(1)} %all-to-all-done.got_ref, f32[16,128]{1,0:T(8,128)S(1)} %get-tuple-element.28.d_ref, f32[16,128]{1,0:T(8,128)S(1)} %get-tuple-element.29.c_ref), custom_call_target="tpu_custom_call" | custom-call | tf_op jit(solution)/shard_map/scan_forward/pallas_call | solution.py:225
  23.1 0.7 copy-done.19
  23.9 10.1 %all-to-all-start.1 = ((f32[24,16,128]{2,1,0:T(8,128)}), f32[24,16,128]{2,1,0:T(8,128)S(1)}, u32[]{:S(2)}, u32[]{:S(2)}) async-start(f32[24,16,128]{2,1,0:T(8,128)} %get-tuple-element.30), calls=%async_computation.1 | async-start | bytes 393216 | tf_op jit(solution)/shard_map/all_to_all | solution.py:238
  34.0 0.1 constant_dynamic-slice_fusion
  34.1 1.1 back.1
  35.3 0.9 copy-done.9
  36.2 3.1 %collective-permute-start = (bf16[384,512]{1,0:T(8,128)(2,1)S(1)}, bf16[384,512]{1,0:T(8,128)(2,1)S(1)}, u32[]{:S(2)}, u32[]{:S(2)}) collective-permute-start(bf16[384,512]{1,0:T(8,128)(2,1)S(1)} %get-tuple-element.33), channel_id=1, source_target_pairs={{0,4},{4,8},{8,12},{12,0},{1,5},{5,9},{9,13},{13,1},{2,6},{6,10},{... | collective-permute-start | bytes 1179656 | tf_op jit(solution)/shard_map/ppermute | solution.py:243
  39.3 4.4 %collective-permute-start.1 = (bf16[384,512]{1,0:T(8,128)(2,1)S(1)}, bf16[384,512]{1,0:T(8,128)(2,1)S(1)}, u32[]{:S(2)}, u32[]{:S(2)}) collective-permute-start(bf16[384,512]{1,0:T(8,128)(2,1)S(1)} %get-tuple-element.34), channel_id=1, source_target_pairs={{0,8},{4,12},{8,0},{12,4},{1,9},{5,13},{9,1},{13,5},{2,10},{6,14},... | collective-permute-start | bytes 1179656 | tf_op jit(solution)/shard_map/ppermute | solution.py:243
  43.6 3.1 %collective-permute-start.2 = (bf16[384,512]{1,0:T(8,128)(2,1)S(1)}, bf16[384,512]{1,0:T(8,128)(2,1)S(1)}, u32[]{:S(2)}, u32[]{:S(2)}) collective-permute-start(bf16[384,512]{1,0:T(8,128)(2,1)S(1)} %get-tuple-element.35), channel_id=1, source_target_pairs={{0,12},{4,0},{8,4},{12,8},{1,13},{5,1},{9,5},{13,9},{2,14},{6,2},{... | collective-permute-start | bytes 1179656 | tf_op jit(solution)/shard_map/ppermute | solution.py:243
  46.7 2.5 %collective-permute-done.r1 = bf16[384,512]{1,0:T(8,128)(2,1)S(1)} collective-permute-done((bf16[384,512]{1,0:T(8,128)(2,1)S(1)}, bf16[384,512]{1,0:T(8,128)(2,1)S(1)}, u32[]{:S(2)}, u32[]{:S(2)}) %collective-permute-start) | collective-permute-done | bytes 393248 | tf_op jit(solution)/shard_map/ppermute | solution.py:243
  49.3 9.4 %collective-permute-done.1.r2 = bf16[384,512]{1,0:T(8,128)(2,1)S(1)} collective-permute-done((bf16[384,512]{1,0:T(8,128)(2,1)S(1)}, bf16[384,512]{1,0:T(8,128)(2,1)S(1)}, u32[]{:S(2)}, u32[]{:S(2)}) %collective-permute-start.1) | collective-permute-done | bytes 393248 | tf_op jit(solution)/shard_map/ppermute | solution.py:243
  58.7 0.7 copy-done.11
  59.4 0.8 collective-permute-done.2.r3
  60.2 0.7 copy-done.13
  60.9 0.0 all-to-all-done.1.s_ref
  60.9 1.1 copy-done.10
  62.1 1.0 copy-done.12
  63.1 1.0 copy-done.14
  64.1 0.9 copy-done.20
  65.0 2.1 %meet.1 = (bf16[4,192,512]{2,1,0:T(8,128)(2,1)S(1)}, bf16[2,96,256]{2,1,0:T(8,128)(2,1)S(1)}) custom-call(s32[3]{0:T(128)S(1)} %pad_add_fusion.at_ref.refs_0_, f32[24,16,128]{2,1,0:T(8,128)S(1)} %all-to-all-done.1.s_ref, f32[16,128]{1,0:T(8,128)S(1)} %get-tuple-element.28.d_ref, f32[16,128]{1,0:T(8,128)S(1)} %get-tuple-element.29.c_ref, ...), custom_call_target="tpu_custom_call" | custom-call | tf_op jit(solution)/shard_map/meet/pallas_call | solution.py:225
  67.1 0.0 copy-start.29
  67.1 23.3 %all_to_all.29.z_ref = bf16[4,192,512]{2,1,0:T(8,128)(2,1)S(1)} all-to-all(bf16[4,192,512]{2,1,0:T(8,128)(2,1)S(1)} %get-tuple-element.36), channel_id=1, replica_groups=mesh['y'=8,'zh'=3,'core'=2,'x'=4,'zl'=4] {'zl'}, dimensions={0} | all-to-all | bytes 1572864 | tf_op jit(solution)/shard_map/all_to_all | solution.py:238
  90.4 2.8 %scan_backward.1 = (f32[512,128]{1,0:T(8,128)S(1)}, f32[24,16,128]{2,1,0:T(8,128)}, f32[2,96,256]{2,1,0:T(8,128)S(1)}) custom-call(bf16[4,192,512]{2,1,0:T(8,128)(2,1)S(1)} %all_to_all.29.z_ref, bf16[2,448,256]{2,1,0:T(8,128)(2,1)S(1)} %all-to-all-done.got_ref, f32[16,128]{1,0:T(8,128)S(1)} %get-tuple-element.28.d_ref, f32[16,128]{1,0:T(8,128)S(1)} %get-tuple-element.29.c_ref), custom_call_target="tpu_custom_call" | custom-call | tf_op jit(solution)/shard_map/scan_backward/pallas_call | solution.py:225
  93.2 0.9 copy-done.1
  94.1 0.7 copy-done.23
  94.8 0.7 copy-done.25
  95.5 11.5 %all-to-all-start.3 = ((f32[24,16,128]{2,1,0:T(8,128)}), f32[24,16,128]{2,1,0:T(8,128)S(1)}, u32[]{:S(2)}, u32[]{:S(2)}) async-start(f32[24,16,128]{2,1,0:T(8,128)} %get-tuple-element.39), calls=%async_computation.3 | async-start | bytes 393216 | tf_op jit(solution)/shard_map/all_to_all | solution.py:238
  107.1 1.0 slice.4
  108.1 5.8 %collective-permute-start.5 = (bf16[384,512]{1,0:T(8,128)(2,1)S(1)}, bf16[384,512]{1,0:T(8,128)(2,1)S(1)}, u32[]{:S(2)}, u32[]{:S(2)}) collective-permute-start(bf16[384,512]{1,0:T(8,128)(2,1)S(1)} %bitcast.15), channel_id=1, source_target_pairs={{0,12},{4,0},{8,4},{12,8},{1,13},{5,1},{9,5},{13,9},{2,14},{6,2},{... | collective-permute-start | bytes 1179656 | tf_op jit(solution)/shard_map/ppermute | solution.py:243
  113.9 3.4 %collective-permute-start.4 = (bf16[384,512]{1,0:T(8,128)(2,1)S(1)}, bf16[384,512]{1,0:T(8,128)(2,1)S(1)}, u32[]{:S(2)}, u32[]{:S(2)}) collective-permute-start(bf16[384,512]{1,0:T(8,128)(2,1)S(1)} %bitcast.16), channel_id=1, source_target_pairs={{0,8},{4,12},{8,0},{12,4},{1,9},{5,13},{9,1},{13,5},{2,10},{6,14},... | collective-permute-start | bytes 1179656 | tf_op jit(solution)/shard_map/ppermute | solution.py:243
  117.4 1.9 collective-permute-start.3
  119.3 2.1 %collective-permute-done.5.p3 = bf16[384,512]{1,0:T(8,128)(2,1)S(1)} collective-permute-done((bf16[384,512]{1,0:T(8,128)(2,1)S(1)}, bf16[384,512]{1,0:T(8,128)(2,1)S(1)}, u32[]{:S(2)}, u32[]{:S(2)}) %collective-permute-start.5) | collective-permute-done | bytes 393248 | tf_op jit(solution)/shard_map/ppermute | solution.py:243
  121.4 4.6 %collective-permute-done.4.p2 = bf16[384,512]{1,0:T(8,128)(2,1)S(1)} collective-permute-done((bf16[384,512]{1,0:T(8,128)(2,1)S(1)}, bf16[384,512]{1,0:T(8,128)(2,1)S(1)}, u32[]{:S(2)}, u32[]{:S(2)}) %collective-permute-start.4) | collective-permute-done | bytes 393248 | tf_op jit(solution)/shard_map/ppermute | solution.py:243
  126.0 10.8 %collective-permute-done.3.p1 = bf16[384,512]{1,0:T(8,128)(2,1)S(1)} collective-permute-done((bf16[384,512]{1,0:T(8,128)(2,1)S(1)}, bf16[384,512]{1,0:T(8,128)(2,1)S(1)}, u32[]{:S(2)}, u32[]{:S(2)}) %collective-permute-start.3) | collective-permute-done | bytes 393248 | tf_op jit(solution)/shard_map/ppermute | solution.py:243
  136.8 1.1 weight.1
  137.9 0.9 copy-done.2
  138.8 0.8 copy-done.3
  139.6 0.7 copy-done.5
  140.3 0.8 copy-done.7
  141.1 0.0 all-to-all-done.3.s_ref
  141.1 11.6 %all-to-all-start.4 = ((bf16[24,64,256]{2,1,0:T(8,128)(2,1)}), bf16[24,64,256]{2,1,0:T(8,128)(2,1)}, u32[]{:S(2)}, u32[]{:S(2)}) async-start(bf16[24,64,256]{2,1,0:T(8,128)(2,1)} %bitcast.20), calls=%async_computation.4 | async-start | bytes 1572864 | tf_op jit(solution)/shard_map/all_to_all | solution.py:238
  152.7 1.0 copy-done.4
  153.7 1.0 copy-done.6
  154.7 2.0 %mixed.1 = (f32[256,256]{1,0:T(8,128)S(1)}, f32[256,256]{1,0:T(8,128)}) custom-call(s32[3]{0:T(128)S(1)} %pad_add_fusion.at_ref.refs_0_, bf16[384,512]{1,0:T(8,128)(2,1)S(1)} %bitcast.19, bf16[384,512]{1,0:T(8,128)(2,1)S(1)} %copy-done.8, bf16[384,512]{1,0:T(8,128)(2,1)S(1)} %copy-done.6, bf16[384,512]{1,0:T(8,128)(2,1)S(1)} %copy-done.4, ...), custom_call_target="tpu_custom_call" | custom-call | tf_op jit(solution)/shard_map/mixed/pallas_call | solution.py:225
  156.7 3.0 %collective-permute-start.6 = (f32[256,256]{1,0:T(8,128)}, f32[256,256]{1,0:T(8,128)S(1)}, u32[]{:S(2)}, u32[]{:S(2)}) collective-permute-start(f32[256,256]{1,0:T(8,128)} %get-tuple-element.38), channel_id=1, source_target_pairs={{0,16},{16,0},{1,17},{17,1},{2,18},{18,2},{3,19},{19,3},{4,20},{20... | collective-permute-start | bytes 786440 | tf_op jit(solution)/shard_map/ppermute | solution.py:243
  159.7 2.1 %heads_backward.1 = (bf16[192,256]{1,0:T(8,128)(2,1)S(1)}, bf16[192,256]{1,0:T(8,128)(2,1)S(1)}) custom-call(s32[3]{0:T(128)S(1)} %pad_add_fusion.at_ref.refs_0_, f32[24,16,128]{2,1,0:T(8,128)S(1)} %all-to-all-done.3.s_ref, f32[16,128]{1,0:T(8,128)S(1)} %get-tuple-element.28.d_ref, f32[16,128]{1,0:T(8,128)S(1)} %get-tuple-element.29.c_ref, ...), custom_call_target="tpu_custom_call" | custom-call | tf_op jit(solution)/shard_map/heads_backward/pallas_call | solution.py:225
  161.8 1.9 %collective-permute-start.7 = (bf16[192,256]{1,0:T(8,128)(2,1)S(1)}, bf16[192,256]{1,0:T(8,128)(2,1)S(1)}, u32[]{:S(2)}, u32[]{:S(2)}) collective-permute-start(bf16[192,256]{1,0:T(8,128)(2,1)S(1)} %get-tuple-element.44), channel_id=1, source_target_pairs={{0,16},{16,0},{1,17},{17,1},{2,18},{18,2},{3,19},{19,3},{4,20},{20... | collective-permute-start | bytes 294920 | tf_op jit(solution)/shard_map/ppermute | solution.py:243
  163.8 21.0 %all-to-all-done.4.refs_1_ = bf16[24,64,256]{2,1,0:T(8,128)(2,1)} async-done(((bf16[24,64,256]{2,1,0:T(8,128)(2,1)}), bf16[24,64,256]{2,1,0:T(8,128)(2,1)}, u32[]{:S(2)}, u32[]{:S(2)}) %all-to-all-start.4) | async-done | bytes 786464 | tf_op jit(solution)/shard_map/all_to_all | solution.py:238
  184.8 1.3 total.1
  186.1 2.7 %collective-permute-start.8 = (f32[32,256]{1,0:T(8,128)S(1)}, f32[32,256]{1,0:T(8,128)S(1)}, u32[]{:S(2)}, u32[]{:S(2)}) collective-permute-start(f32[32,256]{1,0:T(8,128)S(1)} %get-tuple-element.50), channel_id=1, source_target_pairs={{0,16},{16,0},{1,17},{17,1},{2,18},{18,2},{3,19},{19,3},{4,20},{20... | collective-permute-start | bytes 98312 | tf_op jit(solution)/shard_map/ppermute | solution.py:243
  188.8 0.9 copy-done.22
  189.8 1.3 finish.1
  191.1 1.2 join.1
  (45 shorter events, 0.1 us)
Async XLA Ops:
  0.6 33.4 %copy-start = (bf16[3072,256]{1,0:T(8,128)(2,1)S(1)}, bf16[3072,256]{1,0:T(8,128)(2,1)}, u32[]{:S(2)}) copy-start(bf16[3072,256]{1,0:T(8,128)(2,1)} %param.12) | copy-start | bytes 4718596
  0.6 1.0 copy-start.15
  1.7 0.9 copy-start.17
  2.6 0.9 copy-start.27
  3.5 0.9 copy-start.28
  4.4 14.8 %copy-start.31 = (f32[192,16]{0,1:T(8,128)S(1)}, f32[192,16]{0,1:T(8,128)}, u32[]{:S(2)}) copy-start(f32[192,16]{0,1:T(8,128)} %param.11) | copy-start | bytes 36868
  4.4 14.8 %copy-start.32 = (f32[192,16]{0,1:T(8,128)S(1)}, f32[192,16]{0,1:T(8,128)}, u32[]{:S(2)}) copy-start(f32[192,16]{0,1:T(8,128)} %param.10) | copy-start | bytes 36868
  5.2 15.3 %all-to-all-start = ((bf16[2,448,256]{2,1,0:T(8,128)(2,1)}), bf16[2,448,256]{2,1,0:T(8,128)(2,1)S(1)}, u32[]{:S(2)}, u32[]{:S(2)}) async-start(bf16[2,448,256]{2,1,0:T(8,128)(2,1)} %pack.1), calls=%async_computation | async-start | bytes 917504 | tf_op jit(solution)/shard_map/all_to_all | solution.py:238
  23.1 0.7 copy-start.19
  23.9 37.1 %all-to-all-start.1 = ((f32[24,16,128]{2,1,0:T(8,128)}), f32[24,16,128]{2,1,0:T(8,128)S(1)}, u32[]{:S(2)}, u32[]{:S(2)}) async-start(f32[24,16,128]{2,1,0:T(8,128)} %get-tuple-element.30), calls=%async_computation.1 | async-start | bytes 393216 | tf_op jit(solution)/shard_map/all_to_all | solution.py:238
  35.2 0.9 copy-start.9
  36.2 13.1 %collective-permute-start = (bf16[384,512]{1,0:T(8,128)(2,1)S(1)}, bf16[384,512]{1,0:T(8,128)(2,1)S(1)}, u32[]{:S(2)}, u32[]{:S(2)}) collective-permute-start(bf16[384,512]{1,0:T(8,128)(2,1)S(1)} %get-tuple-element.33), channel_id=1, source_target_pairs={{0,4},{4,8},{8,12},{12,0},{1,5},{5,9},{9,13},{13,1},{2,6},{6,10},{... | collective-permute-start | bytes 1179656 | tf_op jit(solution)/shard_map/ppermute | solution.py:243
  39.3 19.4 %collective-permute-start.1 = (bf16[384,512]{1,0:T(8,128)(2,1)S(1)}, bf16[384,512]{1,0:T(8,128)(2,1)S(1)}, u32[]{:S(2)}, u32[]{:S(2)}) collective-permute-start(bf16[384,512]{1,0:T(8,128)(2,1)S(1)} %get-tuple-element.34), channel_id=1, source_target_pairs={{0,8},{4,12},{8,0},{12,4},{1,9},{5,13},{9,1},{13,5},{2,10},{6,14},... | collective-permute-start | bytes 1179656 | tf_op jit(solution)/shard_map/ppermute | solution.py:243
  43.6 16.5 %collective-permute-start.2 = (bf16[384,512]{1,0:T(8,128)(2,1)S(1)}, bf16[384,512]{1,0:T(8,128)(2,1)S(1)}, u32[]{:S(2)}, u32[]{:S(2)}) collective-permute-start(bf16[384,512]{1,0:T(8,128)(2,1)S(1)} %get-tuple-element.35), channel_id=1, source_target_pairs={{0,12},{4,0},{8,4},{12,8},{1,13},{5,1},{9,5},{13,9},{2,14},{6,2},{... | collective-permute-start | bytes 1179656 | tf_op jit(solution)/shard_map/ppermute | solution.py:243
  58.7 0.7 copy-start.11
  60.2 0.7 copy-start.13
  60.9 1.1 copy-start.10
  62.1 1.0 copy-start.12
  63.1 1.0 copy-start.14
  64.1 0.9 copy-start.20
  67.1 28.4 %copy-start.29 = (bf16[2,96,256]{2,1,0:T(8,128)(2,1)}, bf16[2,96,256]{2,1,0:T(8,128)(2,1)S(1)}, u32[]{:S(2)}) copy-start(bf16[2,96,256]{2,1,0:T(8,128)(2,1)S(1)} %get-tuple-element.41.f_ref) | copy-start | bytes 294916
  93.2 0.9 copy-start.1
  94.1 0.7 copy-start.23
  94.8 0.7 copy-start.25
  95.5 45.5 %all-to-all-start.3 = ((f32[24,16,128]{2,1,0:T(8,128)}), f32[24,16,128]{2,1,0:T(8,128)S(1)}, u32[]{:S(2)}, u32[]{:S(2)}) async-start(f32[24,16,128]{2,1,0:T(8,128)} %get-tuple-element.39), calls=%async_computation.3 | async-start | bytes 393216 | tf_op jit(solution)/shard_map/all_to_all | solution.py:238
  108.1 13.2 %collective-permute-start.5 = (bf16[384,512]{1,0:T(8,128)(2,1)S(1)}, bf16[384,512]{1,0:T(8,128)(2,1)S(1)}, u32[]{:S(2)}, u32[]{:S(2)}) collective-permute-start(bf16[384,512]{1,0:T(8,128)(2,1)S(1)} %bitcast.15), channel_id=1, source_target_pairs={{0,12},{4,0},{8,4},{12,8},{1,13},{5,1},{9,5},{13,9},{2,14},{6,2},{... | collective-permute-start | bytes 1179656 | tf_op jit(solution)/shard_map/ppermute | solution.py:243
  113.9 12.1 %collective-permute-start.4 = (bf16[384,512]{1,0:T(8,128)(2,1)S(1)}, bf16[384,512]{1,0:T(8,128)(2,1)S(1)}, u32[]{:S(2)}, u32[]{:S(2)}) collective-permute-start(bf16[384,512]{1,0:T(8,128)(2,1)S(1)} %bitcast.16), channel_id=1, source_target_pairs={{0,8},{4,12},{8,0},{12,4},{1,9},{5,13},{9,1},{13,5},{2,10},{6,14},... | collective-permute-start | bytes 1179656 | tf_op jit(solution)/shard_map/ppermute | solution.py:243
  117.4 19.4 %collective-permute-start.3 = (bf16[384,512]{1,0:T(8,128)(2,1)S(1)}, bf16[384,512]{1,0:T(8,128)(2,1)S(1)}, u32[]{:S(2)}, u32[]{:S(2)}) collective-permute-start(bf16[384,512]{1,0:T(8,128)(2,1)S(1)} %bitcast.17), channel_id=1, source_target_pairs={{0,4},{4,8},{8,12},{12,0},{1,5},{5,9},{9,13},{13,1},{2,6},{6,10},{... | collective-permute-start | bytes 1179656 | tf_op jit(solution)/shard_map/ppermute | solution.py:243
  137.9 0.9 copy-start.2
  138.8 0.8 copy-start.3
  139.6 0.7 copy-start.5
  140.3 0.8 copy-start.7
  141.1 11.6 %copy-start.8 = (bf16[384,512]{1,0:T(8,128)(2,1)S(1)}, bf16[384,512]{1,0:T(8,128)(2,1)}, u32[]{:S(2)}) copy-start(bf16[384,512]{1,0:T(8,128)(2,1)} %copy-done.7) | copy-start | bytes 1179652
  141.1 43.7 %all-to-all-start.4 = ((bf16[24,64,256]{2,1,0:T(8,128)(2,1)}), bf16[24,64,256]{2,1,0:T(8,128)(2,1)}, u32[]{:S(2)}, u32[]{:S(2)}) async-start(bf16[24,64,256]{2,1,0:T(8,128)(2,1)} %bitcast.20), calls=%async_computation.4 | async-start | bytes 1572864 | tf_op jit(solution)/shard_map/all_to_all | solution.py:238
  152.7 1.0 copy-start.4
  153.7 1.0 copy-start.6
  154.7 5.0 %copy-start.24 = (f32[512,128]{1,0:T(8,128)S(1)}, f32[512,128]{1,0:T(8,128)}, u32[]{:S(2)}) copy-start(f32[512,128]{1,0:T(8,128)} %copy-done.23) | copy-start | bytes 786436
  154.7 5.0 %copy-start.26 = (f32[2,96,256]{2,1,0:T(8,128)S(1)}, f32[2,96,256]{2,1,0:T(8,128)}, u32[]{:S(2)}) copy-start(f32[2,96,256]{2,1,0:T(8,128)} %copy-done.25) | copy-start | bytes 589828
  154.7 5.0 %copy-start.30 = (bf16[2,96,256]{2,1,0:T(8,128)(2,1)S(1)}, bf16[2,96,256]{2,1,0:T(8,128)(2,1)}, u32[]{:S(2)}) copy-start(bf16[2,96,256]{2,1,0:T(8,128)(2,1)} %copy-done.29) | copy-start | bytes 294916
  154.7 34.1 %copy-start.16 = (bf16[192,256]{1,0:T(8,128)(2,1)S(1)}, bf16[192,256]{1,0:T(8,128)(2,1)}, u32[]{:S(2)}) copy-start(bf16[192,256]{1,0:T(8,128)(2,1)} %i_ref.3) | copy-start | bytes 294916
  156.7 5.1 %copy-start.21 = (f32[256,256]{1,0:T(8,128)}, f32[256,256]{1,0:T(8,128)S(1)}, u32[]{:S(2)}) copy-start(f32[256,256]{1,0:T(8,128)S(1)} %get-tuple-element.37.m_ref) | copy-start | bytes 786436
  156.7 32.1 %copy-start.18 = (bf16[192,256]{1,0:T(8,128)(2,1)S(1)}, bf16[192,256]{1,0:T(8,128)(2,1)}, u32[]{:S(2)}) copy-start(bf16[192,256]{1,0:T(8,128)(2,1)} %v_ref.3) | copy-start | bytes 294916
  156.7 32.1 %collective-permute-start.6 = (f32[256,256]{1,0:T(8,128)}, f32[256,256]{1,0:T(8,128)S(1)}, u32[]{:S(2)}, u32[]{:S(2)}) collective-permute-start(f32[256,256]{1,0:T(8,128)} %get-tuple-element.38), channel_id=1, source_target_pairs={{0,16},{16,0},{1,17},{17,1},{2,18},{18,2},{3,19},{19,3},{4,20},{20... | collective-permute-start | bytes 786440 | tf_op jit(solution)/shard_map/ppermute | solution.py:243
  161.8 26.9 %collective-permute-start.7 = (bf16[192,256]{1,0:T(8,128)(2,1)S(1)}, bf16[192,256]{1,0:T(8,128)(2,1)S(1)}, u32[]{:S(2)}, u32[]{:S(2)}) collective-permute-start(bf16[192,256]{1,0:T(8,128)(2,1)S(1)} %get-tuple-element.44), channel_id=1, source_target_pairs={{0,16},{16,0},{1,17},{17,1},{2,18},{18,2},{3,19},{19,3},{4,20},{20... | collective-permute-start | bytes 294920 | tf_op jit(solution)/shard_map/ppermute | solution.py:243
  186.1 5.0 %collective-permute-start.8 = (f32[32,256]{1,0:T(8,128)S(1)}, f32[32,256]{1,0:T(8,128)S(1)}, u32[]{:S(2)}, u32[]{:S(2)}) collective-permute-start(f32[32,256]{1,0:T(8,128)S(1)} %get-tuple-element.50), channel_id=1, source_target_pairs={{0,16},{16,0},{1,17},{17,1},{2,18},{18,2},{3,19},{19,3},{4,20},{20... | collective-permute-start | bytes 98312 | tf_op jit(solution)/shard_map/ppermute | solution.py:243
  188.8 1.0 copy-start.22

commit v3 on v1

v3 whole, which is shorter than its diff:
```python
import math

import jax
import jax.numpy as jnp
from jax import lax
from jax.experimental import pallas as pl
from jax.experimental.pallas import tpu as pltpu
from jax.sharding import Mesh
from jax.sharding import PartitionSpec as P

f32 = jnp.float32
bf16 = jnp.bfloat16
SUB = 32
LANES = 128
CORE, X, CHIP = 0, 1, 2


def to_columns(tile):
    rows, width = tile.shape
    pad = jnp.zeros((LANES - rows, width), f32)
    return jnp.concatenate([tile, pad], axis=0).T


def back_kernel(w_ref, g_ref, out_ref):
    chan = 6 * SUB
    grads = g_ref[...]
    for j in range(w_ref.shape[0] // chan):
        part = lax.dot_general(
            w_ref[pl.ds(j * chan, chan), :],
            grads,
            (((1,), (1,)), ((), ())),
            preferred_element_type=f32,
        ).astype(bf16)
        for b in range(6):
            dst = j * chan + (b % 2) * 3 * SUB + (b // 2) * SUB
            out_ref[pl.ds(dst, SUB), :] = part[b * SUB : (b + 1) * SUB]


def pack_kernel(at_ref, i_ref, v_ref, o_ref, g_ref, own_ref, other_ref):
    tok = g_ref.shape[0]
    half = i_ref.shape[0] // 2
    core = at_ref[CORE]
    for h, ref in ((core, own_ref), (1 - core, other_ref)):
        ref[:tok] = g_ref[...]
        for b in range(half // SUB):
            src = pl.ds(pl.multiple_of(2 * SUB * b + SUB * h, SUB), SUB)
            gated = (i_ref[src, :].astype(f32) * v_ref[src, :].astype(f32)).astype(bf16)
            ref[pl.ds(tok + SUB * b, SUB), :] = gated
            ref[pl.ds(tok + half + SUB * b, SUB), :] = o_ref[src, :]


def both_kernel(at_ref, own_ref, other_ref, out_ref):
    core = at_ref[CORE]
    out_ref[core] = own_ref[...]
    out_ref[1 - core] = other_ref[...]


def modes_kernel(at_ref, d_ref, c_ref, od_ref, oc_ref):
    chan = lax.broadcasted_iota(jnp.int32, (d_ref.shape[1], LANES), 0)
    lane = lax.broadcasted_iota(jnp.int32, (d_ref.shape[1], LANES), 1)
    wanted = lane + SUB * (lane // SUB) + SUB * at_ref[CORE]
    pick = jnp.where((chan == wanted) & (lane < d_ref.shape[1] // 2), 1.0, 0.0).astype(f32)
    for src, dst in ((d_ref, od_ref), (c_ref, oc_ref)):
        dst[...] = jnp.dot(
            src[...], pick, precision=lax.Precision.HIGHEST, preferred_element_type=f32
        )


def sum_kernel(p_ref, out_ref):
    total = p_ref[0].astype(f32)
    for i in range(1, p_ref.shape[0]):
        total = total + p_ref[i].astype(f32)
    out_ref[...] = total.astype(bf16)


def scan_kernel(at_ref, got_ref, z_ref, d_ref, c_ref, yf_ref, yb_ref, bs_ref, s_ref, gt, bt):
    tok = got_ref.shape[2]
    half = (got_ref.shape[1] - tok) // 2
    for h in range(2):
        at = pl.ds(h * tok, tok)
        gt[at, :] = to_columns(got_ref[h, tok : tok + half].astype(f32))
        total = z_ref[0, h].astype(f32)
        for q in range(1, z_ref.shape[0]):
            total = total + z_ref[q, h].astype(f32)
        bs_ref[h] = total
        outer = got_ref[h, tok + half :].astype(f32)
        bt[at, :] = to_columns((total * outer).astype(bf16).astype(f32))
    rate = jnp.exp(-d_ref[...])
    coef = c_ref[...]
    length = gt.shape[0]

    def step(i, carry):
        sf, sb = carry
        lo = pl.ds(pl.multiple_of(i * 8, 8), 8)
        hi = pl.ds(pl.multiple_of(length - 8 - i * 8, 8), 8)
        gs, bs = gt[lo, :], bt[hi, :]
        fs, rs = [], [None] * 8
        for t in range(8):
            sf = sf * rate + gs[t : t + 1, :]
            sb = sb * rate + bs[7 - t : 8 - t, :]
            fs.append(jnp.sum(sf * coef, axis=0, keepdims=True))
            rs[7 - t] = jnp.sum(sb * coef, axis=0, keepdims=True)
        yf_ref[lo, :] = jnp.concatenate(fs, axis=0)
        yb_ref[hi, :] = jnp.concatenate(rs, axis=0)
        return sf, sb

    zero = jnp.zeros_like(coef)
    sf, sb = lax.fori_loop(0, length // 8, step, (zero, zero))
    for m in range(s_ref.shape[0]):
        s_ref[m] = jnp.where(m > at_ref[CHIP], sf, sb)


def heads_kernel(at_ref, s_ref, d_ref, c_ref, yf_ref, yb_ref, got_ref, bs_ref, p_ref, own_ref, other_ref, ft, bt):
    me = at_ref[CHIP]
    tok = got_ref.shape[2]
    half = (got_ref.shape[1] - tok) // 2
    decay = d_ref[...]
    rate = jnp.exp(-decay)
    coef = c_ref[...]
    length = ft.shape[0]
    chips = s_ref.shape[0]
    jump = jnp.exp(-decay * float(length))
    pf = jnp.zeros_like(coef)
    pb = jnp.zeros_like(coef)
    for m in range(chips):
        pf = jnp.where(m < me, pf * jump + s_ref[m], pf)
        back = chips - 1 - m
        pb = jnp.where(back > me, pb * jump + s_ref[back], pb)

    def step(i, carry):
        pf, pb = carry
        lo = pl.ds(pl.multiple_of(i * 8, 8), 8)
        hi = pl.ds(pl.multiple_of(length - 8 - i * 8, 8), 8)
        fs, rs = [], [None] * 8
        for t in range(8):
            pf = pf * rate
            pb = pb * rate
            fs.append(jnp.sum(pf, axis=0, keepdims=True))
            rs[7 - t] = jnp.sum(pb, axis=0, keepdims=True)
        ft[lo, :] = yf_ref[lo, :] + jnp.concatenate(fs, axis=0)
        bt[hi, :] = yb_ref[hi, :] + jnp.concatenate(rs, axis=0)
        return pf, pb

    lax.fori_loop(0, length // 8, step, (pf * coef, pb * coef))
    core = at_ref[CORE]
    for h, ref in ((core, own_ref), (1 - core, other_ref)):
        at = pl.ds(pl.multiple_of(h * tok, tok), tok)
        filtered = ft[at, :].T[:half].astype(bf16).astype(f32)
        product = (got_ref[h, tok + half :].astype(f32) * filtered).astype(bf16)
        for q in range(p_ref.shape[0]):
            p_ref[q, :, at] = product
        ref[:half] = bt[at, :].T[:half].astype(bf16)
        ref[half:] = (bs_ref[h] * filtered).astype(bf16)


def weight_kernel(p_ref, got_ref, out_ref):
    tok = got_ref.shape[2]
    grads = got_ref[:, :tok, :].reshape(2 * tok, -1)
    out_ref[...] = jnp.dot(p_ref[...], grads, preferred_element_type=f32).astype(bf16)


def mixed_kernel(at_ref, p_ref, w_ref, own_ref, other_ref, total):
    tok = own_ref.shape[1]
    total[...] = lax.dot_general(
        w_ref[...], p_ref[...], (((0,), (0,)), ((), ())), preferred_element_type=f32
    )
    core = at_ref[CORE]
    own_ref[...] = total[:, pl.ds(pl.multiple_of(core * tok, tok), tok)]
    other_ref[...] = total[:, pl.ds(pl.multiple_of((1 - core) * tok, tok), tok)]


def finish_kernel(at_ref, m_ref, mr_ref, g_ref, gr_ref, i_ref, v_ref, mixed_ref, go_ref, gi_ref, gv_ref):
    mixed_ref[...] = (m_ref[...] + mr_ref[...]).T.astype(bf16)
    half = g_ref.shape[0] // 2
    core = at_ref[CORE]
    for h, ref in ((core, g_ref), (1 - core, gr_ref)):
        for b in range(half // SUB):
            at = pl.ds(pl.multiple_of(2 * SUB * b + SUB * h, SUB), SUB)
            back = ref[pl.ds(SUB * b, SUB), :].astype(f32)
            go_ref[at, :] = ref[pl.ds(half + SUB * b, SUB), :]
            gi_ref[at, :] = (back * v_ref[at, :].astype(f32)).astype(bf16)
            gv_ref[at, :] = (back * i_ref[at, :].astype(f32)).astype(bf16)


def total_kernel(scale, p_ref, out_ref):
    for h in range(2):
        total = p_ref[h].astype(f32)
        for m in range(1, p_ref.shape[0] // 2):
            total = total + p_ref[2 * m + h].astype(f32)
        out_ref[pl.ds(h * SUB, SUB), :] = total * scale


def call(kernel, name, outs, args, scratch=(), indexed=True):
    specs = [pl.BlockSpec(memory_space=pltpu.VMEM)] * len(args)
    if indexed:
        specs[0] = pl.BlockSpec(memory_space=pltpu.SMEM)
    return pl.pallas_call(
        kernel,
        out_shape=tuple(jax.ShapeDtypeStruct(s, t) for s, t in outs),
        in_specs=specs,
        out_specs=tuple([pl.BlockSpec(memory_space=pltpu.VMEM)] * len(outs)),
        scratch_shapes=[pltpu.VMEM(s, f32) for s in scratch],
        compiler_params=pltpu.CompilerParams(vmem_limit_bytes=24 * 2**20),
        name=name,
    )(*args)


def swap(x, axes):
    return lax.all_to_all(x, axes, 0, 0, tiled=True)


def spread(x, axis):
    n, rows, m = x.shape
    return swap(x.reshape(n * rows, m), axis)


def other_core(x):
    return lax.ppermute(x, "core", [(0, 1), (1, 0)])


def shards(outer_gate, inner_gate, value_proj, residues, decays, out_weight, out_grad):
    chan, tok = outer_gate.shape
    half = chan // 2
    length = 2 * tok
    all_chan, cols = out_weight.shape
    modes = decays.shape[1]
    core = lax.axis_index("core")
    chips = lax.axis_size(("y", "zh"))
    nx, nz = lax.axis_size("x"), lax.axis_size("zl")
    at = jnp.stack([core, lax.axis_index("x"), lax.axis_index(("y", "zh"))]).astype(jnp.int32)

    (part,) = call(
        back_kernel, "back", [((all_chan, tok), bf16)], (out_weight, out_grad), indexed=False
    )
    part = swap(part, "x").reshape(nx, all_chan // nx, tok)

    own, other = call(
        pack_kernel,
        "pack",
        [((tok + chan, cols), bf16)] * 2,
        (at, inner_gate, value_proj, outer_gate, out_grad),
    )
    (got,) = call(
        both_kernel, "both", [((2, tok + chan, cols), bf16)], (at, own, other_core(other))
    )
    coef = residues * jnp.sqrt(-jnp.expm1(-2.0 * decays))
    small = ((modes, LANES), f32)
    decay, coef = call(modes_kernel, "modes", [small, small], (at, decays.T, coef.T))
    weight = lax.dynamic_index_in_dim(
        out_weight.reshape(-1, 2, SUB, cols), core, 1, keepdims=False
    ).reshape(-1, cols)

    (part,) = call(sum_kernel, "sum", [((all_chan // nx, tok), bf16)], (part,), indexed=False)
    part = swap(part, ("zl", "core")).reshape(nz, 2, half, tok)

    columns = ((length, LANES), f32)
    yf, yb, back_sum, states = call(
        scan_kernel,
        "scan",
        [columns, columns, ((2, half, tok), f32), ((chips, modes, LANES), f32)],
        (at, got, part, decay, coef),
        scratch=[(length, LANES)] * 2,
    )
    states = swap(states, ("y", "zh"))
    product, grads, grads_other = call(
        heads_kernel,
        "heads",
        [((nz, half, length), bf16)] + [((chan, tok), bf16)] * 2,
        (at, states, decay, coef, yf, yb, got, back_sum),
        scratch=[(length, LANES)] * 2,
    )
    product = spread(product, "zl")
    product = spread(jnp.broadcast_to(product[None], (nx,) + product.shape), "x")

    (partial,) = call(
        weight_kernel,
        "weight",
        [((product.shape[0], cols), bf16)],
        (product, got),
        indexed=False,
    )
    partial = swap(partial, ("y", "zh", "core")).reshape(2 * chips, SUB, cols)

    mixed, mixed_other = call(
        mixed_kernel,
        "mixed",
        [((cols, tok), f32)] * 2,
        (at, product, weight),
        scratch=[(cols, length)],
    )
    outs = call(
        finish_kernel,
        "finish",
        [((tok, cols), bf16)] + [((chan, tok), bf16)] * 3,
        (
            at,
            mixed,
            other_core(mixed_other),
            grads,
            other_core(grads_other),
            inner_gate,
            value_proj,
        ),
    )
    *outs, partial = lax.optimization_barrier((*outs, partial))
    scale = 1.0 / math.sqrt(length * chips)
    (grad_weight,) = call(
        lambda *refs: total_kernel(scale, *refs),
        "total",
        [((2 * SUB, cols), f32)],
        (partial,),
        indexed=False,
    )
    return (*outs, grad_weight)


def solution(mesh):
    fine = Mesh(mesh.devices.reshape(8, 3, 2, 4, 4), ("y", "zh", "core", "x", "zl"))
    seq, col = ("y", "zh", "core"), ("x", "zl")
    return jax.shard_map(
        shards,
        mesh=fine,
        in_specs=(
            P(col, seq),
            P(col, seq),
            P(col, seq),
            P(col, None),
            P(col, None),
            P(None, col),
            P(seq, col),
        ),
        out_specs=(P(seq, col), P(col, seq), P(col, seq), P(col, seq), P(seq, col)),
        check_vma=False,
    )
```

time: 169 us -> 165 us (0.976)
  blocking collectives: 95.9 us -> 82.7 us
  Pallas kernels: 4.94 us -> 14.7 us
  starting transfers between devices: 22.6 us -> 31.6 us
  waiting for transfers between devices: 23.2 us -> 31.1 us
  other arithmetic: 6.39 us -> 0.1 us
  matrix products: 5.23 us -> 0 us
  local copies, waits for them, and re-layouts: 8.66 us -> 3.43 us
    all_gather x1 -> x0, blocking collectives: 12.2 us -> none  [shards(): product = lax.all_gather(product, 'zl', axis=0, tiled=True)]
    pallas_call x2 -> x11, Pallas kernels: 4.94 us -> 14.7 us  [call(): pl.pallas_call(kernel, out_shape=tuple((jax.ShapeDtypeStruct(s, t) for s,...]
    ppermute x0 -> x3, starting transfers between devices: none -> 6.25 us  [other_core(): return lax.ppermute(x, 'core', [(0, 1), (1, 0)])]
    all_to_all x3 -> x2, waiting for transfers between devices: 23.2 us -> 29.3 us  [swap(): return lax.all_to_all(x, axes, 0, 0, tiled=True)]
    dot_general x3 -> x0, matrix products: 5.23 us -> none  [the longest x1 2.41 us: shards(): jnp.dot(product, grads, preferred_element_type=f32).astype(bf16)]
    convert_element_type x5 -> x0, other arithmetic: 3.06 us -> none  [the longest x1 0.97 us: shards(): gated = (inner * value).astype(bf16)]
    unnamed x18 -> x20, local copies, waits for them, and re-layouts: 0.25 us -> 3.24 us
    all_to_all x3 -> x2, starting transfers between devices: 22.6 us -> 25.4 us  [swap(): return lax.all_to_all(x, axes, 0, 0, tiled=True)]
  transfers between devices with their start and end apart: 3 -> 5, of which waited for: 3 -> 4; matrix products, arithmetic and copies ran while one was open for 4% -> 0% of each run, Pallas kernels for 0% -> 3%
where the time goes in v3:
time: 165 us; the launch traced here: 164 us
  blocking collectives  82.7 us (50%)
  starting transfers between devices  31.6 us (19%)
  waiting for transfers between devices  31.1 us (19%)
  Pallas kernels  14.7 us (9%)
  local copies, waits for them, and re-layouts  3.43 us (2%)
    all_to_all x4, blocking collectives, swap(): return lax.all_to_all(x, axes, 0, 0, tiled=True)  82.7 us
    all_to_all x2, waiting for transfers between devices, swap(): return lax.all_to_all(x, axes, 0, 0, tiled=True)  29.3 us
    all_to_all x2, starting transfers between devices, swap(): return lax.all_to_all(x, axes, 0, 0, tiled=True)  25.4 us
    pallas_call x11, Pallas kernels, call(): pl.pallas_call(kernel, out_shape=tuple((jax.ShapeDtypeStruct(s, t) for s,...  14.7 us
    ppermute x3, starting transfers between devices, other_core(): return lax.ppermute(x, 'core', [(0, 1), (1, 0)])  6.25 us
  transfers between devices with their start and end apart: 5, of which 4 were waited for; matrix products, arithmetic and copies ran while one was open for 0% of the time, Pallas kernels for 3%

profile of v3, /device:TPU:1, one launch (start us, length us, event | category | flops | bytes accessed | tf_op | source)
XLA Modules:
  0.0 164.5 jit_solution(8725777696772466852)
XLA Ops:
  0.6 0.0 copy-start
  0.6 1.4 copy-done
  2.0 0.0 copy-start.3
  2.0 0.9 copy-done.3
  2.9 0.8 back.1
  3.8 17.2 %all_to_all.46.p_ref = bf16[4,768,256]{2,1,0:T(8,128)(2,1)S(1)} all-to-all(bf16[4,768,256]{2,1,0:T(8,128)(2,1)S(1)} %bitcast.18), channel_id=1, replica_groups=mesh['y'=8,'zh'=3,'core'=2,'x'=4,'zl'=4] {'x'}, dimensions={0} | all-to-all | bytes 3145728 | tf_op jit(solution)/shard_map/all_to_all | solution.py:209
  21.0 0.0 copy-start.4
  21.0 0.0 copy-start.5
  21.0 0.0 copy-start.6
  21.0 0.0 copy-start.7
  21.0 0.0 copy-start.8
  21.0 0.0 copy-start.9
  21.0 0.9 sum.1
  22.0 16.4 %all-to-all-start.1 = ((bf16[8,96,256]{2,1,0:T(8,128)(2,1)}), bf16[8,96,256]{2,1,0:T(8,128)(2,1)S(1)}, u32[]{:S(2)}, u32[]{:S(2)}) async-start(bf16[8,96,256]{2,1,0:T(8,128)(2,1)} %bitcast.4), calls=%async_computation.1 | async-start | bytes 786432 | tf_op jit(solution)/shard_map/all_to_all | solution.py:209
  38.3 0.1 pad_add_fusion.at_ref
  38.4 0.0 copy-done.4
  38.4 0.0 copy-done.5
  38.4 0.0 copy-done.6
  38.4 0.0 copy-done.7
  38.4 0.6 pack.1
  39.0 1.9 %collective-permute-start = (bf16[448,256]{1,0:T(8,128)(2,1)S(1)}, bf16[448,256]{1,0:T(8,128)(2,1)S(1)}, u32[]{:S(2)}, u32[]{:S(2)}) collective-permute-start(bf16[448,256]{1,0:T(8,128)(2,1)S(1)} %get-tuple-element.28), channel_id=1, source_target_pairs={{0,16},{16,0},{1,17},{17,1},{2,18},{18,2},{3,19},{19,3},{4,20},{20... | collective-permute-start | bytes 688136 | tf_op jit(solution)/shard_map/ppermute | solution.py:218
  41.0 0.0 copy-done.8
  41.0 0.0 copy-done.9
  41.0 0.8 modes.1
  41.8 0.6 collective-permute-done.other_ref
  42.4 0.6 both.1.got_ref
  43.0 7.0 %all-to-all-done.1 = bf16[8,96,256]{2,1,0:T(8,128)(2,1)S(1)} async-done(((bf16[8,96,256]{2,1,0:T(8,128)(2,1)}), bf16[8,96,256]{2,1,0:T(8,128)(2,1)S(1)}, u32[]{:S(2)}, u32[]{:S(2)}) %all-to-all-start.1) | async-done | bytes 393248 | tf_op jit(solution)/shard_map/all_to_all | solution.py:209
  50.0 3.4 %scan.1 = (f32[512,128]{1,0:T(8,128)S(1)}, f32[512,128]{1,0:T(8,128)S(1)}, f32[2,96,256]{2,1,0:T(8,128)S(1)}, f32[24,16,128]{2,1,0:T(8,128)S(1)}) custom-call(s32[3]{0:T(128)S(1)} %pad_add_fusion.at_ref, bf16[2,448,256]{2,1,0:T(8,128)(2,1)S(1)} %both.1.got_ref, bf16[4,2,96,256]{3,2,1,0:T(8,128)(2,1)S(1)} %bitcast.22, f32[16,128]{1,0:T(8,128)S(1)} %get-tuple-element.29.d_ref, ...), custom_call_target="tpu_custom_call" | custom-call | tf_op jit(solution)/shard_map/scan/pallas_call | solution.py:197
  53.4 31.8 %all_to_all.47.s_ref = f32[24,16,128]{2,1,0:T(8,128)S(1)} all-to-all(f32[24,16,128]{2,1,0:T(8,128)S(1)} %get-tuple-element.31), channel_id=1, replica_groups=mesh['y'=8,'zh'=3,'core'=2,'x'=4,'zl'=4] {'y','zh'}, dimensions={0} | all-to-all | bytes 393216 | tf_op jit(solution)/shard_map/all_to_all | solution.py:209
  85.2 2.7 %heads.1 = (bf16[4,96,512]{2,1,0:T(8,128)(2,1)S(1)}, bf16[192,256]{1,0:T(8,128)(2,1)S(1)}, bf16[192,256]{1,0:T(8,128)(2,1)S(1)}) custom-call(s32[3]{0:T(128)S(1)} %pad_add_fusion.at_ref, f32[24,16,128]{2,1,0:T(8,128)S(1)} %all_to_all.47.s_ref, f32[16,128]{1,0:T(8,128)S(1)} %get-tuple-element.29.d_ref, f32[16,128]{1,0:T(8,128)S(1)} %get-tuple-element.30.c_ref, ...), custom_call_target="tpu_custom_call" | custom-call | tf_op jit(solution)/shard_map/heads/pallas_call | solution.py:197
  87.9 12.8 %all_to_all.48 = bf16[4,96,512]{2,1,0:T(8,128)(2,1)S(1)} all-to-all(bf16[4,96,512]{2,1,0:T(8,128)(2,1)S(1)} %get-tuple-element.35), channel_id=1, replica_groups=mesh['y'=8,'zh'=3,'core'=2,'x'=4,'zl'=4] {'zl'}, dimensions={0} | all-to-all | bytes 786432 | tf_op jit(solution)/shard_map/all_to_all | solution.py:209
  100.7 0.1 broadcast_in_dim.9
  100.8 20.9 %all_to_all.49 = bf16[4,384,512]{2,1,0:T(8,128)(2,1)S(1)} all-to-all(bf16[4,384,512]{2,1,0:T(8,128)(2,1)S(1)} %broadcast_in_dim.9), channel_id=1, replica_groups=mesh['y'=8,'zh'=3,'core'=2,'x'=4,'zl'=4] {'x'}, dimensions={0} | all-to-all | bytes 3145728 | tf_op jit(solution)/shard_map/all_to_all | solution.py:209
  121.7 0.6 weight.1
  122.2 0.0 copy-start.2
  122.3 0.9 copy-done.2
  123.2 0.0 copy-start.1
  123.2 9.0 %all-to-all-start.5 = ((bf16[48,32,256]{2,1,0:T(8,128)(2,1)}), bf16[48,32,256]{2,1,0:T(8,128)(2,1)}, u32[]{:S(2)}, u32[]{:S(2)}) async-start(bf16[48,32,256]{2,1,0:T(8,128)(2,1)} %bitcast.21), calls=%async_computation.5 | async-start | bytes 1572864 | tf_op jit(solution)/shard_map/all_to_all | solution.py:209
  132.2 0.0 copy-done.1
  132.2 0.1 constant_dynamic-slice_fusion
  132.3 1.2 mixed.1
  133.5 2.3 %collective-permute-start.1 = (f32[256,256]{1,0:T(8,128)S(1)}, f32[256,256]{1,0:T(8,128)S(1)}, u32[]{:S(2)}, u32[]{:S(2)}) collective-permute-start(f32[256,256]{1,0:T(8,128)S(1)} %get-tuple-element.37), channel_id=1, source_target_pairs={{0,16},{16,0},{1,17},{17,1},{2,18},{18,2},{3,19},{19,3},{4,20},{20... | collective-permute-start | bytes 786440 | tf_op jit(solution)/shard_map/ppermute | solution.py:218
  135.8 2.0 %collective-permute-start.2 = (bf16[192,256]{1,0:T(8,128)(2,1)S(1)}, bf16[192,256]{1,0:T(8,128)(2,1)S(1)}, u32[]{:S(2)}, u32[]{:S(2)}) collective-permute-start(bf16[192,256]{1,0:T(8,128)(2,1)S(1)} %get-tuple-element.39), channel_id=1, source_target_pairs={{0,16},{16,0},{1,17},{17,1},{2,18},{18,2},{3,19},{19,3},{4,20},{20... | collective-permute-start | bytes 294920 | tf_op jit(solution)/shard_map/ppermute | solution.py:218
  137.8 1.2 collective-permute-done.2.gr_ref
  139.0 0.0 collective-permute-done.1.mr_ref
  139.0 1.3 finish.1
  140.3 22.3 %all-to-all-done.5.refs_0_ = bf16[48,32,256]{2,1,0:T(8,128)(2,1)} async-done(((bf16[48,32,256]{2,1,0:T(8,128)(2,1)}), bf16[48,32,256]{2,1,0:T(8,128)(2,1)}, u32[]{:S(2)}, u32[]{:S(2)}) %all-to-all-start.5) | async-done | bytes 786464 | tf_op jit(solution)/shard_map/all_to_all | solution.py:209
  162.6 1.9 %total.1 = f32[64,256]{1,0:T(8,128)} custom-call(bf16[48,32,256]{2,1,0:T(8,128)(2,1)} %all-to-all-done.5.refs_0_), custom_call_target="tpu_custom_call" | custom-call | tf_op jit(solution)/shard_map/total/pallas_call | solution.py:197
  (1 shorter events, 0.0 us)
Async XLA Ops:
  0.6 1.4 copy-start
  2.0 0.9 copy-start.3
  21.0 17.4 %copy-start.4 = (bf16[256,256]{1,0:T(8,128)(2,1)S(1)}, bf16[256,256]{1,0:T(8,128)(2,1)}, u32[]{:S(2)}) copy-start(bf16[256,256]{1,0:T(8,128)(2,1)} %g_ref.3) | copy-start | bytes 393220
  21.0 17.4 %copy-start.5 = (bf16[192,256]{1,0:T(8,128)(2,1)S(1)}, bf16[192,256]{1,0:T(8,128)(2,1)}, u32[]{:S(2)}) copy-start(bf16[192,256]{1,0:T(8,128)(2,1)} %i_ref.3) | copy-start | bytes 294916
  21.0 17.4 %copy-start.6 = (bf16[192,256]{1,0:T(8,128)(2,1)S(1)}, bf16[192,256]{1,0:T(8,128)(2,1)}, u32[]{:S(2)}) copy-start(bf16[192,256]{1,0:T(8,128)(2,1)} %v_ref.3) | copy-start | bytes 294916
  21.0 17.4 %copy-start.7 = (bf16[192,256]{1,0:T(8,128)(2,1)S(1)}, bf16[192,256]{1,0:T(8,128)(2,1)}, u32[]{:S(2)}) copy-start(bf16[192,256]{1,0:T(8,128)(2,1)} %o_ref.1) | copy-start | bytes 294916
  21.0 20.0 %copy-start.8 = (f32[192,16]{0,1:T(8,128)S(1)}, f32[192,16]{0,1:T(8,128)}, u32[]{:S(2)}) copy-start(f32[192,16]{0,1:T(8,128)} %param.11) | copy-start | bytes 36868
  21.0 20.0 %copy-start.9 = (f32[192,16]{0,1:T(8,128)S(1)}, f32[192,16]{0,1:T(8,128)}, u32[]{:S(2)}) copy-start(f32[192,16]{0,1:T(8,128)} %param.10) | copy-start | bytes 36868
  22.0 28.1 %all-to-all-start.1 = ((bf16[8,96,256]{2,1,0:T(8,128)(2,1)}), bf16[8,96,256]{2,1,0:T(8,128)(2,1)S(1)}, u32[]{:S(2)}, u32[]{:S(2)}) async-start(bf16[8,96,256]{2,1,0:T(8,128)(2,1)} %bitcast.4), calls=%async_computation.1 | async-start | bytes 786432 | tf_op jit(solution)/shard_map/all_to_all | solution.py:209
  39.0 3.4 %collective-permute-start = (bf16[448,256]{1,0:T(8,128)(2,1)S(1)}, bf16[448,256]{1,0:T(8,128)(2,1)S(1)}, u32[]{:S(2)}, u32[]{:S(2)}) collective-permute-start(bf16[448,256]{1,0:T(8,128)(2,1)S(1)} %get-tuple-element.28), channel_id=1, source_target_pairs={{0,16},{16,0},{1,17},{17,1},{2,18},{18,2},{3,19},{19,3},{4,20},{20... | collective-permute-start | bytes 688136 | tf_op jit(solution)/shard_map/ppermute | solution.py:218
  122.2 0.9 copy-start.2
  123.2 9.0 %copy-start.1 = (bf16[3072,256]{1,0:T(8,128)(2,1)S(1)}, bf16[3072,256]{1,0:T(8,128)(2,1)}, u32[]{:S(2)}) copy-start(bf16[3072,256]{1,0:T(8,128)(2,1)} %w_ref.1) | copy-start | bytes 4718596
  123.2 39.4 %all-to-all-start.5 = ((bf16[48,32,256]{2,1,0:T(8,128)(2,1)}), bf16[48,32,256]{2,1,0:T(8,128)(2,1)}, u32[]{:S(2)}, u32[]{:S(2)}) async-start(bf16[48,32,256]{2,1,0:T(8,128)(2,1)} %bitcast.21), calls=%async_computation.5 | async-start | bytes 1572864 | tf_op jit(solution)/shard_map/all_to_all | solution.py:209
  133.5 5.5 %collective-permute-start.1 = (f32[256,256]{1,0:T(8,128)S(1)}, f32[256,256]{1,0:T(8,128)S(1)}, u32[]{:S(2)}, u32[]{:S(2)}) collective-permute-start(f32[256,256]{1,0:T(8,128)S(1)} %get-tuple-element.37), channel_id=1, source_target_pairs={{0,16},{16,0},{1,17},{17,1},{2,18},{18,2},{3,19},{19,3},{4,20},{20... | collective-permute-start | bytes 786440 | tf_op jit(solution)/shard_map/ppermute | solution.py:218
  135.8 3.2 %collective-permute-start.2 = (bf16[192,256]{1,0:T(8,128)(2,1)S(1)}, bf16[192,256]{1,0:T(8,128)(2,1)S(1)}, u32[]{:S(2)}, u32[]{:S(2)}) collective-permute-start(bf16[192,256]{1,0:T(8,128)(2,1)S(1)} %get-tuple-element.39), channel_id=1, source_target_pairs={{0,16},{16,0},{1,17},{17,1},{2,18},{18,2},{3,19},{19,3},{4,20},{20... | collective-permute-start | bytes 294920 | tf_op jit(solution)/shard_map/ppermute | solution.py:218

commit v4 on v2

v4 whole, which is shorter than its diff:
```python
import math

import jax
import jax.numpy as jnp
from jax import lax
from jax.experimental import pallas as pl
from jax.experimental.pallas import tpu as pltpu
from jax.sharding import Mesh
from jax.sharding import PartitionSpec as P

f32 = jnp.float32
bf16 = jnp.bfloat16
SUB = 32
LANES = 128
CORE, X, ZL, CHIP = "core", "x", "zl", ("y", "zh")


def to_columns(tile):
    rows, width = tile.shape
    pad = jnp.zeros((LANES - rows, width), f32)
    return jnp.concatenate([tile, pad], axis=0).T


def pack_kernel(i_hbm, v_hbm, o_hbm, g_hbm, own_ref, other_ref, i_ref, v_ref, o_ref, g_ref, sems):
    copies = [
        pltpu.make_async_copy(src, dst, sems.at[k])
        for k, (src, dst) in enumerate(
            ((i_hbm, i_ref), (v_hbm, v_ref), (o_hbm, o_ref), (g_hbm, g_ref))
        )
    ]
    for copy in copies:
        copy.start()
    for copy in copies:
        copy.wait()
    tok = g_ref.shape[0]
    half = i_ref.shape[0] // 2
    core = lax.axis_index(CORE)
    for h, ref in ((core, own_ref), (1 - core, other_ref)):
        ref[:tok] = g_ref[...]
        for b in range(half // SUB):
            src = pl.ds(pl.multiple_of(2 * SUB * b + SUB * h, SUB), SUB)
            gated = (i_ref[src, :].astype(f32) * v_ref[src, :].astype(f32)).astype(bf16)
            ref[pl.ds(tok + SUB * b, SUB), :] = gated
            ref[pl.ds(tok + half + SUB * b, SUB), :] = o_ref[src, :]


def both_kernel(own_ref, other_ref, out_ref):
    core = lax.axis_index(CORE)
    out_ref[core] = own_ref[...]
    out_ref[1 - core] = other_ref[...]


def modes_kernel(d_ref, c_ref, od_ref, oc_ref):
    chan = lax.broadcasted_iota(jnp.int32, (d_ref.shape[1], LANES), 0)
    lane = lax.broadcasted_iota(jnp.int32, (d_ref.shape[1], LANES), 1)
    wanted = lane + SUB * (lane // SUB) + SUB * lax.axis_index(CORE)
    pick = jnp.where((chan == wanted) & (lane < d_ref.shape[1] // 2), 1.0, 0.0).astype(f32)
    for src, dst in ((d_ref, od_ref), (c_ref, oc_ref)):
        dst[...] = jnp.dot(
            src[...], pick, precision=lax.Precision.HIGHEST, preferred_element_type=f32
        )


def weight_rows(w_ref, core, block, count):
    blocks = w_ref.shape[0] // (2 * SUB * count)
    rows = []
    for b in range(blocks):
        start = 2 * SUB * (block * blocks + b) + SUB * core
        rows.append(w_ref[pl.ds(pl.multiple_of(start, SUB), SUB), :])
    return jnp.concatenate(rows, axis=0)


def back_kernel(w_ref, got_ref, own_ref, *sent_refs):
    tok = got_ref.shape[2]
    n = 1 + len(sent_refs)
    for k, ref in enumerate((own_ref,) + sent_refs):
        w = weight_rows(w_ref, lax.axis_index(CORE), lax.rem(lax.axis_index(X) + k, n), n)
        for h in range(2):
            part = lax.dot_general(
                w, got_ref[h, :tok], (((1,), (1,)), ((), ())), preferred_element_type=f32
            )
            ref[:, pl.ds(h * tok, tok)] = part.astype(ref.dtype)


def sum_kernel(p0, p1, p2, p3, own_ref, *sent_refs):
    rows = own_ref.shape[0]
    n = 1 + len(sent_refs)
    for k, ref in enumerate((own_ref,) + sent_refs):
        block = lax.rem(lax.axis_index(ZL) + k, n)
        at = pl.ds(pl.multiple_of(block * rows, rows), rows)
        total = p0[at, :] + p1[at, :].astype(f32) + p2[at, :].astype(f32) + p3[at, :].astype(f32)
        ref[...] = total.astype(ref.dtype)


def scan(src, y_ref, rate, coef, reverse):
    length = src.shape[0]

    def step(i, state):
        lo = length - 8 - i * 8 if reverse else i * 8
        at = pl.ds(pl.multiple_of(lo, 8), 8)
        block = src[at, :]
        rows = [None] * 8
        for t in range(8):
            u = 7 - t if reverse else t
            state = state * rate + block[u : u + 1, :]
            rows[u] = jnp.sum(state * coef, axis=0, keepdims=True)
        y_ref[at, :] = jnp.concatenate(rows, axis=0)
        return state

    return lax.fori_loop(0, length // 8, step, jnp.zeros_like(coef))


def heads(y_ref, out, state, rate, reverse):
    length = y_ref.shape[0]

    def step(i, state):
        lo = length - 8 - i * 8 if reverse else i * 8
        at = pl.ds(pl.multiple_of(lo, 8), 8)
        rows = [None] * 8
        for t in range(8):
            u = 7 - t if reverse else t
            state = state * rate
            rows[u] = jnp.sum(state, axis=0, keepdims=True)
        out[at, :] = y_ref[at, :] + jnp.concatenate(rows, axis=0)
        return state

    lax.fori_loop(0, length // 8, step, state)


def scan_forward_kernel(got_ref, d_ref, c_ref, y_ref, s_ref, gt):
    tok = got_ref.shape[2]
    half = (got_ref.shape[1] - tok) // 2
    for h in range(2):
        gt[pl.ds(h * tok, tok), :] = to_columns(got_ref[h, tok : tok + half].astype(f32))
    state = scan(gt, y_ref, jnp.exp(-d_ref[...]), c_ref[...], False)
    for m in range(s_ref.shape[0]):
        s_ref[m] = state


def heads_forward_kernel(s_ref, d_ref, c_ref, y_ref, got_ref, p_ref, f_ref, ft):
    tok = got_ref.shape[2]
    half = f_ref.shape[1]
    decay = d_ref[...]
    jump = jnp.exp(-decay * float(ft.shape[0]))
    state = jnp.zeros_like(decay)
    for m in range(s_ref.shape[0]):
        state = jnp.where(m < lax.axis_index(CHIP), state * jump + s_ref[m], state)
    heads(y_ref, ft, state * c_ref[...], jnp.exp(-decay), False)
    for h in range(2):
        at = pl.ds(h * tok, tok)
        filtered = ft[at, :].T[:half].astype(bf16)
        f_ref[h] = filtered
        product = (got_ref[h, tok + half :].astype(f32) * filtered.astype(f32)).astype(bf16)
        for q in range(p_ref.shape[0]):
            p_ref[q, :, at] = product


def scan_backward_kernel(p0, p1, p2, p3, got_ref, d_ref, c_ref, y_ref, s_ref, b_ref, bt):
    tok = got_ref.shape[2]
    half = p0.shape[0]
    for h in range(2):
        at = pl.ds(h * tok, tok)
        total = p0[:, at] + p1[:, at].astype(f32) + p2[:, at].astype(f32) + p3[:, at].astype(f32)
        b_ref[h] = total
        outer = got_ref[h, tok + half :].astype(f32)
        bt[at, :] = to_columns((total * outer).astype(bf16).astype(f32))
    state = scan(bt, y_ref, jnp.exp(-d_ref[...]), c_ref[...], True)
    first = state.astype(bf16)
    s_ref[:, :LANES] = first
    s_ref[:, LANES:] = (state - first.astype(f32)).astype(bf16)


def weight_kernel(p_ref, got_ref, s_ref, out_ref):
    tok = got_ref.shape[2]
    chips = out_ref.shape[0]
    grads = got_ref[:, :tok, :].reshape(2 * tok, -1)
    part = jnp.dot(p_ref[...], grads, preferred_element_type=f32).astype(bf16)
    out_ref[:, : 2 * SUB, :] = part.reshape(chips, 2 * SUB, -1)
    for m in range(chips):
        out_ref[m, 2 * SUB :, :] = s_ref[...]


def mixed_kernel(p_ref, w_ref, own_ref, other_ref, total):
    tok = own_ref.shape[1]
    total[...] = lax.dot_general(
        weight_rows(w_ref, lax.axis_index(CORE), 0, 1),
        p_ref[...],
        (((0,), (0,)), ((), ())),
        preferred_element_type=f32,
    )
    core = lax.axis_index(CORE)
    own_ref[...] = total[:, pl.ds(pl.multiple_of(core * tok, tok), tok)]
    other_ref[...] = total[:, pl.ds(pl.multiple_of((1 - core) * tok, tok), tok)]


def last_kernel(scale, t_ref, d_ref, c_ref, y_ref, f_ref, b_ref, own_ref, other_ref, bt):
    half, tok = f_ref.shape[1:]
    rows = 2 * SUB
    decay = d_ref[...]
    jump = jnp.exp(-decay * float(2 * tok))
    state = jnp.zeros_like(decay)
    for m in range(t_ref.shape[0] - 1, -1, -1):
        two = t_ref[m, rows:, :].astype(f32)
        state = jnp.where(
            m > lax.axis_index(CHIP), state * jump + (two[:, :LANES] + two[:, LANES:]), state
        )
    heads(y_ref, bt, state * c_ref[...], jnp.exp(-decay), True)
    core = lax.axis_index(CORE)
    for h, ref in ((core, own_ref), (1 - core, other_ref)):
        at = pl.ds(pl.multiple_of(h * tok, tok), tok)
        ref[:half] = bt[at, :].T[:half].astype(bf16).astype(f32)
        ref[half : 2 * half] = (b_ref[h] * f_ref[h].astype(f32)).astype(bf16).astype(f32)
        mine = pl.ds(pl.multiple_of(h * SUB, SUB), SUB)
        total = t_ref[0, mine, :].astype(f32)
        for m in range(1, t_ref.shape[0]):
            total = total + t_ref[m, mine, :].astype(f32)
        ref[2 * half :] = total * scale


def finish_kernel(m_ref, mr_ref, own_ref, other_ref, i_ref, v_ref, mixed_ref, go_ref, gi_ref, gv_ref, gw_ref):
    mixed_ref[...] = (m_ref[...] + mr_ref[...]).T.astype(bf16)
    half = i_ref.shape[0] // 2
    core = lax.axis_index(CORE)
    for h, ref in ((core, own_ref), (1 - core, other_ref)):
        for b in range(half // SUB):
            at = pl.ds(pl.multiple_of(2 * SUB * b + SUB * h, SUB), SUB)
            back = ref[pl.ds(SUB * b, SUB), :]
            go_ref[at, :] = ref[pl.ds(half + SUB * b, SUB), :].astype(bf16)
            gi_ref[at, :] = (back * v_ref[at, :].astype(f32)).astype(bf16)
            gv_ref[at, :] = (back * i_ref[at, :].astype(f32)).astype(bf16)
        gw_ref[pl.ds(pl.multiple_of(SUB * h, SUB), SUB), :] = ref[2 * half :]


def call(kernel, name, outs, args, scratch=(), cost=None):
    specs = [pl.BlockSpec(memory_space=pltpu.VMEM)] * len(args)
    return pl.pallas_call(
        kernel,
        out_shape=tuple(jax.ShapeDtypeStruct(s, t) for s, t in outs),
        in_specs=specs,
        out_specs=tuple([pl.BlockSpec(memory_space=pltpu.VMEM)] * len(outs)),
        scratch_shapes=[pltpu.VMEM(s, f32) for s in scratch],
        compiler_params=pltpu.CompilerParams(vmem_limit_bytes=24 * 2**20),
        cost_estimate=cost,
        name=name,
    )(*args)


LONG = pl.CostEstimate(flops=10**11, bytes_accessed=0, transcendentals=0)


def swap(x, axes):
    return lax.all_to_all(x, axes, 0, 0, tiled=True)


def spread(x, axis):
    n, rows, m = x.shape
    return swap(x.reshape(n * rows, m), axis)


def shift(x, axis, k):
    n = lax.axis_size(axis)
    return lax.ppermute(x, axis, [(i, (i + k) % n) for i in range(n)])


def other_core(x):
    return lax.ppermute(x, "core", [(0, 1), (1, 0)])


def shards(outer_gate, inner_gate, value_proj, residues, decays, out_weight, out_grad):
    chan, tok = outer_gate.shape
    half = chan // 2
    length = 2 * tok
    all_chan, cols = out_weight.shape
    modes = decays.shape[1]
    chips = lax.axis_size(("y", "zh"))
    nx, nz = lax.axis_size("x"), lax.axis_size("zl")

    packed = ((tok + chan, cols), bf16)
    vmem = pl.BlockSpec(memory_space=pltpu.VMEM)
    anywhere = pl.BlockSpec(memory_space=pl.ANY)
    own, other = pl.pallas_call(
        pack_kernel,
        out_shape=(jax.ShapeDtypeStruct(*packed),) * 2,
        in_specs=[anywhere] * 4,
        out_specs=(vmem,) * 2,
        scratch_shapes=[pltpu.VMEM((chan, tok), bf16)] * 3
        + [pltpu.VMEM((tok, cols), bf16), pltpu.SemaphoreType.DMA((4,))],
        name="pack",
    )(inner_gate, value_proj, outer_gate, out_grad)
    (got,) = call(
        both_kernel, "both", [((2, tok + chan, cols), bf16)], (own, other_core(other))
    )
    coef = residues * jnp.sqrt(-jnp.expm1(-2.0 * decays))
    small = ((modes, LANES), f32)
    decay, coef = call(modes_kernel, "modes", [small, small], (decays.T, coef.T))

    rows = nz * half
    parts = call(
        back_kernel,
        "back",
        [((rows, length), f32)] + [((rows, length), bf16)] * (nx - 1),
        (out_weight, got),
    )
    got, own = lax.optimization_barrier((got, parts[0]))
    parts = [own] + [shift(part, "x", k) for k, part in enumerate(parts) if k]
    columns = ((length, LANES), f32)
    yf, states = call(
        scan_forward_kernel,
        "scan_forward",
        [columns, ((chips, modes, LANES), f32)],
        (got, decay, coef),
        scratch=[(length, LANES)],
    )
    states = swap(states, ("y", "zh"))
    parts = call(
        sum_kernel,
        "sum",
        [((half, length), f32)] + [((half, length), bf16)] * (nz - 1),
        parts,
        cost=LONG,
    )
    states, *parts = lax.optimization_barrier((states, *parts))
    product, filtered = call(
        heads_forward_kernel,
        "heads_forward",
        [((nz, half, length), bf16), ((2, half, tok), bf16)],
        (states, decay, coef, yf, got),
        scratch=[(length, LANES)],
    )
    product = spread(product, "zl")

    *parts, product = lax.optimization_barrier((*parts, product))
    parts = [parts[0]] + [shift(part, "zl", k) for k, part in enumerate(parts) if k]
    product = spread(jnp.broadcast_to(product[None], (nx,) + product.shape), "x")
    yb, state, back_sum = call(
        scan_backward_kernel,
        "scan_backward",
        [columns, ((modes, 2 * LANES), bf16), ((2, half, tok), f32)],
        (*parts, got, decay, coef),
        scratch=[(length, LANES)],
    )

    (partial,) = call(
        weight_kernel,
        "weight",
        [((chips, 2 * SUB + modes, cols), bf16)],
        (product, got, state),
    )
    partial = swap(partial, ("y", "zh"))
    mixed, mixed_other = call(
        mixed_kernel,
        "mixed",
        [((cols, tok), f32)] * 2,
        (product, out_weight),
        scratch=[(cols, length)],
    )
    mixed_other = other_core(mixed_other)
    scale = 1.0 / math.sqrt(length * chips)
    own, other = call(
        lambda *refs: last_kernel(scale, *refs),
        "last",
        [((chan + SUB, cols), f32)] * 2,
        (partial, decay, coef, yb, filtered, back_sum),
        scratch=[(length, LANES)],
    )
    return call(
        finish_kernel,
        "finish",
        [((tok, cols), bf16)] + [((chan, tok), bf16)] * 3 + [((2 * SUB, cols), f32)],
        (mixed, mixed_other, own, other_core(other), inner_gate, value_proj),
    )


def solution(mesh):
    fine = Mesh(mesh.devices.reshape(8, 3, 2, 4, 4), ("y", "zh", "core", "x", "zl"))
    seq, col = ("y", "zh", "core"), ("x", "zl")
    return jax.shard_map(
        shards,
        mesh=fine,
        in_specs=(
            P(col, seq),
            P(col, seq),
            P(col, seq),
            P(col, None),
            P(col, None),
            P(None, col),
            P(seq, col),
        ),
        out_specs=(P(seq, col), P(col, seq), P(col, seq), P(col, seq), P(seq, col)),
        check_vma=False,
    )
```

time: 193 us -> 161 us (0.83)
  the two profiles are of different devices: /device:TPU:1 before, /device:TPU:195 now
where the time goes in v4:
time: 161 us; the launch traced here: 160 us
  waiting for transfers between devices  70.5 us (44%)
  starting transfers between devices  52 us (32%)
  Pallas kernels  14.4 us (9%)
  blocking collectives  13.8 us (9%)
  local copies, waits for them, and re-layouts  8.71 us (5%)
    all_to_all x3, waiting for transfers between devices, swap(): return lax.all_to_all(x, axes, 0, 0, tiled=True)  62.4 us
    all_to_all x3, starting transfers between devices, swap(): return lax.all_to_all(x, axes, 0, 0, tiled=True)  25.7 us
    ppermute x6, starting transfers between devices, shift(): return lax.ppermute(x, axis, [(i, (i + k) % n) for i in range(n)])  16.8 us
    all_to_all x1, blocking collectives, swap(): return lax.all_to_all(x, axes, 0, 0, tiled=True)  13.8 us
    pallas_call x11, Pallas kernels, call(): pl.pallas_call(kernel, out_shape=tuple((jax.ShapeDtypeStruct(s, t) for s,...  12.5 us
    ppermute x3, starting transfers between devices, other_core(): return lax.ppermute(x, 'core', [(0, 1), (1, 0)])  9.55 us
    unnamed x30, local copies, waits for them, and re-layouts  7.39 us
    ppermute x6, waiting for transfers between devices, shift(): return lax.ppermute(x, axis, [(i, (i + k) % n) for i in range(n)])  5.65 us
  transfers between devices with their start and end apart: 12, of which 7 were waited for; matrix products, arithmetic and copies ran while one was open for 0% of the time, Pallas kernels for 5%

profile of v4, /device:TPU:195, one launch (start us, length us, event | category | flops | bytes accessed | tf_op | source)
XLA Modules:
  0.0 160.3 jit_solution(12418825557343406550)
XLA Ops:
  0.6 0.0 copy-start.8
  0.6 0.0 copy-start.14
  0.7 1.9 %pack.1 = (bf16[448,256]{1,0:T(8,128)(2,1)}, bf16[448,256]{1,0:T(8,128)(2,1)}) custom-call(bf16[192,256]{1,0:T(8,128)(2,1)} %i_ref.1, bf16[192,256]{1,0:T(8,128)(2,1)} %v_ref.1, bf16[192,256]{1,0:T(8,128)(2,1)} %o_hbm.1, bf16[256,256]{1,0:T(8,128)(2,1)} %g_hbm.1), custom_call_target="tpu_custom_call" | custom-call | tf_op jit(solution)/shard_map/pack/pallas_call | solution.py:281
  2.5 2.6 %collective-permute-start = (bf16[448,256]{1,0:T(8,128)(2,1)}, bf16[448,256]{1,0:T(8,128)(2,1)S(1)}, u32[]{:S(2)}, u32[]{:S(2)}) collective-permute-start(bf16[448,256]{1,0:T(8,128)(2,1)} %get-tuple-element.41), channel_id=1, source_target_pairs={{0,16},{16,0},{1,17},{17,1},{2,18},{18,2},{3,19},{19,3},{4,20},{20... | collective-permute-start | bytes 688136 | tf_op jit(solution)/shard_map/ppermute | solution.py:266
  5.1 1.3 collective-permute-done.other_ref
  6.4 0.0 copy-start.5
  6.4 0.9 copy-done.5
  7.4 0.0 copy-start
  7.4 1.4 copy-done
  8.8 1.3 back.1
  10.2 3.1 %collective-permute-start.1 = (bf16[384,512]{1,0:T(8,128)(2,1)}, bf16[384,512]{1,0:T(8,128)(2,1)S(1)}, u32[]{:S(2)}, u32[]{:S(2)}) collective-permute-start(bf16[384,512]{1,0:T(8,128)(2,1)} %get-tuple-element.48), channel_id=1, source_target_pairs={{0,4},{4,8},{8,12},{12,0},{1,5},{5,9},{9,13},{13,1},{2,6},{6,10},{... | collective-permute-start | bytes 1179656 | tf_op jit(solution)/shard_map/ppermute | solution.py:262
  13.3 2.7 %collective-permute-start.2 = (bf16[384,512]{1,0:T(8,128)(2,1)}, bf16[384,512]{1,0:T(8,128)(2,1)S(1)}, u32[]{:S(2)}, u32[]{:S(2)}) collective-permute-start(bf16[384,512]{1,0:T(8,128)(2,1)} %get-tuple-element.49), channel_id=1, source_target_pairs={{0,8},{4,12},{8,0},{12,4},{1,9},{5,13},{9,1},{13,5},{2,10},{6,14},... | collective-permute-start | bytes 1179656 | tf_op jit(solution)/shard_map/ppermute | solution.py:262
  16.0 3.8 %collective-permute-start.3 = (bf16[384,512]{1,0:T(8,128)(2,1)S(1)}, bf16[384,512]{1,0:T(8,128)(2,1)S(1)}, u32[]{:S(2)}, u32[]{:S(2)}) collective-permute-start(bf16[384,512]{1,0:T(8,128)(2,1)S(1)} %get-tuple-element.50), channel_id=1, source_target_pairs={{0,12},{4,0},{8,4},{12,8},{1,13},{5,1},{9,5},{13,9},{2,14},{6,2},{... | collective-permute-start | bytes 1179656 | tf_op jit(solution)/shard_map/ppermute | solution.py:262
  19.8 0.0 copy-done.8
  19.8 0.0 copy-done.14
  19.9 0.3 modes.1
  20.1 2.7 %scan_forward.1 = (f32[512,128]{1,0:T(8,128)S(1)}, f32[24,16,128]{2,1,0:T(8,128)}) custom-call(bf16[2,448,256]{2,1,0:T(8,128)(2,1)S(1)} %both.1.got_ref, f32[16,128]{1,0:T(8,128)S(1)} %get-tuple-element.44.d_ref.refs_1_, f32[16,128]{1,0:T(8,128)S(1)} %get-tuple-element.45.c_ref.refs_2_), custom_call_target="tpu_custom_call" | custom-call | tf_op jit(solution)/shard_map/scan_forward/pallas_call | solution.py:236
  22.8 16.5 %all-to-all-start = ((f32[24,16,128]{2,1,0:T(8,128)}), f32[24,16,128]{2,1,0:T(8,128)S(1)}, u32[]{:S(2)}, u32[]{:S(2)}) async-start(f32[24,16,128]{2,1,0:T(8,128)} %get-tuple-element.46), calls=%async_computation | async-start | bytes 393216 | tf_op jit(solution)/shard_map/all_to_all | solution.py:252
  39.3 0.0 collective-permute-done.1.p1
  39.3 0.0 collective-permute-done.2.p2
  39.3 0.0 collective-permute-done.3.p3
  39.3 0.0 copy-start.9
  39.3 0.8 copy-done.9
  40.1 0.0 copy-start.10
  40.1 1.0 copy-done.10
  41.1 0.2 sum.1
  41.3 0.0 copy-start.11
  41.3 0.0 copy-start.12
  41.3 0.0 copy-start.13
  41.3 14.6 %all-to-all-done.s_ref = f32[24,16,128]{2,1,0:T(8,128)S(1)} async-done(((f32[24,16,128]{2,1,0:T(8,128)}), f32[24,16,128]{2,1,0:T(8,128)S(1)}, u32[]{:S(2)}, u32[]{:S(2)}) %all-to-all-start) | async-done | bytes 196640 | tf_op jit(solution)/shard_map/all_to_all | solution.py:252
  55.9 1.4 heads_forward.1
  57.3 0.0 copy-start.6
  57.3 13.8 %all_to_all.27 = bf16[4,96,512]{2,1,0:T(8,128)(2,1)S(1)} all-to-all(bf16[4,96,512]{2,1,0:T(8,128)(2,1)S(1)} %get-tuple-element.61), channel_id=1, replica_groups=mesh['y'=8,'zh'=3,'core'=2,'x'=4,'zl'=4] {'zl'}, dimensions={0} | all-to-all | bytes 786432 | tf_op jit(solution)/shard_map/all_to_all | solution.py:252
  71.1 1.3 broadcast_in_dim.2
  72.4 0.0 copy-done.11
  72.4 0.0 copy-done.12
  72.4 0.0 copy-done.13
  72.4 0.0 copy-done.6
  72.4 4.7 %all-to-all-start.2 = ((bf16[4,384,512]{2,1,0:T(8,128)(2,1)}), bf16[4,384,512]{2,1,0:T(8,128)(2,1)S(1)}, u32[]{:S(2)}, u32[]{:S(2)}) async-start(bf16[4,384,512]{2,1,0:T(8,128)(2,1)} %broadcast_in_dim.2), calls=%async_computation.2 | async-start | bytes 3145728 | tf_op jit(solution)/shard_map/all_to_all | solution.py:252
  77.1 2.9 %collective-permute-start.5 = (bf16[96,512]{1,0:T(8,128)(2,1)}, bf16[96,512]{1,0:T(8,128)(2,1)S(1)}, u32[]{:S(2)}, u32[]{:S(2)}) collective-permute-start(bf16[96,512]{1,0:T(8,128)(2,1)} %copy-done.13), channel_id=1, source_target_pairs={{0,1},{1,2},{2,3},{3,0},{4,5},{5,6},{6,7},{7,4},{8,9},{9,10},{10,1... | collective-permute-start | bytes 294920 | tf_op jit(solution)/shard_map/ppermute | solution.py:262
  80.0 1.9 %collective-permute-start.6 = (bf16[96,512]{1,0:T(8,128)(2,1)}, bf16[96,512]{1,0:T(8,128)(2,1)S(1)}, u32[]{:S(2)}, u32[]{:S(2)}) collective-permute-start(bf16[96,512]{1,0:T(8,128)(2,1)} %copy-done.12), channel_id=1, source_target_pairs={{0,2},{1,3},{2,0},{3,1},{4,6},{5,7},{6,4},{7,5},{8,10},{9,11},{10,... | collective-permute-start | bytes 294920 | tf_op jit(solution)/shard_map/ppermute | solution.py:262
  81.9 2.4 %collective-permute-start.7 = (bf16[96,512]{1,0:T(8,128)(2,1)}, bf16[96,512]{1,0:T(8,128)(2,1)S(1)}, u32[]{:S(2)}, u32[]{:S(2)}) collective-permute-start(bf16[96,512]{1,0:T(8,128)(2,1)} %copy-done.11), channel_id=1, source_target_pairs={{0,3},{1,0},{2,1},{3,2},{4,7},{5,4},{6,5},{7,6},{8,11},{9,8},{10,9... | collective-permute-start | bytes 294920 | tf_op jit(solution)/shard_map/ppermute | solution.py:262
  84.3 0.0 collective-permute-done.5.p1
  84.3 3.2 %collective-permute-done.6.p2 = bf16[96,512]{1,0:T(8,128)(2,1)S(1)} collective-permute-done((bf16[96,512]{1,0:T(8,128)(2,1)}, bf16[96,512]{1,0:T(8,128)(2,1)S(1)}, u32[]{:S(2)}, u32[]{:S(2)}) %collective-permute-start.6) | collective-permute-done | bytes 98336 | tf_op jit(solution)/shard_map/ppermute | solution.py:262
  87.5 2.5 %collective-permute-done.7.p3 = bf16[96,512]{1,0:T(8,128)(2,1)S(1)} collective-permute-done((bf16[96,512]{1,0:T(8,128)(2,1)}, bf16[96,512]{1,0:T(8,128)(2,1)S(1)}, u32[]{:S(2)}, u32[]{:S(2)}) %collective-permute-start.7) | collective-permute-done | bytes 98336 | tf_op jit(solution)/shard_map/ppermute | solution.py:262
  89.9 2.2 %scan_backward.1 = (f32[512,128]{1,0:T(8,128)S(1)}, bf16[16,256]{1,0:T(8,128)(2,1)S(1)}, f32[2,96,256]{2,1,0:T(8,128)S(1)}) custom-call(f32[96,512]{1,0:T(8,128)S(1)} %get-tuple-element.65.p0, bf16[96,512]{1,0:T(8,128)(2,1)S(1)} %collective-permute-done.5.p1, bf16[96,512]{1,0:T(8,128)(2,1)S(1)} %collective-permute-done.6.p2, ...), custom_call_target="tpu_custom_call" | custom-call | tf_op jit(solution)/shard_map/scan_backward/pallas_call | solution.py:236
  92.1 3.4 %all-to-all-done.2 = bf16[4,384,512]{2,1,0:T(8,128)(2,1)S(1)} async-done(((bf16[4,384,512]{2,1,0:T(8,128)(2,1)}), bf16[4,384,512]{2,1,0:T(8,128)(2,1)S(1)}, u32[]{:S(2)}, u32[]{:S(2)}) %all-to-all-start.2) | async-done | bytes 1572896 | tf_op jit(solution)/shard_map/all_to_all | solution.py:252
  95.5 0.6 weight.1
  96.1 0.0 copy-start.2
  96.1 1.0 copy-done.2
  97.1 4.5 %all-to-all-start.3 = ((bf16[24,80,256]{2,1,0:T(8,128)(2,1)}), bf16[24,80,256]{2,1,0:T(8,128)(2,1)S(1)}, u32[]{:S(2)}, u32[]{:S(2)}) async-start(bf16[24,80,256]{2,1,0:T(8,128)(2,1)} %copy-done.2), calls=%async_computation.3 | async-start | bytes 1966080 | tf_op jit(solution)/shard_map/all_to_all | solution.py:252
  101.6 0.0 copy-start.1
  101.6 1.4 copy-done.1
  103.0 1.4 mixed.1
  104.4 4.2 %collective-permute-start.4 = (f32[256,256]{1,0:T(8,128)}, f32[256,256]{1,0:T(8,128)S(1)}, u32[]{:S(2)}, u32[]{:S(2)}) collective-permute-start(f32[256,256]{1,0:T(8,128)} %get-tuple-element.64), channel_id=1, source_target_pairs={{0,16},{16,0},{1,17},{17,1},{2,18},{18,2},{3,19},{19,3},{4,20},{20... | collective-permute-start | bytes 786440 | tf_op jit(solution)/shard_map/ppermute | solution.py:266
  108.6 44.4 %all-to-all-done.3.refs_0_ = bf16[24,80,256]{2,1,0:T(8,128)(2,1)S(1)} async-done(((bf16[24,80,256]{2,1,0:T(8,128)(2,1)}), bf16[24,80,256]{2,1,0:T(8,128)(2,1)S(1)}, u32[]{:S(2)}, u32[]{:S(2)}) %all-to-all-start.3) | async-done | bytes 983072 | tf_op jit(solution)/shard_map/all_to_all | solution.py:252
  153.0 0.9 copy-done.7
  153.9 1.7 %last.1 = (f32[224,256]{1,0:T(8,128)S(1)}, f32[224,256]{1,0:T(8,128)S(1)}) custom-call(bf16[24,80,256]{2,1,0:T(8,128)(2,1)S(1)} %all-to-all-done.3.refs_0_, f32[16,128]{1,0:T(8,128)S(1)} %get-tuple-element.44.d_ref.refs_1_, f32[16,128]{1,0:T(8,128)S(1)} %get-tuple-element.45.c_ref.refs_2_, f32[512,128]{1,0:T(8,128)S(1)} %get-tuple-element.70.refs_3_, ...), custom_call_target="tpu_custom_call" | custom-call | tf_op jit(solution)/shard_map/last/pallas_call | solution.py:236
  155.6 2.7 %collective-permute-start.8 = (f32[224,256]{1,0:T(8,128)S(1)}, f32[224,256]{1,0:T(8,128)S(1)}, u32[]{:S(2)}, u32[]{:S(2)}) collective-permute-start(f32[224,256]{1,0:T(8,128)S(1)} %get-tuple-element.74), channel_id=1, source_target_pairs={{0,16},{16,0},{1,17},{17,1},{2,18},{18,2},{3,19},{19,3},{4,20},{20... | collective-permute-start | bytes 688136 | tf_op jit(solution)/shard_map/ppermute | solution.py:266
  158.4 0.0 collective-permute-done.4.mr_ref
  158.4 1.1 collective-permute-done.8.other_ref
  159.5 0.0 copy-done.3
  159.5 0.0 copy-done.4
  159.5 0.8 finish.1
  (5 shorter events, 0.1 us)
Async XLA Ops:
  0.6 19.2 %copy-start.8 = (f32[192,16]{0,1:T(8,128)S(1)}, f32[192,16]{0,1:T(8,128)}, u32[]{:S(2)}) copy-start(f32[192,16]{0,1:T(8,128)} %param.11) | copy-start | bytes 36868
  0.6 19.2 %copy-start.14 = (f32[192,16]{0,1:T(8,128)S(1)}, f32[192,16]{0,1:T(8,128)}, u32[]{:S(2)}) copy-start(f32[192,16]{0,1:T(8,128)} %param.10) | copy-start | bytes 36868
  2.5 3.9 %collective-permute-start = (bf16[448,256]{1,0:T(8,128)(2,1)}, bf16[448,256]{1,0:T(8,128)(2,1)S(1)}, u32[]{:S(2)}, u32[]{:S(2)}) collective-permute-start(bf16[448,256]{1,0:T(8,128)(2,1)} %get-tuple-element.41), channel_id=1, source_target_pairs={{0,16},{16,0},{1,17},{17,1},{2,18},{18,2},{3,19},{19,3},{4,20},{20... | collective-permute-start | bytes 688136 | tf_op jit(solution)/shard_map/ppermute | solution.py:266
  6.4 0.9 copy-start.5
  7.4 1.4 copy-start
  10.2 29.1 %collective-permute-start.1 = (bf16[384,512]{1,0:T(8,128)(2,1)}, bf16[384,512]{1,0:T(8,128)(2,1)S(1)}, u32[]{:S(2)}, u32[]{:S(2)}) collective-permute-start(bf16[384,512]{1,0:T(8,128)(2,1)} %get-tuple-element.48), channel_id=1, source_target_pairs={{0,4},{4,8},{8,12},{12,0},{1,5},{5,9},{9,13},{13,1},{2,6},{6,10},{... | collective-permute-start | bytes 1179656 | tf_op jit(solution)/shard_map/ppermute | solution.py:262
  13.3 26.0 %collective-permute-start.2 = (bf16[384,512]{1,0:T(8,128)(2,1)}, bf16[384,512]{1,0:T(8,128)(2,1)S(1)}, u32[]{:S(2)}, u32[]{:S(2)}) collective-permute-start(bf16[384,512]{1,0:T(8,128)(2,1)} %get-tuple-element.49), channel_id=1, source_target_pairs={{0,8},{4,12},{8,0},{12,4},{1,9},{5,13},{9,1},{13,5},{2,10},{6,14},... | collective-permute-start | bytes 1179656 | tf_op jit(solution)/shard_map/ppermute | solution.py:262
  16.0 23.3 %collective-permute-start.3 = (bf16[384,512]{1,0:T(8,128)(2,1)S(1)}, bf16[384,512]{1,0:T(8,128)(2,1)S(1)}, u32[]{:S(2)}, u32[]{:S(2)}) collective-permute-start(bf16[384,512]{1,0:T(8,128)(2,1)S(1)} %get-tuple-element.50), channel_id=1, source_target_pairs={{0,12},{4,0},{8,4},{12,8},{1,13},{5,1},{9,5},{13,9},{2,14},{6,2},{... | collective-permute-start | bytes 1179656 | tf_op jit(solution)/shard_map/ppermute | solution.py:262
  22.8 33.1 %all-to-all-start = ((f32[24,16,128]{2,1,0:T(8,128)}), f32[24,16,128]{2,1,0:T(8,128)S(1)}, u32[]{:S(2)}, u32[]{:S(2)}) async-start(f32[24,16,128]{2,1,0:T(8,128)} %get-tuple-element.46), calls=%async_computation | async-start | bytes 393216 | tf_op jit(solution)/shard_map/all_to_all | solution.py:252
  39.3 0.8 copy-start.9
  40.1 1.0 copy-start.10
  41.3 31.1 %copy-start.11 = (bf16[96,512]{1,0:T(8,128)(2,1)}, bf16[96,512]{1,0:T(8,128)(2,1)S(1)}, u32[]{:S(2)}) copy-start(bf16[96,512]{1,0:T(8,128)(2,1)S(1)} %get-tuple-element.68) | copy-start | bytes 294916
  41.3 31.1 %copy-start.12 = (bf16[96,512]{1,0:T(8,128)(2,1)}, bf16[96,512]{1,0:T(8,128)(2,1)S(1)}, u32[]{:S(2)}) copy-start(bf16[96,512]{1,0:T(8,128)(2,1)S(1)} %get-tuple-element.67) | copy-start | bytes 294916
  41.3 31.1 %copy-start.13 = (bf16[96,512]{1,0:T(8,128)(2,1)}, bf16[96,512]{1,0:T(8,128)(2,1)S(1)}, u32[]{:S(2)}) copy-start(bf16[96,512]{1,0:T(8,128)(2,1)S(1)} %get-tuple-element.66) | copy-start | bytes 294916
  57.3 15.1 %copy-start.6 = (bf16[2,96,256]{2,1,0:T(8,128)(2,1)}, bf16[2,96,256]{2,1,0:T(8,128)(2,1)S(1)}, u32[]{:S(2)}) copy-start(bf16[2,96,256]{2,1,0:T(8,128)(2,1)S(1)} %get-tuple-element.71.refs_4_) | copy-start | bytes 294916
  72.4 23.1 %all-to-all-start.2 = ((bf16[4,384,512]{2,1,0:T(8,128)(2,1)}), bf16[4,384,512]{2,1,0:T(8,128)(2,1)S(1)}, u32[]{:S(2)}, u32[]{:S(2)}) async-start(bf16[4,384,512]{2,1,0:T(8,128)(2,1)} %broadcast_in_dim.2), calls=%async_computation.2 | async-start | bytes 3145728 | tf_op jit(solution)/shard_map/all_to_all | solution.py:252
  77.1 7.2 %collective-permute-start.5 = (bf16[96,512]{1,0:T(8,128)(2,1)}, bf16[96,512]{1,0:T(8,128)(2,1)S(1)}, u32[]{:S(2)}, u32[]{:S(2)}) collective-permute-start(bf16[96,512]{1,0:T(8,128)(2,1)} %copy-done.13), channel_id=1, source_target_pairs={{0,1},{1,2},{2,3},{3,0},{4,5},{5,6},{6,7},{7,4},{8,9},{9,10},{10,1... | collective-permute-start | bytes 294920 | tf_op jit(solution)/shard_map/ppermute | solution.py:262
  80.0 7.5 %collective-permute-start.6 = (bf16[96,512]{1,0:T(8,128)(2,1)}, bf16[96,512]{1,0:T(8,128)(2,1)S(1)}, u32[]{:S(2)}, u32[]{:S(2)}) collective-permute-start(bf16[96,512]{1,0:T(8,128)(2,1)} %copy-done.12), channel_id=1, source_target_pairs={{0,2},{1,3},{2,0},{3,1},{4,6},{5,7},{6,4},{7,5},{8,10},{9,11},{10,... | collective-permute-start | bytes 294920 | tf_op jit(solution)/shard_map/ppermute | solution.py:262
  81.9 8.1 %collective-permute-start.7 = (bf16[96,512]{1,0:T(8,128)(2,1)}, bf16[96,512]{1,0:T(8,128)(2,1)S(1)}, u32[]{:S(2)}, u32[]{:S(2)}) collective-permute-start(bf16[96,512]{1,0:T(8,128)(2,1)} %copy-done.11), channel_id=1, source_target_pairs={{0,3},{1,0},{2,1},{3,2},{4,7},{5,4},{6,5},{7,6},{8,11},{9,8},{10,9... | collective-permute-start | bytes 294920 | tf_op jit(solution)/shard_map/ppermute | solution.py:262
  96.1 1.0 copy-start.2
  97.1 56.0 %all-to-all-start.3 = ((bf16[24,80,256]{2,1,0:T(8,128)(2,1)}), bf16[24,80,256]{2,1,0:T(8,128)(2,1)S(1)}, u32[]{:S(2)}, u32[]{:S(2)}) async-start(bf16[24,80,256]{2,1,0:T(8,128)(2,1)} %copy-done.2), calls=%async_computation.3 | async-start | bytes 1966080 | tf_op jit(solution)/shard_map/all_to_all | solution.py:252
  101.6 1.4 copy-start.1
  103.0 56.5 %copy-start.3 = (bf16[192,256]{1,0:T(8,128)(2,1)S(1)}, bf16[192,256]{1,0:T(8,128)(2,1)}, u32[]{:S(2)}) copy-start(bf16[192,256]{1,0:T(8,128)(2,1)} %i_ref.1) | copy-start | bytes 294916
  103.0 56.5 %copy-start.4 = (bf16[192,256]{1,0:T(8,128)(2,1)S(1)}, bf16[192,256]{1,0:T(8,128)(2,1)}, u32[]{:S(2)}) copy-start(bf16[192,256]{1,0:T(8,128)(2,1)} %v_ref.1) | copy-start | bytes 294916
  104.4 54.0 %collective-permute-start.4 = (f32[256,256]{1,0:T(8,128)}, f32[256,256]{1,0:T(8,128)S(1)}, u32[]{:S(2)}, u32[]{:S(2)}) collective-permute-start(f32[256,256]{1,0:T(8,128)} %get-tuple-element.64), channel_id=1, source_target_pairs={{0,16},{16,0},{1,17},{17,1},{2,18},{18,2},{3,19},{19,3},{4,20},{20... | collective-permute-start | bytes 786440 | tf_op jit(solution)/shard_map/ppermute | solution.py:266
  153.0 0.9 copy-start.7
  155.6 3.8 %collective-permute-start.8 = (f32[224,256]{1,0:T(8,128)S(1)}, f32[224,256]{1,0:T(8,128)S(1)}, u32[]{:S(2)}, u32[]{:S(2)}) collective-permute-start(f32[224,256]{1,0:T(8,128)S(1)} %get-tuple-element.74), channel_id=1, source_target_pairs={{0,16},{16,0},{1,17},{17,1},{2,18},{18,2},{3,19},{19,3},{4,20},{20... | collective-permute-start | bytes 688136 | tf_op jit(solution)/shard_map/ppermute | solution.py:266

commit v5 on v4

--- a/solution.py
+++ b/solution.py
@@ -12,7 +12,7 @@
 bf16 = jnp.bfloat16
 SUB = 32
 LANES = 128
-CORE, X, ZL, CHIP = "core", "x", "zl", ("y", "zh")
+CORE, ZL, Y, ZH, CHIP = "core", "zl", "y", "zh", ("y", "zh")
 
 
 def to_columns(tile):
@@ -70,26 +70,37 @@
     return jnp.concatenate(rows, axis=0)
 
 
-def back_kernel(w_ref, got_ref, own_ref, *sent_refs):
-    tok = got_ref.shape[2]
-    n = 1 + len(sent_refs)
-    for k, ref in enumerate((own_ref,) + sent_refs):
-        w = weight_rows(w_ref, lax.axis_index(CORE), lax.rem(lax.axis_index(X) + k, n), n)
-        for h in range(2):
-            part = lax.dot_general(
-                w, got_ref[h, :tok], (((1,), (1,)), ((), ())), preferred_element_type=f32
-            )
-            ref[:, pl.ds(h * tok, tok)] = part.astype(ref.dtype)
-
-
-def sum_kernel(p0, p1, p2, p3, own_ref, *sent_refs):
-    rows = own_ref.shape[0]
-    n = 1 + len(sent_refs)
-    for k, ref in enumerate((own_ref,) + sent_refs):
-        block = lax.rem(lax.axis_index(ZL) + k, n)
-        at = pl.ds(pl.multiple_of(block * rows, rows), rows)
-        total = p0[at, :] + p1[at, :].astype(f32) + p2[at, :].astype(f32) + p3[at, :].astype(f32)
-        ref[...] = total.astype(ref.dtype)
+def back_kernel(w_ref, g_ref, out_ref):
+    chan = 6 * SUB
+    grads = g_ref[...]
+    for j in range(w_ref.shape[0] // chan):
+        part = lax.dot_general(
+            w_ref[pl.ds(j * chan, chan), :],
+            grads,
+            (((1,), (1,)), ((), ())),
+            preferred_element_type=f32,
+        ).astype(bf16)
+        for b in range(6):
+            dst = j * chan + (b % 2) * 3 * SUB + (b // 2) * SUB
+            out_ref[pl.ds(dst, SUB), :] = part[b * SUB : (b + 1) * SUB]
+
+
+def split_kernel(p_ref, *outs):
+    rows = p_ref.shape[0] // len(outs)
+    for k, ref in enumerate(outs):
+        block = lax.rem(lax.axis_index(ZL) + k, len(outs))
+        ref[...] = p_ref[pl.ds(pl.multiple_of(block * rows, rows), rows), :]
+
+
+def sum_kernel(p0, p1, p2, p3, own_ref, other_ref):
+    half = own_ref.shape[0]
+    core = lax.axis_index(CORE)
+    for h, ref in ((core, own_ref), (1 - core, other_ref)):
+        at = pl.ds(pl.multiple_of(h * half, half), half)
+        total = p0[at, :].astype(f32)
+        for p in (p1, p2, p3):
+            total = total + p[at, :].astype(f32)
+        ref[...] = total
 
 
 def scan(src, y_ref, rate, coef, reverse):
@@ -155,29 +166,64 @@
             p_ref[q, :, at] = product
 
 
-def scan_backward_kernel(p0, p1, p2, p3, got_ref, d_ref, c_ref, y_ref, s_ref, b_ref, bt):
+def scan_backward_kernel(own_ref, other_ref, got_ref, d_ref, c_ref, y_ref, s_ref, b_ref, bt):
     tok = got_ref.shape[2]
-    half = p0.shape[0]
+    half = own_ref.shape[0]
+    core = lax.axis_index(CORE)
+    b_ref[core] = own_ref[...]
+    b_ref[1 - core] = other_ref[...]
     for h in range(2):
-        at = pl.ds(h * tok, tok)
-        total = p0[:, at] + p1[:, at].astype(f32) + p2[:, at].astype(f32) + p3[:, at].astype(f32)
-        b_ref[h] = total
         outer = got_ref[h, tok + half :].astype(f32)
-        bt[at, :] = to_columns((total * outer).astype(bf16).astype(f32))
+        bt[pl.ds(h * tok, tok), :] = to_columns((b_ref[h] * outer).astype(bf16).astype(f32))
     state = scan(bt, y_ref, jnp.exp(-d_ref[...]), c_ref[...], True)
+    put_state(s_ref, state)
+
+
+def put_state(ref, state):
     first = state.astype(bf16)
-    s_ref[:, :LANES] = first
-    s_ref[:, LANES:] = (state - first.astype(f32)).astype(bf16)
+    ref[:, :LANES] = first
+    ref[:, LANES:] = (state - first.astype(f32)).astype(bf16)
+
+
+def get_state(ref):
+    both = ref.astype(f32)
+    return both[:, :LANES] + both[:, LANES:]
 
 
 def weight_kernel(p_ref, got_ref, s_ref, out_ref):
     tok = got_ref.shape[2]
-    chips = out_ref.shape[0]
+    n = out_ref.shape[0]
+    rows = p_ref.shape[0] // n
     grads = got_ref[:, :tok, :].reshape(2 * tok, -1)
-    part = jnp.dot(p_ref[...], grads, preferred_element_type=f32).astype(bf16)
-    out_ref[:, : 2 * SUB, :] = part.reshape(chips, 2 * SUB, -1)
-    for m in range(chips):
-        out_ref[m, 2 * SUB :, :] = s_ref[...]
+    for y in range(n):
+        part = jnp.dot(p_ref[pl.ds(y * rows, rows), :], grads, preferred_element_type=f32)
+        out_ref[y, :rows, :] = part.astype(bf16)
+        out_ref[y, rows:, :] = s_ref[...]
+
+
+def middle_kernel(t_ref, d_ref, out_ref):
+    n = t_ref.shape[0]
+    zs, rows = out_ref.shape[0], 2 * SUB
+    length = 2.0 * t_ref.shape[2]
+    decay = d_ref[...]
+    y, zh = lax.axis_index(Y), lax.axis_index(ZH)
+    jump = jnp.exp(-decay * (zs * length))
+    later = jnp.zeros_like(decay)
+    here = jnp.zeros_like(decay)
+    for k in range(n - 1, -1, -1):
+        state = get_state(t_ref[k, zs * rows :, :])
+        later = jnp.where(k > y, later * jump + state, later)
+        here = jnp.where(k == y, state, here)
+    for z in range(zs):
+        total = t_ref[0, pl.ds(z * rows, rows), :].astype(f32)
+        for k in range(1, n):
+            total = total + t_ref[k, pl.ds(z * rows, rows), :].astype(f32)
+        out_ref[z, :rows, :] = total.astype(bf16)
+        far = (zs - 1 + zh - z).astype(f32) * length
+        near = jnp.maximum(zh - z - 1, 0).astype(f32) * length
+        carry = jnp.exp(-decay * far) * later
+        carry = jnp.where(zh > z, carry + jnp.exp(-decay * near) * here, carry)
+        put_state(out_ref.at[z, rows:, :], carry)
 
 
 def mixed_kernel(p_ref, w_ref, own_ref, other_ref, total):
@@ -197,13 +243,9 @@
     half, tok = f_ref.shape[1:]
     rows = 2 * SUB
     decay = d_ref[...]
-    jump = jnp.exp(-decay * float(2 * tok))
-    state = jnp.zeros_like(decay)
-    for m in range(t_ref.shape[0] - 1, -1, -1):
-        two = t_ref[m, rows:, :].astype(f32)
-        state = jnp.where(
-            m > lax.axis_index(CHIP), state * jump + (two[:, :LANES] + two[:, LANES:]), state
-        )
+    state = get_state(t_ref[0, rows:, :])
+    for m in range(1, t_ref.shape[0]):
+        state = state + get_state(t_ref[m, rows:, :])
     heads(y_ref, bt, state * c_ref[...], jnp.exp(-decay), True)
     core = lax.axis_index(CORE)
     for h, ref in ((core, own_ref), (1 - core, other_ref)):
@@ -245,9 +287,6 @@
     )(*args)
 
 
-LONG = pl.CostEstimate(flops=10**11, bytes_accessed=0, transcendentals=0)
-
-
 def swap(x, axes):
     return lax.all_to_all(x, axes, 0, 0, tiled=True)
 
@@ -272,8 +311,11 @@
     length = 2 * tok
     all_chan, cols = out_weight.shape
     modes = decays.shape[1]
-    chips = lax.axis_size(("y", "zh"))
-    nx, nz = lax.axis_size("x"), lax.axis_size("zl")
+    ny, nh, nx, nz = (lax.axis_size(axis) for axis in ("y", "zh", "x", "zl"))
+    chips = ny * nh
+
+    (part,) = call(back_kernel, "back", [((all_chan, tok), bf16)], (out_weight, out_grad))
+    part = lax.psum_scatter(part, "x", scatter_dimension=0, tiled=True)
 
     packed = ((tok + chan, cols), bf16)
     vmem = pl.BlockSpec(memory_space=pltpu.VMEM)
@@ -294,15 +336,6 @@
     small = ((modes, LANES), f32)
     decay, coef = call(modes_kernel, "modes", [small, small], (decays.T, coef.T))
 
-    rows = nz * half
-    parts = call(
-        back_kernel,
-        "back",
-        [((rows, length), f32)] + [((rows, length), bf16)] * (nx - 1),
-        (out_weight, got),
-    )
-    got, own = lax.optimization_barrier((got, parts[0]))
-    parts = [own] + [shift(part, "x", k) for k, part in enumerate(parts) if k]
     columns = ((length, LANES), f32)
     yf, states = call(
         scan_forward_kernel,
@@ -312,14 +345,6 @@
         scratch=[(length, LANES)],
     )
     states = swap(states, ("y", "zh"))
-    parts = call(
-        sum_kernel,
-        "sum",
-        [((half, length), f32)] + [((half, length), bf16)] * (nz - 1),
-        parts,
-        cost=LONG,
-    )
-    states, *parts = lax.optimization_barrier((states, *parts))
     product, filtered = call(
         heads_forward_kernel,
         "heads_forward",
@@ -329,24 +354,34 @@
     )
     product = spread(product, "zl")
 
-    *parts, product = lax.optimization_barrier((*parts, product))
-    parts = [parts[0]] + [shift(part, "zl", k) for k, part in enumerate(parts) if k]
+    part, product = lax.optimization_barrier((part, product))
+    own, *parts = call(split_kernel, "split", [((chan, tok), bf16)] * nz, (part,))
+    own, other = call(
+        sum_kernel,
+        "sum",
+        [((half, tok), f32)] * 2,
+        (own, *(shift(part, "zl", k + 1) for k, part in enumerate(parts))),
+    )
     product = spread(jnp.broadcast_to(product[None], (nx,) + product.shape), "x")
     yb, state, back_sum = call(
         scan_backward_kernel,
         "scan_backward",
         [columns, ((modes, 2 * LANES), bf16), ((2, half, tok), f32)],
-        (*parts, got, decay, coef),
+        (own, other_core(other), got, decay, coef),
         scratch=[(length, LANES)],
     )
 
     (partial,) = call(
         weight_kernel,
         "weight",
-        [((chips, 2 * SUB + modes, cols), bf16)],
+        [((ny, nh * 2 * SUB + modes, cols), bf16)],
         (product, got, state),
     )
-    partial = swap(partial, ("y", "zh"))
+    partial = swap(partial, "y")
+    (partial,) = call(
+        middle_kernel, "middle", [((nh, 2 * SUB + modes, cols), bf16)], (partial, decay)
+    )
+    partial = swap(partial, "zh")
     mixed, mixed_other = call(
         mixed_kernel,
         "mixed",

time: 161 us -> 159 us (0.988)
  the two profiles are of different devices: /device:TPU:195 before, /device:TPU:1 now
where the time goes in v5:
time: 159 us; the launch traced here: 158 us
  blocking collectives  67.7 us (43%)
  starting transfers between devices  41.7 us (26%)
  Pallas kernels  14.9 us (9%)
  between operations  14.3 us (9%)
  local copies, waits for them, and re-layouts  11 us (7%)
  waiting for transfers between devices  8.16 us (5%)
    all_to_all x3, blocking collectives, swap(): return lax.all_to_all(x, axes, 0, 0, tiled=True)  67.7 us
    ppermute x4, starting transfers between devices, other_core(): return lax.ppermute(x, 'core', [(0, 1), (1, 0)])  25.2 us
    pallas_call x13, Pallas kernels, call(): pl.pallas_call(kernel, out_shape=tuple((jax.ShapeDtypeStruct(s, t) for s,...  13 us
    unnamed x34, local copies, waits for them, and re-layouts  9.71 us
    ppermute x3, starting transfers between devices, shift(): return lax.ppermute(x, axis, [(i, (i + k) % n) for i in range(n)])  9 us
    all_to_all x2, starting transfers between devices, swap(): return lax.all_to_all(x, axes, 0, 0, tiled=True)  7.48 us
    ppermute x3, waiting for transfers between devices, shift(): return lax.ppermute(x, axis, [(i, (i + k) % n) for i in range(n)])  3.66 us
  transfers between devices with their start and end apart: 10, of which 6 were waited for; matrix products, arithmetic and copies ran while one was open for 0% of the time, Pallas kernels for 7%

profile of v5, /device:TPU:1, one launch (start us, length us, event | category | flops | bytes accessed | tf_op | source)
XLA Modules:
  0.0 157.8 jit_solution(10379234662824282665)
XLA Ops:
  7.2 0.0 reduce-scatter.2.cloned.1.call-start
  7.2 0.0 copy-start
  7.2 1.4 copy-done
  8.6 0.0 copy-start.2
  8.6 0.9 copy-done.2
  9.5 2.0 %back.1 = bf16[3072,256]{1,0:T(8,128)(2,1)} custom-call(bf16[3072,256]{1,0:T(8,128)(2,1)S(1)} %copy-done, bf16[256,256]{1,0:T(8,128)(2,1)S(1)} %copy-done.2), custom_call_target="tpu_custom_call" | custom-call | tf_op jit(solution)/shard_map/back/pallas_call | solution.py:278
  11.5 0.0 copy-start.16
  11.6 0.0 reduce-scatter.2.cloned.1.call-update
  11.6 1.9 %pack.1 = (bf16[448,256]{1,0:T(8,128)(2,1)}, bf16[448,256]{1,0:T(8,128)(2,1)}) custom-call(bf16[192,256]{1,0:T(8,128)(2,1)} %i_ref.1, bf16[192,256]{1,0:T(8,128)(2,1)} %v_ref.1, bf16[192,256]{1,0:T(8,128)(2,1)} %o_hbm.1, bf16[256,256]{1,0:T(8,128)(2,1)} %g_hbm.1), custom_call_target="tpu_custom_call" | custom-call | tf_op jit(solution)/shard_map/pack/pallas_call | solution.py:323
  13.5 12.4 %collective-permute-start = (bf16[448,256]{1,0:T(8,128)(2,1)}, bf16[448,256]{1,0:T(8,128)(2,1)S(1)}, u32[]{:S(2)}, u32[]{:S(2)}) collective-permute-start(bf16[448,256]{1,0:T(8,128)(2,1)} %get-tuple-element.29), channel_id=1, source_target_pairs={{0,16},{16,0},{1,17},{17,1},{2,18},{18,2},{3,19},{19,3},{4,20},{20... | collective-permute-start | bytes 688136 | tf_op jit(solution)/shard_map/ppermute | solution.py:305
  25.9 0.0 copy-done.15
  25.9 0.0 copy-done.16
  26.0 0.3 modes.1
  26.2 1.0 collective-permute-done.other_ref
  27.2 0.0 copy-start.10
  27.2 0.9 copy-done.10
  28.2 2.0 %scan_forward.1 = (f32[512,128]{1,0:T(8,128)S(1)}, f32[24,16,128]{2,1,0:T(8,128)S(1)}) custom-call(bf16[2,448,256]{2,1,0:T(8,128)(2,1)S(1)} %both.1.got_ref, f32[16,128]{1,0:T(8,128)S(1)} %get-tuple-element.30.d_ref.refs_1_, f32[16,128]{1,0:T(8,128)S(1)} %get-tuple-element.31.c_ref.refs_2_), custom_call_target="tpu_custom_call" | custom-call | tf_op jit(solution)/shard_map/scan_forward/pallas_call | solution.py:278
  30.2 22.3 %all_to_all.32.s_ref = f32[24,16,128]{2,1,0:T(8,128)S(1)} all-to-all(f32[24,16,128]{2,1,0:T(8,128)S(1)} %get-tuple-element.32), channel_id=1, replica_groups=mesh['y'=8,'zh'=3,'core'=2,'x'=4,'zl'=4] {'y','zh'}, dimensions={0} | all-to-all | bytes 393216 | tf_op jit(solution)/shard_map/all_to_all | solution.py:291
  52.4 1.4 heads_forward.1
  53.9 0.0 copy-start.13
  53.9 0.6 copy-done.13
  54.5 18.6 %all_to_all.33 = bf16[4,96,512]{2,1,0:T(8,128)(2,1)S(1)} all-to-all(bf16[4,96,512]{2,1,0:T(8,128)(2,1)S(1)} %get-tuple-element.34), channel_id=1, replica_groups=mesh['y'=8,'zh'=3,'core'=2,'x'=4,'zl'=4] {'zl'}, dimensions={0} | all-to-all | bytes 786432 | tf_op jit(solution)/shard_map/all_to_all | solution.py:291
  73.0 0.0 reduce-scatter.2.cloned.1.call-done.p_ref
  73.0 1.3 broadcast_in_dim.2
  74.4 0.0 copy-start.3
  74.4 4.1 %all-to-all-start.2 = ((bf16[4,384,512]{2,1,0:T(8,128)(2,1)}), bf16[4,384,512]{2,1,0:T(8,128)(2,1)S(1)}, u32[]{:S(2)}, u32[]{:S(2)}) async-start(bf16[4,384,512]{2,1,0:T(8,128)(2,1)} %broadcast_in_dim.2), calls=%async_computation.3 | async-start | bytes 3145728 | tf_op jit(solution)/shard_map/all_to_all | solution.py:291
  78.5 0.0 copy-done.3
  78.5 1.9 %collective-permute-start.2 = (bf16[192,256]{1,0:T(8,128)(2,1)S(1)}, bf16[192,256]{1,0:T(8,128)(2,1)S(1)}, u32[]{:S(2)}, u32[]{:S(2)}) collective-permute-start(bf16[192,256]{1,0:T(8,128)(2,1)S(1)} %get-tuple-element.40), channel_id=1, source_target_pairs={{0,1},{1,2},{2,3},{3,0},{4,5},{5,6},{6,7},{7,4},{8,9},{9,10},{10,1... | collective-permute-start | bytes 294920 | tf_op jit(solution)/shard_map/ppermute | solution.py:301
  80.5 4.5 %collective-permute-start.3 = (bf16[192,256]{1,0:T(8,128)(2,1)S(1)}, bf16[192,256]{1,0:T(8,128)(2,1)S(1)}, u32[]{:S(2)}, u32[]{:S(2)}) collective-permute-start(bf16[192,256]{1,0:T(8,128)(2,1)S(1)} %get-tuple-element.41), channel_id=1, source_target_pairs={{0,2},{1,3},{2,0},{3,1},{4,6},{5,7},{6,4},{7,5},{8,10},{9,11},{10,... | collective-permute-start | bytes 294920 | tf_op jit(solution)/shard_map/ppermute | solution.py:301
  84.9 2.6 %collective-permute-start.4 = (bf16[192,256]{1,0:T(8,128)(2,1)S(1)}, bf16[192,256]{1,0:T(8,128)(2,1)S(1)}, u32[]{:S(2)}, u32[]{:S(2)}) collective-permute-start(bf16[192,256]{1,0:T(8,128)(2,1)S(1)} %get-tuple-element.42), channel_id=1, source_target_pairs={{0,3},{1,0},{2,1},{3,2},{4,7},{5,4},{6,5},{7,6},{8,11},{9,8},{10,9... | collective-permute-start | bytes 294920 | tf_op jit(solution)/shard_map/ppermute | solution.py:301
  87.5 0.0 collective-permute-done.2.p1
  87.6 1.9 %collective-permute-done.3.p2 = bf16[192,256]{1,0:T(8,128)(2,1)S(1)} collective-permute-done((bf16[192,256]{1,0:T(8,128)(2,1)S(1)}, bf16[192,256]{1,0:T(8,128)(2,1)S(1)}, u32[]{:S(2)}, u32[]{:S(2)}) %collective-permute-start.3) | collective-permute-done | bytes 98336 | tf_op jit(solution)/shard_map/ppermute | solution.py:301
  89.4 1.8 %collective-permute-done.4.p3 = bf16[192,256]{1,0:T(8,128)(2,1)S(1)} collective-permute-done((bf16[192,256]{1,0:T(8,128)(2,1)S(1)}, bf16[192,256]{1,0:T(8,128)(2,1)S(1)}, u32[]{:S(2)}, u32[]{:S(2)}) %collective-permute-start.4) | collective-permute-done | bytes 98336 | tf_op jit(solution)/shard_map/ppermute | solution.py:301
  91.3 4.5 %collective-permute-start.5 = (f32[96,256]{1,0:T(8,128)S(1)}, f32[96,256]{1,0:T(8,128)S(1)}, u32[]{:S(2)}, u32[]{:S(2)}) collective-permute-start(f32[96,256]{1,0:T(8,128)S(1)} %get-tuple-element.44), channel_id=1, source_target_pairs={{0,16},{16,0},{1,17},{17,1},{2,18},{18,2},{3,19},{19,3},{4,20},{20... | collective-permute-start | bytes 294920 | tf_op jit(solution)/shard_map/ppermute | solution.py:305
  95.7 0.9 collective-permute-done.5.other_ref
  96.7 2.1 %scan_backward.1 = (f32[512,128]{1,0:T(8,128)S(1)}, bf16[16,256]{1,0:T(8,128)(2,1)S(1)}, f32[2,96,256]{2,1,0:T(8,128)S(1)}) custom-call(f32[96,256]{1,0:T(8,128)S(1)} %get-tuple-element.43.own_ref, f32[96,256]{1,0:T(8,128)S(1)} %collective-permute-done.5.other_ref, bf16[2,448,256]{2,1,0:T(8,128)(2,1)S(1)} %both.1.got_ref, ...), custom_call_target="tpu_custom_call" | custom-call | tf_op jit(solution)/shard_map/scan_backward/pallas_call | solution.py:278
  98.8 0.0 copy-start.6
  98.8 0.7 copy-done.6
  99.5 0.0 copy-start.11
  99.5 0.7 copy-done.11
  100.2 0.0 all-to-all-done.2
  100.2 0.6 weight.1
  100.8 0.0 copy-start.1
  100.8 26.9 %all_to_all.34.t_ref = bf16[8,208,256]{2,1,0:T(8,128)(2,1)S(1)} all-to-all(bf16[8,208,256]{2,1,0:T(8,128)(2,1)S(1)} %weight.1), channel_id=1, replica_groups=mesh['y'=8,'zh'=3,'core'=2,'x'=4,'zl'=4] {'y'}, dimensions={0} | all-to-all | bytes 1703936 | tf_op jit(solution)/shard_map/all_to_all | solution.py:291
  127.7 0.8 middle.1
  128.5 3.3 %all-to-all-start.4 = ((bf16[3,80,256]{2,1,0:T(8,128)(2,1)}), bf16[3,80,256]{2,1,0:T(8,128)(2,1)S(1)}, u32[]{:S(2)}, u32[]{:S(2)}) async-start(bf16[3,80,256]{2,1,0:T(8,128)(2,1)} %middle.1), calls=%async_computation.5 | async-start | bytes 245760 | tf_op jit(solution)/shard_map/all_to_all | solution.py:291
  131.8 0.0 copy-done.1
  131.8 0.0 copy-start.4
  131.8 0.0 copy-start.5
  131.8 1.4 mixed.1
  133.2 0.7 copy-done.8
  133.9 3.3 %collective-permute-start.1 = (f32[256,256]{1,0:T(8,128)}, f32[256,256]{1,0:T(8,128)S(1)}, u32[]{:S(2)}, u32[]{:S(2)}) collective-permute-start(f32[256,256]{1,0:T(8,128)} %get-tuple-element.37), channel_id=1, source_target_pairs={{0,16},{16,0},{1,17},{17,1},{2,18},{18,2},{3,19},{19,3},{4,20},{20... | collective-permute-start | bytes 786440 | tf_op jit(solution)/shard_map/ppermute | solution.py:305
  137.3 1.5 all-to-all-done.4.refs_0_
  138.8 0.9 copy-done.7
  139.7 0.9 copy-done.12
  140.6 0.9 copy-done.14
  141.5 1.5 last.1
  143.1 5.0 %collective-permute-start.6 = (f32[224,256]{1,0:T(8,128)S(1)}, f32[224,256]{1,0:T(8,128)S(1)}, u32[]{:S(2)}, u32[]{:S(2)}) collective-permute-start(f32[224,256]{1,0:T(8,128)S(1)} %get-tuple-element.50), channel_id=1, source_target_pairs={{0,16},{16,0},{1,17},{17,1},{2,18},{18,2},{3,19},{19,3},{4,20},{20... | collective-permute-start | bytes 688136 | tf_op jit(solution)/shard_map/ppermute | solution.py:305
  148.0 0.0 collective-permute-done.1.mr_ref
  148.1 1.1 collective-permute-done.6.other_ref
  149.1 0.0 copy-done.4
  149.1 0.0 copy-done.5
  149.2 0.9 copy-done.9
  150.1 0.8 finish.1
  (10 shorter events, 0.2 us)
Async XLA Ops:
  7.2 65.9 %reduce-scatter.2.cloned.1.call-start = ((), (), s32[]{:S(2)}) async-start(), calls=%async_computation.6 | async-start | bytes 1966080 | tf_op jit(solution)/shard_map/reduce_scatter | solution.py:318
  7.2 1.4 copy-start
  8.6 0.9 copy-start.2
  11.5 14.4 %copy-start.15 = (f32[192,16]{0,1:T(8,128)S(1)}, f32[192,16]{0,1:T(8,128)}, u32[]{:S(2)}) copy-start(f32[192,16]{0,1:T(8,128)} %param.11) | copy-start | bytes 36868
  11.5 14.4 %copy-start.16 = (f32[192,16]{0,1:T(8,128)S(1)}, f32[192,16]{0,1:T(8,128)}, u32[]{:S(2)}) copy-start(f32[192,16]{0,1:T(8,128)} %param.10) | copy-start | bytes 36868
  13.5 13.7 %collective-permute-start = (bf16[448,256]{1,0:T(8,128)(2,1)}, bf16[448,256]{1,0:T(8,128)(2,1)S(1)}, u32[]{:S(2)}, u32[]{:S(2)}) collective-permute-start(bf16[448,256]{1,0:T(8,128)(2,1)} %get-tuple-element.29), channel_id=1, source_target_pairs={{0,16},{16,0},{1,17},{17,1},{2,18},{18,2},{3,19},{19,3},{4,20},{20... | collective-permute-start | bytes 688136 | tf_op jit(solution)/shard_map/ppermute | solution.py:305
  27.2 0.9 copy-start.10
  53.9 0.6 copy-start.13
  74.4 4.1 %copy-start.3 = (bf16[768,256]{1,0:T(8,128)(2,1)S(1)}, bf16[768,256]{1,0:T(8,128)(2,1)}, u32[]{:S(2)}) copy-start(bf16[768,256]{1,0:T(8,128)(2,1)} %reduce-scatter.2.cloned.1.call-done.p_ref) | copy-start | bytes 1179652
  74.4 25.8 %all-to-all-start.2 = ((bf16[4,384,512]{2,1,0:T(8,128)(2,1)}), bf16[4,384,512]{2,1,0:T(8,128)(2,1)S(1)}, u32[]{:S(2)}, u32[]{:S(2)}) async-start(bf16[4,384,512]{2,1,0:T(8,128)(2,1)} %broadcast_in_dim.2), calls=%async_computation.3 | async-start | bytes 3145728 | tf_op jit(solution)/shard_map/all_to_all | solution.py:291
  78.5 9.0 %collective-permute-start.2 = (bf16[192,256]{1,0:T(8,128)(2,1)S(1)}, bf16[192,256]{1,0:T(8,128)(2,1)S(1)}, u32[]{:S(2)}, u32[]{:S(2)}) collective-permute-start(bf16[192,256]{1,0:T(8,128)(2,1)S(1)} %get-tuple-element.40), channel_id=1, source_target_pairs={{0,1},{1,2},{2,3},{3,0},{4,5},{5,6},{6,7},{7,4},{8,9},{9,10},{10,1... | collective-permute-start | bytes 294920 | tf_op jit(solution)/shard_map/ppermute | solution.py:301
  80.5 9.0 %collective-permute-start.3 = (bf16[192,256]{1,0:T(8,128)(2,1)S(1)}, bf16[192,256]{1,0:T(8,128)(2,1)S(1)}, u32[]{:S(2)}, u32[]{:S(2)}) collective-permute-start(bf16[192,256]{1,0:T(8,128)(2,1)S(1)} %get-tuple-element.41), channel_id=1, source_target_pairs={{0,2},{1,3},{2,0},{3,1},{4,6},{5,7},{6,4},{7,5},{8,10},{9,11},{10,... | collective-permute-start | bytes 294920 | tf_op jit(solution)/shard_map/ppermute | solution.py:301
  84.9 6.3 %collective-permute-start.4 = (bf16[192,256]{1,0:T(8,128)(2,1)S(1)}, bf16[192,256]{1,0:T(8,128)(2,1)S(1)}, u32[]{:S(2)}, u32[]{:S(2)}) collective-permute-start(bf16[192,256]{1,0:T(8,128)(2,1)S(1)} %get-tuple-element.42), channel_id=1, source_target_pairs={{0,3},{1,0},{2,1},{3,2},{4,7},{5,4},{6,5},{7,6},{8,11},{9,8},{10,9... | collective-permute-start | bytes 294920 | tf_op jit(solution)/shard_map/ppermute | solution.py:301
  91.3 5.4 %collective-permute-start.5 = (f32[96,256]{1,0:T(8,128)S(1)}, f32[96,256]{1,0:T(8,128)S(1)}, u32[]{:S(2)}, u32[]{:S(2)}) collective-permute-start(f32[96,256]{1,0:T(8,128)S(1)} %get-tuple-element.44), channel_id=1, source_target_pairs={{0,16},{16,0},{1,17},{17,1},{2,18},{18,2},{3,19},{19,3},{4,20},{20... | collective-permute-start | bytes 294920 | tf_op jit(solution)/shard_map/ppermute | solution.py:305
  98.8 0.7 copy-start.6
  99.5 0.7 copy-start.11
  100.8 31.0 %copy-start.1 = (bf16[3072,256]{1,0:T(8,128)(2,1)S(1)}, bf16[3072,256]{1,0:T(8,128)(2,1)}, u32[]{:S(2)}) copy-start(bf16[3072,256]{1,0:T(8,128)(2,1)} %w_ref.3) | copy-start | bytes 4718596
  128.5 10.3 %all-to-all-start.4 = ((bf16[3,80,256]{2,1,0:T(8,128)(2,1)}), bf16[3,80,256]{2,1,0:T(8,128)(2,1)S(1)}, u32[]{:S(2)}, u32[]{:S(2)}) async-start(bf16[3,80,256]{2,1,0:T(8,128)(2,1)} %middle.1), calls=%async_computation.5 | async-start | bytes 245760 | tf_op jit(solution)/shard_map/all_to_all | solution.py:291
  131.8 17.3 %copy-start.4 = (bf16[192,256]{1,0:T(8,128)(2,1)S(1)}, bf16[192,256]{1,0:T(8,128)(2,1)}, u32[]{:S(2)}) copy-start(bf16[192,256]{1,0:T(8,128)(2,1)} %i_ref.1) | copy-start | bytes 294916
  131.8 17.3 %copy-start.5 = (bf16[192,256]{1,0:T(8,128)(2,1)S(1)}, bf16[192,256]{1,0:T(8,128)(2,1)}, u32[]{:S(2)}) copy-start(bf16[192,256]{1,0:T(8,128)(2,1)} %v_ref.1) | copy-start | bytes 294916
  133.2 0.7 copy-start.8
  133.9 14.1 %collective-permute-start.1 = (f32[256,256]{1,0:T(8,128)}, f32[256,256]{1,0:T(8,128)S(1)}, u32[]{:S(2)}, u32[]{:S(2)}) collective-permute-start(f32[256,256]{1,0:T(8,128)} %get-tuple-element.37), channel_id=1, source_target_pairs={{0,16},{16,0},{1,17},{17,1},{2,18},{18,2},{3,19},{19,3},{4,20},{20... | collective-permute-start | bytes 786440 | tf_op jit(solution)/shard_map/ppermute | solution.py:305
  138.8 1.0 copy-start.7
  139.7 0.9 copy-start.12
  140.6 0.9 copy-start.14
  143.1 6.1 %collective-permute-start.6 = (f32[224,256]{1,0:T(8,128)S(1)}, f32[224,256]{1,0:T(8,128)S(1)}, u32[]{:S(2)}, u32[]{:S(2)}) collective-permute-start(f32[224,256]{1,0:T(8,128)S(1)} %get-tuple-element.50), channel_id=1, source_target_pairs={{0,16},{16,0},{1,17},{17,1},{2,18},{18,2},{3,19},{19,3},{4,20},{20... | collective-permute-start | bytes 688136 | tf_op jit(solution)/shard_map/ppermute | solution.py:305
  149.1 1.0 copy-start.9
Sparse Core Ops, SparseCore 0:
  11.7 40.3 reduce-scatter.1

commit v6 on v5

--- a/solution.py
+++ b/solution.py
@@ -12,7 +12,7 @@
 bf16 = jnp.bfloat16
 SUB = 32
 LANES = 128
-CORE, ZL, Y, ZH, CHIP = "core", "zl", "y", "zh", ("y", "zh")
+CORE, X, ZL, Y, ZH, CHIP = "core", "x", "zl", "y", "zh", ("y", "zh")
 
 
 def to_columns(tile):
@@ -22,16 +22,7 @@
 
 
 def pack_kernel(i_hbm, v_hbm, o_hbm, g_hbm, own_ref, other_ref, i_ref, v_ref, o_ref, g_ref, sems):
-    copies = [
-        pltpu.make_async_copy(src, dst, sems.at[k])
-        for k, (src, dst) in enumerate(
-            ((i_hbm, i_ref), (v_hbm, v_ref), (o_hbm, o_ref), (g_hbm, g_ref))
-        )
-    ]
-    for copy in copies:
-        copy.start()
-    for copy in copies:
-        copy.wait()
+    fetch(sems, (i_hbm, i_ref), (v_hbm, v_ref), (o_hbm, o_ref), (g_hbm, g_ref))
     tok = g_ref.shape[0]
     half = i_ref.shape[0] // 2
     core = lax.axis_index(CORE)
@@ -44,10 +35,17 @@
             ref[pl.ds(tok + half + SUB * b, SUB), :] = o_ref[src, :]
 
 
-def both_kernel(own_ref, other_ref, out_ref):
-    core = lax.axis_index(CORE)
-    out_ref[core] = own_ref[...]
-    out_ref[1 - core] = other_ref[...]
+def fetch(sems, *pairs):
+    copies = [pltpu.make_async_copy(src, dst, sems.at[k]) for k, (src, dst) in enumerate(pairs)]
+    for copy in copies:
+        copy.start()
+    for copy in copies:
+        copy.wait()
+
+
+def both_kernel(own_hbm, other_hbm, out_ref, sems):
+    core = lax.axis_index(CORE)
+    fetch(sems, (own_hbm, out_ref.at[core]), (other_hbm, out_ref.at[1 - core]))
 
 
 def modes_kernel(d_ref, c_ref, od_ref, oc_ref):
@@ -70,26 +68,32 @@
     return jnp.concatenate(rows, axis=0)
 
 
-def back_kernel(w_ref, g_ref, out_ref):
+def back_kernel(w_ref, g_ref, *outs):
     chan = 6 * SUB
+    n = len(outs)
+    rows = w_ref.shape[0] // n
     grads = g_ref[...]
-    for j in range(w_ref.shape[0] // chan):
-        part = lax.dot_general(
-            w_ref[pl.ds(j * chan, chan), :],
-            grads,
-            (((1,), (1,)), ((), ())),
-            preferred_element_type=f32,
-        ).astype(bf16)
-        for b in range(6):
-            dst = j * chan + (b % 2) * 3 * SUB + (b // 2) * SUB
-            out_ref[pl.ds(dst, SUB), :] = part[b * SUB : (b + 1) * SUB]
-
-
-def split_kernel(p_ref, *outs):
-    rows = p_ref.shape[0] // len(outs)
+    for k, ref in enumerate(outs):
+        block = lax.rem(lax.axis_index(X) + k, n)
+        for j in range(rows // chan):
+            at = pl.ds(pl.multiple_of(block * rows + j * chan, chan), chan)
+            part = lax.dot_general(
+                w_ref[at, :], grads, (((1,), (1,)), ((), ())), preferred_element_type=f32
+            ).astype(bf16)
+            for b in range(6):
+                dst = j * chan + (b % 2) * 3 * SUB + (b // 2) * SUB
+                ref[pl.ds(dst, SUB), :] = part[b * SUB : (b + 1) * SUB]
+
+
+def split_kernel(p0, p1, p2, p3, *outs):
+    rows = p0.shape[0] // len(outs)
     for k, ref in enumerate(outs):
         block = lax.rem(lax.axis_index(ZL) + k, len(outs))
-        ref[...] = p_ref[pl.ds(pl.multiple_of(block * rows, rows), rows), :]
+        at = pl.ds(pl.multiple_of(block * rows, rows), rows)
+        total = p0[at, :].astype(f32)
+        for p in (p1, p2, p3):
+            total = total + p[at, :].astype(f32)
+        ref[...] = total.astype(bf16)
 
 
 def sum_kernel(p0, p1, p2, p3, own_ref, other_ref):
@@ -166,15 +170,16 @@
             p_ref[q, :, at] = product
 
 
-def scan_backward_kernel(own_ref, other_ref, got_ref, d_ref, c_ref, y_ref, s_ref, b_ref, bt):
+def scan_backward_kernel(own_ref, other_ref, f_ref, got_ref, d_ref, c_ref, y_ref, s_ref, go_ref, gx_ref, bt):
     tok = got_ref.shape[2]
     half = own_ref.shape[0]
     core = lax.axis_index(CORE)
-    b_ref[core] = own_ref[...]
-    b_ref[1 - core] = other_ref[...]
-    for h in range(2):
+    for h, ref, out in ((core, own_ref, go_ref), (1 - core, other_ref, gx_ref)):
+        total = ref[...]
+        out[...] = (total * f_ref[h].astype(f32)).astype(bf16)
         outer = got_ref[h, tok + half :].astype(f32)
-        bt[pl.ds(h * tok, tok), :] = to_columns((b_ref[h] * outer).astype(bf16).astype(f32))
+        at = pl.ds(pl.multiple_of(h * tok, tok), tok)
+        bt[at, :] = to_columns((total * outer).astype(bf16).astype(f32))
     state = scan(bt, y_ref, jnp.exp(-d_ref[...]), c_ref[...], True)
     put_state(s_ref, state)
 
@@ -239,52 +244,69 @@
     other_ref[...] = total[:, pl.ds(pl.multiple_of((1 - core) * tok, tok), tok)]
 
 
-def last_kernel(scale, t_ref, d_ref, c_ref, y_ref, f_ref, b_ref, own_ref, other_ref, bt):
-    half, tok = f_ref.shape[1:]
+def last_kernel(scale, d_ref, c_ref, t_hbm, y_hbm, own_ref, other_ref, t_ref, y_ref, bt, sems):
+    fetch(sems, (t_hbm, t_ref), (y_hbm, y_ref))
     rows = 2 * SUB
-    decay = d_ref[...]
+    tok = y_ref.shape[0] // 2
+    half = own_ref.shape[0] - SUB
     state = get_state(t_ref[0, rows:, :])
     for m in range(1, t_ref.shape[0]):
         state = state + get_state(t_ref[m, rows:, :])
-    heads(y_ref, bt, state * c_ref[...], jnp.exp(-decay), True)
-    core = lax.axis_index(CORE)
-    for h, ref in ((core, own_ref), (1 - core, other_ref)):
-        at = pl.ds(pl.multiple_of(h * tok, tok), tok)
-        ref[:half] = bt[at, :].T[:half].astype(bf16).astype(f32)
-        ref[half : 2 * half] = (b_ref[h] * f_ref[h].astype(f32)).astype(bf16).astype(f32)
+    core = lax.axis_index(CORE)
+    for h, ref in ((core, own_ref), (1 - core, other_ref)):
         mine = pl.ds(pl.multiple_of(h * SUB, SUB), SUB)
         total = t_ref[0, mine, :].astype(f32)
         for m in range(1, t_ref.shape[0]):
             total = total + t_ref[m, mine, :].astype(f32)
-        ref[2 * half :] = total * scale
-
-
-def finish_kernel(m_ref, mr_ref, own_ref, other_ref, i_ref, v_ref, mixed_ref, go_ref, gi_ref, gv_ref, gw_ref):
+        ref[half:] = total * scale
+    heads(y_ref, bt, state * c_ref[...], jnp.exp(-d_ref[...]), True)
+    for h, ref in ((core, own_ref), (1 - core, other_ref)):
+        at = pl.ds(pl.multiple_of(h * tok, tok), tok)
+        ref[:half] = bt[at, :].T[:half].astype(bf16).astype(f32)
+
+
+def halves(core, own_ref, other_ref, count):
+    for h, ref in ((core, own_ref), (1 - core, other_ref)):
+        for b in range(count):
+            at = pl.ds(pl.multiple_of(2 * SUB * b + SUB * h, SUB), SUB)
+            yield at, ref, pl.ds(SUB * b, SUB)
+
+
+def finish_kernel(m_ref, mr_ref, own_ref, other_ref, mixed_ref, go_ref):
     mixed_ref[...] = (m_ref[...] + mr_ref[...]).T.astype(bf16)
+    for at, ref, src in halves(lax.axis_index(CORE), own_ref, other_ref, own_ref.shape[0] // SUB):
+        go_ref[at, :] = ref[src, :]
+
+
+def end_kernel(own_hbm, other_hbm, i_hbm, v_hbm, gi_ref, gv_ref, gw_ref, own_ref, other_ref, i_ref, v_ref, sems):
+    fetch(sems, (own_hbm, own_ref), (other_hbm, other_ref), (i_hbm, i_ref), (v_hbm, v_ref))
     half = i_ref.shape[0] // 2
     core = lax.axis_index(CORE)
-    for h, ref in ((core, own_ref), (1 - core, other_ref)):
-        for b in range(half // SUB):
-            at = pl.ds(pl.multiple_of(2 * SUB * b + SUB * h, SUB), SUB)
-            back = ref[pl.ds(SUB * b, SUB), :]
-            go_ref[at, :] = ref[pl.ds(half + SUB * b, SUB), :].astype(bf16)
-            gi_ref[at, :] = (back * v_ref[at, :].astype(f32)).astype(bf16)
-            gv_ref[at, :] = (back * i_ref[at, :].astype(f32)).astype(bf16)
-        gw_ref[pl.ds(pl.multiple_of(SUB * h, SUB), SUB), :] = ref[2 * half :]
-
-
-def call(kernel, name, outs, args, scratch=(), cost=None):
-    specs = [pl.BlockSpec(memory_space=pltpu.VMEM)] * len(args)
+    for at, ref, src in halves(core, own_ref, other_ref, half // SUB):
+        back = ref[src, :]
+        gi_ref[at, :] = (back * v_ref[at, :].astype(f32)).astype(bf16)
+        gv_ref[at, :] = (back * i_ref[at, :].astype(f32)).astype(bf16)
+    for h, ref in ((core, own_ref), (1 - core, other_ref)):
+        gw_ref[pl.ds(pl.multiple_of(SUB * h, SUB), SUB), :] = ref[half:]
+
+
+def call(kernel, name, outs, args, scratch=(), cost=None, remote=0, limit=24):
+    specs = [pl.BlockSpec(memory_space=pltpu.VMEM)] * (len(args) - remote)
+    specs += [pl.BlockSpec(memory_space=pl.ANY)] * remote
     return pl.pallas_call(
         kernel,
         out_shape=tuple(jax.ShapeDtypeStruct(s, t) for s, t in outs),
         in_specs=specs,
         out_specs=tuple([pl.BlockSpec(memory_space=pltpu.VMEM)] * len(outs)),
-        scratch_shapes=[pltpu.VMEM(s, f32) for s in scratch],
-        compiler_params=pltpu.CompilerParams(vmem_limit_bytes=24 * 2**20),
+        scratch_shapes=[pltpu.VMEM(s, t) for s, t in scratch]
+        + ([pltpu.SemaphoreType.DMA((remote,))] if remote else []),
+        compiler_params=None if limit is None else pltpu.CompilerParams(vmem_limit_bytes=limit * 2**20),
         cost_estimate=cost,
         name=name,
     )(*args)
+
+
+LONG = pl.CostEstimate(flops=10**11, bytes_accessed=0, transcendentals=0)
 
 
 def swap(x, axes):
@@ -314,23 +336,19 @@
     ny, nh, nx, nz = (lax.axis_size(axis) for axis in ("y", "zh", "x", "zl"))
     chips = ny * nh
 
-    (part,) = call(back_kernel, "back", [((all_chan, tok), bf16)], (out_weight, out_grad))
-    part = lax.psum_scatter(part, "x", scatter_dimension=0, tiled=True)
-
     packed = ((tok + chan, cols), bf16)
-    vmem = pl.BlockSpec(memory_space=pltpu.VMEM)
-    anywhere = pl.BlockSpec(memory_space=pl.ANY)
-    own, other = pl.pallas_call(
+    gate = ((chan, tok), bf16)
+    own, other = call(
         pack_kernel,
-        out_shape=(jax.ShapeDtypeStruct(*packed),) * 2,
-        in_specs=[anywhere] * 4,
-        out_specs=(vmem,) * 2,
-        scratch_shapes=[pltpu.VMEM((chan, tok), bf16)] * 3
-        + [pltpu.VMEM((tok, cols), bf16), pltpu.SemaphoreType.DMA((4,))],
-        name="pack",
-    )(inner_gate, value_proj, outer_gate, out_grad)
+        "pack",
+        [packed] * 2,
+        (inner_gate, value_proj, outer_gate, out_grad),
+        scratch=[gate] * 3 + [((tok, cols), bf16)],
+        remote=4,
+        limit=None,
+    )
     (got,) = call(
-        both_kernel, "both", [((2, tok + chan, cols), bf16)], (own, other_core(other))
+        both_kernel, "both", [((2, tok + chan, cols), bf16)], (own, other_core(other)), remote=2
     )
     coef = residues * jnp.sqrt(-jnp.expm1(-2.0 * decays))
     small = ((modes, LANES), f32)
@@ -342,7 +360,7 @@
         "scan_forward",
         [columns, ((chips, modes, LANES), f32)],
         (got, decay, coef),
-        scratch=[(length, LANES)],
+        scratch=[columns],
     )
     states = swap(states, ("y", "zh"))
     product, filtered = call(
@@ -350,12 +368,17 @@
         "heads_forward",
         [((nz, half, length), bf16), ((2, half, tok), bf16)],
         (states, decay, coef, yf, got),
-        scratch=[(length, LANES)],
-    )
+        scratch=[columns],
+    )
+
+    parts = call(
+        back_kernel, "back", [((all_chan // nx, tok), bf16)] * nx, (out_weight, out_grad)
+    )
+    product, *parts = lax.optimization_barrier((product, *parts))
     product = spread(product, "zl")
-
-    part, product = lax.optimization_barrier((part, product))
-    own, *parts = call(split_kernel, "split", [((chan, tok), bf16)] * nz, (part,))
+    parts = [parts[0]] + [shift(part, "x", k) for k, part in enumerate(parts) if k]
+
+    own, *parts = call(split_kernel, "split", [gate] * nz, parts, cost=LONG)
     own, other = call(
         sum_kernel,
         "sum",
@@ -363,12 +386,12 @@
         (own, *(shift(part, "zl", k + 1) for k, part in enumerate(parts))),
     )
     product = spread(jnp.broadcast_to(product[None], (nx,) + product.shape), "x")
-    yb, state, back_sum = call(
+    yb, state, grad_outer, grad_outer_other = call(
         scan_backward_kernel,
         "scan_backward",
-        [columns, ((modes, 2 * LANES), bf16), ((2, half, tok), f32)],
-        (own, other_core(other), got, decay, coef),
-        scratch=[(length, LANES)],
+        [columns, ((modes, 2 * LANES), bf16)] + [((half, tok), bf16)] * 2,
+        (own, other_core(other), filtered, got, decay, coef),
+        scratch=[columns],
     )
 
     (partial,) = call(
@@ -387,23 +410,34 @@
         "mixed",
         [((cols, tok), f32)] * 2,
         (product, out_weight),
-        scratch=[(cols, length)],
-    )
-    mixed_other = other_core(mixed_other)
+        scratch=[((cols, length), f32)],
+    )
+    mixed, grad_outer = call(
+        finish_kernel,
+        "finish",
+        [((tok, cols), bf16), gate],
+        (mixed, other_core(mixed_other), grad_outer, other_core(grad_outer_other)),
+    )
+    mixed, grad_outer, partial = lax.optimization_barrier((mixed, grad_outer, partial))
     scale = 1.0 / math.sqrt(length * chips)
+    late = ((half + SUB, cols), f32)
     own, other = call(
         lambda *refs: last_kernel(scale, *refs),
         "last",
-        [((chan + SUB, cols), f32)] * 2,
-        (partial, decay, coef, yb, filtered, back_sum),
-        scratch=[(length, LANES)],
-    )
-    return call(
-        finish_kernel,
-        "finish",
-        [((tok, cols), bf16)] + [((chan, tok), bf16)] * 3 + [((2 * SUB, cols), f32)],
-        (mixed, mixed_other, own, other_core(other), inner_gate, value_proj),
-    )
+        [late] * 2,
+        (decay, coef, partial.reshape(nh, 2 * SUB + modes, cols), yb),
+        scratch=[((nh, 2 * SUB + modes, cols), bf16), columns, columns],
+        remote=2,
+    )
+    grad_inner, grad_value, grad_weight = call(
+        end_kernel,
+        "end",
+        [gate, gate, ((2 * SUB, cols), f32)],
+        (own, other_core(other), inner_gate, value_proj),
+        scratch=[late, late, gate, gate],
+        remote=4,
+    )
+    return (mixed, grad_outer, grad_inner, grad_value, grad_weight)
 
 
 def solution(mesh):

time: 159 us -> 156 us (0.981)
  blocking collectives: 67.7 us -> 0 us
  starting transfers between devices: 41.7 us -> 84.6 us
  waiting for transfers between devices: 8.16 us -> 43 us
  between operations: 14.3 us -> 0.87 us
  Pallas kernels: 14.9 us -> 20.4 us
  local copies, waits for them, and re-layouts: 11 us -> 5.55 us
    all_to_all x3 -> x0, blocking collectives: 67.7 us -> none  [swap(): return lax.all_to_all(x, axes, 0, 0, tiled=True)]
    all_to_all x2 -> x5, waiting for transfers between devices: 1.49 us -> 29.9 us  [swap(): return lax.all_to_all(x, axes, 0, 0, tiled=True)]
    all_to_all x2 -> x5, starting transfers between devices: 7.48 us -> 30.5 us  [swap(): return lax.all_to_all(x, axes, 0, 0, tiled=True)]
    ppermute x3 -> x6, starting transfers between devices: 9 us -> 21 us  [shift(): return lax.ppermute(x, axis, [(i, (i + k) % n) for i in range(n)])]
    ppermute x4 -> x5, starting transfers between devices: 25.2 us -> 33.1 us  [other_core(): return lax.ppermute(x, 'core', [(0, 1), (1, 0)])]
    pallas_call x13 -> x15, Pallas kernels: 13 us -> 20.4 us  [call(): pl.pallas_call(kernel, out_shape=tuple((jax.ShapeDtypeStruct(s, t) for s,...]
    ppermute x3 -> x6, waiting for transfers between devices: 3.66 us -> 10.3 us  [shift(): return lax.ppermute(x, axis, [(i, (i + k) % n) for i in range(n)])]
    unnamed x34 -> x20, local copies, waits for them, and re-layouts: 9.71 us -> 4.25 us
  transfers between devices with their start and end apart: 10 -> 16, of which waited for: 6 -> 10; matrix products, arithmetic and copies ran while one was open for 0% -> 1% of each run, Pallas kernels for 7% -> 6%
where the time goes in v6:
time: 156 us; the launch traced here: 155 us
  starting transfers between devices  84.6 us (54%)
  waiting for transfers between devices  43 us (28%)
  Pallas kernels  20.4 us (13%)
  local copies, waits for them, and re-layouts  5.55 us (4%)
    ppermute x5, starting transfers between devices, other_core(): return lax.ppermute(x, 'core', [(0, 1), (1, 0)])  33.1 us
    all_to_all x5, starting transfers between devices, swap(): return lax.all_to_all(x, axes, 0, 0, tiled=True)  30.5 us
    all_to_all x5, waiting for transfers between devices, swap(): return lax.all_to_all(x, axes, 0, 0, tiled=True)  29.9 us
    ppermute x6, starting transfers between devices, shift(): return lax.ppermute(x, axis, [(i, (i + k) % n) for i in range(n)])  21 us
    pallas_call x15, Pallas kernels, call(): pl.pallas_call(kernel, out_shape=tuple((jax.ShapeDtypeStruct(s, t) for s,...  20.4 us
    ppermute x6, waiting for transfers between devices, shift(): return lax.ppermute(x, axis, [(i, (i + k) % n) for i in range(n)])  10.3 us
    unnamed x20, local copies, waits for them, and re-layouts  4.25 us
  transfers between devices with their start and end apart: 16, of which 10 were waited for; matrix products, arithmetic and copies ran while one was open for 1% of the time, Pallas kernels for 6%

profile of v6, /device:TPU:1, one launch (start us, length us, event | category | flops | bytes accessed | tf_op | source)
XLA Modules:
  0.0 155.2 jit_solution(15274654137488089132)
XLA Ops:
  0.6 0.0 copy-start.3
  0.6 0.0 copy-start
  0.7 2.0 %pack.1 = (bf16[448,256]{1,0:T(8,128)(2,1)}, bf16[448,256]{1,0:T(8,128)(2,1)}) custom-call(bf16[192,256]{1,0:T(8,128)(2,1)} %i_hbm.3, bf16[192,256]{1,0:T(8,128)(2,1)} %v_hbm.3, bf16[192,256]{1,0:T(8,128)(2,1)} %o_hbm.1, bf16[256,256]{1,0:T(8,128)(2,1)} %g_ref.1), custom_call_target="tpu_custom_call" | custom-call | tf_op jit(solution)/shard_map/pack/pallas_call | solution.py:296
  2.7 12.4 %collective-permute-start = (bf16[448,256]{1,0:T(8,128)(2,1)}, bf16[448,256]{1,0:T(8,128)(2,1)S(1)}, u32[]{:S(2)}, u32[]{:S(2)}) collective-permute-start(bf16[448,256]{1,0:T(8,128)(2,1)} %get-tuple-element.45), channel_id=1, source_target_pairs={{0,16},{16,0},{1,17},{17,1},{2,18},{18,2},{3,19},{19,3},{4,20},{20... | collective-permute-start | bytes 688136 | tf_op jit(solution)/shard_map/ppermute | solution.py:327
  15.1 0.8 multiply_bitcast_fusion.c_ref
  15.9 0.0 copy-start.9
  15.9 0.7 copy-done.9
  16.6 0.3 modes.1
  16.8 0.0 collective-permute-done.other_hbm
  16.8 0.0 copy-start.8
  16.8 1.0 copy-done.8
  17.8 0.6 both.1.got_ref
  18.4 2.7 %scan_forward.1 = (f32[512,128]{1,0:T(8,128)S(1)}, f32[24,16,128]{2,1,0:T(8,128)}) custom-call(bf16[2,448,256]{2,1,0:T(8,128)(2,1)S(1)} %both.1.got_ref, f32[16,128]{1,0:T(8,128)S(1)} %get-tuple-element.46.d_ref.refs_0_, f32[16,128]{1,0:T(8,128)S(1)} %get-tuple-element.47.c_ref.refs_1_), custom_call_target="tpu_custom_call" | custom-call | tf_op jit(solution)/shard_map/scan_forward/pallas_call | solution.py:296
  21.1 10.1 %all-to-all-start = ((f32[24,16,128]{2,1,0:T(8,128)}), f32[24,16,128]{2,1,0:T(8,128)S(1)}, u32[]{:S(2)}, u32[]{:S(2)}) async-start(f32[24,16,128]{2,1,0:T(8,128)} %get-tuple-element.48), calls=%async_computation | async-start | bytes 393216 | tf_op jit(solution)/shard_map/all_to_all | solution.py:313
  31.2 0.0 copy-done.3
  31.2 0.0 copy-done
  31.2 1.5 back.1
  32.7 10.9 %all-to-all-done.s_ref = f32[24,16,128]{2,1,0:T(8,128)S(1)} async-done(((f32[24,16,128]{2,1,0:T(8,128)}), f32[24,16,128]{2,1,0:T(8,128)S(1)}, u32[]{:S(2)}, u32[]{:S(2)}) %all-to-all-start) | async-done | bytes 196640 | tf_op jit(solution)/shard_map/all_to_all | solution.py:313
  43.5 2.1 %heads_forward.1 = (bf16[4,96,512]{2,1,0:T(8,128)(2,1)}, bf16[2,96,256]{2,1,0:T(8,128)(2,1)S(1)}) custom-call(f32[24,16,128]{2,1,0:T(8,128)S(1)} %all-to-all-done.s_ref, f32[16,128]{1,0:T(8,128)S(1)} %get-tuple-element.46.d_ref.refs_0_, f32[16,128]{1,0:T(8,128)S(1)} %get-tuple-element.47.c_ref.refs_1_, f32[512,128]{1,0:T(8,128)S(1)} %get-tuple-element.49.y_ref, ...), custom_call_target="tpu_custom_call" | custom-call | tf_op jit(solution)/shard_map/heads_forward/pallas_call | solution.py:296
  45.7 8.7 %all-to-all-start.1 = ((bf16[4,96,512]{2,1,0:T(8,128)(2,1)}), bf16[4,96,512]{2,1,0:T(8,128)(2,1)S(1)}, u32[]{:S(2)}, u32[]{:S(2)}) async-start(bf16[4,96,512]{2,1,0:T(8,128)(2,1)} %get-tuple-element.55), calls=%async_computation.1 | async-start | bytes 786432 | tf_op jit(solution)/shard_map/all_to_all | solution.py:313
  54.4 3.1 %collective-permute-start.2 = (bf16[768,256]{1,0:T(8,128)(2,1)}, bf16[768,256]{1,0:T(8,128)(2,1)}, u32[]{:S(2)}, u32[]{:S(2)}) collective-permute-start(bf16[768,256]{1,0:T(8,128)(2,1)} %get-tuple-element.59), channel_id=1, source_target_pairs={{0,4},{4,8},{8,12},{12,0},{1,5},{5,9},{9,13},{13,1},{2,6},{6,10},{... | collective-permute-start | bytes 1179656 | tf_op jit(solution)/shard_map/ppermute | solution.py:323
  57.5 4.4 %collective-permute-start.3 = (bf16[768,256]{1,0:T(8,128)(2,1)}, bf16[768,256]{1,0:T(8,128)(2,1)}, u32[]{:S(2)}, u32[]{:S(2)}) collective-permute-start(bf16[768,256]{1,0:T(8,128)(2,1)} %get-tuple-element.60), channel_id=1, source_target_pairs={{0,8},{4,12},{8,0},{12,4},{1,9},{5,13},{9,1},{13,5},{2,10},{6,14},... | collective-permute-start | bytes 1179656 | tf_op jit(solution)/shard_map/ppermute | solution.py:323
  61.9 3.1 %collective-permute-start.4 = (bf16[768,256]{1,0:T(8,128)(2,1)S(1)}, bf16[768,256]{1,0:T(8,128)(2,1)}, u32[]{:S(2)}, u32[]{:S(2)}) collective-permute-start(bf16[768,256]{1,0:T(8,128)(2,1)S(1)} %get-tuple-element.61), channel_id=1, source_target_pairs={{0,12},{4,0},{8,4},{12,8},{1,13},{5,1},{9,5},{13,9},{2,14},{6,2},{... | collective-permute-start | bytes 1179656 | tf_op jit(solution)/shard_map/ppermute | solution.py:323
  64.9 0.7 all-to-all-done.1
  65.7 1.3 broadcast_in_dim.9
  67.0 3.9 %all-to-all-start.2 = ((bf16[4,384,512]{2,1,0:T(8,128)(2,1)}), bf16[4,384,512]{2,1,0:T(8,128)(2,1)S(1)}, u32[]{:S(2)}, u32[]{:S(2)}) async-start(bf16[4,384,512]{2,1,0:T(8,128)(2,1)} %broadcast_in_dim.9), calls=%async_computation.2 | async-start | bytes 3145728 | tf_op jit(solution)/shard_map/all_to_all | solution.py:313
  70.9 0.0 collective-permute-done.2.p1
  70.9 6.1 %collective-permute-done.3.p2 = bf16[768,256]{1,0:T(8,128)(2,1)} collective-permute-done((bf16[768,256]{1,0:T(8,128)(2,1)}, bf16[768,256]{1,0:T(8,128)(2,1)}, u32[]{:S(2)}, u32[]{:S(2)}) %collective-permute-start.3) | collective-permute-done | bytes 393248 | tf_op jit(solution)/shard_map/ppermute | solution.py:323
  77.0 1.7 %collective-permute-done.4.p3 = bf16[768,256]{1,0:T(8,128)(2,1)} collective-permute-done((bf16[768,256]{1,0:T(8,128)(2,1)S(1)}, bf16[768,256]{1,0:T(8,128)(2,1)}, u32[]{:S(2)}, u32[]{:S(2)}) %collective-permute-start.4) | collective-permute-done | bytes 393248 | tf_op jit(solution)/shard_map/ppermute | solution.py:323
  78.6 1.4 split.1
  80.0 3.4 %collective-permute-start.5 = (bf16[192,256]{1,0:T(8,128)(2,1)S(1)}, bf16[192,256]{1,0:T(8,128)(2,1)S(1)}, u32[]{:S(2)}, u32[]{:S(2)}) collective-permute-start(bf16[192,256]{1,0:T(8,128)(2,1)S(1)} %get-tuple-element.63), channel_id=1, source_target_pairs={{0,1},{1,2},{2,3},{3,0},{4,5},{5,6},{6,7},{7,4},{8,9},{9,10},{10,1... | collective-permute-start | bytes 294920 | tf_op jit(solution)/shard_map/ppermute | solution.py:323
  83.4 4.0 %collective-permute-start.6 = (bf16[192,256]{1,0:T(8,128)(2,1)S(1)}, bf16[192,256]{1,0:T(8,128)(2,1)S(1)}, u32[]{:S(2)}, u32[]{:S(2)}) collective-permute-start(bf16[192,256]{1,0:T(8,128)(2,1)S(1)} %get-tuple-element.64), channel_id=1, source_target_pairs={{0,2},{1,3},{2,0},{3,1},{4,6},{5,7},{6,4},{7,5},{8,10},{9,11},{10,... | collective-permute-start | bytes 294920 | tf_op jit(solution)/shard_map/ppermute | solution.py:323
  87.4 3.1 %collective-permute-start.7 = (bf16[192,256]{1,0:T(8,128)(2,1)S(1)}, bf16[192,256]{1,0:T(8,128)(2,1)S(1)}, u32[]{:S(2)}, u32[]{:S(2)}) collective-permute-start(bf16[192,256]{1,0:T(8,128)(2,1)S(1)} %get-tuple-element.65), channel_id=1, source_target_pairs={{0,3},{1,0},{2,1},{3,2},{4,7},{5,4},{6,5},{7,6},{8,11},{9,8},{10,9... | collective-permute-start | bytes 294920 | tf_op jit(solution)/shard_map/ppermute | solution.py:323
  90.5 0.0 collective-permute-done.5.p1
  90.5 1.6 %collective-permute-done.6.p2 = bf16[192,256]{1,0:T(8,128)(2,1)S(1)} collective-permute-done((bf16[192,256]{1,0:T(8,128)(2,1)S(1)}, bf16[192,256]{1,0:T(8,128)(2,1)S(1)}, u32[]{:S(2)}, u32[]{:S(2)}) %collective-permute-start.6) | collective-permute-done | bytes 98336 | tf_op jit(solution)/shard_map/ppermute | solution.py:323
  92.1 1.1 collective-permute-done.7.p3
  93.2 6.9 %collective-permute-start.8 = (f32[96,256]{1,0:T(8,128)S(1)}, f32[96,256]{1,0:T(8,128)S(1)}, u32[]{:S(2)}, u32[]{:S(2)}) collective-permute-start(f32[96,256]{1,0:T(8,128)S(1)} %get-tuple-element.67), channel_id=1, source_target_pairs={{0,16},{16,0},{1,17},{17,1},{2,18},{18,2},{3,19},{19,3},{4,20},{20... | collective-permute-start | bytes 294920 | tf_op jit(solution)/shard_map/ppermute | solution.py:327
  100.1 0.9 collective-permute-done.8.other_ref
  101.0 2.1 %scan_backward.1 = (f32[512,128]{1,0:T(8,128)S(1)}, bf16[16,256]{1,0:T(8,128)(2,1)S(1)}, bf16[96,256]{1,0:T(8,128)(2,1)S(1)}, bf16[96,256]{1,0:T(8,128)(2,1)S(1)}) custom-call(f32[96,256]{1,0:T(8,128)S(1)} %get-tuple-element.66.own_ref, f32[96,256]{1,0:T(8,128)S(1)} %collective-permute-done.8.other_ref, bf16[2,96,256]{2,1,0:T(8,128)(2,1)S(1)} %get-tuple-element.68.f_ref, ...), custom_call_target="tpu_custom_call" | custom-call | tf_op jit(solution)/shard_map/scan_backward/pallas_call | solution.py:296
  103.2 0.0 all-to-all-done.2
  103.2 0.6 weight.1
  103.8 0.0 copy-start.2
  103.8 0.9 copy-done.2
  104.7 0.0 copy-start.1
  104.7 4.4 %all-to-all-start.3 = ((bf16[8,208,256]{2,1,0:T(8,128)(2,1)}), bf16[8,208,256]{2,1,0:T(8,128)(2,1)}, u32[]{:S(2)}, u32[]{:S(2)}) async-start(bf16[8,208,256]{2,1,0:T(8,128)(2,1)} %copy-done.2), calls=%async_computation.3 | async-start | bytes 1703936 | tf_op jit(solution)/shard_map/all_to_all | solution.py:313
  109.0 0.0 copy-done.1
  109.0 1.4 mixed.1
  110.4 0.7 copy-done.6
  111.2 2.4 %collective-permute-start.1 = (f32[256,256]{1,0:T(8,128)}, f32[256,256]{1,0:T(8,128)S(1)}, u32[]{:S(2)}, u32[]{:S(2)}) collective-permute-start(f32[256,256]{1,0:T(8,128)} %get-tuple-element.57), channel_id=1, source_target_pairs={{0,16},{16,0},{1,17},{17,1},{2,18},{18,2},{3,19},{19,3},{4,20},{20... | collective-permute-start | bytes 786440 | tf_op jit(solution)/shard_map/ppermute | solution.py:327
  113.5 18.3 %all-to-all-done.3.t_ref = bf16[8,208,256]{2,1,0:T(8,128)(2,1)} async-done(((bf16[8,208,256]{2,1,0:T(8,128)(2,1)}), bf16[8,208,256]{2,1,0:T(8,128)(2,1)}, u32[]{:S(2)}, u32[]{:S(2)}) %all-to-all-start.3) | async-done | bytes 852000 | tf_op jit(solution)/shard_map/all_to_all | solution.py:313
  131.8 1.9 %middle.1 = bf16[3,80,256]{2,1,0:T(8,128)(2,1)} custom-call(bf16[8,208,256]{2,1,0:T(8,128)(2,1)} %all-to-all-done.3.t_ref, f32[16,128]{1,0:T(8,128)S(1)} %get-tuple-element.46.d_ref.refs_0_), custom_call_target="tpu_custom_call" | custom-call | tf_op jit(solution)/shard_map/middle/pallas_call | solution.py:296
  133.8 3.4 %all-to-all-start.4 = ((bf16[3,80,256]{2,1,0:T(8,128)(2,1)}), bf16[3,80,256]{2,1,0:T(8,128)(2,1)S(1)}, u32[]{:S(2)}, u32[]{:S(2)}) async-start(bf16[3,80,256]{2,1,0:T(8,128)(2,1)} %middle.1), calls=%async_computation.4 | async-start | bytes 245760 | tf_op jit(solution)/shard_map/all_to_all | solution.py:313
  137.2 4.8 %collective-permute-start.9 = (bf16[96,256]{1,0:T(8,128)(2,1)S(1)}, bf16[96,256]{1,0:T(8,128)(2,1)S(1)}, u32[]{:S(2)}, u32[]{:S(2)}) collective-permute-start(bf16[96,256]{1,0:T(8,128)(2,1)S(1)} %get-tuple-element.70), channel_id=1, source_target_pairs={{0,16},{16,0},{1,17},{17,1},{2,18},{18,2},{3,19},{19,3},{4,20},{20... | collective-permute-start | bytes 147464 | tf_op jit(solution)/shard_map/ppermute | solution.py:327
  142.1 0.9 collective-permute-done.9.other_ref
  142.9 0.0 collective-permute-done.1.mr_ref
  142.9 0.9 copy-done.7
  143.9 0.8 finish.1
  144.6 0.0 all-to-all-done.4.refs_2_
  144.6 1.7 %last.1 = (f32[128,256]{1,0:T(8,128)S(1)}, f32[128,256]{1,0:T(8,128)S(1)}) custom-call(f32[16,128]{1,0:T(8,128)S(1)} %get-tuple-element.46.d_ref.refs_0_, f32[16,128]{1,0:T(8,128)S(1)} %get-tuple-element.47.c_ref.refs_1_, bf16[3,80,256]{2,1,0:T(8,128)(2,1)S(1)} %all-to-all-done.4.refs_2_, f32[512,128]{1,0:T(8,128)S(1)} %get-tuple-element.77.refs_3_), custom_call_target="tpu_custom_call" | custom-call | tf_op jit(solution)/shard_map/last/pallas_call | solution.py:296
  146.3 6.5 %collective-permute-start.10 = (f32[128,256]{1,0:T(8,128)S(1)}, f32[128,256]{1,0:T(8,128)S(1)}, u32[]{:S(2)}, u32[]{:S(2)}) collective-permute-start(f32[128,256]{1,0:T(8,128)S(1)} %get-tuple-element.79), channel_id=1, source_target_pairs={{0,16},{16,0},{1,17},{17,1},{2,18},{18,2},{3,19},{19,3},{4,20},{20... | collective-permute-start | bytes 393224 | tf_op jit(solution)/shard_map/ppermute | solution.py:327
  152.9 1.0 collective-permute-done.10.other_hbm
  153.9 0.0 copy-done.4
  153.9 0.0 copy-done.5
  153.9 1.4 end.1
  (5 shorter events, 0.1 us)
Async XLA Ops:
  0.6 30.6 %copy-start.3 = (bf16[256,256]{1,0:T(8,128)(2,1)S(1)}, bf16[256,256]{1,0:T(8,128)(2,1)}, u32[]{:S(2)}) copy-start(bf16[256,256]{1,0:T(8,128)(2,1)} %g_ref.1) | copy-start | bytes 393220
  0.6 30.6 %copy-start = (bf16[3072,256]{1,0:T(8,128)(2,1)S(1)}, bf16[3072,256]{1,0:T(8,128)(2,1)}, u32[]{:S(2)}) copy-start(bf16[3072,256]{1,0:T(8,128)(2,1)} %w_ref.3) | copy-start | bytes 4718596
  2.7 14.2 %collective-permute-start = (bf16[448,256]{1,0:T(8,128)(2,1)}, bf16[448,256]{1,0:T(8,128)(2,1)S(1)}, u32[]{:S(2)}, u32[]{:S(2)}) collective-permute-start(bf16[448,256]{1,0:T(8,128)(2,1)} %get-tuple-element.45), channel_id=1, source_target_pairs={{0,16},{16,0},{1,17},{17,1},{2,18},{18,2},{3,19},{19,3},{4,20},{20... | collective-permute-start | bytes 688136 | tf_op jit(solution)/shard_map/ppermute | solution.py:327
  15.9 0.7 copy-start.9
  16.8 1.0 copy-start.8
  21.1 22.5 %all-to-all-start = ((f32[24,16,128]{2,1,0:T(8,128)}), f32[24,16,128]{2,1,0:T(8,128)S(1)}, u32[]{:S(2)}, u32[]{:S(2)}) async-start(f32[24,16,128]{2,1,0:T(8,128)} %get-tuple-element.48), calls=%async_computation | async-start | bytes 393216 | tf_op jit(solution)/shard_map/all_to_all | solution.py:313
  45.7 20.0 %all-to-all-start.1 = ((bf16[4,96,512]{2,1,0:T(8,128)(2,1)}), bf16[4,96,512]{2,1,0:T(8,128)(2,1)S(1)}, u32[]{:S(2)}, u32[]{:S(2)}) async-start(bf16[4,96,512]{2,1,0:T(8,128)(2,1)} %get-tuple-element.55), calls=%async_computation.1 | async-start | bytes 786432 | tf_op jit(solution)/shard_map/all_to_all | solution.py:313
  54.4 16.5 %collective-permute-start.2 = (bf16[768,256]{1,0:T(8,128)(2,1)}, bf16[768,256]{1,0:T(8,128)(2,1)}, u32[]{:S(2)}, u32[]{:S(2)}) collective-permute-start(bf16[768,256]{1,0:T(8,128)(2,1)} %get-tuple-element.59), channel_id=1, source_target_pairs={{0,4},{4,8},{8,12},{12,0},{1,5},{5,9},{9,13},{13,1},{2,6},{6,10},{... | collective-permute-start | bytes 1179656 | tf_op jit(solution)/shard_map/ppermute | solution.py:323
  57.5 19.5 %collective-permute-start.3 = (bf16[768,256]{1,0:T(8,128)(2,1)}, bf16[768,256]{1,0:T(8,128)(2,1)}, u32[]{:S(2)}, u32[]{:S(2)}) collective-permute-start(bf16[768,256]{1,0:T(8,128)(2,1)} %get-tuple-element.60), channel_id=1, source_target_pairs={{0,8},{4,12},{8,0},{12,4},{1,9},{5,13},{9,1},{13,5},{2,10},{6,14},... | collective-permute-start | bytes 1179656 | tf_op jit(solution)/shard_map/ppermute | solution.py:323
  61.9 16.8 %collective-permute-start.4 = (bf16[768,256]{1,0:T(8,128)(2,1)S(1)}, bf16[768,256]{1,0:T(8,128)(2,1)}, u32[]{:S(2)}, u32[]{:S(2)}) collective-permute-start(bf16[768,256]{1,0:T(8,128)(2,1)S(1)} %get-tuple-element.61), channel_id=1, source_target_pairs={{0,12},{4,0},{8,4},{12,8},{1,13},{5,1},{9,5},{13,9},{2,14},{6,2},{... | collective-permute-start | bytes 1179656 | tf_op jit(solution)/shard_map/ppermute | solution.py:323
  67.0 36.2 %all-to-all-start.2 = ((bf16[4,384,512]{2,1,0:T(8,128)(2,1)}), bf16[4,384,512]{2,1,0:T(8,128)(2,1)S(1)}, u32[]{:S(2)}, u32[]{:S(2)}) async-start(bf16[4,384,512]{2,1,0:T(8,128)(2,1)} %broadcast_in_dim.9), calls=%async_computation.2 | async-start | bytes 3145728 | tf_op jit(solution)/shard_map/all_to_all | solution.py:313
  80.0 10.5 %collective-permute-start.5 = (bf16[192,256]{1,0:T(8,128)(2,1)S(1)}, bf16[192,256]{1,0:T(8,128)(2,1)S(1)}, u32[]{:S(2)}, u32[]{:S(2)}) collective-permute-start(bf16[192,256]{1,0:T(8,128)(2,1)S(1)} %get-tuple-element.63), channel_id=1, source_target_pairs={{0,1},{1,2},{2,3},{3,0},{4,5},{5,6},{6,7},{7,4},{8,9},{9,10},{10,1... | collective-permute-start | bytes 294920 | tf_op jit(solution)/shard_map/ppermute | solution.py:323
  83.4 8.7 %collective-permute-start.6 = (bf16[192,256]{1,0:T(8,128)(2,1)S(1)}, bf16[192,256]{1,0:T(8,128)(2,1)S(1)}, u32[]{:S(2)}, u32[]{:S(2)}) collective-permute-start(bf16[192,256]{1,0:T(8,128)(2,1)S(1)} %get-tuple-element.64), channel_id=1, source_target_pairs={{0,2},{1,3},{2,0},{3,1},{4,6},{5,7},{6,4},{7,5},{8,10},{9,11},{10,... | collective-permute-start | bytes 294920 | tf_op jit(solution)/shard_map/ppermute | solution.py:323
  87.4 5.7 %collective-permute-start.7 = (bf16[192,256]{1,0:T(8,128)(2,1)S(1)}, bf16[192,256]{1,0:T(8,128)(2,1)S(1)}, u32[]{:S(2)}, u32[]{:S(2)}) collective-permute-start(bf16[192,256]{1,0:T(8,128)(2,1)S(1)} %get-tuple-element.65), channel_id=1, source_target_pairs={{0,3},{1,0},{2,1},{3,2},{4,7},{5,4},{6,5},{7,6},{8,11},{9,8},{10,9... | collective-permute-start | bytes 294920 | tf_op jit(solution)/shard_map/ppermute | solution.py:323
  93.2 7.8 %collective-permute-start.8 = (f32[96,256]{1,0:T(8,128)S(1)}, f32[96,256]{1,0:T(8,128)S(1)}, u32[]{:S(2)}, u32[]{:S(2)}) collective-permute-start(f32[96,256]{1,0:T(8,128)S(1)} %get-tuple-element.67), channel_id=1, source_target_pairs={{0,16},{16,0},{1,17},{17,1},{2,18},{18,2},{3,19},{19,3},{4,20},{20... | collective-permute-start | bytes 294920 | tf_op jit(solution)/shard_map/ppermute | solution.py:327
  103.8 0.9 copy-start.2
  104.7 4.4 %copy-start.1 = (bf16[3072,256]{1,0:T(8,128)(2,1)S(1)}, bf16[3072,256]{1,0:T(8,128)(2,1)}, u32[]{:S(2)}) copy-start(bf16[3072,256]{1,0:T(8,128)(2,1)} %w_ref.3) | copy-start | bytes 4718596
  104.7 27.2 %all-to-all-start.3 = ((bf16[8,208,256]{2,1,0:T(8,128)(2,1)}), bf16[8,208,256]{2,1,0:T(8,128)(2,1)}, u32[]{:S(2)}, u32[]{:S(2)}) async-start(bf16[8,208,256]{2,1,0:T(8,128)(2,1)} %copy-done.2), calls=%async_computation.3 | async-start | bytes 1703936 | tf_op jit(solution)/shard_map/all_to_all | solution.py:313
  110.4 0.7 copy-start.6
  111.2 42.7 %copy-start.4 = (bf16[192,256]{1,0:T(8,128)(2,1)S(1)}, bf16[192,256]{1,0:T(8,128)(2,1)}, u32[]{:S(2)}) copy-start(bf16[192,256]{1,0:T(8,128)(2,1)} %i_hbm.3) | copy-start | bytes 294916
  111.2 42.7 %copy-start.5 = (bf16[192,256]{1,0:T(8,128)(2,1)S(1)}, bf16[192,256]{1,0:T(8,128)(2,1)}, u32[]{:S(2)}) copy-start(bf16[192,256]{1,0:T(8,128)(2,1)} %v_hbm.3) | copy-start | bytes 294916
  111.2 31.8 %collective-permute-start.1 = (f32[256,256]{1,0:T(8,128)}, f32[256,256]{1,0:T(8,128)S(1)}, u32[]{:S(2)}, u32[]{:S(2)}) collective-permute-start(f32[256,256]{1,0:T(8,128)} %get-tuple-element.57), channel_id=1, source_target_pairs={{0,16},{16,0},{1,17},{17,1},{2,18},{18,2},{3,19},{19,3},{4,20},{20... | collective-permute-start | bytes 786440 | tf_op jit(solution)/shard_map/ppermute | solution.py:327
  133.8 10.9 %all-to-all-start.4 = ((bf16[3,80,256]{2,1,0:T(8,128)(2,1)}), bf16[3,80,256]{2,1,0:T(8,128)(2,1)S(1)}, u32[]{:S(2)}, u32[]{:S(2)}) async-start(bf16[3,80,256]{2,1,0:T(8,128)(2,1)} %middle.1), calls=%async_computation.4 | async-start | bytes 245760 | tf_op jit(solution)/shard_map/all_to_all | solution.py:313
  137.2 5.7 %collective-permute-start.9 = (bf16[96,256]{1,0:T(8,128)(2,1)S(1)}, bf16[96,256]{1,0:T(8,128)(2,1)S(1)}, u32[]{:S(2)}, u32[]{:S(2)}) collective-permute-start(bf16[96,256]{1,0:T(8,128)(2,1)S(1)} %get-tuple-element.70), channel_id=1, source_target_pairs={{0,16},{16,0},{1,17},{17,1},{2,18},{18,2},{3,19},{19,3},{4,20},{20... | collective-permute-start | bytes 147464 | tf_op jit(solution)/shard_map/ppermute | solution.py:327
  142.9 1.0 copy-start.7
  146.3 7.5 %collective-permute-start.10 = (f32[128,256]{1,0:T(8,128)S(1)}, f32[128,256]{1,0:T(8,128)S(1)}, u32[]{:S(2)}, u32[]{:S(2)}) collective-permute-start(f32[128,256]{1,0:T(8,128)S(1)} %get-tuple-element.79), channel_id=1, source_target_pairs={{0,16},{16,0},{1,17},{17,1},{2,18},{18,2},{3,19},{19,3},{4,20},{20... | collective-permute-start | bytes 393224 | tf_op jit(solution)/shard_map/ppermute | solution.py:327

commit v7 on v6

--- a/solution.py
+++ b/solution.py
@@ -142,11 +142,14 @@
     lax.fori_loop(0, length // 8, step, state)
 
 
-def scan_forward_kernel(got_ref, d_ref, c_ref, y_ref, s_ref, gt):
-    tok = got_ref.shape[2]
-    half = (got_ref.shape[1] - tok) // 2
-    for h in range(2):
-        gt[pl.ds(h * tok, tok), :] = to_columns(got_ref[h, tok : tok + half].astype(f32))
+def scan_forward_kernel(d_ref, c_ref, own_hbm, other_hbm, y_ref, s_ref, own_ref, other_ref, gt, sems):
+    half, tok = own_ref.shape
+    gated = pl.ds(tok, half)
+    fetch(sems, (own_hbm.at[gated], own_ref), (other_hbm.at[gated], other_ref))
+    core = lax.axis_index(CORE)
+    for h, ref in ((core, own_ref), (1 - core, other_ref)):
+        at = pl.ds(pl.multiple_of(h * tok, tok), tok)
+        gt[at, :] = to_columns(ref[...].astype(f32))
     state = scan(gt, y_ref, jnp.exp(-d_ref[...]), c_ref[...], False)
     for m in range(s_ref.shape[0]):
         s_ref[m] = state
@@ -195,15 +198,20 @@
     return both[:, :LANES] + both[:, LANES:]
 
 
-def weight_kernel(p_ref, got_ref, s_ref, out_ref):
+def weight_kernel(p_ref, got_ref, s_ref, out_hbm, out_ref, sems):
     tok = got_ref.shape[2]
     n = out_ref.shape[0]
     rows = p_ref.shape[0] // n
     grads = got_ref[:, :tok, :].reshape(2 * tok, -1)
+    copies = []
     for y in range(n):
         part = jnp.dot(p_ref[pl.ds(y * rows, rows), :], grads, preferred_element_type=f32)
         out_ref[y, :rows, :] = part.astype(bf16)
         out_ref[y, rows:, :] = s_ref[...]
+        copies.append(pltpu.make_async_copy(out_ref.at[y], out_hbm.at[y], sems.at[y]))
+        copies[-1].start()
+    for copy in copies:
+        copy.wait()
 
 
 def middle_kernel(t_ref, d_ref, out_ref):
@@ -347,9 +355,7 @@
         remote=4,
         limit=None,
     )
-    (got,) = call(
-        both_kernel, "both", [((2, tok + chan, cols), bf16)], (own, other_core(other)), remote=2
-    )
+    other = other_core(other)
     coef = residues * jnp.sqrt(-jnp.expm1(-2.0 * decays))
     small = ((modes, LANES), f32)
     decay, coef = call(modes_kernel, "modes", [small, small], (decays.T, coef.T))
@@ -359,10 +365,14 @@
         scan_forward_kernel,
         "scan_forward",
         [columns, ((chips, modes, LANES), f32)],
-        (got, decay, coef),
-        scratch=[columns],
+        (decay, coef, own, other),
+        scratch=[((half, tok), bf16)] * 2 + [columns],
+        remote=2,
     )
     states = swap(states, ("y", "zh"))
+    (got,) = call(
+        both_kernel, "both", [((2, tok + chan, cols), bf16)], (own, other), remote=2
+    )
     product, filtered = call(
         heads_forward_kernel,
         "heads_forward",
@@ -374,11 +384,11 @@
     parts = call(
         back_kernel, "back", [((all_chan // nx, tok), bf16)] * nx, (out_weight, out_grad)
     )
-    product, *parts = lax.optimization_barrier((product, *parts))
     product = spread(product, "zl")
     parts = [parts[0]] + [shift(part, "x", k) for k, part in enumerate(parts) if k]
 
-    own, *parts = call(split_kernel, "split", [gate] * nz, parts, cost=LONG)
+    parts = call(split_kernel, "split", [gate] * nz, parts, cost=LONG)
+    own, *parts, product = lax.optimization_barrier((*parts, product))
     own, other = call(
         sum_kernel,
         "sum",
@@ -394,12 +404,16 @@
         scratch=[columns],
     )
 
-    (partial,) = call(
+    sums = (ny, nh * 2 * SUB + modes, cols)
+    partial = pl.pallas_call(
         weight_kernel,
-        "weight",
-        [((ny, nh * 2 * SUB + modes, cols), bf16)],
-        (product, got, state),
-    )
+        out_shape=jax.ShapeDtypeStruct(sums, bf16),
+        in_specs=[pl.BlockSpec(memory_space=pltpu.VMEM)] * 3,
+        out_specs=pl.BlockSpec(memory_space=pl.ANY),
+        scratch_shapes=[pltpu.VMEM(sums, bf16), pltpu.SemaphoreType.DMA((ny,))],
+        compiler_params=pltpu.CompilerParams(vmem_limit_bytes=24 * 2**20),
+        name="weight",
+    )(product, got, state)
     partial = swap(partial, "y")
     (partial,) = call(
         middle_kernel, "middle", [((nh, 2 * SUB + modes, cols), bf16)], (partial, decay)

time: 156 us -> 148 us (0.949)
  waiting for transfers between devices: 43 us -> 35.2 us
  starting transfers between devices: 84.6 us -> 79.6 us
  Pallas kernels: 20.4 us -> 22.8 us
  local copies, waits for them, and re-layouts: 5.55 us -> 7.85 us
    all_to_all x5, waiting for transfers between devices: 29.9 us -> 24 us  [swap(): return lax.all_to_all(x, axes, 0, 0, tiled=True)]
    ppermute x5, starting transfers between devices: 33.1 us -> 27.9 us  [other_core(): return lax.ppermute(x, 'core', [(0, 1), (1, 0)])]
    pallas_call x0 -> x1, Pallas kernels: none -> 3.12 us  [shards(): pl.pallas_call(weight_kernel, out_shape=jax.ShapeDtypeStruct(sums, bf16),...]
    unnamed x20 -> x22, local copies, waits for them, and re-layouts: 4.25 us -> 6.56 us
    ppermute x6, waiting for transfers between devices: 10.3 us -> 8.38 us  [shift(): return lax.ppermute(x, axis, [(i, (i + k) % n) for i in range(n)])]
    all_to_all x5, starting transfers between devices: 30.5 us -> 32.2 us  [swap(): return lax.all_to_all(x, axes, 0, 0, tiled=True)]
    pallas_call x15 -> x14, Pallas kernels: 20.4 us -> 19.7 us  [call(): pl.pallas_call(kernel, out_shape=tuple((jax.ShapeDtypeStruct(s, t) for s,...]
  transfers between devices with their start and end apart: 16 -> 16, of which waited for: 10 -> 10; matrix products, arithmetic and copies ran while one was open for 1% -> 1% of each run, Pallas kernels for 6% -> 8%
where the time goes in v7:
time: 148 us; the launch traced here: 147 us
  starting transfers between devices  79.6 us (54%)
  waiting for transfers between devices  35.2 us (24%)
  Pallas kernels  22.8 us (15%)
  local copies, waits for them, and re-layouts  7.85 us (5%)
    all_to_all x5, starting transfers between devices, swap(): return lax.all_to_all(x, axes, 0, 0, tiled=True)  32.2 us
    ppermute x5, starting transfers between devices, other_core(): return lax.ppermute(x, 'core', [(0, 1), (1, 0)])  27.9 us
    all_to_all x5, waiting for transfers between devices, swap(): return lax.all_to_all(x, axes, 0, 0, tiled=True)  24 us
    pallas_call x14, Pallas kernels, call(): pl.pallas_call(kernel, out_shape=tuple((jax.ShapeDtypeStruct(s, t) for s,...  19.7 us
    ppermute x6, starting transfers between devices, shift(): return lax.ppermute(x, axis, [(i, (i + k) % n) for i in range(n)])  19.5 us
    ppermute x6, waiting for transfers between devices, shift(): return lax.ppermute(x, axis, [(i, (i + k) % n) for i in range(n)])  8.38 us
    unnamed x22, local copies, waits for them, and re-layouts  6.56 us
    pallas_call x1, Pallas kernels, shards(): pl.pallas_call(weight_kernel, out_shape=jax.ShapeDtypeStruct(sums, bf16),...  3.12 us
  transfers between devices with their start and end apart: 16, of which 10 were waited for; matrix products, arithmetic and copies ran while one was open for 1% of the time, Pallas kernels for 8%

profile of v7, /device:TPU:1, one launch (start us, length us, event | category | flops | bytes accessed | tf_op | source)
XLA Modules:
  0.0 147.1 jit_solution(3141609545390900791)
XLA Ops:
  0.6 1.9 %pack.1 = (bf16[448,256]{1,0:T(8,128)(2,1)}, bf16[448,256]{1,0:T(8,128)(2,1)}) custom-call(bf16[192,256]{1,0:T(8,128)(2,1)} %i_hbm.3, bf16[192,256]{1,0:T(8,128)(2,1)} %v_hbm.3, bf16[192,256]{1,0:T(8,128)(2,1)} %o_hbm.1, bf16[256,256]{1,0:T(8,128)(2,1)} %g_hbm.1), custom_call_target="tpu_custom_call" | custom-call | tf_op jit(solution)/shard_map/pack/pallas_call | solution.py:304
  2.5 12.4 %collective-permute-start.3 = (bf16[448,256]{1,0:T(8,128)(2,1)}, bf16[448,256]{1,0:T(8,128)(2,1)S(1)}, u32[]{:S(2)}, u32[]{:S(2)}) collective-permute-start(bf16[448,256]{1,0:T(8,128)(2,1)} %get-tuple-element.55), channel_id=1, source_target_pairs={{0,16},{16,0},{1,17},{17,1},{2,18},{18,2},{3,19},{19,3},{4,20},{20... | collective-permute-start | bytes 688136 | tf_op jit(solution)/shard_map/ppermute | solution.py:335
  15.0 0.8 multiply_bitcast_fusion.c_ref
  15.7 0.0 copy-start.10
  15.7 0.7 copy-done.10
  16.4 0.3 modes.1
  16.7 0.0 collective-permute-done.3.other_hbm
  16.7 1.0 copy-done.3
  17.7 0.0 copy-start.4
  17.7 2.8 %scan_forward.1 = (f32[512,128]{1,0:T(8,128)S(1)}, f32[24,16,128]{2,1,0:T(8,128)}) custom-call(f32[16,128]{1,0:T(8,128)S(1)} %get-tuple-element.52.d_ref.refs_0_, f32[16,128]{1,0:T(8,128)S(1)} %get-tuple-element.53.c_ref.refs_1_, bf16[448,256]{1,0:T(8,128)(2,1)S(1)} %copy-done.3, bf16[448,256]{1,0:T(8,128)(2,1)S(1)} %collective-permute-done.3.other_hbm), custom_call_target="tpu_custom_call" | custom-call | tf_op jit(solution)/shard_map/scan_forward/pallas_call | solution.py:304
  20.5 10.2 %all-to-all-start = ((f32[24,16,128]{2,1,0:T(8,128)}), f32[24,16,128]{2,1,0:T(8,128)S(1)}, u32[]{:S(2)}, u32[]{:S(2)}) async-start(f32[24,16,128]{2,1,0:T(8,128)} %get-tuple-element.56), calls=%async_computation | async-start | bytes 393216 | tf_op jit(solution)/shard_map/all_to_all | solution.py:321
  30.6 0.0 copy-start
  30.7 1.4 copy-done
  32.1 0.0 copy-start.5
  32.1 0.9 copy-done.5
  33.0 1.5 back.1
  34.4 3.1 %collective-permute-start = (bf16[768,256]{1,0:T(8,128)(2,1)}, bf16[768,256]{1,0:T(8,128)(2,1)S(1)}, u32[]{:S(2)}, u32[]{:S(2)}) collective-permute-start(bf16[768,256]{1,0:T(8,128)(2,1)} %get-tuple-element.45), channel_id=1, source_target_pairs={{0,4},{4,8},{8,12},{12,0},{1,5},{5,9},{9,13},{13,1},{2,6},{6,10},{... | collective-permute-start | bytes 1179656 | tf_op jit(solution)/shard_map/ppermute | solution.py:331
  37.5 4.4 %collective-permute-start.1 = (bf16[768,256]{1,0:T(8,128)(2,1)}, bf16[768,256]{1,0:T(8,128)(2,1)S(1)}, u32[]{:S(2)}, u32[]{:S(2)}) collective-permute-start(bf16[768,256]{1,0:T(8,128)(2,1)} %get-tuple-element.46), channel_id=1, source_target_pairs={{0,8},{4,12},{8,0},{12,4},{1,9},{5,13},{9,1},{13,5},{2,10},{6,14},... | collective-permute-start | bytes 1179656 | tf_op jit(solution)/shard_map/ppermute | solution.py:331
  41.9 3.1 %collective-permute-start.2 = (bf16[768,256]{1,0:T(8,128)(2,1)S(1)}, bf16[768,256]{1,0:T(8,128)(2,1)}, u32[]{:S(2)}, u32[]{:S(2)}) collective-permute-start(bf16[768,256]{1,0:T(8,128)(2,1)S(1)} %get-tuple-element.47), channel_id=1, source_target_pairs={{0,12},{4,0},{8,4},{12,8},{1,13},{5,1},{9,5},{13,9},{2,14},{6,2},{... | collective-permute-start | bytes 1179656 | tf_op jit(solution)/shard_map/ppermute | solution.py:331
  45.0 0.0 copy-done.4
  45.0 0.6 both.1.got_ref
  45.6 0.0 all-to-all-done.s_ref
  45.6 2.2 %heads_forward.1 = (bf16[4,96,512]{2,1,0:T(8,128)(2,1)}, bf16[2,96,256]{2,1,0:T(8,128)(2,1)S(1)}) custom-call(f32[24,16,128]{2,1,0:T(8,128)S(1)} %all-to-all-done.s_ref, f32[16,128]{1,0:T(8,128)S(1)} %get-tuple-element.52.d_ref.refs_0_, f32[16,128]{1,0:T(8,128)S(1)} %get-tuple-element.53.c_ref.refs_1_, f32[512,128]{1,0:T(8,128)S(1)} %get-tuple-element.57.y_ref, ...), custom_call_target="tpu_custom_call" | custom-call | tf_op jit(solution)/shard_map/heads_forward/pallas_call | solution.py:304
  47.8 6.0 %all-to-all-start.1 = ((bf16[4,96,512]{2,1,0:T(8,128)(2,1)}), bf16[4,96,512]{2,1,0:T(8,128)(2,1)S(1)}, u32[]{:S(2)}, u32[]{:S(2)}) async-start(bf16[4,96,512]{2,1,0:T(8,128)(2,1)} %get-tuple-element.58), calls=%async_computation.1 | async-start | bytes 786432 | tf_op jit(solution)/shard_map/all_to_all | solution.py:321
  53.8 0.0 collective-permute-done.p1
  53.8 3.7 %collective-permute-done.1.p2 = bf16[768,256]{1,0:T(8,128)(2,1)S(1)} collective-permute-done((bf16[768,256]{1,0:T(8,128)(2,1)}, bf16[768,256]{1,0:T(8,128)(2,1)S(1)}, u32[]{:S(2)}, u32[]{:S(2)}) %collective-permute-start.1) | collective-permute-done | bytes 393248 | tf_op jit(solution)/shard_map/ppermute | solution.py:331
  57.6 1.3 collective-permute-done.2.p3
  58.9 1.2 split.1
  60.1 4.9 %all-to-all-done.1 = bf16[4,96,512]{2,1,0:T(8,128)(2,1)S(1)} async-done(((bf16[4,96,512]{2,1,0:T(8,128)(2,1)}), bf16[4,96,512]{2,1,0:T(8,128)(2,1)S(1)}, u32[]{:S(2)}, u32[]{:S(2)}) %all-to-all-start.1) | async-done | bytes 393248 | tf_op jit(solution)/shard_map/all_to_all | solution.py:321
  65.0 1.3 broadcast_in_dim.2
  66.3 4.0 %all-to-all-start.2 = ((bf16[4,384,512]{2,1,0:T(8,128)(2,1)}), bf16[4,384,512]{2,1,0:T(8,128)(2,1)S(1)}, u32[]{:S(2)}, u32[]{:S(2)}) async-start(bf16[4,384,512]{2,1,0:T(8,128)(2,1)} %broadcast_in_dim.2), calls=%async_computation.2 | async-start | bytes 3145728 | tf_op jit(solution)/shard_map/all_to_all | solution.py:321
  70.3 1.9 %collective-permute-start.5 = (bf16[192,256]{1,0:T(8,128)(2,1)S(1)}, bf16[192,256]{1,0:T(8,128)(2,1)S(1)}, u32[]{:S(2)}, u32[]{:S(2)}) collective-permute-start(bf16[192,256]{1,0:T(8,128)(2,1)S(1)} %get-tuple-element.63), channel_id=1, source_target_pairs={{0,1},{1,2},{2,3},{3,0},{4,5},{5,6},{6,7},{7,4},{8,9},{9,10},{10,1... | collective-permute-start | bytes 294920 | tf_op jit(solution)/shard_map/ppermute | solution.py:331
  72.3 3.0 %collective-permute-start.6 = (bf16[192,256]{1,0:T(8,128)(2,1)S(1)}, bf16[192,256]{1,0:T(8,128)(2,1)S(1)}, u32[]{:S(2)}, u32[]{:S(2)}) collective-permute-start(bf16[192,256]{1,0:T(8,128)(2,1)S(1)} %get-tuple-element.64), channel_id=1, source_target_pairs={{0,2},{1,3},{2,0},{3,1},{4,6},{5,7},{6,4},{7,5},{8,10},{9,11},{10,... | collective-permute-start | bytes 294920 | tf_op jit(solution)/shard_map/ppermute | solution.py:331
  75.3 4.1 %collective-permute-start.7 = (bf16[192,256]{1,0:T(8,128)(2,1)S(1)}, bf16[192,256]{1,0:T(8,128)(2,1)S(1)}, u32[]{:S(2)}, u32[]{:S(2)}) collective-permute-start(bf16[192,256]{1,0:T(8,128)(2,1)S(1)} %get-tuple-element.65), channel_id=1, source_target_pairs={{0,3},{1,0},{2,1},{3,2},{4,7},{5,4},{6,5},{7,6},{8,11},{9,8},{10,9... | collective-permute-start | bytes 294920 | tf_op jit(solution)/shard_map/ppermute | solution.py:331
  79.3 0.0 collective-permute-done.5.p1
  79.4 1.7 %collective-permute-done.6.p2 = bf16[192,256]{1,0:T(8,128)(2,1)S(1)} collective-permute-done((bf16[192,256]{1,0:T(8,128)(2,1)S(1)}, bf16[192,256]{1,0:T(8,128)(2,1)S(1)}, u32[]{:S(2)}, u32[]{:S(2)}) %collective-permute-start.6) | collective-permute-done | bytes 98336 | tf_op jit(solution)/shard_map/ppermute | solution.py:331
  81.1 1.6 %collective-permute-done.7.p3 = bf16[192,256]{1,0:T(8,128)(2,1)S(1)} collective-permute-done((bf16[192,256]{1,0:T(8,128)(2,1)S(1)}, bf16[192,256]{1,0:T(8,128)(2,1)S(1)}, u32[]{:S(2)}, u32[]{:S(2)}) %collective-permute-start.7) | collective-permute-done | bytes 98336 | tf_op jit(solution)/shard_map/ppermute | solution.py:331
  82.7 4.1 %collective-permute-start.8 = (f32[96,256]{1,0:T(8,128)S(1)}, f32[96,256]{1,0:T(8,128)S(1)}, u32[]{:S(2)}, u32[]{:S(2)}) collective-permute-start(f32[96,256]{1,0:T(8,128)S(1)} %get-tuple-element.67), channel_id=1, source_target_pairs={{0,16},{16,0},{1,17},{17,1},{2,18},{18,2},{3,19},{19,3},{4,20},{20... | collective-permute-start | bytes 294920 | tf_op jit(solution)/shard_map/ppermute | solution.py:335
  86.8 0.9 collective-permute-done.8.other_ref
  87.8 2.1 %scan_backward.1 = (f32[512,128]{1,0:T(8,128)S(1)}, bf16[16,256]{1,0:T(8,128)(2,1)S(1)}, bf16[96,256]{1,0:T(8,128)(2,1)S(1)}, bf16[96,256]{1,0:T(8,128)(2,1)S(1)}) custom-call(f32[96,256]{1,0:T(8,128)S(1)} %get-tuple-element.66.own_ref, f32[96,256]{1,0:T(8,128)S(1)} %collective-permute-done.8.other_ref, bf16[2,96,256]{2,1,0:T(8,128)(2,1)S(1)} %get-tuple-element.68.f_ref, ...), custom_call_target="tpu_custom_call" | custom-call | tf_op jit(solution)/shard_map/scan_backward/pallas_call | solution.py:304
  89.9 0.0 all-to-all-done.2
  89.9 3.1 %weight.1 = bf16[8,208,256]{2,1,0:T(8,128)(2,1)S(1)} custom-call(bf16[1536,512]{1,0:T(8,128)(2,1)S(1)} %bitcast.5, bf16[2,448,256]{2,1,0:T(8,128)(2,1)S(1)} %both.1.got_ref, bf16[16,256]{1,0:T(8,128)(2,1)S(1)} %get-tuple-element.73.s_ref), custom_call_target="tpu_custom_call" | custom-call | tf_op jit(solution)/shard_map/weight/pallas_call | solution.py:408
  93.1 0.0 copy-start.2
  93.1 0.9 copy-done.2
  94.0 4.3 %all-to-all-start.3 = ((bf16[8,208,256]{2,1,0:T(8,128)(2,1)}), bf16[8,208,256]{2,1,0:T(8,128)(2,1)}, u32[]{:S(2)}, u32[]{:S(2)}) async-start(bf16[8,208,256]{2,1,0:T(8,128)(2,1)} %copy-done.2), calls=%async_computation.3 | async-start | bytes 1703936 | tf_op jit(solution)/shard_map/all_to_all | solution.py:321
  98.3 0.0 copy-done.1
  98.3 1.4 mixed.1
  99.7 0.7 copy-done.8
  100.4 4.1 %collective-permute-start.4 = (f32[256,256]{1,0:T(8,128)}, f32[256,256]{1,0:T(8,128)S(1)}, u32[]{:S(2)}, u32[]{:S(2)}) collective-permute-start(f32[256,256]{1,0:T(8,128)} %get-tuple-element.61), channel_id=1, source_target_pairs={{0,16},{16,0},{1,17},{17,1},{2,18},{18,2},{3,19},{19,3},{4,20},{20... | collective-permute-start | bytes 786440 | tf_op jit(solution)/shard_map/ppermute | solution.py:335
  104.5 17.2 %all-to-all-done.3.t_ref = bf16[8,208,256]{2,1,0:T(8,128)(2,1)} async-done(((bf16[8,208,256]{2,1,0:T(8,128)(2,1)}), bf16[8,208,256]{2,1,0:T(8,128)(2,1)}, u32[]{:S(2)}, u32[]{:S(2)}) %all-to-all-start.3) | async-done | bytes 852000 | tf_op jit(solution)/shard_map/all_to_all | solution.py:321
  121.8 1.9 %middle.1 = bf16[3,80,256]{2,1,0:T(8,128)(2,1)} custom-call(bf16[8,208,256]{2,1,0:T(8,128)(2,1)} %all-to-all-done.3.t_ref, f32[16,128]{1,0:T(8,128)S(1)} %get-tuple-element.52.d_ref.refs_0_), custom_call_target="tpu_custom_call" | custom-call | tf_op jit(solution)/shard_map/middle/pallas_call | solution.py:304
  123.7 7.7 %all-to-all-start.4 = ((bf16[3,80,256]{2,1,0:T(8,128)(2,1)}), bf16[3,80,256]{2,1,0:T(8,128)(2,1)S(1)}, u32[]{:S(2)}, u32[]{:S(2)}) async-start(bf16[3,80,256]{2,1,0:T(8,128)(2,1)} %middle.1), calls=%async_computation.4 | async-start | bytes 245760 | tf_op jit(solution)/shard_map/all_to_all | solution.py:321
  131.4 2.7 %collective-permute-start.9 = (bf16[96,256]{1,0:T(8,128)(2,1)S(1)}, bf16[96,256]{1,0:T(8,128)(2,1)S(1)}, u32[]{:S(2)}, u32[]{:S(2)}) collective-permute-start(bf16[96,256]{1,0:T(8,128)(2,1)S(1)} %get-tuple-element.70), channel_id=1, source_target_pairs={{0,16},{16,0},{1,17},{17,1},{2,18},{18,2},{3,19},{19,3},{4,20},{20... | collective-permute-start | bytes 147464 | tf_op jit(solution)/shard_map/ppermute | solution.py:335
  134.1 0.9 collective-permute-done.9.other_ref
  134.9 0.0 collective-permute-done.4.mr_ref
  134.9 0.9 copy-done.9
  135.9 0.8 finish.1
  136.6 1.9 %all-to-all-done.4.refs_2_ = bf16[3,80,256]{2,1,0:T(8,128)(2,1)S(1)} async-done(((bf16[3,80,256]{2,1,0:T(8,128)(2,1)}), bf16[3,80,256]{2,1,0:T(8,128)(2,1)S(1)}, u32[]{:S(2)}, u32[]{:S(2)}) %all-to-all-start.4) | async-done | bytes 122912 | tf_op jit(solution)/shard_map/all_to_all | solution.py:321
  138.5 1.7 %last.1 = (f32[128,256]{1,0:T(8,128)S(1)}, f32[128,256]{1,0:T(8,128)S(1)}) custom-call(f32[16,128]{1,0:T(8,128)S(1)} %get-tuple-element.52.d_ref.refs_0_, f32[16,128]{1,0:T(8,128)S(1)} %get-tuple-element.53.c_ref.refs_1_, bf16[3,80,256]{2,1,0:T(8,128)(2,1)S(1)} %all-to-all-done.4.refs_2_, f32[512,128]{1,0:T(8,128)S(1)} %get-tuple-element.77.refs_3_), custom_call_target="tpu_custom_call" | custom-call | tf_op jit(solution)/shard_map/last/pallas_call | solution.py:304
  140.2 4.6 %collective-permute-start.10 = (f32[128,256]{1,0:T(8,128)S(1)}, f32[128,256]{1,0:T(8,128)S(1)}, u32[]{:S(2)}, u32[]{:S(2)}) collective-permute-start(f32[128,256]{1,0:T(8,128)S(1)} %get-tuple-element.79), channel_id=1, source_target_pairs={{0,16},{16,0},{1,17},{17,1},{2,18},{18,2},{3,19},{19,3},{4,20},{20... | collective-permute-start | bytes 393224 | tf_op jit(solution)/shard_map/ppermute | solution.py:335
  144.8 1.0 collective-permute-done.10.other_hbm
  145.7 0.0 copy-done.6
  145.7 0.0 copy-done.7
  145.7 1.4 end.1
  (7 shorter events, 0.1 us)
Async XLA Ops:
  2.5 14.2 %collective-permute-start.3 = (bf16[448,256]{1,0:T(8,128)(2,1)}, bf16[448,256]{1,0:T(8,128)(2,1)S(1)}, u32[]{:S(2)}, u32[]{:S(2)}) collective-permute-start(bf16[448,256]{1,0:T(8,128)(2,1)} %get-tuple-element.55), channel_id=1, source_target_pairs={{0,16},{16,0},{1,17},{17,1},{2,18},{18,2},{3,19},{19,3},{4,20},{20... | collective-permute-start | bytes 688136 | tf_op jit(solution)/shard_map/ppermute | solution.py:335
  15.7 0.7 copy-start.10
  16.7 1.0 copy-start.3
  17.7 27.3 %copy-start.4 = (bf16[448,256]{1,0:T(8,128)(2,1)S(1)}, bf16[448,256]{1,0:T(8,128)(2,1)}, u32[]{:S(2)}) copy-start(bf16[448,256]{1,0:T(8,128)(2,1)} %get-tuple-element.54.own_hbm) | copy-start | bytes 688132
  20.5 25.1 %all-to-all-start = ((f32[24,16,128]{2,1,0:T(8,128)}), f32[24,16,128]{2,1,0:T(8,128)S(1)}, u32[]{:S(2)}, u32[]{:S(2)}) async-start(f32[24,16,128]{2,1,0:T(8,128)} %get-tuple-element.56), calls=%async_computation | async-start | bytes 393216 | tf_op jit(solution)/shard_map/all_to_all | solution.py:321
  30.6 1.4 copy-start
  32.1 0.9 copy-start.5
  34.4 19.4 %collective-permute-start = (bf16[768,256]{1,0:T(8,128)(2,1)}, bf16[768,256]{1,0:T(8,128)(2,1)S(1)}, u32[]{:S(2)}, u32[]{:S(2)}) collective-permute-start(bf16[768,256]{1,0:T(8,128)(2,1)} %get-tuple-element.45), channel_id=1, source_target_pairs={{0,4},{4,8},{8,12},{12,0},{1,5},{5,9},{9,13},{13,1},{2,6},{6,10},{... | collective-permute-start | bytes 1179656 | tf_op jit(solution)/shard_map/ppermute | solution.py:331
  37.5 20.0 %collective-permute-start.1 = (bf16[768,256]{1,0:T(8,128)(2,1)}, bf16[768,256]{1,0:T(8,128)(2,1)S(1)}, u32[]{:S(2)}, u32[]{:S(2)}) collective-permute-start(bf16[768,256]{1,0:T(8,128)(2,1)} %get-tuple-element.46), channel_id=1, source_target_pairs={{0,8},{4,12},{8,0},{12,4},{1,9},{5,13},{9,1},{13,5},{2,10},{6,14},... | collective-permute-start | bytes 1179656 | tf_op jit(solution)/shard_map/ppermute | solution.py:331
  41.9 17.0 %collective-permute-start.2 = (bf16[768,256]{1,0:T(8,128)(2,1)S(1)}, bf16[768,256]{1,0:T(8,128)(2,1)}, u32[]{:S(2)}, u32[]{:S(2)}) collective-permute-start(bf16[768,256]{1,0:T(8,128)(2,1)S(1)} %get-tuple-element.47), channel_id=1, source_target_pairs={{0,12},{4,0},{8,4},{12,8},{1,13},{5,1},{9,5},{13,9},{2,14},{6,2},{... | collective-permute-start | bytes 1179656 | tf_op jit(solution)/shard_map/ppermute | solution.py:331
  47.8 17.2 %all-to-all-start.1 = ((bf16[4,96,512]{2,1,0:T(8,128)(2,1)}), bf16[4,96,512]{2,1,0:T(8,128)(2,1)S(1)}, u32[]{:S(2)}, u32[]{:S(2)}) async-start(bf16[4,96,512]{2,1,0:T(8,128)(2,1)} %get-tuple-element.58), calls=%async_computation.1 | async-start | bytes 786432 | tf_op jit(solution)/shard_map/all_to_all | solution.py:321
  66.3 23.6 %all-to-all-start.2 = ((bf16[4,384,512]{2,1,0:T(8,128)(2,1)}), bf16[4,384,512]{2,1,0:T(8,128)(2,1)S(1)}, u32[]{:S(2)}, u32[]{:S(2)}) async-start(bf16[4,384,512]{2,1,0:T(8,128)(2,1)} %broadcast_in_dim.2), calls=%async_computation.2 | async-start | bytes 3145728 | tf_op jit(solution)/shard_map/all_to_all | solution.py:321
  70.3 9.0 %collective-permute-start.5 = (bf16[192,256]{1,0:T(8,128)(2,1)S(1)}, bf16[192,256]{1,0:T(8,128)(2,1)S(1)}, u32[]{:S(2)}, u32[]{:S(2)}) collective-permute-start(bf16[192,256]{1,0:T(8,128)(2,1)S(1)} %get-tuple-element.63), channel_id=1, source_target_pairs={{0,1},{1,2},{2,3},{3,0},{4,5},{5,6},{6,7},{7,4},{8,9},{9,10},{10,1... | collective-permute-start | bytes 294920 | tf_op jit(solution)/shard_map/ppermute | solution.py:331
  72.3 8.8 %collective-permute-start.6 = (bf16[192,256]{1,0:T(8,128)(2,1)S(1)}, bf16[192,256]{1,0:T(8,128)(2,1)S(1)}, u32[]{:S(2)}, u32[]{:S(2)}) collective-permute-start(bf16[192,256]{1,0:T(8,128)(2,1)S(1)} %get-tuple-element.64), channel_id=1, source_target_pairs={{0,2},{1,3},{2,0},{3,1},{4,6},{5,7},{6,4},{7,5},{8,10},{9,11},{10,... | collective-permute-start | bytes 294920 | tf_op jit(solution)/shard_map/ppermute | solution.py:331
  75.3 7.4 %collective-permute-start.7 = (bf16[192,256]{1,0:T(8,128)(2,1)S(1)}, bf16[192,256]{1,0:T(8,128)(2,1)S(1)}, u32[]{:S(2)}, u32[]{:S(2)}) collective-permute-start(bf16[192,256]{1,0:T(8,128)(2,1)S(1)} %get-tuple-element.65), channel_id=1, source_target_pairs={{0,3},{1,0},{2,1},{3,2},{4,7},{5,4},{6,5},{7,6},{8,11},{9,8},{10,9... | collective-permute-start | bytes 294920 | tf_op jit(solution)/shard_map/ppermute | solution.py:331
  82.7 5.1 %collective-permute-start.8 = (f32[96,256]{1,0:T(8,128)S(1)}, f32[96,256]{1,0:T(8,128)S(1)}, u32[]{:S(2)}, u32[]{:S(2)}) collective-permute-start(f32[96,256]{1,0:T(8,128)S(1)} %get-tuple-element.67), channel_id=1, source_target_pairs={{0,16},{16,0},{1,17},{17,1},{2,18},{18,2},{3,19},{19,3},{4,20},{20... | collective-permute-start | bytes 294920 | tf_op jit(solution)/shard_map/ppermute | solution.py:335
  93.1 0.9 copy-start.2
  94.0 4.4 %copy-start.1 = (bf16[3072,256]{1,0:T(8,128)(2,1)S(1)}, bf16[3072,256]{1,0:T(8,128)(2,1)}, u32[]{:S(2)}) copy-start(bf16[3072,256]{1,0:T(8,128)(2,1)} %w_ref.3) | copy-start | bytes 4718596
  94.0 27.8 %all-to-all-start.3 = ((bf16[8,208,256]{2,1,0:T(8,128)(2,1)}), bf16[8,208,256]{2,1,0:T(8,128)(2,1)}, u32[]{:S(2)}, u32[]{:S(2)}) async-start(bf16[8,208,256]{2,1,0:T(8,128)(2,1)} %copy-done.2), calls=%async_computation.3 | async-start | bytes 1703936 | tf_op jit(solution)/shard_map/all_to_all | solution.py:321
  99.7 0.7 copy-start.8
  100.4 45.3 %copy-start.6 = (bf16[192,256]{1,0:T(8,128)(2,1)S(1)}, bf16[192,256]{1,0:T(8,128)(2,1)}, u32[]{:S(2)}) copy-start(bf16[192,256]{1,0:T(8,128)(2,1)} %i_hbm.3) | copy-start | bytes 294916
  100.4 45.3 %copy-start.7 = (bf16[192,256]{1,0:T(8,128)(2,1)S(1)}, bf16[192,256]{1,0:T(8,128)(2,1)}, u32[]{:S(2)}) copy-start(bf16[192,256]{1,0:T(8,128)(2,1)} %v_hbm.3) | copy-start | bytes 294916
  100.4 34.5 %collective-permute-start.4 = (f32[256,256]{1,0:T(8,128)}, f32[256,256]{1,0:T(8,128)S(1)}, u32[]{:S(2)}, u32[]{:S(2)}) collective-permute-start(f32[256,256]{1,0:T(8,128)} %get-tuple-element.61), channel_id=1, source_target_pairs={{0,16},{16,0},{1,17},{17,1},{2,18},{18,2},{3,19},{19,3},{4,20},{20... | collective-permute-start | bytes 786440 | tf_op jit(solution)/shard_map/ppermute | solution.py:335
  123.7 14.8 %all-to-all-start.4 = ((bf16[3,80,256]{2,1,0:T(8,128)(2,1)}), bf16[3,80,256]{2,1,0:T(8,128)(2,1)S(1)}, u32[]{:S(2)}, u32[]{:S(2)}) async-start(bf16[3,80,256]{2,1,0:T(8,128)(2,1)} %middle.1), calls=%async_computation.4 | async-start | bytes 245760 | tf_op jit(solution)/shard_map/all_to_all | solution.py:321
  131.4 3.5 %collective-permute-start.9 = (bf16[96,256]{1,0:T(8,128)(2,1)S(1)}, bf16[96,256]{1,0:T(8,128)(2,1)S(1)}, u32[]{:S(2)}, u32[]{:S(2)}) collective-permute-start(bf16[96,256]{1,0:T(8,128)(2,1)S(1)} %get-tuple-element.70), channel_id=1, source_target_pairs={{0,16},{16,0},{1,17},{17,1},{2,18},{18,2},{3,19},{19,3},{4,20},{20... | collective-permute-start | bytes 147464 | tf_op jit(solution)/shard_map/ppermute | solution.py:335
  134.9 1.0 copy-start.9
  140.2 5.5 %collective-permute-start.10 = (f32[128,256]{1,0:T(8,128)S(1)}, f32[128,256]{1,0:T(8,128)S(1)}, u32[]{:S(2)}, u32[]{:S(2)}) collective-permute-start(f32[128,256]{1,0:T(8,128)S(1)} %get-tuple-element.79), channel_id=1, source_target_pairs={{0,16},{16,0},{1,17},{17,1},{2,18},{18,2},{3,19},{19,3},{4,20},{20... | collective-permute-start | bytes 393224 | tf_op jit(solution)/shard_map/ppermute | solution.py:335

commit v8 on v7

--- a/solution.py
+++ b/solution.py
@@ -48,24 +48,20 @@
     fetch(sems, (own_hbm, out_ref.at[core]), (other_hbm, out_ref.at[1 - core]))
 
 
-def modes_kernel(d_ref, c_ref, od_ref, oc_ref):
+def modes_kernel(d_ref, c_ref, od_ref, oc_ref, ad_ref, ac_ref):
     chan = lax.broadcasted_iota(jnp.int32, (d_ref.shape[1], LANES), 0)
     lane = lax.broadcasted_iota(jnp.int32, (d_ref.shape[1], LANES), 1)
-    wanted = lane + SUB * (lane // SUB) + SUB * lax.axis_index(CORE)
-    pick = jnp.where((chan == wanted) & (lane < d_ref.shape[1] // 2), 1.0, 0.0).astype(f32)
-    for src, dst in ((d_ref, od_ref), (c_ref, oc_ref)):
-        dst[...] = jnp.dot(
-            src[...], pick, precision=lax.Precision.HIGHEST, preferred_element_type=f32
-        )
-
-
-def weight_rows(w_ref, core, block, count):
-    blocks = w_ref.shape[0] // (2 * SUB * count)
-    rows = []
-    for b in range(blocks):
-        start = 2 * SUB * (block * blocks + b) + SUB * core
-        rows.append(w_ref[pl.ds(pl.multiple_of(start, SUB), SUB), :])
-    return jnp.concatenate(rows, axis=0)
+    for src, own, both in ((d_ref, od_ref, ad_ref), (c_ref, oc_ref, ac_ref)):
+        for h in range(2):
+            wanted = lane + SUB * (lane // SUB) + SUB * h
+            pick = jnp.where((chan == wanted) & (lane < d_ref.shape[1] // 2), 1.0, 0.0)
+            both[h] = jnp.dot(
+                src[...],
+                pick.astype(f32),
+                precision=lax.Precision.HIGHEST,
+                preferred_element_type=f32,
+            )
+        own[...] = both[lax.axis_index(CORE)]
 
 
 def back_kernel(w_ref, g_ref, *outs):
@@ -173,7 +169,7 @@
             p_ref[q, :, at] = product
 
 
-def scan_backward_kernel(own_ref, other_ref, f_ref, got_ref, d_ref, c_ref, y_ref, s_ref, go_ref, gx_ref, bt):
+def scan_backward_kernel(own_ref, other_ref, f_ref, got_ref, d_ref, c_ref, yo_ref, yx_ref, s_ref, go_ref, gx_ref, bt, y_ref):
     tok = got_ref.shape[2]
     half = own_ref.shape[0]
     core = lax.axis_index(CORE)
@@ -185,6 +181,8 @@
         bt[at, :] = to_columns((total * outer).astype(bf16).astype(f32))
     state = scan(bt, y_ref, jnp.exp(-d_ref[...]), c_ref[...], True)
     put_state(s_ref, state)
+    yo_ref[...] = y_ref[pl.ds(pl.multiple_of(core * tok, tok), tok), :]
+    yx_ref[...] = y_ref[pl.ds(pl.multiple_of((1 - core) * tok, tok), tok), :]
 
 
 def put_state(ref, state):
@@ -198,25 +196,20 @@
     return both[:, :LANES] + both[:, LANES:]
 
 
-def weight_kernel(p_ref, got_ref, s_ref, out_hbm, out_ref, sems):
+def weight_kernel(p_ref, got_ref, s_ref, out_ref):
     tok = got_ref.shape[2]
     n = out_ref.shape[0]
     rows = p_ref.shape[0] // n
     grads = got_ref[:, :tok, :].reshape(2 * tok, -1)
-    copies = []
     for y in range(n):
         part = jnp.dot(p_ref[pl.ds(y * rows, rows), :], grads, preferred_element_type=f32)
         out_ref[y, :rows, :] = part.astype(bf16)
         out_ref[y, rows:, :] = s_ref[...]
-        copies.append(pltpu.make_async_copy(out_ref.at[y], out_hbm.at[y], sems.at[y]))
-        copies[-1].start()
-    for copy in copies:
-        copy.wait()
 
 
 def middle_kernel(t_ref, d_ref, out_ref):
     n = t_ref.shape[0]
-    zs, rows = out_ref.shape[0], 2 * SUB
+    zs, rows = out_ref.shape[0] // 2, 2 * SUB
     length = 2.0 * t_ref.shape[2]
     decay = d_ref[...]
     y, zh = lax.axis_index(Y), lax.axis_index(ZH)
@@ -231,12 +224,22 @@
         total = t_ref[0, pl.ds(z * rows, rows), :].astype(f32)
         for k in range(1, n):
             total = total + t_ref[k, pl.ds(z * rows, rows), :].astype(f32)
-        out_ref[z, :rows, :] = total.astype(bf16)
         far = (zs - 1 + zh - z).astype(f32) * length
         near = jnp.maximum(zh - z - 1, 0).astype(f32) * length
         carry = jnp.exp(-decay * far) * later
         carry = jnp.where(zh > z, carry + jnp.exp(-decay * near) * here, carry)
-        put_state(out_ref.at[z, rows:, :], carry)
+        for h in range(2):
+            out_ref[2 * z + h, :SUB, :] = total[h * SUB : (h + 1) * SUB].astype(bf16)
+            put_state(out_ref.at[2 * z + h, SUB:, :], carry)
+
+
+def weight_rows(w_ref, core, block, count):
+    blocks = w_ref.shape[0] // (2 * SUB * count)
+    rows = []
+    for b in range(blocks):
+        start = 2 * SUB * (block * blocks + b) + SUB * core
+        rows.append(w_ref[pl.ds(pl.multiple_of(start, SUB), SUB), :])
+    return jnp.concatenate(rows, axis=0)
 
 
 def mixed_kernel(p_ref, w_ref, own_ref, other_ref, total):
@@ -252,27 +255,6 @@
     other_ref[...] = total[:, pl.ds(pl.multiple_of((1 - core) * tok, tok), tok)]
 
 
-def last_kernel(scale, d_ref, c_ref, t_hbm, y_hbm, own_ref, other_ref, t_ref, y_ref, bt, sems):
-    fetch(sems, (t_hbm, t_ref), (y_hbm, y_ref))
-    rows = 2 * SUB
-    tok = y_ref.shape[0] // 2
-    half = own_ref.shape[0] - SUB
-    state = get_state(t_ref[0, rows:, :])
-    for m in range(1, t_ref.shape[0]):
-        state = state + get_state(t_ref[m, rows:, :])
-    core = lax.axis_index(CORE)
-    for h, ref in ((core, own_ref), (1 - core, other_ref)):
-        mine = pl.ds(pl.multiple_of(h * SUB, SUB), SUB)
-        total = t_ref[0, mine, :].astype(f32)
-        for m in range(1, t_ref.shape[0]):
-            total = total + t_ref[m, mine, :].astype(f32)
-        ref[half:] = total * scale
-    heads(y_ref, bt, state * c_ref[...], jnp.exp(-d_ref[...]), True)
-    for h, ref in ((core, own_ref), (1 - core, other_ref)):
-        at = pl.ds(pl.multiple_of(h * tok, tok), tok)
-        ref[:half] = bt[at, :].T[:half].astype(bf16).astype(f32)
-
-
 def halves(core, own_ref, other_ref, count):
     for h, ref in ((core, own_ref), (1 - core, other_ref)):
         for b in range(count):
@@ -286,16 +268,28 @@
         go_ref[at, :] = ref[src, :]
 
 
-def end_kernel(own_hbm, other_hbm, i_hbm, v_hbm, gi_ref, gv_ref, gw_ref, own_ref, other_ref, i_ref, v_ref, sems):
-    fetch(sems, (own_hbm, own_ref), (other_hbm, other_ref), (i_hbm, i_ref), (v_hbm, v_ref))
+def last_kernel(scale, d_ref, c_ref, t_hbm, yo_hbm, yx_hbm, i_hbm, v_hbm, gi_ref, gv_ref, gw_ref, t_ref, yo_ref, yx_ref, i_ref, v_ref, bt, sems):
+    fetch(sems, (t_hbm, t_ref), (yo_hbm, yo_ref), (yx_hbm, yx_ref), (i_hbm, i_ref), (v_hbm, v_ref))
+    tok = yo_ref.shape[0]
     half = i_ref.shape[0] // 2
     core = lax.axis_index(CORE)
-    for at, ref, src in halves(core, own_ref, other_ref, half // SUB):
-        back = ref[src, :]
-        gi_ref[at, :] = (back * v_ref[at, :].astype(f32)).astype(bf16)
-        gv_ref[at, :] = (back * i_ref[at, :].astype(f32)).astype(bf16)
-    for h, ref in ((core, own_ref), (1 - core, other_ref)):
-        gw_ref[pl.ds(pl.multiple_of(SUB * h, SUB), SUB), :] = ref[half:]
+    later = (1 - core).astype(f32) * tok
+    for h, y_ref in ((core, yo_ref), (1 - core, yx_ref)):
+        state = get_state(t_ref[h, SUB:, :])
+        total = t_ref[h, :SUB, :].astype(f32)
+        for z in range(1, t_ref.shape[0] // 2):
+            state = state + get_state(t_ref[2 * z + h, SUB:, :])
+            total = total + t_ref[2 * z + h, :SUB, :].astype(f32)
+        gw_ref[pl.ds(pl.multiple_of(SUB * h, SUB), SUB), :] = total * scale
+        decay = d_ref[h]
+        state = state * jnp.exp(-decay * later) * c_ref[h]
+        heads(y_ref, bt, state, jnp.exp(-decay), True)
+        back = bt[...].T[:half].astype(bf16).astype(f32)
+        for b in range(half // SUB):
+            at = pl.ds(pl.multiple_of(2 * SUB * b + SUB * h, SUB), SUB)
+            part = back[SUB * b : SUB * (b + 1)]
+            gi_ref[at, :] = (part * v_ref[at, :].astype(f32)).astype(bf16)
+            gv_ref[at, :] = (part * i_ref[at, :].astype(f32)).astype(bf16)
 
 
 def call(kernel, name, outs, args, scratch=(), cost=None, remote=0, limit=24):
@@ -358,7 +352,10 @@
     other = other_core(other)
     coef = residues * jnp.sqrt(-jnp.expm1(-2.0 * decays))
     small = ((modes, LANES), f32)
-    decay, coef = call(modes_kernel, "modes", [small, small], (decays.T, coef.T))
+    pair = ((2, modes, LANES), f32)
+    decay, coef, decay_both, coef_both = call(
+        modes_kernel, "modes", [small, small, pair, pair], (decays.T, coef.T)
+    )
 
     columns = ((length, LANES), f32)
     yf, states = call(
@@ -396,29 +393,25 @@
         (own, *(shift(part, "zl", k + 1) for k, part in enumerate(parts))),
     )
     product = spread(jnp.broadcast_to(product[None], (nx,) + product.shape), "x")
-    yb, state, grad_outer, grad_outer_other = call(
+    half_columns = ((tok, LANES), f32)
+    yb, yb_other, state, grad_outer, grad_outer_other = call(
         scan_backward_kernel,
         "scan_backward",
-        [columns, ((modes, 2 * LANES), bf16)] + [((half, tok), bf16)] * 2,
+        [half_columns] * 2 + [((modes, 2 * LANES), bf16)] + [((half, tok), bf16)] * 2,
         (own, other_core(other), filtered, got, decay, coef),
-        scratch=[columns],
-    )
-
-    sums = (ny, nh * 2 * SUB + modes, cols)
-    partial = pl.pallas_call(
+        scratch=[columns] * 2,
+    )
+
+    (partial,) = call(
         weight_kernel,
-        out_shape=jax.ShapeDtypeStruct(sums, bf16),
-        in_specs=[pl.BlockSpec(memory_space=pltpu.VMEM)] * 3,
-        out_specs=pl.BlockSpec(memory_space=pl.ANY),
-        scratch_shapes=[pltpu.VMEM(sums, bf16), pltpu.SemaphoreType.DMA((ny,))],
-        compiler_params=pltpu.CompilerParams(vmem_limit_bytes=24 * 2**20),
-        name="weight",
-    )(product, got, state)
+        "weight",
+        [((ny, nh * 2 * SUB + modes, cols), bf16)],
+        (product, got, state),
+    )
     partial = swap(partial, "y")
-    (partial,) = call(
-        middle_kernel, "middle", [((nh, 2 * SUB + modes, cols), bf16)], (partial, decay)
-    )
-    partial = swap(partial, "zh")
+    last = ((2 * nh, SUB + modes, cols), bf16)
+    (partial,) = call(middle_kernel, "middle", [last], (partial, decay))
+    partial = swap(partial, ("zh", "core"))
     mixed, mixed_other = call(
         mixed_kernel,
         "mixed",
@@ -434,22 +427,21 @@
     )
     mixed, grad_outer, partial = lax.optimization_barrier((mixed, grad_outer, partial))
     scale = 1.0 / math.sqrt(length * chips)
-    late = ((half + SUB, cols), f32)
-    own, other = call(
+    grad_inner, grad_value, grad_weight = call(
         lambda *refs: last_kernel(scale, *refs),
         "last",
-        [late] * 2,
-        (decay, coef, partial.reshape(nh, 2 * SUB + modes, cols), yb),
-        scratch=[((nh, 2 * SUB + modes, cols), bf16), columns, columns],
-        remote=2,
-    )
-    grad_inner, grad_value, grad_weight = call(
-        end_kernel,
-        "end",
         [gate, gate, ((2 * SUB, cols), f32)],
-        (own, other_core(other), inner_gate, value_proj),
-        scratch=[late, late, gate, gate],
-        remote=4,
+        (
+            decay_both,
+            coef_both,
+            partial.reshape(last[0]),
+            yb,
+            other_core(yb_other),
+            inner_gate,
+            value_proj,
+        ),
+        scratch=[last, half_columns, half_columns, gate, gate, half_columns],
+        remote=5,
     )
     return (mixed, grad_outer, grad_inner, grad_value, grad_weight)
 

time: 148 us -> 145 us (0.980)
  blocking collectives: 0 us -> 28.1 us
  waiting for transfers between devices: 35.2 us -> 16 us
  starting transfers between devices: 79.6 us -> 70.3 us
  Pallas kernels: 22.8 us -> 19.6 us
    all_to_all x0 -> x1, blocking collectives: none -> 28.1 us  [swap(): return lax.all_to_all(x, axes, 0, 0, tiled=True)]
    all_to_all x5 -> x4, waiting for transfers between devices: 24 us -> 5.22 us  [swap(): return lax.all_to_all(x, axes, 0, 0, tiled=True)]
    ppermute x5, starting transfers between devices: 27.9 us -> 22.8 us  [other_core(): return lax.ppermute(x, 'core', [(0, 1), (1, 0)])]
    all_to_all x5 -> x4, starting transfers between devices: 32.2 us -> 28 us  [swap(): return lax.all_to_all(x, axes, 0, 0, tiled=True)]
    pallas_call x1 -> x0, Pallas kernels: 3.12 us -> none  [shards(): pl.pallas_call(weight_kernel, out_shape=jax.ShapeDtypeStruct(sums, bf16),...]
    unnamed x22 -> x28, local copies, waits for them, and re-layouts: 6.56 us -> 6.86 us
  transfers between devices with their start and end apart: 16 -> 15, of which waited for: 10 -> 8; matrix products, arithmetic and copies ran while one was open for 1% -> 1% of each run, Pallas kernels for 8% -> 7%
where the time goes in v8:
time: 145 us; the launch traced here: 144 us
  starting transfers between devices  70.3 us (48%)
  blocking collectives  28.1 us (19%)
  Pallas kernels  19.6 us (14%)
  waiting for transfers between devices  16 us (11%)
  local copies, waits for them, and re-layouts  8.16 us (6%)
    all_to_all x1, blocking collectives, swap(): return lax.all_to_all(x, axes, 0, 0, tiled=True)  28.1 us
    all_to_all x4, starting transfers between devices, swap(): return lax.all_to_all(x, axes, 0, 0, tiled=True)  28 us
    ppermute x5, starting transfers between devices, other_core(): return lax.ppermute(x, 'core', [(0, 1), (1, 0)])  22.8 us
    pallas_call x14, Pallas kernels, call(): pl.pallas_call(kernel, out_shape=tuple((jax.ShapeDtypeStruct(s, t) for s,...  19.6 us
    ppermute x6, starting transfers between devices, shift(): return lax.ppermute(x, axis, [(i, (i + k) % n) for i in range(n)])  19.5 us
    ppermute x6, waiting for transfers between devices, shift(): return lax.ppermute(x, axis, [(i, (i + k) % n) for i in range(n)])  8.64 us
    unnamed x28, local copies, waits for them, and re-layouts  6.86 us
    all_to_all x4, waiting for transfers between devices, swap(): return lax.all_to_all(x, axes, 0, 0, tiled=True)  5.22 us
  transfers between devices with their start and end apart: 15, of which 8 were waited for; matrix products, arithmetic and copies ran while one was open for 1% of the time, Pallas kernels for 7%

profile of v8, /device:TPU:1, one launch (start us, length us, event | category | flops | bytes accessed | tf_op | source)
XLA Modules:
  0.0 143.8 jit_solution(2496669012195419025)
XLA Ops:
  0.6 1.9 %pack.1 = (bf16[448,256]{1,0:T(8,128)(2,1)}, bf16[448,256]{1,0:T(8,128)(2,1)}) custom-call(bf16[192,256]{1,0:T(8,128)(2,1)} %refs_5_.1, bf16[192,256]{1,0:T(8,128)(2,1)} %refs_6_.1, bf16[192,256]{1,0:T(8,128)(2,1)} %o_hbm.1, bf16[256,256]{1,0:T(8,128)(2,1)} %g_hbm.1), custom_call_target="tpu_custom_call" | custom-call | tf_op jit(solution)/shard_map/pack/pallas_call | solution.py:298
  2.5 12.4 %collective-permute-start.3 = (bf16[448,256]{1,0:T(8,128)(2,1)}, bf16[448,256]{1,0:T(8,128)(2,1)S(1)}, u32[]{:S(2)}, u32[]{:S(2)}) collective-permute-start(bf16[448,256]{1,0:T(8,128)(2,1)} %get-tuple-element.56), channel_id=1, source_target_pairs={{0,16},{16,0},{1,17},{17,1},{2,18},{18,2},{3,19},{19,3},{4,20},{20... | collective-permute-start | bytes 688136 | tf_op jit(solution)/shard_map/ppermute | solution.py:329
  15.0 0.8 multiply_bitcast_fusion.c_ref
  15.7 0.0 copy-start.9
  15.7 0.7 copy-done.9
  16.4 0.4 modes.1
  16.9 0.0 collective-permute-done.3.other_hbm
  16.9 0.0 copy-start.2
  16.9 0.9 copy-done.2
  17.8 2.8 %scan_forward.1 = (f32[512,128]{1,0:T(8,128)S(1)}, f32[24,16,128]{2,1,0:T(8,128)}) custom-call(f32[16,128]{1,0:T(8,128)S(1)} %get-tuple-element.53.d_ref, f32[16,128]{1,0:T(8,128)S(1)} %get-tuple-element.54.c_ref, bf16[448,256]{1,0:T(8,128)(2,1)S(1)} %copy-done.2, bf16[448,256]{1,0:T(8,128)(2,1)S(1)} %collective-permute-done.3.other_hbm), custom_call_target="tpu_custom_call" | custom-call | tf_op jit(solution)/shard_map/scan_forward/pallas_call | solution.py:298
  20.6 10.2 %all-to-all-start = ((f32[24,16,128]{2,1,0:T(8,128)}), f32[24,16,128]{2,1,0:T(8,128)S(1)}, u32[]{:S(2)}, u32[]{:S(2)}) async-start(f32[24,16,128]{2,1,0:T(8,128)} %get-tuple-element.57), calls=%async_computation | async-start | bytes 393216 | tf_op jit(solution)/shard_map/all_to_all | solution.py:315
  30.8 0.0 copy-start
  30.8 1.4 copy-done
  32.2 0.9 copy-done.4
  33.1 1.7 %back.1 = (bf16[768,256]{1,0:T(8,128)(2,1)S(1)}, bf16[768,256]{1,0:T(8,128)(2,1)}, bf16[768,256]{1,0:T(8,128)(2,1)}, bf16[768,256]{1,0:T(8,128)(2,1)}) custom-call(bf16[3072,256]{1,0:T(8,128)(2,1)S(1)} %copy-done, bf16[256,256]{1,0:T(8,128)(2,1)S(1)} %copy-done.4), custom_call_target="tpu_custom_call" | custom-call | tf_op jit(solution)/shard_map/back/pallas_call | solution.py:298
  34.8 3.1 %collective-permute-start = (bf16[768,256]{1,0:T(8,128)(2,1)}, bf16[768,256]{1,0:T(8,128)(2,1)S(1)}, u32[]{:S(2)}, u32[]{:S(2)}) collective-permute-start(bf16[768,256]{1,0:T(8,128)(2,1)} %get-tuple-element.46), channel_id=1, source_target_pairs={{0,4},{4,8},{8,12},{12,0},{1,5},{5,9},{9,13},{13,1},{2,6},{6,10},{... | collective-permute-start | bytes 1179656 | tf_op jit(solution)/shard_map/ppermute | solution.py:325
  38.0 4.4 %collective-permute-start.1 = (bf16[768,256]{1,0:T(8,128)(2,1)}, bf16[768,256]{1,0:T(8,128)(2,1)S(1)}, u32[]{:S(2)}, u32[]{:S(2)}) collective-permute-start(bf16[768,256]{1,0:T(8,128)(2,1)} %get-tuple-element.47), channel_id=1, source_target_pairs={{0,8},{4,12},{8,0},{12,4},{1,9},{5,13},{9,1},{13,5},{2,10},{6,14},... | collective-permute-start | bytes 1179656 | tf_op jit(solution)/shard_map/ppermute | solution.py:325
  42.3 3.1 %collective-permute-start.2 = (bf16[768,256]{1,0:T(8,128)(2,1)}, bf16[768,256]{1,0:T(8,128)(2,1)}, u32[]{:S(2)}, u32[]{:S(2)}) collective-permute-start(bf16[768,256]{1,0:T(8,128)(2,1)} %get-tuple-element.48), channel_id=1, source_target_pairs={{0,12},{4,0},{8,4},{12,8},{1,13},{5,1},{9,5},{13,9},{2,14},{6,2},{... | collective-permute-start | bytes 1179656 | tf_op jit(solution)/shard_map/ppermute | solution.py:325
  45.4 0.0 copy-done.3
  45.4 0.6 both.1.got_ref
  46.0 0.0 copy-done.10
  46.1 0.0 all-to-all-done.s_ref
  46.1 2.2 %heads_forward.1 = (bf16[4,96,512]{2,1,0:T(8,128)(2,1)}, bf16[2,96,256]{2,1,0:T(8,128)(2,1)S(1)}) custom-call(f32[24,16,128]{2,1,0:T(8,128)S(1)} %all-to-all-done.s_ref, f32[16,128]{1,0:T(8,128)S(1)} %get-tuple-element.53.d_ref, f32[16,128]{1,0:T(8,128)S(1)} %get-tuple-element.54.c_ref, f32[512,128]{1,0:T(8,128)S(1)} %get-tuple-element.58.y_ref, ...), custom_call_target="tpu_custom_call" | custom-call | tf_op jit(solution)/shard_map/heads_forward/pallas_call | solution.py:298
  48.2 5.8 %all-to-all-start.1 = ((bf16[4,96,512]{2,1,0:T(8,128)(2,1)}), bf16[4,96,512]{2,1,0:T(8,128)(2,1)S(1)}, u32[]{:S(2)}, u32[]{:S(2)}) async-start(bf16[4,96,512]{2,1,0:T(8,128)(2,1)} %get-tuple-element.59), calls=%async_computation.1 | async-start | bytes 786432 | tf_op jit(solution)/shard_map/all_to_all | solution.py:315
  54.0 0.0 collective-permute-done.p1
  54.0 4.0 %collective-permute-done.1.p2 = bf16[768,256]{1,0:T(8,128)(2,1)S(1)} collective-permute-done((bf16[768,256]{1,0:T(8,128)(2,1)}, bf16[768,256]{1,0:T(8,128)(2,1)S(1)}, u32[]{:S(2)}, u32[]{:S(2)}) %collective-permute-start.1) | collective-permute-done | bytes 393248 | tf_op jit(solution)/shard_map/ppermute | solution.py:325
  58.0 1.3 collective-permute-done.2.p3
  59.3 1.2 split.1
  60.5 4.7 %all-to-all-done.1 = bf16[4,96,512]{2,1,0:T(8,128)(2,1)S(1)} async-done(((bf16[4,96,512]{2,1,0:T(8,128)(2,1)}), bf16[4,96,512]{2,1,0:T(8,128)(2,1)S(1)}, u32[]{:S(2)}, u32[]{:S(2)}) %all-to-all-start.1) | async-done | bytes 393248 | tf_op jit(solution)/shard_map/all_to_all | solution.py:315
  65.2 1.3 broadcast_in_dim.2
  66.5 4.0 %all-to-all-start.2 = ((bf16[4,384,512]{2,1,0:T(8,128)(2,1)}), bf16[4,384,512]{2,1,0:T(8,128)(2,1)S(1)}, u32[]{:S(2)}, u32[]{:S(2)}) async-start(bf16[4,384,512]{2,1,0:T(8,128)(2,1)} %broadcast_in_dim.2), calls=%async_computation.2 | async-start | bytes 3145728 | tf_op jit(solution)/shard_map/all_to_all | solution.py:315
  70.5 1.9 %collective-permute-start.5 = (bf16[192,256]{1,0:T(8,128)(2,1)S(1)}, bf16[192,256]{1,0:T(8,128)(2,1)S(1)}, u32[]{:S(2)}, u32[]{:S(2)}) collective-permute-start(bf16[192,256]{1,0:T(8,128)(2,1)S(1)} %get-tuple-element.64), channel_id=1, source_target_pairs={{0,1},{1,2},{2,3},{3,0},{4,5},{5,6},{6,7},{7,4},{8,9},{9,10},{10,1... | collective-permute-start | bytes 294920 | tf_op jit(solution)/shard_map/ppermute | solution.py:325
  72.4 3.0 %collective-permute-start.6 = (bf16[192,256]{1,0:T(8,128)(2,1)S(1)}, bf16[192,256]{1,0:T(8,128)(2,1)S(1)}, u32[]{:S(2)}, u32[]{:S(2)}) collective-permute-start(bf16[192,256]{1,0:T(8,128)(2,1)S(1)} %get-tuple-element.65), channel_id=1, source_target_pairs={{0,2},{1,3},{2,0},{3,1},{4,6},{5,7},{6,4},{7,5},{8,10},{9,11},{10,... | collective-permute-start | bytes 294920 | tf_op jit(solution)/shard_map/ppermute | solution.py:325
  75.4 4.1 %collective-permute-start.7 = (bf16[192,256]{1,0:T(8,128)(2,1)S(1)}, bf16[192,256]{1,0:T(8,128)(2,1)S(1)}, u32[]{:S(2)}, u32[]{:S(2)}) collective-permute-start(bf16[192,256]{1,0:T(8,128)(2,1)S(1)} %get-tuple-element.66), channel_id=1, source_target_pairs={{0,3},{1,0},{2,1},{3,2},{4,7},{5,4},{6,5},{7,6},{8,11},{9,8},{10,9... | collective-permute-start | bytes 294920 | tf_op jit(solution)/shard_map/ppermute | solution.py:325
  79.5 0.0 collective-permute-done.5.p1
  79.5 1.7 %collective-permute-done.6.p2 = bf16[192,256]{1,0:T(8,128)(2,1)S(1)} collective-permute-done((bf16[192,256]{1,0:T(8,128)(2,1)S(1)}, bf16[192,256]{1,0:T(8,128)(2,1)S(1)}, u32[]{:S(2)}, u32[]{:S(2)}) %collective-permute-start.6) | collective-permute-done | bytes 98336 | tf_op jit(solution)/shard_map/ppermute | solution.py:325
  81.2 1.6 %collective-permute-done.7.p3 = bf16[192,256]{1,0:T(8,128)(2,1)S(1)} collective-permute-done((bf16[192,256]{1,0:T(8,128)(2,1)S(1)}, bf16[192,256]{1,0:T(8,128)(2,1)S(1)}, u32[]{:S(2)}, u32[]{:S(2)}) %collective-permute-start.7) | collective-permute-done | bytes 98336 | tf_op jit(solution)/shard_map/ppermute | solution.py:325
  82.9 4.1 %collective-permute-start.8 = (f32[96,256]{1,0:T(8,128)S(1)}, f32[96,256]{1,0:T(8,128)S(1)}, u32[]{:S(2)}, u32[]{:S(2)}) collective-permute-start(f32[96,256]{1,0:T(8,128)S(1)} %get-tuple-element.68), channel_id=1, source_target_pairs={{0,16},{16,0},{1,17},{17,1},{2,18},{18,2},{3,19},{19,3},{4,20},{20... | collective-permute-start | bytes 294920 | tf_op jit(solution)/shard_map/ppermute | solution.py:329
  87.0 0.9 collective-permute-done.8.other_ref
  87.9 2.8 %scan_backward.1 = (f32[256,128]{1,0:T(8,128)S(1)}, f32[256,128]{1,0:T(8,128)}, bf16[16,256]{1,0:T(8,128)(2,1)S(1)}, bf16[96,256]{1,0:T(8,128)(2,1)S(1)}, bf16[96,256]{1,0:T(8,128)(2,1)S(1)}) custom-call(f32[96,256]{1,0:T(8,128)S(1)} %get-tuple-element.67.own_ref, f32[96,256]{1,0:T(8,128)S(1)} %collective-permute-done.8.other_ref, ...), custom_call_target="tpu_custom_call" | custom-call | tf_op jit(solution)/shard_map/scan_backward/pallas_call | solution.py:298
  90.7 0.6 copy-done.7
  91.4 0.6 copy-done.12
  92.0 0.0 all-to-all-done.2
  92.0 0.6 weight.1
  92.6 0.0 copy-start.1
  92.6 28.1 %all_to_all.32.t_ref = bf16[8,208,256]{2,1,0:T(8,128)(2,1)S(1)} all-to-all(bf16[8,208,256]{2,1,0:T(8,128)(2,1)S(1)} %weight.1), channel_id=1, replica_groups=mesh['y'=8,'zh'=3,'core'=2,'x'=4,'zl'=4] {'y'}, dimensions={0} | all-to-all | bytes 1703936 | tf_op jit(solution)/shard_map/all_to_all | solution.py:315
  120.7 0.8 middle.1
  121.5 8.1 %all-to-all-start.4 = ((bf16[6,48,256]{2,1,0:T(8,128)(2,1)}), bf16[6,48,256]{2,1,0:T(8,128)(2,1)S(1)}, u32[]{:S(2)}, u32[]{:S(2)}) async-start(bf16[6,48,256]{2,1,0:T(8,128)(2,1)} %middle.1), calls=%async_computation.4 | async-start | bytes 294912 | tf_op jit(solution)/shard_map/all_to_all | solution.py:315
  129.6 0.0 copy-done.1
  129.6 0.0 copy-start.6
  129.6 0.7 mixed.1
  130.3 1.9 %collective-permute-start.4 = (f32[256,256]{1,0:T(8,128)S(1)}, f32[256,256]{1,0:T(8,128)S(1)}, u32[]{:S(2)}, u32[]{:S(2)}) collective-permute-start(f32[256,256]{1,0:T(8,128)S(1)} %get-tuple-element.62), channel_id=1, source_target_pairs={{0,16},{16,0},{1,17},{17,1},{2,18},{18,2},{3,19},{19,3},{4,20},{20... | collective-permute-start | bytes 786440 | tf_op jit(solution)/shard_map/ppermute | solution.py:329
  132.2 2.4 %collective-permute-start.10 = (f32[256,128]{1,0:T(8,128)}, f32[256,128]{1,0:T(8,128)S(1)}, u32[]{:S(2)}, u32[]{:S(2)}) collective-permute-start(f32[256,128]{1,0:T(8,128)} %get-tuple-element.81), channel_id=1, source_target_pairs={{0,16},{16,0},{1,17},{17,1},{2,18},{18,2},{3,19},{19,3},{4,20},{20... | collective-permute-start | bytes 393224 | tf_op jit(solution)/shard_map/ppermute | solution.py:329
  134.6 0.0 copy-done.13
  134.6 1.9 %collective-permute-start.9 = (bf16[96,256]{1,0:T(8,128)(2,1)S(1)}, bf16[96,256]{1,0:T(8,128)(2,1)S(1)}, u32[]{:S(2)}, u32[]{:S(2)}) collective-permute-start(bf16[96,256]{1,0:T(8,128)(2,1)S(1)} %copy-done.13), channel_id=1, source_target_pairs={{0,16},{16,0},{1,17},{17,1},{2,18},{18,2},{3,19},{19,3},{4,20},{20... | collective-permute-start | bytes 147464 | tf_op jit(solution)/shard_map/ppermute | solution.py:329
  136.6 1.2 collective-permute-done.9.other_ref
  137.8 0.0 collective-permute-done.4.mr_ref
  137.8 0.8 finish.1
  138.5 0.5 all-to-all-done.4.refs_2_
  139.1 0.0 collective-permute-done.10.refs_4_
  139.1 0.0 copy-done.6
  139.1 0.9 copy-done.8
  140.0 0.7 copy-done.11
  140.7 3.1 %last.1 = (bf16[192,256]{1,0:T(8,128)(2,1)}, bf16[192,256]{1,0:T(8,128)(2,1)}, f32[64,256]{1,0:T(8,128)}) custom-call(f32[2,16,128]{2,1,0:T(8,128)S(1)} %get-tuple-element.77.refs_0_, f32[2,16,128]{2,1,0:T(8,128)S(1)} %copy-done.11, bf16[6,48,256]{2,1,0:T(8,128)(2,1)S(1)} %all-to-all-done.4.refs_2_, f32[256,128]{1,0:T(8,128)S(1)} %copy-done.8, ...), custom_call_target="tpu_custom_call" | custom-call | tf_op jit(solution)/shard_map/last/pallas_call | solution.py:298
  (11 shorter events, 0.1 us)
Async XLA Ops:
  2.5 14.4 %collective-permute-start.3 = (bf16[448,256]{1,0:T(8,128)(2,1)}, bf16[448,256]{1,0:T(8,128)(2,1)S(1)}, u32[]{:S(2)}, u32[]{:S(2)}) collective-permute-start(bf16[448,256]{1,0:T(8,128)(2,1)} %get-tuple-element.56), channel_id=1, source_target_pairs={{0,16},{16,0},{1,17},{17,1},{2,18},{18,2},{3,19},{19,3},{4,20},{20... | collective-permute-start | bytes 688136 | tf_op jit(solution)/shard_map/ppermute | solution.py:329
  15.7 0.7 copy-start.9
  16.9 29.2 %copy-start.10 = (f32[2,16,128]{2,1,0:T(8,128)}, f32[2,16,128]{2,1,0:T(8,128)S(1)}, u32[]{:S(2)}) copy-start(f32[2,16,128]{2,1,0:T(8,128)S(1)} %get-tuple-element.78.refs_1_) | copy-start | bytes 49156
  16.9 0.9 copy-start.2
  17.8 27.6 %copy-start.3 = (bf16[448,256]{1,0:T(8,128)(2,1)S(1)}, bf16[448,256]{1,0:T(8,128)(2,1)}, u32[]{:S(2)}) copy-start(bf16[448,256]{1,0:T(8,128)(2,1)} %get-tuple-element.55.own_hbm) | copy-start | bytes 688132
  20.6 25.4 %all-to-all-start = ((f32[24,16,128]{2,1,0:T(8,128)}), f32[24,16,128]{2,1,0:T(8,128)S(1)}, u32[]{:S(2)}, u32[]{:S(2)}) async-start(f32[24,16,128]{2,1,0:T(8,128)} %get-tuple-element.57), calls=%async_computation | async-start | bytes 393216 | tf_op jit(solution)/shard_map/all_to_all | solution.py:315
  30.8 1.4 copy-start
  32.2 0.9 copy-start.4
  34.8 19.1 %collective-permute-start = (bf16[768,256]{1,0:T(8,128)(2,1)}, bf16[768,256]{1,0:T(8,128)(2,1)S(1)}, u32[]{:S(2)}, u32[]{:S(2)}) collective-permute-start(bf16[768,256]{1,0:T(8,128)(2,1)} %get-tuple-element.46), channel_id=1, source_target_pairs={{0,4},{4,8},{8,12},{12,0},{1,5},{5,9},{9,13},{13,1},{2,6},{6,10},{... | collective-permute-start | bytes 1179656 | tf_op jit(solution)/shard_map/ppermute | solution.py:325
  38.0 20.0 %collective-permute-start.1 = (bf16[768,256]{1,0:T(8,128)(2,1)}, bf16[768,256]{1,0:T(8,128)(2,1)S(1)}, u32[]{:S(2)}, u32[]{:S(2)}) collective-permute-start(bf16[768,256]{1,0:T(8,128)(2,1)} %get-tuple-element.47), channel_id=1, source_target_pairs={{0,8},{4,12},{8,0},{12,4},{1,9},{5,13},{9,1},{13,5},{2,10},{6,14},... | collective-permute-start | bytes 1179656 | tf_op jit(solution)/shard_map/ppermute | solution.py:325
  42.3 17.0 %collective-permute-start.2 = (bf16[768,256]{1,0:T(8,128)(2,1)}, bf16[768,256]{1,0:T(8,128)(2,1)}, u32[]{:S(2)}, u32[]{:S(2)}) collective-permute-start(bf16[768,256]{1,0:T(8,128)(2,1)} %get-tuple-element.48), channel_id=1, source_target_pairs={{0,12},{4,0},{8,4},{12,8},{1,13},{5,1},{9,5},{13,9},{2,14},{6,2},{... | collective-permute-start | bytes 1179656 | tf_op jit(solution)/shard_map/ppermute | solution.py:325
  48.2 17.0 %all-to-all-start.1 = ((bf16[4,96,512]{2,1,0:T(8,128)(2,1)}), bf16[4,96,512]{2,1,0:T(8,128)(2,1)S(1)}, u32[]{:S(2)}, u32[]{:S(2)}) async-start(bf16[4,96,512]{2,1,0:T(8,128)(2,1)} %get-tuple-element.59), calls=%async_computation.1 | async-start | bytes 786432 | tf_op jit(solution)/shard_map/all_to_all | solution.py:315
  66.5 25.5 %all-to-all-start.2 = ((bf16[4,384,512]{2,1,0:T(8,128)(2,1)}), bf16[4,384,512]{2,1,0:T(8,128)(2,1)S(1)}, u32[]{:S(2)}, u32[]{:S(2)}) async-start(bf16[4,384,512]{2,1,0:T(8,128)(2,1)} %broadcast_in_dim.2), calls=%async_computation.2 | async-start | bytes 3145728 | tf_op jit(solution)/shard_map/all_to_all | solution.py:315
  70.5 9.0 %collective-permute-start.5 = (bf16[192,256]{1,0:T(8,128)(2,1)S(1)}, bf16[192,256]{1,0:T(8,128)(2,1)S(1)}, u32[]{:S(2)}, u32[]{:S(2)}) collective-permute-start(bf16[192,256]{1,0:T(8,128)(2,1)S(1)} %get-tuple-element.64), channel_id=1, source_target_pairs={{0,1},{1,2},{2,3},{3,0},{4,5},{5,6},{6,7},{7,4},{8,9},{9,10},{10,1... | collective-permute-start | bytes 294920 | tf_op jit(solution)/shard_map/ppermute | solution.py:325
  72.4 8.8 %collective-permute-start.6 = (bf16[192,256]{1,0:T(8,128)(2,1)S(1)}, bf16[192,256]{1,0:T(8,128)(2,1)S(1)}, u32[]{:S(2)}, u32[]{:S(2)}) collective-permute-start(bf16[192,256]{1,0:T(8,128)(2,1)S(1)} %get-tuple-element.65), channel_id=1, source_target_pairs={{0,2},{1,3},{2,0},{3,1},{4,6},{5,7},{6,4},{7,5},{8,10},{9,11},{10,... | collective-permute-start | bytes 294920 | tf_op jit(solution)/shard_map/ppermute | solution.py:325
  75.4 7.4 %collective-permute-start.7 = (bf16[192,256]{1,0:T(8,128)(2,1)S(1)}, bf16[192,256]{1,0:T(8,128)(2,1)S(1)}, u32[]{:S(2)}, u32[]{:S(2)}) collective-permute-start(bf16[192,256]{1,0:T(8,128)(2,1)S(1)} %get-tuple-element.66), channel_id=1, source_target_pairs={{0,3},{1,0},{2,1},{3,2},{4,7},{5,4},{6,5},{7,6},{8,11},{9,8},{10,9... | collective-permute-start | bytes 294920 | tf_op jit(solution)/shard_map/ppermute | solution.py:325
  82.9 5.1 %collective-permute-start.8 = (f32[96,256]{1,0:T(8,128)S(1)}, f32[96,256]{1,0:T(8,128)S(1)}, u32[]{:S(2)}, u32[]{:S(2)}) collective-permute-start(f32[96,256]{1,0:T(8,128)S(1)} %get-tuple-element.68), channel_id=1, source_target_pairs={{0,16},{16,0},{1,17},{17,1},{2,18},{18,2},{3,19},{19,3},{4,20},{20... | collective-permute-start | bytes 294920 | tf_op jit(solution)/shard_map/ppermute | solution.py:329
  90.7 0.6 copy-start.7
  91.4 0.6 copy-start.12
  92.6 37.0 %copy-start.1 = (bf16[3072,256]{1,0:T(8,128)(2,1)S(1)}, bf16[3072,256]{1,0:T(8,128)(2,1)}, u32[]{:S(2)}) copy-start(bf16[3072,256]{1,0:T(8,128)(2,1)} %w_ref.3) | copy-start | bytes 4718596
  121.5 17.6 %all-to-all-start.4 = ((bf16[6,48,256]{2,1,0:T(8,128)(2,1)}), bf16[6,48,256]{2,1,0:T(8,128)(2,1)S(1)}, u32[]{:S(2)}, u32[]{:S(2)}) async-start(bf16[6,48,256]{2,1,0:T(8,128)(2,1)} %middle.1), calls=%async_computation.4 | async-start | bytes 294912 | tf_op jit(solution)/shard_map/all_to_all | solution.py:315
  129.6 5.0 %copy-start.13 = (bf16[96,256]{1,0:T(8,128)(2,1)S(1)}, bf16[96,256]{1,0:T(8,128)(2,1)}, u32[]{:S(2)}) copy-start(bf16[96,256]{1,0:T(8,128)(2,1)} %copy-done.12) | copy-start | bytes 147460
  129.6 9.5 %copy-start.5 = (bf16[192,256]{1,0:T(8,128)(2,1)S(1)}, bf16[192,256]{1,0:T(8,128)(2,1)}, u32[]{:S(2)}) copy-start(bf16[192,256]{1,0:T(8,128)(2,1)} %refs_5_.1) | copy-start | bytes 294916
  129.6 9.5 %copy-start.6 = (bf16[192,256]{1,0:T(8,128)(2,1)S(1)}, bf16[192,256]{1,0:T(8,128)(2,1)}, u32[]{:S(2)}) copy-start(bf16[192,256]{1,0:T(8,128)(2,1)} %refs_6_.1) | copy-start | bytes 294916
  130.3 7.5 %collective-permute-start.4 = (f32[256,256]{1,0:T(8,128)S(1)}, f32[256,256]{1,0:T(8,128)S(1)}, u32[]{:S(2)}, u32[]{:S(2)}) collective-permute-start(f32[256,256]{1,0:T(8,128)S(1)} %get-tuple-element.62), channel_id=1, source_target_pairs={{0,16},{16,0},{1,17},{17,1},{2,18},{18,2},{3,19},{19,3},{4,20},{20... | collective-permute-start | bytes 786440 | tf_op jit(solution)/shard_map/ppermute | solution.py:329
  132.2 6.9 %collective-permute-start.10 = (f32[256,128]{1,0:T(8,128)}, f32[256,128]{1,0:T(8,128)S(1)}, u32[]{:S(2)}, u32[]{:S(2)}) collective-permute-start(f32[256,128]{1,0:T(8,128)} %get-tuple-element.81), channel_id=1, source_target_pairs={{0,16},{16,0},{1,17},{17,1},{2,18},{18,2},{3,19},{19,3},{4,20},{20... | collective-permute-start | bytes 393224 | tf_op jit(solution)/shard_map/ppermute | solution.py:329
  134.6 3.1 %collective-permute-start.9 = (bf16[96,256]{1,0:T(8,128)(2,1)S(1)}, bf16[96,256]{1,0:T(8,128)(2,1)S(1)}, u32[]{:S(2)}, u32[]{:S(2)}) collective-permute-start(bf16[96,256]{1,0:T(8,128)(2,1)S(1)} %copy-done.13), channel_id=1, source_target_pairs={{0,16},{16,0},{1,17},{17,1},{2,18},{18,2},{3,19},{19,3},{4,20},{20... | collective-permute-start | bytes 147464 | tf_op jit(solution)/shard_map/ppermute | solution.py:329
  139.1 0.9 copy-start.8
  140.0 0.7 copy-start.11

commit v9 on v8

--- a/solution.py
+++ b/solution.py
@@ -242,8 +242,8 @@
     return jnp.concatenate(rows, axis=0)
 
 
-def mixed_kernel(p_ref, w_ref, own_ref, other_ref, total):
-    tok = own_ref.shape[1]
+def mixed_kernel(p_ref, w_ref, y_ref, g_ref, own_ref, other_ref, total):
+    cols, tok = own_ref.shape
     total[...] = lax.dot_general(
         weight_rows(w_ref, lax.axis_index(CORE), 0, 1),
         p_ref[...],
@@ -252,7 +252,9 @@
     )
     core = lax.axis_index(CORE)
     own_ref[...] = total[:, pl.ds(pl.multiple_of(core * tok, tok), tok)]
-    other_ref[...] = total[:, pl.ds(pl.multiple_of((1 - core) * tok, tok), tok)]
+    other_ref[:cols, :tok] = total[:, pl.ds(pl.multiple_of((1 - core) * tok, tok), tok)]
+    other_ref[:cols, tok:] = y_ref[...]
+    other_ref[cols:, :tok] = g_ref[...].astype(f32)
 
 
 def halves(core, own_ref, other_ref, count):
@@ -262,15 +264,19 @@
             yield at, ref, pl.ds(SUB * b, SUB)
 
 
-def finish_kernel(m_ref, mr_ref, own_ref, other_ref, mixed_ref, go_ref):
-    mixed_ref[...] = (m_ref[...] + mr_ref[...]).T.astype(bf16)
-    for at, ref, src in halves(lax.axis_index(CORE), own_ref, other_ref, own_ref.shape[0] // SUB):
-        go_ref[at, :] = ref[src, :]
-
-
-def last_kernel(scale, d_ref, c_ref, t_hbm, yo_hbm, yx_hbm, i_hbm, v_hbm, gi_ref, gv_ref, gw_ref, t_ref, yo_ref, yx_ref, i_ref, v_ref, bt, sems):
-    fetch(sems, (t_hbm, t_ref), (yo_hbm, yo_ref), (yx_hbm, yx_ref), (i_hbm, i_ref), (v_hbm, v_ref))
-    tok = yo_ref.shape[0]
+def finish_kernel(m_ref, x_ref, g_ref, mixed_ref, go_ref):
+    cols, tok = m_ref.shape
+    mixed_ref[...] = (m_ref[...] + x_ref[:cols, :tok]).T.astype(bf16)
+    core = lax.axis_index(CORE)
+    for at, ref, src in halves(core, g_ref, x_ref.at[cols:, :tok], g_ref.shape[0] // SUB):
+        go_ref[at, :] = ref[src, :].astype(bf16)
+
+
+def last_kernel(scale, t_hbm, yo_hbm, x_hbm, i_hbm, v_hbm, d_hbm, c_hbm, gi_ref, gv_ref, gw_ref, t_ref, yo_ref, yx_ref, i_ref, v_ref, d_ref, c_ref, bt, sems):
+    tok, lanes = yx_ref.shape
+    part = x_hbm.at[pl.ds(0, tok), pl.ds(tok, lanes)]
+    pairs = ((t_hbm, t_ref), (yo_hbm, yo_ref), (part, yx_ref), (i_hbm, i_ref), (v_hbm, v_ref))
+    fetch(sems, *pairs, (d_hbm, d_ref), (c_hbm, c_ref))
     half = i_ref.shape[0] // 2
     core = lax.axis_index(CORE)
     later = (1 - core).astype(f32) * tok
@@ -415,15 +421,16 @@
     mixed, mixed_other = call(
         mixed_kernel,
         "mixed",
-        [((cols, tok), f32)] * 2,
-        (product, out_weight),
+        [((cols, tok), f32), ((cols + half, tok + LANES), f32)],
+        (product, out_weight, yb_other, grad_outer_other),
         scratch=[((cols, length), f32)],
     )
+    got = other_core(mixed_other)
     mixed, grad_outer = call(
         finish_kernel,
         "finish",
         [((tok, cols), bf16), gate],
-        (mixed, other_core(mixed_other), grad_outer, other_core(grad_outer_other)),
+        (mixed, got, grad_outer),
     )
     mixed, grad_outer, partial = lax.optimization_barrier((mixed, grad_outer, partial))
     scale = 1.0 / math.sqrt(length * chips)
@@ -431,17 +438,9 @@
         lambda *refs: last_kernel(scale, *refs),
         "last",
         [gate, gate, ((2 * SUB, cols), f32)],
-        (
-            decay_both,
-            coef_both,
-            partial.reshape(last[0]),
-            yb,
-            other_core(yb_other),
-            inner_gate,
-            value_proj,
-        ),
-        scratch=[last, half_columns, half_columns, gate, gate, half_columns],
-        remote=5,
+        (partial.reshape(last[0]), yb, got, inner_gate, value_proj, decay_both, coef_both),
+        scratch=[last, half_columns, half_columns, gate, gate, pair, pair, half_columns],
+        remote=7,
     )
     return (mixed, grad_outer, grad_inner, grad_value, grad_weight)
 

time: 145 us -> 146 us (level)
  blocking collectives: 28.1 us -> 0 us
  waiting for transfers between devices: 16 us -> 42.3 us
  local copies, waits for them, and re-layouts: 8.16 us -> 10.3 us
    all_to_all x1 -> x0, blocking collectives: 28.1 us -> none  [swap(): return lax.all_to_all(x, axes, 0, 0, tiled=True)]
    all_to_all x4 -> x5, waiting for transfers between devices: 5.22 us -> 32.7 us  [swap(): return lax.all_to_all(x, axes, 0, 0, tiled=True)]
    ppermute x5 -> x3, starting transfers between devices: 22.8 us -> 19.1 us  [other_core(): return lax.ppermute(x, 'core', [(0, 1), (1, 0)])]
    all_to_all x4 -> x5, starting transfers between devices: 28 us -> 31.4 us  [swap(): return lax.all_to_all(x, axes, 0, 0, tiled=True)]
    unnamed x28 -> x38, local copies, waits for them, and re-layouts: 6.86 us -> 8.97 us
  transfers between devices with their start and end apart: 15 -> 14, of which waited for: 8 -> 8; matrix products, arithmetic and copies ran while one was open for 1% -> 1% of each run, Pallas kernels for 7% -> 9%
where the time goes in v9:
time: 146 us; the launch traced here: 145 us
  starting transfers between devices  70.1 us (48%)
  waiting for transfers between devices  42.3 us (29%)
  Pallas kernels  20.8 us (14%)
  local copies, waits for them, and re-layouts  10.3 us (7%)
    all_to_all x5, waiting for transfers between devices, swap(): return lax.all_to_all(x, axes, 0, 0, tiled=True)  32.7 us
    all_to_all x5, starting transfers between devices, swap(): return lax.all_to_all(x, axes, 0, 0, tiled=True)  31.4 us
    pallas_call x14, Pallas kernels, call(): pl.pallas_call(kernel, out_shape=tuple((jax.ShapeDtypeStruct(s, t) for s,...  20.8 us
    ppermute x6, starting transfers between devices, shift(): return lax.ppermute(x, axis, [(i, (i + k) % n) for i in range(n)])  19.5 us
    ppermute x3, starting transfers between devices, other_core(): return lax.ppermute(x, 'core', [(0, 1), (1, 0)])  19.1 us
    unnamed x38, local copies, waits for them, and re-layouts  8.97 us
    ppermute x6, waiting for transfers between devices, shift(): return lax.ppermute(x, axis, [(i, (i + k) % n) for i in range(n)])  8.66 us
  transfers between devices with their start and end apart: 14, of which 8 were waited for; matrix products, arithmetic and copies ran while one was open for 1% of the time, Pallas kernels for 9%

profile of v9, /device:TPU:1, one launch (start us, length us, event | category | flops | bytes accessed | tf_op | source)
XLA Modules:
  0.0 145.1 jit_solution(5141960192837970492)
XLA Ops:
  0.6 1.9 %pack.1 = (bf16[448,256]{1,0:T(8,128)(2,1)}, bf16[448,256]{1,0:T(8,128)(2,1)}) custom-call(bf16[192,256]{1,0:T(8,128)(2,1)} %refs_3_.1, bf16[192,256]{1,0:T(8,128)(2,1)} %refs_4_.1, bf16[192,256]{1,0:T(8,128)(2,1)} %o_hbm.1, bf16[256,256]{1,0:T(8,128)(2,1)} %g_hbm.1), custom_call_target="tpu_custom_call" | custom-call | tf_op jit(solution)/shard_map/pack/pallas_call | solution.py:304
  2.5 12.4 %collective-permute-start.3 = (bf16[448,256]{1,0:T(8,128)(2,1)}, bf16[448,256]{1,0:T(8,128)(2,1)S(1)}, u32[]{:S(2)}, u32[]{:S(2)}) collective-permute-start(bf16[448,256]{1,0:T(8,128)(2,1)} %get-tuple-element.56), channel_id=1, source_target_pairs={{0,16},{16,0},{1,17},{17,1},{2,18},{18,2},{3,19},{19,3},{4,20},{20... | collective-permute-start | bytes 688136 | tf_op jit(solution)/shard_map/ppermute | solution.py:335
  15.0 0.8 multiply_bitcast_fusion.c_ref
  15.7 0.0 copy-start.10
  15.7 0.7 copy-done.10
  16.4 0.4 modes.1
  16.9 0.6 copy-done.15
  17.5 0.0 collective-permute-done.3.other_hbm
  17.5 0.9 copy-done.3
  18.4 2.8 %scan_forward.1 = (f32[512,128]{1,0:T(8,128)S(1)}, f32[24,16,128]{2,1,0:T(8,128)}) custom-call(f32[16,128]{1,0:T(8,128)S(1)} %get-tuple-element.53.d_ref, f32[16,128]{1,0:T(8,128)S(1)} %get-tuple-element.54.c_ref, bf16[448,256]{1,0:T(8,128)(2,1)S(1)} %copy-done.3, bf16[448,256]{1,0:T(8,128)(2,1)S(1)} %collective-permute-done.3.other_hbm), custom_call_target="tpu_custom_call" | custom-call | tf_op jit(solution)/shard_map/scan_forward/pallas_call | solution.py:304
  21.2 10.2 %all-to-all-start = ((f32[24,16,128]{2,1,0:T(8,128)}), f32[24,16,128]{2,1,0:T(8,128)S(1)}, u32[]{:S(2)}, u32[]{:S(2)}) async-start(f32[24,16,128]{2,1,0:T(8,128)} %get-tuple-element.57), calls=%async_computation | async-start | bytes 393216 | tf_op jit(solution)/shard_map/all_to_all | solution.py:321
  31.4 0.0 copy-start
  31.4 1.4 copy-done
  32.8 0.9 copy-done.5
  33.7 1.7 %back.1 = (bf16[768,256]{1,0:T(8,128)(2,1)S(1)}, bf16[768,256]{1,0:T(8,128)(2,1)}, bf16[768,256]{1,0:T(8,128)(2,1)}, bf16[768,256]{1,0:T(8,128)(2,1)}) custom-call(bf16[3072,256]{1,0:T(8,128)(2,1)S(1)} %copy-done, bf16[256,256]{1,0:T(8,128)(2,1)S(1)} %copy-done.5), custom_call_target="tpu_custom_call" | custom-call | tf_op jit(solution)/shard_map/back/pallas_call | solution.py:304
  35.5 3.1 %collective-permute-start = (bf16[768,256]{1,0:T(8,128)(2,1)}, bf16[768,256]{1,0:T(8,128)(2,1)S(1)}, u32[]{:S(2)}, u32[]{:S(2)}) collective-permute-start(bf16[768,256]{1,0:T(8,128)(2,1)} %get-tuple-element.46), channel_id=1, source_target_pairs={{0,4},{4,8},{8,12},{12,0},{1,5},{5,9},{9,13},{13,1},{2,6},{6,10},{... | collective-permute-start | bytes 1179656 | tf_op jit(solution)/shard_map/ppermute | solution.py:331
  38.6 4.4 %collective-permute-start.1 = (bf16[768,256]{1,0:T(8,128)(2,1)}, bf16[768,256]{1,0:T(8,128)(2,1)S(1)}, u32[]{:S(2)}, u32[]{:S(2)}) collective-permute-start(bf16[768,256]{1,0:T(8,128)(2,1)} %get-tuple-element.47), channel_id=1, source_target_pairs={{0,8},{4,12},{8,0},{12,4},{1,9},{5,13},{9,1},{13,5},{2,10},{6,14},... | collective-permute-start | bytes 1179656 | tf_op jit(solution)/shard_map/ppermute | solution.py:331
  42.9 3.1 %collective-permute-start.2 = (bf16[768,256]{1,0:T(8,128)(2,1)}, bf16[768,256]{1,0:T(8,128)(2,1)}, u32[]{:S(2)}, u32[]{:S(2)}) collective-permute-start(bf16[768,256]{1,0:T(8,128)(2,1)} %get-tuple-element.48), channel_id=1, source_target_pairs={{0,12},{4,0},{8,4},{12,8},{1,13},{5,1},{9,5},{13,9},{2,14},{6,2},{... | collective-permute-start | bytes 1179656 | tf_op jit(solution)/shard_map/ppermute | solution.py:331
  46.0 0.0 copy-done.4
  46.0 0.6 both.1.got_ref
  46.6 0.0 copy-done.17
  46.7 0.0 all-to-all-done.s_ref
  46.7 2.2 %heads_forward.1 = (bf16[4,96,512]{2,1,0:T(8,128)(2,1)}, bf16[2,96,256]{2,1,0:T(8,128)(2,1)S(1)}) custom-call(f32[24,16,128]{2,1,0:T(8,128)S(1)} %all-to-all-done.s_ref, f32[16,128]{1,0:T(8,128)S(1)} %get-tuple-element.53.d_ref, f32[16,128]{1,0:T(8,128)S(1)} %get-tuple-element.54.c_ref, f32[512,128]{1,0:T(8,128)S(1)} %get-tuple-element.58.y_ref, ...), custom_call_target="tpu_custom_call" | custom-call | tf_op jit(solution)/shard_map/heads_forward/pallas_call | solution.py:304
  48.8 5.8 %all-to-all-start.1 = ((bf16[4,96,512]{2,1,0:T(8,128)(2,1)}), bf16[4,96,512]{2,1,0:T(8,128)(2,1)S(1)}, u32[]{:S(2)}, u32[]{:S(2)}) async-start(bf16[4,96,512]{2,1,0:T(8,128)(2,1)} %get-tuple-element.59), calls=%async_computation.1 | async-start | bytes 786432 | tf_op jit(solution)/shard_map/all_to_all | solution.py:321
  54.6 0.0 collective-permute-done.p1
  54.6 4.0 %collective-permute-done.1.p2 = bf16[768,256]{1,0:T(8,128)(2,1)S(1)} collective-permute-done((bf16[768,256]{1,0:T(8,128)(2,1)}, bf16[768,256]{1,0:T(8,128)(2,1)S(1)}, u32[]{:S(2)}, u32[]{:S(2)}) %collective-permute-start.1) | collective-permute-done | bytes 393248 | tf_op jit(solution)/shard_map/ppermute | solution.py:331
  58.6 1.3 collective-permute-done.2.p3
  59.9 1.2 split.1
  61.1 4.6 %all-to-all-done.1 = bf16[4,96,512]{2,1,0:T(8,128)(2,1)S(1)} async-done(((bf16[4,96,512]{2,1,0:T(8,128)(2,1)}), bf16[4,96,512]{2,1,0:T(8,128)(2,1)S(1)}, u32[]{:S(2)}, u32[]{:S(2)}) %all-to-all-start.1) | async-done | bytes 393248 | tf_op jit(solution)/shard_map/all_to_all | solution.py:321
  65.8 1.3 broadcast_in_dim.2
  67.1 4.0 %all-to-all-start.2 = ((bf16[4,384,512]{2,1,0:T(8,128)(2,1)}), bf16[4,384,512]{2,1,0:T(8,128)(2,1)S(1)}, u32[]{:S(2)}, u32[]{:S(2)}) async-start(bf16[4,384,512]{2,1,0:T(8,128)(2,1)} %broadcast_in_dim.2), calls=%async_computation.2 | async-start | bytes 3145728 | tf_op jit(solution)/shard_map/all_to_all | solution.py:321
  71.1 1.9 %collective-permute-start.4 = (bf16[192,256]{1,0:T(8,128)(2,1)S(1)}, bf16[192,256]{1,0:T(8,128)(2,1)S(1)}, u32[]{:S(2)}, u32[]{:S(2)}) collective-permute-start(bf16[192,256]{1,0:T(8,128)(2,1)S(1)} %get-tuple-element.62), channel_id=1, source_target_pairs={{0,1},{1,2},{2,3},{3,0},{4,5},{5,6},{6,7},{7,4},{8,9},{9,10},{10,1... | collective-permute-start | bytes 294920 | tf_op jit(solution)/shard_map/ppermute | solution.py:331
  73.0 3.0 %collective-permute-start.5 = (bf16[192,256]{1,0:T(8,128)(2,1)S(1)}, bf16[192,256]{1,0:T(8,128)(2,1)S(1)}, u32[]{:S(2)}, u32[]{:S(2)}) collective-permute-start(bf16[192,256]{1,0:T(8,128)(2,1)S(1)} %get-tuple-element.63), channel_id=1, source_target_pairs={{0,2},{1,3},{2,0},{3,1},{4,6},{5,7},{6,4},{7,5},{8,10},{9,11},{10,... | collective-permute-start | bytes 294920 | tf_op jit(solution)/shard_map/ppermute | solution.py:331
  76.0 4.1 %collective-permute-start.6 = (bf16[192,256]{1,0:T(8,128)(2,1)S(1)}, bf16[192,256]{1,0:T(8,128)(2,1)S(1)}, u32[]{:S(2)}, u32[]{:S(2)}) collective-permute-start(bf16[192,256]{1,0:T(8,128)(2,1)S(1)} %get-tuple-element.64), channel_id=1, source_target_pairs={{0,3},{1,0},{2,1},{3,2},{4,7},{5,4},{6,5},{7,6},{8,11},{9,8},{10,9... | collective-permute-start | bytes 294920 | tf_op jit(solution)/shard_map/ppermute | solution.py:331
  80.1 0.0 collective-permute-done.4.p1
  80.1 1.7 %collective-permute-done.5.p2 = bf16[192,256]{1,0:T(8,128)(2,1)S(1)} collective-permute-done((bf16[192,256]{1,0:T(8,128)(2,1)S(1)}, bf16[192,256]{1,0:T(8,128)(2,1)S(1)}, u32[]{:S(2)}, u32[]{:S(2)}) %collective-permute-start.5) | collective-permute-done | bytes 98336 | tf_op jit(solution)/shard_map/ppermute | solution.py:331
  81.8 1.6 %collective-permute-done.6.p3 = bf16[192,256]{1,0:T(8,128)(2,1)S(1)} collective-permute-done((bf16[192,256]{1,0:T(8,128)(2,1)S(1)}, bf16[192,256]{1,0:T(8,128)(2,1)S(1)}, u32[]{:S(2)}, u32[]{:S(2)}) %collective-permute-start.6) | collective-permute-done | bytes 98336 | tf_op jit(solution)/shard_map/ppermute | solution.py:331
  83.5 4.1 %collective-permute-start.7 = (f32[96,256]{1,0:T(8,128)S(1)}, f32[96,256]{1,0:T(8,128)S(1)}, u32[]{:S(2)}, u32[]{:S(2)}) collective-permute-start(f32[96,256]{1,0:T(8,128)S(1)} %get-tuple-element.66), channel_id=1, source_target_pairs={{0,16},{16,0},{1,17},{17,1},{2,18},{18,2},{3,19},{19,3},{4,20},{20... | collective-permute-start | bytes 294920 | tf_op jit(solution)/shard_map/ppermute | solution.py:335
  87.6 0.9 collective-permute-done.7.other_ref
  88.5 2.2 %scan_backward.1 = (f32[256,128]{1,0:T(8,128)S(1)}, f32[256,128]{1,0:T(8,128)S(1)}, bf16[16,256]{1,0:T(8,128)(2,1)S(1)}, bf16[96,256]{1,0:T(8,128)(2,1)S(1)}, bf16[96,256]{1,0:T(8,128)(2,1)S(1)}) custom-call(f32[96,256]{1,0:T(8,128)S(1)} %get-tuple-element.65.own_ref, f32[96,256]{1,0:T(8,128)S(1)} %collective-permute-done.7.other_ref, ...), custom_call_target="tpu_custom_call" | custom-call | tf_op jit(solution)/shard_map/scan_backward/pallas_call | solution.py:304
  90.7 0.0 copy-start.8
  90.7 0.6 copy-done.8
  91.3 0.6 copy-done.11
  91.9 0.6 copy-done.13
  92.6 0.0 all-to-all-done.2
  92.6 0.6 weight.1
  93.2 0.0 copy-start.2
  93.2 0.9 copy-done.2
  94.1 4.4 %all-to-all-start.3 = ((bf16[8,208,256]{2,1,0:T(8,128)(2,1)}), bf16[8,208,256]{2,1,0:T(8,128)(2,1)}, u32[]{:S(2)}, u32[]{:S(2)}) async-start(bf16[8,208,256]{2,1,0:T(8,128)(2,1)} %copy-done.2), calls=%async_computation.3 | async-start | bytes 1703936 | tf_op jit(solution)/shard_map/all_to_all | solution.py:321
  98.4 0.0 copy-done.1
  98.4 0.0 copy-start.14
  98.4 0.8 copy-done.14
  99.2 1.5 %mixed.1 = (f32[256,256]{1,0:T(8,128)S(1)}, f32[352,384]{1,0:T(8,128)}) custom-call(bf16[1536,512]{1,0:T(8,128)(2,1)S(1)} %bitcast.6, bf16[3072,256]{1,0:T(8,128)(2,1)S(1)} %copy-done.1, f32[256,128]{1,0:T(8,128)S(1)} %get-tuple-element.68.y_ref, bf16[96,256]{1,0:T(8,128)(2,1)S(1)} %copy-done.14), custom_call_target="tpu_custom_call" | custom-call | tf_op jit(solution)/shard_map/mixed/pallas_call | solution.py:304
  100.7 2.6 %collective-permute-start.8 = (f32[352,384]{1,0:T(8,128)}, f32[352,384]{1,0:T(8,128)S(1)}, u32[]{:S(2)}, u32[]{:S(2)}) collective-permute-start(f32[352,384]{1,0:T(8,128)} %get-tuple-element.71), channel_id=1, source_target_pairs={{0,16},{16,0},{1,17},{17,1},{2,18},{18,2},{3,19},{19,3},{4,20},{20... | collective-permute-start | bytes 1622024 | tf_op jit(solution)/shard_map/ppermute | solution.py:335
  103.3 20.1 %all-to-all-done.3.t_ref = bf16[8,208,256]{2,1,0:T(8,128)(2,1)} async-done(((bf16[8,208,256]{2,1,0:T(8,128)(2,1)}), bf16[8,208,256]{2,1,0:T(8,128)(2,1)}, u32[]{:S(2)}, u32[]{:S(2)}) %all-to-all-start.3) | async-done | bytes 852000 | tf_op jit(solution)/shard_map/all_to_all | solution.py:321
  123.4 1.9 %middle.1 = bf16[6,48,256]{2,1,0:T(8,128)(2,1)} custom-call(bf16[8,208,256]{2,1,0:T(8,128)(2,1)} %all-to-all-done.3.t_ref, f32[16,128]{1,0:T(8,128)S(1)} %get-tuple-element.53.d_ref), custom_call_target="tpu_custom_call" | custom-call | tf_op jit(solution)/shard_map/middle/pallas_call | solution.py:304
  125.4 7.1 %all-to-all-start.4 = ((bf16[6,48,256]{2,1,0:T(8,128)(2,1)}), bf16[6,48,256]{2,1,0:T(8,128)(2,1)S(1)}, u32[]{:S(2)}, u32[]{:S(2)}) async-start(bf16[6,48,256]{2,1,0:T(8,128)(2,1)} %middle.1), calls=%async_computation.4 | async-start | bytes 294912 | tf_op jit(solution)/shard_map/all_to_all | solution.py:321
  132.5 0.0 collective-permute-done.8.x_ref.refs_2_
  132.5 0.8 copy-done.12
  133.3 0.8 finish.1
  134.1 7.9 %all-to-all-done.4.refs_0_ = bf16[6,48,256]{2,1,0:T(8,128)(2,1)S(1)} async-done(((bf16[6,48,256]{2,1,0:T(8,128)(2,1)}), bf16[6,48,256]{2,1,0:T(8,128)(2,1)S(1)}, u32[]{:S(2)}, u32[]{:S(2)}) %all-to-all-start.4) | async-done | bytes 147488 | tf_op jit(solution)/shard_map/all_to_all | solution.py:321
  142.0 0.0 copy-done.16
  142.0 0.0 copy-done.18
  142.0 3.0 %last.1 = (bf16[192,256]{1,0:T(8,128)(2,1)}, bf16[192,256]{1,0:T(8,128)(2,1)}, f32[64,256]{1,0:T(8,128)}) custom-call(bf16[6,48,256]{2,1,0:T(8,128)(2,1)S(1)} %all-to-all-done.4.refs_0_, f32[256,128]{1,0:T(8,128)S(1)} %copy-done.9, f32[352,384]{1,0:T(8,128)S(1)} %collective-permute-done.8.x_ref.refs_2_, bf16[192,256]{1,0:T(8,128)(2,1)S(1)} %copy-done.6, ...), custom_call_target="tpu_custom_call" | custom-call | tf_op jit(solution)/shard_map/last/pallas_call | solution.py:304
  (18 shorter events, 0.1 us)
Async XLA Ops:
  2.5 15.0 %collective-permute-start.3 = (bf16[448,256]{1,0:T(8,128)(2,1)}, bf16[448,256]{1,0:T(8,128)(2,1)S(1)}, u32[]{:S(2)}, u32[]{:S(2)}) collective-permute-start(bf16[448,256]{1,0:T(8,128)(2,1)} %get-tuple-element.56), channel_id=1, source_target_pairs={{0,16},{16,0},{1,17},{17,1},{2,18},{18,2},{3,19},{19,3},{4,20},{20... | collective-permute-start | bytes 688136 | tf_op jit(solution)/shard_map/ppermute | solution.py:335
  15.7 0.7 copy-start.10
  16.9 0.6 copy-start.15
  17.5 29.2 %copy-start.17 = (f32[2,16,128]{2,1,0:T(8,128)}, f32[2,16,128]{2,1,0:T(8,128)S(1)}, u32[]{:S(2)}) copy-start(f32[2,16,128]{2,1,0:T(8,128)S(1)} %get-tuple-element.81.refs_6_) | copy-start | bytes 49156
  17.5 0.9 copy-start.3
  18.4 27.6 %copy-start.4 = (bf16[448,256]{1,0:T(8,128)(2,1)S(1)}, bf16[448,256]{1,0:T(8,128)(2,1)}, u32[]{:S(2)}) copy-start(bf16[448,256]{1,0:T(8,128)(2,1)} %get-tuple-element.55.own_hbm) | copy-start | bytes 688132
  21.2 25.4 %all-to-all-start = ((f32[24,16,128]{2,1,0:T(8,128)}), f32[24,16,128]{2,1,0:T(8,128)S(1)}, u32[]{:S(2)}, u32[]{:S(2)}) async-start(f32[24,16,128]{2,1,0:T(8,128)} %get-tuple-element.57), calls=%async_computation | async-start | bytes 393216 | tf_op jit(solution)/shard_map/all_to_all | solution.py:321
  31.4 1.4 copy-start
  32.8 0.9 copy-start.5
  35.5 19.1 %collective-permute-start = (bf16[768,256]{1,0:T(8,128)(2,1)}, bf16[768,256]{1,0:T(8,128)(2,1)S(1)}, u32[]{:S(2)}, u32[]{:S(2)}) collective-permute-start(bf16[768,256]{1,0:T(8,128)(2,1)} %get-tuple-element.46), channel_id=1, source_target_pairs={{0,4},{4,8},{8,12},{12,0},{1,5},{5,9},{9,13},{13,1},{2,6},{6,10},{... | collective-permute-start | bytes 1179656 | tf_op jit(solution)/shard_map/ppermute | solution.py:331
  38.6 20.0 %collective-permute-start.1 = (bf16[768,256]{1,0:T(8,128)(2,1)}, bf16[768,256]{1,0:T(8,128)(2,1)S(1)}, u32[]{:S(2)}, u32[]{:S(2)}) collective-permute-start(bf16[768,256]{1,0:T(8,128)(2,1)} %get-tuple-element.47), channel_id=1, source_target_pairs={{0,8},{4,12},{8,0},{12,4},{1,9},{5,13},{9,1},{13,5},{2,10},{6,14},... | collective-permute-start | bytes 1179656 | tf_op jit(solution)/shard_map/ppermute | solution.py:331
  42.9 17.0 %collective-permute-start.2 = (bf16[768,256]{1,0:T(8,128)(2,1)}, bf16[768,256]{1,0:T(8,128)(2,1)}, u32[]{:S(2)}, u32[]{:S(2)}) collective-permute-start(bf16[768,256]{1,0:T(8,128)(2,1)} %get-tuple-element.48), channel_id=1, source_target_pairs={{0,12},{4,0},{8,4},{12,8},{1,13},{5,1},{9,5},{13,9},{2,14},{6,2},{... | collective-permute-start | bytes 1179656 | tf_op jit(solution)/shard_map/ppermute | solution.py:331
  48.8 17.0 %all-to-all-start.1 = ((bf16[4,96,512]{2,1,0:T(8,128)(2,1)}), bf16[4,96,512]{2,1,0:T(8,128)(2,1)S(1)}, u32[]{:S(2)}, u32[]{:S(2)}) async-start(bf16[4,96,512]{2,1,0:T(8,128)(2,1)} %get-tuple-element.59), calls=%async_computation.1 | async-start | bytes 786432 | tf_op jit(solution)/shard_map/all_to_all | solution.py:321
  67.1 25.5 %all-to-all-start.2 = ((bf16[4,384,512]{2,1,0:T(8,128)(2,1)}), bf16[4,384,512]{2,1,0:T(8,128)(2,1)S(1)}, u32[]{:S(2)}, u32[]{:S(2)}) async-start(bf16[4,384,512]{2,1,0:T(8,128)(2,1)} %broadcast_in_dim.2), calls=%async_computation.2 | async-start | bytes 3145728 | tf_op jit(solution)/shard_map/all_to_all | solution.py:321
  71.1 9.0 %collective-permute-start.4 = (bf16[192,256]{1,0:T(8,128)(2,1)S(1)}, bf16[192,256]{1,0:T(8,128)(2,1)S(1)}, u32[]{:S(2)}, u32[]{:S(2)}) collective-permute-start(bf16[192,256]{1,0:T(8,128)(2,1)S(1)} %get-tuple-element.62), channel_id=1, source_target_pairs={{0,1},{1,2},{2,3},{3,0},{4,5},{5,6},{6,7},{7,4},{8,9},{9,10},{10,1... | collective-permute-start | bytes 294920 | tf_op jit(solution)/shard_map/ppermute | solution.py:331
  73.0 8.8 %collective-permute-start.5 = (bf16[192,256]{1,0:T(8,128)(2,1)S(1)}, bf16[192,256]{1,0:T(8,128)(2,1)S(1)}, u32[]{:S(2)}, u32[]{:S(2)}) collective-permute-start(bf16[192,256]{1,0:T(8,128)(2,1)S(1)} %get-tuple-element.63), channel_id=1, source_target_pairs={{0,2},{1,3},{2,0},{3,1},{4,6},{5,7},{6,4},{7,5},{8,10},{9,11},{10,... | collective-permute-start | bytes 294920 | tf_op jit(solution)/shard_map/ppermute | solution.py:331
  76.0 7.4 %collective-permute-start.6 = (bf16[192,256]{1,0:T(8,128)(2,1)S(1)}, bf16[192,256]{1,0:T(8,128)(2,1)S(1)}, u32[]{:S(2)}, u32[]{:S(2)}) collective-permute-start(bf16[192,256]{1,0:T(8,128)(2,1)S(1)} %get-tuple-element.64), channel_id=1, source_target_pairs={{0,3},{1,0},{2,1},{3,2},{4,7},{5,4},{6,5},{7,6},{8,11},{9,8},{10,9... | collective-permute-start | bytes 294920 | tf_op jit(solution)/shard_map/ppermute | solution.py:331
  83.5 5.1 %collective-permute-start.7 = (f32[96,256]{1,0:T(8,128)S(1)}, f32[96,256]{1,0:T(8,128)S(1)}, u32[]{:S(2)}, u32[]{:S(2)}) collective-permute-start(f32[96,256]{1,0:T(8,128)S(1)} %get-tuple-element.66), channel_id=1, source_target_pairs={{0,16},{16,0},{1,17},{17,1},{2,18},{18,2},{3,19},{19,3},{4,20},{20... | collective-permute-start | bytes 294920 | tf_op jit(solution)/shard_map/ppermute | solution.py:335
  90.7 0.7 copy-start.8
  91.3 0.6 copy-start.11
  91.9 0.6 copy-start.13
  93.2 0.9 copy-start.2
  94.1 4.4 %copy-start.1 = (bf16[3072,256]{1,0:T(8,128)(2,1)S(1)}, bf16[3072,256]{1,0:T(8,128)(2,1)}, u32[]{:S(2)}) copy-start(bf16[3072,256]{1,0:T(8,128)(2,1)} %w_ref.3) | copy-start | bytes 4718596
  94.1 29.4 %all-to-all-start.3 = ((bf16[8,208,256]{2,1,0:T(8,128)(2,1)}), bf16[8,208,256]{2,1,0:T(8,128)(2,1)}, u32[]{:S(2)}, u32[]{:S(2)}) async-start(bf16[8,208,256]{2,1,0:T(8,128)(2,1)} %copy-done.2), calls=%async_computation.3 | async-start | bytes 1703936 | tf_op jit(solution)/shard_map/all_to_all | solution.py:321
  98.4 0.8 copy-start.14
  100.7 41.3 %copy-start.6 = (bf16[192,256]{1,0:T(8,128)(2,1)S(1)}, bf16[192,256]{1,0:T(8,128)(2,1)}, u32[]{:S(2)}) copy-start(bf16[192,256]{1,0:T(8,128)(2,1)} %refs_3_.1) | copy-start | bytes 294916
  100.7 41.3 %copy-start.7 = (bf16[192,256]{1,0:T(8,128)(2,1)S(1)}, bf16[192,256]{1,0:T(8,128)(2,1)}, u32[]{:S(2)}) copy-start(bf16[192,256]{1,0:T(8,128)(2,1)} %refs_4_.1) | copy-start | bytes 294916
  100.7 41.3 %copy-start.9 = (f32[256,128]{1,0:T(8,128)S(1)}, f32[256,128]{1,0:T(8,128)}, u32[]{:S(2)}) copy-start(f32[256,128]{1,0:T(8,128)} %copy-done.8) | copy-start | bytes 393220
  100.7 41.3 %copy-start.16 = (f32[2,16,128]{2,1,0:T(8,128)S(1)}, f32[2,16,128]{2,1,0:T(8,128)}, u32[]{:S(2)}) copy-start(f32[2,16,128]{2,1,0:T(8,128)} %copy-done.15) | copy-start | bytes 49156
  100.7 41.3 %copy-start.18 = (f32[2,16,128]{2,1,0:T(8,128)S(1)}, f32[2,16,128]{2,1,0:T(8,128)}, u32[]{:S(2)}) copy-start(f32[2,16,128]{2,1,0:T(8,128)} %copy-done.17) | copy-start | bytes 49156
  100.7 31.8 %collective-permute-start.8 = (f32[352,384]{1,0:T(8,128)}, f32[352,384]{1,0:T(8,128)S(1)}, u32[]{:S(2)}, u32[]{:S(2)}) collective-permute-start(f32[352,384]{1,0:T(8,128)} %get-tuple-element.71), channel_id=1, source_target_pairs={{0,16},{16,0},{1,17},{17,1},{2,18},{18,2},{3,19},{19,3},{4,20},{20... | collective-permute-start | bytes 1622024 | tf_op jit(solution)/shard_map/ppermute | solution.py:335
  125.4 16.6 %all-to-all-start.4 = ((bf16[6,48,256]{2,1,0:T(8,128)(2,1)}), bf16[6,48,256]{2,1,0:T(8,128)(2,1)S(1)}, u32[]{:S(2)}, u32[]{:S(2)}) async-start(bf16[6,48,256]{2,1,0:T(8,128)(2,1)} %middle.1), calls=%async_computation.4 | async-start | bytes 294912 | tf_op jit(solution)/shard_map/all_to_all | solution.py:321
  132.5 0.8 copy-start.12

commit v10 on v8

--- a/solution.py
+++ b/solution.py
@@ -157,8 +157,9 @@
     decay = d_ref[...]
     jump = jnp.exp(-decay * float(ft.shape[0]))
     state = jnp.zeros_like(decay)
-    for m in range(s_ref.shape[0]):
-        state = jnp.where(m < lax.axis_index(CHIP), state * jump + s_ref[m], state)
+    chips = s_ref.shape[0]
+    for m in range(chips):
+        state = jnp.where(m < lax.axis_index(CHIP), state * jump + s_ref[chips - 1 - m], state)
     heads(y_ref, ft, state * c_ref[...], jnp.exp(-decay), False)
     for h in range(2):
         at = pl.ds(h * tok, tok)
@@ -203,8 +204,8 @@
     grads = got_ref[:, :tok, :].reshape(2 * tok, -1)
     for y in range(n):
         part = jnp.dot(p_ref[pl.ds(y * rows, rows), :], grads, preferred_element_type=f32)
-        out_ref[y, :rows, :] = part.astype(bf16)
-        out_ref[y, rows:, :] = s_ref[...]
+        out_ref[n - 1 - y, :rows, :] = part.astype(bf16)
+        out_ref[n - 1 - y, rows:, :] = s_ref[...]
 
 
 def middle_kernel(t_ref, d_ref, out_ref):
@@ -217,7 +218,7 @@
     later = jnp.zeros_like(decay)
     here = jnp.zeros_like(decay)
     for k in range(n - 1, -1, -1):
-        state = get_state(t_ref[k, zs * rows :, :])
+        state = get_state(t_ref[n - 1 - k, zs * rows :, :])
         later = jnp.where(k > y, later * jump + state, later)
         here = jnp.where(k == y, state, here)
     for z in range(zs):
@@ -229,8 +230,9 @@
         carry = jnp.exp(-decay * far) * later
         carry = jnp.where(zh > z, carry + jnp.exp(-decay * near) * here, carry)
         for h in range(2):
-            out_ref[2 * z + h, :SUB, :] = total[h * SUB : (h + 1) * SUB].astype(bf16)
-            put_state(out_ref.at[2 * z + h, SUB:, :], carry)
+            slot = 2 * (zs - z) - 1 - h
+            out_ref[slot, :SUB, :] = total[h * SUB : (h + 1) * SUB].astype(bf16)
+            put_state(out_ref.at[slot, SUB:, :], carry)
 
 
 def weight_rows(w_ref, core, block, count):
@@ -268,18 +270,19 @@
         go_ref[at, :] = ref[src, :]
 
 
-def last_kernel(scale, d_ref, c_ref, t_hbm, yo_hbm, yx_hbm, i_hbm, v_hbm, gi_ref, gv_ref, gw_ref, t_ref, yo_ref, yx_ref, i_ref, v_ref, bt, sems):
-    fetch(sems, (t_hbm, t_ref), (yo_hbm, yo_ref), (yx_hbm, yx_ref), (i_hbm, i_ref), (v_hbm, v_ref))
+def last_kernel(scale, t_hbm, yo_hbm, yx_hbm, i_hbm, v_hbm, d_hbm, c_hbm, gi_ref, gv_ref, gw_ref, t_ref, yo_ref, yx_ref, i_ref, v_ref, d_ref, c_ref, bt, sems):
+    pairs = ((t_hbm, t_ref), (yo_hbm, yo_ref), (yx_hbm, yx_ref), (i_hbm, i_ref), (v_hbm, v_ref))
+    fetch(sems, *pairs, (d_hbm, d_ref), (c_hbm, c_ref))
     tok = yo_ref.shape[0]
     half = i_ref.shape[0] // 2
     core = lax.axis_index(CORE)
     later = (1 - core).astype(f32) * tok
     for h, y_ref in ((core, yo_ref), (1 - core, yx_ref)):
-        state = get_state(t_ref[h, SUB:, :])
-        total = t_ref[h, :SUB, :].astype(f32)
+        state = get_state(t_ref[1 - h, SUB:, :])
+        total = t_ref[1 - h, :SUB, :].astype(f32)
         for z in range(1, t_ref.shape[0] // 2):
-            state = state + get_state(t_ref[2 * z + h, SUB:, :])
-            total = total + t_ref[2 * z + h, :SUB, :].astype(f32)
+            state = state + get_state(t_ref[2 * z + 1 - h, SUB:, :])
+            total = total + t_ref[2 * z + 1 - h, :SUB, :].astype(f32)
         gw_ref[pl.ds(pl.multiple_of(SUB * h, SUB), SUB), :] = total * scale
         decay = d_ref[h]
         state = state * jnp.exp(-decay * later) * c_ref[h]
@@ -315,6 +318,11 @@
     return lax.all_to_all(x, axes, 0, 0, tiled=True)
 
 
+def swap_back(x, axes):
+    order = [list(range(lax.axis_size(axes)))[::-1]]
+    return lax.all_to_all(x, axes, 0, 0, axis_index_groups=order, tiled=True)
+
+
 def spread(x, axis):
     n, rows, m = x.shape
     return swap(x.reshape(n * rows, m), axis)
@@ -366,7 +374,7 @@
         scratch=[((half, tok), bf16)] * 2 + [columns],
         remote=2,
     )
-    states = swap(states, ("y", "zh"))
+    states = swap_back(states, ("y", "zh"))
     (got,) = call(
         both_kernel, "both", [((2, tok + chan, cols), bf16)], (own, other), remote=2
     )
@@ -408,10 +416,10 @@
         [((ny, nh * 2 * SUB + modes, cols), bf16)],
         (product, got, state),
     )
-    partial = swap(partial, "y")
+    partial = swap_back(partial, "y")
     last = ((2 * nh, SUB + modes, cols), bf16)
     (partial,) = call(middle_kernel, "middle", [last], (partial, decay))
-    partial = swap(partial, ("zh", "core"))
+    partial = swap_back(partial, ("zh", "core"))
     mixed, mixed_other = call(
         mixed_kernel,
         "mixed",
@@ -432,16 +440,17 @@
         "last",
         [gate, gate, ((2 * SUB, cols), f32)],
         (
-            decay_both,
-            coef_both,
             partial.reshape(last[0]),
             yb,
             other_core(yb_other),
             inner_gate,
             value_proj,
+            decay_both,
+            coef_both,
         ),
-        scratch=[last, half_columns, half_columns, gate, gate, half_columns],
-        remote=5,
+        scratch=[last, half_columns, half_columns, gate, gate, pair, pair, half_columns],
+        remote=7,
+        limit=None,
     )
     return (mixed, grad_outer, grad_inner, grad_value, grad_weight)
 

time: 145 us -> 141 us (0.972)
  waiting for transfers between devices: 16 us -> 14.1 us
    all_to_all x4 -> x2, starting transfers between devices: 28 us -> 9.01 us  [swap(): return lax.all_to_all(x, axes, 0, 0, tiled=True)]
    all_to_all x0 -> x2, starting transfers between devices: none -> 18.7 us  [swap_back(): return lax.all_to_all(x, axes, 0, 0, axis_index_groups=order, tiled=True)]
    all_to_all x4 -> x2, waiting for transfers between devices: 5.22 us -> 3.11 us  [swap(): return lax.all_to_all(x, axes, 0, 0, tiled=True)]
    unnamed x28 -> x22, local copies, waits for them, and re-layouts: 6.86 us -> 5.92 us
  transfers between devices with their start and end apart: 15 -> 15, of which waited for: 8 -> 7; matrix products, arithmetic and copies ran while one was open for 1% -> 1% of each run, Pallas kernels for 7% -> 7%
where the time goes in v10:
time: 141 us; the launch traced here: 140 us
  starting transfers between devices  71 us (50%)
  blocking collectives  27.1 us (19%)
  Pallas kernels  19.1 us (14%)
  waiting for transfers between devices  14.1 us (10%)
  local copies, waits for them, and re-layouts  7.23 us (5%)
    all_to_all x1, blocking collectives, swap_back(): return lax.all_to_all(x, axes, 0, 0, axis_index_groups=order, tiled=True)  27.1 us
    ppermute x5, starting transfers between devices, other_core(): return lax.ppermute(x, 'core', [(0, 1), (1, 0)])  23.8 us
    ppermute x6, starting transfers between devices, shift(): return lax.ppermute(x, axis, [(i, (i + k) % n) for i in range(n)])  19.5 us
    pallas_call x14, Pallas kernels, call(): pl.pallas_call(kernel, out_shape=tuple((jax.ShapeDtypeStruct(s, t) for s,...  19.1 us
    all_to_all x2, starting transfers between devices, swap_back(): return lax.all_to_all(x, axes, 0, 0, axis_index_groups=order, tiled=True)  18.7 us
    ppermute x6, waiting for transfers between devices, shift(): return lax.ppermute(x, axis, [(i, (i + k) % n) for i in range(n)])  9.22 us
    all_to_all x2, starting transfers between devices, swap(): return lax.all_to_all(x, axes, 0, 0, tiled=True)  9.01 us
    unnamed x22, local copies, waits for them, and re-layouts  5.92 us
  transfers between devices with their start and end apart: 15, of which 7 were waited for; matrix products, arithmetic and copies ran while one was open for 1% of the time, Pallas kernels for 7%

profile of v10, /device:TPU:1, one launch (start us, length us, event | category | flops | bytes accessed | tf_op | source)
XLA Modules:
  0.0 140.2 jit_solution(16801227740595641886)
XLA Ops:
  0.6 1.9 %pack.1 = (bf16[448,256]{1,0:T(8,128)(2,1)}, bf16[448,256]{1,0:T(8,128)(2,1)}) custom-call(bf16[192,256]{1,0:T(8,128)(2,1)} %refs_3_.1, bf16[192,256]{1,0:T(8,128)(2,1)} %refs_4_.1, bf16[192,256]{1,0:T(8,128)(2,1)} %o_hbm.1, bf16[256,256]{1,0:T(8,128)(2,1)} %g_hbm.1), custom_call_target="tpu_custom_call" | custom-call | tf_op jit(solution)/shard_map/pack/pallas_call | solution.py:301
  2.5 12.4 %collective-permute-start.3 = (bf16[448,256]{1,0:T(8,128)(2,1)}, bf16[448,256]{1,0:T(8,128)(2,1)S(1)}, u32[]{:S(2)}, u32[]{:S(2)}) collective-permute-start(bf16[448,256]{1,0:T(8,128)(2,1)} %get-tuple-element.56), channel_id=1, source_target_pairs={{0,16},{16,0},{1,17},{17,1},{2,18},{18,2},{3,19},{19,3},{4,20},{20... | collective-permute-start | bytes 688136 | tf_op jit(solution)/shard_map/ppermute | solution.py:337
  15.0 0.8 multiply_bitcast_fusion.c_ref
  15.7 0.0 copy-start.6
  15.7 0.7 copy-done.6
  16.5 0.4 modes.1
  16.9 0.0 copy-start.7
  16.9 0.6 copy-done.7
  17.5 0.0 copy-start.8
  17.5 0.0 collective-permute-done.3.other_hbm
  17.5 0.9 copy-done.2
  18.4 2.8 %scan_forward.1 = (f32[512,128]{1,0:T(8,128)S(1)}, f32[24,16,128]{2,1,0:T(8,128)}) custom-call(f32[16,128]{1,0:T(8,128)S(1)} %get-tuple-element.53.d_ref, f32[16,128]{1,0:T(8,128)S(1)} %get-tuple-element.54.c_ref, bf16[448,256]{1,0:T(8,128)(2,1)S(1)} %copy-done.2, bf16[448,256]{1,0:T(8,128)(2,1)S(1)} %collective-permute-done.3.other_hbm), custom_call_target="tpu_custom_call" | custom-call | tf_op jit(solution)/shard_map/scan_forward/pallas_call | solution.py:301
  21.3 10.3 %all-to-all-start = ((f32[24,16,128]{2,1,0:T(8,128)}), f32[24,16,128]{2,1,0:T(8,128)S(1)}, u32[]{:S(2)}, u32[]{:S(2)}) async-start(f32[24,16,128]{2,1,0:T(8,128)} %get-tuple-element.57), calls=%async_computation | async-start | bytes 393216 | tf_op jit(solution)/shard_map/all_to_all | solution.py:323
  31.6 0.0 copy-start
  31.6 1.4 copy-done
  33.0 0.9 copy-done.4
  33.9 1.5 %back.1 = (bf16[768,256]{1,0:T(8,128)(2,1)S(1)}, bf16[768,256]{1,0:T(8,128)(2,1)}, bf16[768,256]{1,0:T(8,128)(2,1)}, bf16[768,256]{1,0:T(8,128)(2,1)S(1)}) custom-call(bf16[3072,256]{1,0:T(8,128)(2,1)S(1)} %copy-done, bf16[256,256]{1,0:T(8,128)(2,1)S(1)} %copy-done.4), custom_call_target="tpu_custom_call" | custom-call | tf_op jit(solution)/shard_map/back/pallas_call | solution.py:301
  35.4 3.1 %collective-permute-start = (bf16[768,256]{1,0:T(8,128)(2,1)}, bf16[768,256]{1,0:T(8,128)(2,1)S(1)}, u32[]{:S(2)}, u32[]{:S(2)}) collective-permute-start(bf16[768,256]{1,0:T(8,128)(2,1)} %get-tuple-element.46), channel_id=1, source_target_pairs={{0,4},{4,8},{8,12},{12,0},{1,5},{5,9},{9,13},{13,1},{2,6},{6,10},{... | collective-permute-start | bytes 1179656 | tf_op jit(solution)/shard_map/ppermute | solution.py:333
  38.5 4.4 %collective-permute-start.1 = (bf16[768,256]{1,0:T(8,128)(2,1)}, bf16[768,256]{1,0:T(8,128)(2,1)S(1)}, u32[]{:S(2)}, u32[]{:S(2)}) collective-permute-start(bf16[768,256]{1,0:T(8,128)(2,1)} %get-tuple-element.47), channel_id=1, source_target_pairs={{0,8},{4,12},{8,0},{12,4},{1,9},{5,13},{9,1},{13,5},{2,10},{6,14},... | collective-permute-start | bytes 1179656 | tf_op jit(solution)/shard_map/ppermute | solution.py:333
  42.8 3.1 %collective-permute-start.2 = (bf16[768,256]{1,0:T(8,128)(2,1)S(1)}, bf16[768,256]{1,0:T(8,128)(2,1)}, u32[]{:S(2)}, u32[]{:S(2)}) collective-permute-start(bf16[768,256]{1,0:T(8,128)(2,1)S(1)} %get-tuple-element.48), channel_id=1, source_target_pairs={{0,12},{4,0},{8,4},{12,8},{1,13},{5,1},{9,5},{13,9},{2,14},{6,2},{... | collective-permute-start | bytes 1179656 | tf_op jit(solution)/shard_map/ppermute | solution.py:333
  45.9 0.0 copy-done.3
  45.9 0.6 both.1.got_ref
  46.6 0.0 copy-done.8
  46.6 0.0 all-to-all-done.s_ref
  46.6 2.2 %heads_forward.1 = (bf16[4,96,512]{2,1,0:T(8,128)(2,1)}, bf16[2,96,256]{2,1,0:T(8,128)(2,1)S(1)}) custom-call(f32[24,16,128]{2,1,0:T(8,128)S(1)} %all-to-all-done.s_ref, f32[16,128]{1,0:T(8,128)S(1)} %get-tuple-element.53.d_ref, f32[16,128]{1,0:T(8,128)S(1)} %get-tuple-element.54.c_ref, f32[512,128]{1,0:T(8,128)S(1)} %get-tuple-element.58.y_ref, ...), custom_call_target="tpu_custom_call" | custom-call | tf_op jit(solution)/shard_map/heads_forward/pallas_call | solution.py:301
  48.7 5.4 %all-to-all-start.1 = ((bf16[4,96,512]{2,1,0:T(8,128)(2,1)}), bf16[4,96,512]{2,1,0:T(8,128)(2,1)S(1)}, u32[]{:S(2)}, u32[]{:S(2)}) async-start(bf16[4,96,512]{2,1,0:T(8,128)(2,1)} %get-tuple-element.59), calls=%async_computation.1 | async-start | bytes 786432 | tf_op jit(solution)/shard_map/all_to_all | solution.py:318
  54.2 0.0 collective-permute-done.p1
  54.2 4.0 %collective-permute-done.1.p2 = bf16[768,256]{1,0:T(8,128)(2,1)S(1)} collective-permute-done((bf16[768,256]{1,0:T(8,128)(2,1)}, bf16[768,256]{1,0:T(8,128)(2,1)S(1)}, u32[]{:S(2)}, u32[]{:S(2)}) %collective-permute-start.1) | collective-permute-done | bytes 393248 | tf_op jit(solution)/shard_map/ppermute | solution.py:333
  58.2 1.4 %collective-permute-done.2.p3 = bf16[768,256]{1,0:T(8,128)(2,1)} collective-permute-done((bf16[768,256]{1,0:T(8,128)(2,1)S(1)}, bf16[768,256]{1,0:T(8,128)(2,1)}, u32[]{:S(2)}, u32[]{:S(2)}) %collective-permute-start.2) | collective-permute-done | bytes 393248 | tf_op jit(solution)/shard_map/ppermute | solution.py:333
  59.6 1.2 split.1
  60.8 3.1 %all-to-all-done.1 = bf16[4,96,512]{2,1,0:T(8,128)(2,1)S(1)} async-done(((bf16[4,96,512]{2,1,0:T(8,128)(2,1)}), bf16[4,96,512]{2,1,0:T(8,128)(2,1)S(1)}, u32[]{:S(2)}, u32[]{:S(2)}) %all-to-all-start.1) | async-done | bytes 393248 | tf_op jit(solution)/shard_map/all_to_all | solution.py:318
  63.9 1.3 broadcast_in_dim.2
  65.2 3.6 %all-to-all-start.2 = ((bf16[4,384,512]{2,1,0:T(8,128)(2,1)}), bf16[4,384,512]{2,1,0:T(8,128)(2,1)S(1)}, u32[]{:S(2)}, u32[]{:S(2)}) async-start(bf16[4,384,512]{2,1,0:T(8,128)(2,1)} %broadcast_in_dim.2), calls=%async_computation.2 | async-start | bytes 3145728 | tf_op jit(solution)/shard_map/all_to_all | solution.py:318
  68.8 1.9 %collective-permute-start.5 = (bf16[192,256]{1,0:T(8,128)(2,1)S(1)}, bf16[192,256]{1,0:T(8,128)(2,1)S(1)}, u32[]{:S(2)}, u32[]{:S(2)}) collective-permute-start(bf16[192,256]{1,0:T(8,128)(2,1)S(1)} %get-tuple-element.64), channel_id=1, source_target_pairs={{0,1},{1,2},{2,3},{3,0},{4,5},{5,6},{6,7},{7,4},{8,9},{9,10},{10,1... | collective-permute-start | bytes 294920 | tf_op jit(solution)/shard_map/ppermute | solution.py:333
  70.7 4.5 %collective-permute-start.6 = (bf16[192,256]{1,0:T(8,128)(2,1)S(1)}, bf16[192,256]{1,0:T(8,128)(2,1)S(1)}, u32[]{:S(2)}, u32[]{:S(2)}) collective-permute-start(bf16[192,256]{1,0:T(8,128)(2,1)S(1)} %get-tuple-element.65), channel_id=1, source_target_pairs={{0,2},{1,3},{2,0},{3,1},{4,6},{5,7},{6,4},{7,5},{8,10},{9,11},{10,... | collective-permute-start | bytes 294920 | tf_op jit(solution)/shard_map/ppermute | solution.py:333
  75.2 2.6 %collective-permute-start.7 = (bf16[192,256]{1,0:T(8,128)(2,1)S(1)}, bf16[192,256]{1,0:T(8,128)(2,1)S(1)}, u32[]{:S(2)}, u32[]{:S(2)}) collective-permute-start(bf16[192,256]{1,0:T(8,128)(2,1)S(1)} %get-tuple-element.66), channel_id=1, source_target_pairs={{0,3},{1,0},{2,1},{3,2},{4,7},{5,4},{6,5},{7,6},{8,11},{9,8},{10,9... | collective-permute-start | bytes 294920 | tf_op jit(solution)/shard_map/ppermute | solution.py:333
  77.8 0.0 collective-permute-done.5.p1
  77.8 0.7 collective-permute-done.6.p2
  78.6 3.1 %collective-permute-done.7.p3 = bf16[192,256]{1,0:T(8,128)(2,1)S(1)} collective-permute-done((bf16[192,256]{1,0:T(8,128)(2,1)S(1)}, bf16[192,256]{1,0:T(8,128)(2,1)S(1)}, u32[]{:S(2)}, u32[]{:S(2)}) %collective-permute-start.7) | collective-permute-done | bytes 98336 | tf_op jit(solution)/shard_map/ppermute | solution.py:333
  81.7 4.7 %collective-permute-start.8 = (f32[96,256]{1,0:T(8,128)S(1)}, f32[96,256]{1,0:T(8,128)S(1)}, u32[]{:S(2)}, u32[]{:S(2)}) collective-permute-start(f32[96,256]{1,0:T(8,128)S(1)} %get-tuple-element.68), channel_id=1, source_target_pairs={{0,16},{16,0},{1,17},{17,1},{2,18},{18,2},{3,19},{19,3},{4,20},{20... | collective-permute-start | bytes 294920 | tf_op jit(solution)/shard_map/ppermute | solution.py:337
  86.4 0.9 collective-permute-done.8.other_ref
  87.3 2.2 %scan_backward.1 = (f32[256,128]{1,0:T(8,128)S(1)}, f32[256,128]{1,0:T(8,128)S(1)}, bf16[16,256]{1,0:T(8,128)(2,1)S(1)}, bf16[96,256]{1,0:T(8,128)(2,1)S(1)}, bf16[96,256]{1,0:T(8,128)(2,1)S(1)}) custom-call(f32[96,256]{1,0:T(8,128)S(1)} %get-tuple-element.67.own_ref, f32[96,256]{1,0:T(8,128)S(1)} %collective-permute-done.8.other_ref, ...), custom_call_target="tpu_custom_call" | custom-call | tf_op jit(solution)/shard_map/scan_backward/pallas_call | solution.py:301
  89.5 0.0 copy-start.5
  89.5 0.6 copy-done.5
  90.1 0.0 all-to-all-done.2
  90.1 0.6 weight.1
  90.7 0.0 copy-start.1
  90.7 27.1 %all_to_all.32.t_ref = bf16[8,208,256]{2,1,0:T(8,128)(2,1)S(1)} all-to-all(bf16[8,208,256]{2,1,0:T(8,128)(2,1)S(1)} %weight.1), channel_id=1, replica_groups={{672,576,480,384,288,192,96,0},{673,577,481,385,289,193,97,1},{674,578,..., dimensions={0} | all-to-all | bytes 1703936 | tf_op jit(solution)/shard_map/all_to_all | solution.py:323
  117.8 0.8 middle.1
  118.6 8.4 %all-to-all-start.4 = ((bf16[6,48,256]{2,1,0:T(8,128)(2,1)}), bf16[6,48,256]{2,1,0:T(8,128)(2,1)S(1)}, u32[]{:S(2)}, u32[]{:S(2)}) async-start(bf16[6,48,256]{2,1,0:T(8,128)(2,1)} %middle.1), calls=%async_computation.4 | async-start | bytes 294912 | tf_op jit(solution)/shard_map/all_to_all | solution.py:323
  127.0 0.0 copy-done.1
  127.0 0.7 mixed.1
  127.7 2.3 %collective-permute-start.4 = (f32[256,256]{1,0:T(8,128)S(1)}, f32[256,256]{1,0:T(8,128)S(1)}, u32[]{:S(2)}, u32[]{:S(2)}) collective-permute-start(f32[256,256]{1,0:T(8,128)S(1)} %get-tuple-element.62), channel_id=1, source_target_pairs={{0,16},{16,0},{1,17},{17,1},{2,18},{18,2},{3,19},{19,3},{4,20},{20... | collective-permute-start | bytes 786440 | tf_op jit(solution)/shard_map/ppermute | solution.py:337
  130.0 2.0 %collective-permute-start.10 = (f32[256,128]{1,0:T(8,128)S(1)}, f32[256,128]{1,0:T(8,128)S(1)}, u32[]{:S(2)}, u32[]{:S(2)}) collective-permute-start(f32[256,128]{1,0:T(8,128)S(1)} %get-tuple-element.79), channel_id=1, source_target_pairs={{0,16},{16,0},{1,17},{17,1},{2,18},{18,2},{3,19},{19,3},{4,20},{20... | collective-permute-start | bytes 393224 | tf_op jit(solution)/shard_map/ppermute | solution.py:337
  132.0 2.3 %collective-permute-start.9 = (bf16[96,256]{1,0:T(8,128)(2,1)S(1)}, bf16[96,256]{1,0:T(8,128)(2,1)S(1)}, u32[]{:S(2)}, u32[]{:S(2)}) collective-permute-start(bf16[96,256]{1,0:T(8,128)(2,1)S(1)} %get-tuple-element.71), channel_id=1, source_target_pairs={{0,16},{16,0},{1,17},{17,1},{2,18},{18,2},{3,19},{19,3},{4,20},{20... | collective-permute-start | bytes 147464 | tf_op jit(solution)/shard_map/ppermute | solution.py:337
  134.4 0.9 collective-permute-done.9.other_ref
  135.2 0.0 collective-permute-done.4.mr_ref
  135.2 0.8 finish.1
  136.0 0.0 all-to-all-done.4.refs_0_
  136.0 0.0 collective-permute-done.10.refs_2_
  136.0 0.0 copy-start.10
  136.0 0.6 copy-done.9
  136.7 0.1 copy-done.10
  136.7 3.5 %last.1 = (bf16[192,256]{1,0:T(8,128)(2,1)}, bf16[192,256]{1,0:T(8,128)(2,1)}, f32[64,256]{1,0:T(8,128)}) custom-call(bf16[6,48,256]{2,1,0:T(8,128)(2,1)} %copy-done.9, f32[256,128]{1,0:T(8,128)} %copy-done.5, f32[256,128]{1,0:T(8,128)} %copy-done.10, bf16[192,256]{1,0:T(8,128)(2,1)} %refs_3_.1, bf16[192,256]{1,0:T(8,128)(2,1)} %refs_4_.1, ...), custom_call_target="tpu_custom_call" | custom-call | tf_op jit(solution)/shard_map/last/pallas_call | solution.py:301
  (5 shorter events, 0.1 us)
Async XLA Ops:
  2.5 15.0 %collective-permute-start.3 = (bf16[448,256]{1,0:T(8,128)(2,1)}, bf16[448,256]{1,0:T(8,128)(2,1)S(1)}, u32[]{:S(2)}, u32[]{:S(2)}) collective-permute-start(bf16[448,256]{1,0:T(8,128)(2,1)} %get-tuple-element.56), channel_id=1, source_target_pairs={{0,16},{16,0},{1,17},{17,1},{2,18},{18,2},{3,19},{19,3},{4,20},{20... | collective-permute-start | bytes 688136 | tf_op jit(solution)/shard_map/ppermute | solution.py:337
  15.7 0.7 copy-start.6
  16.9 0.6 copy-start.7
  17.5 29.1 %copy-start.8 = (f32[2,16,128]{2,1,0:T(8,128)}, f32[2,16,128]{2,1,0:T(8,128)S(1)}, u32[]{:S(2)}) copy-start(f32[2,16,128]{2,1,0:T(8,128)S(1)} %get-tuple-element.81.refs_6_) | copy-start | bytes 49156
  17.5 0.9 copy-start.2
  18.4 27.5 %copy-start.3 = (bf16[448,256]{1,0:T(8,128)(2,1)S(1)}, bf16[448,256]{1,0:T(8,128)(2,1)}, u32[]{:S(2)}) copy-start(bf16[448,256]{1,0:T(8,128)(2,1)} %get-tuple-element.55.own_hbm) | copy-start | bytes 688132
  21.3 25.3 %all-to-all-start = ((f32[24,16,128]{2,1,0:T(8,128)}), f32[24,16,128]{2,1,0:T(8,128)S(1)}, u32[]{:S(2)}, u32[]{:S(2)}) async-start(f32[24,16,128]{2,1,0:T(8,128)} %get-tuple-element.57), calls=%async_computation | async-start | bytes 393216 | tf_op jit(solution)/shard_map/all_to_all | solution.py:323
  31.6 1.4 %copy-start = (bf16[3072,256]{1,0:T(8,128)(2,1)S(1)}, bf16[3072,256]{1,0:T(8,128)(2,1)}, u32[]{:S(2)}) copy-start(bf16[3072,256]{1,0:T(8,128)(2,1)} %w_ref.3) | copy-start | bytes 4718596
  33.0 0.9 copy-start.4
  35.4 18.8 %collective-permute-start = (bf16[768,256]{1,0:T(8,128)(2,1)}, bf16[768,256]{1,0:T(8,128)(2,1)S(1)}, u32[]{:S(2)}, u32[]{:S(2)}) collective-permute-start(bf16[768,256]{1,0:T(8,128)(2,1)} %get-tuple-element.46), channel_id=1, source_target_pairs={{0,4},{4,8},{8,12},{12,0},{1,5},{5,9},{9,13},{13,1},{2,6},{6,10},{... | collective-permute-start | bytes 1179656 | tf_op jit(solution)/shard_map/ppermute | solution.py:333
  38.5 19.7 %collective-permute-start.1 = (bf16[768,256]{1,0:T(8,128)(2,1)}, bf16[768,256]{1,0:T(8,128)(2,1)S(1)}, u32[]{:S(2)}, u32[]{:S(2)}) collective-permute-start(bf16[768,256]{1,0:T(8,128)(2,1)} %get-tuple-element.47), channel_id=1, source_target_pairs={{0,8},{4,12},{8,0},{12,4},{1,9},{5,13},{9,1},{13,5},{2,10},{6,14},... | collective-permute-start | bytes 1179656 | tf_op jit(solution)/shard_map/ppermute | solution.py:333
  42.8 16.8 %collective-permute-start.2 = (bf16[768,256]{1,0:T(8,128)(2,1)S(1)}, bf16[768,256]{1,0:T(8,128)(2,1)}, u32[]{:S(2)}, u32[]{:S(2)}) collective-permute-start(bf16[768,256]{1,0:T(8,128)(2,1)S(1)} %get-tuple-element.48), channel_id=1, source_target_pairs={{0,12},{4,0},{8,4},{12,8},{1,13},{5,1},{9,5},{13,9},{2,14},{6,2},{... | collective-permute-start | bytes 1179656 | tf_op jit(solution)/shard_map/ppermute | solution.py:333
  48.7 15.2 %all-to-all-start.1 = ((bf16[4,96,512]{2,1,0:T(8,128)(2,1)}), bf16[4,96,512]{2,1,0:T(8,128)(2,1)S(1)}, u32[]{:S(2)}, u32[]{:S(2)}) async-start(bf16[4,96,512]{2,1,0:T(8,128)(2,1)} %get-tuple-element.59), calls=%async_computation.1 | async-start | bytes 786432 | tf_op jit(solution)/shard_map/all_to_all | solution.py:318
  65.2 24.9 %all-to-all-start.2 = ((bf16[4,384,512]{2,1,0:T(8,128)(2,1)}), bf16[4,384,512]{2,1,0:T(8,128)(2,1)S(1)}, u32[]{:S(2)}, u32[]{:S(2)}) async-start(bf16[4,384,512]{2,1,0:T(8,128)(2,1)} %broadcast_in_dim.2), calls=%async_computation.2 | async-start | bytes 3145728 | tf_op jit(solution)/shard_map/all_to_all | solution.py:318
  68.8 9.0 %collective-permute-start.5 = (bf16[192,256]{1,0:T(8,128)(2,1)S(1)}, bf16[192,256]{1,0:T(8,128)(2,1)S(1)}, u32[]{:S(2)}, u32[]{:S(2)}) collective-permute-start(bf16[192,256]{1,0:T(8,128)(2,1)S(1)} %get-tuple-element.64), channel_id=1, source_target_pairs={{0,1},{1,2},{2,3},{3,0},{4,5},{5,6},{6,7},{7,4},{8,9},{9,10},{10,1... | collective-permute-start | bytes 294920 | tf_op jit(solution)/shard_map/ppermute | solution.py:333
  70.7 7.8 %collective-permute-start.6 = (bf16[192,256]{1,0:T(8,128)(2,1)S(1)}, bf16[192,256]{1,0:T(8,128)(2,1)S(1)}, u32[]{:S(2)}, u32[]{:S(2)}) collective-permute-start(bf16[192,256]{1,0:T(8,128)(2,1)S(1)} %get-tuple-element.65), channel_id=1, source_target_pairs={{0,2},{1,3},{2,0},{3,1},{4,6},{5,7},{6,4},{7,5},{8,10},{9,11},{10,... | collective-permute-start | bytes 294920 | tf_op jit(solution)/shard_map/ppermute | solution.py:333
  75.2 6.4 %collective-permute-start.7 = (bf16[192,256]{1,0:T(8,128)(2,1)S(1)}, bf16[192,256]{1,0:T(8,128)(2,1)S(1)}, u32[]{:S(2)}, u32[]{:S(2)}) collective-permute-start(bf16[192,256]{1,0:T(8,128)(2,1)S(1)} %get-tuple-element.66), channel_id=1, source_target_pairs={{0,3},{1,0},{2,1},{3,2},{4,7},{5,4},{6,5},{7,6},{8,11},{9,8},{10,9... | collective-permute-start | bytes 294920 | tf_op jit(solution)/shard_map/ppermute | solution.py:333
  81.7 5.6 %collective-permute-start.8 = (f32[96,256]{1,0:T(8,128)S(1)}, f32[96,256]{1,0:T(8,128)S(1)}, u32[]{:S(2)}, u32[]{:S(2)}) collective-permute-start(f32[96,256]{1,0:T(8,128)S(1)} %get-tuple-element.68), channel_id=1, source_target_pairs={{0,16},{16,0},{1,17},{17,1},{2,18},{18,2},{3,19},{19,3},{4,20},{20... | collective-permute-start | bytes 294920 | tf_op jit(solution)/shard_map/ppermute | solution.py:337
  89.5 0.7 copy-start.5
  90.7 36.3 %copy-start.1 = (bf16[3072,256]{1,0:T(8,128)(2,1)S(1)}, bf16[3072,256]{1,0:T(8,128)(2,1)}, u32[]{:S(2)}) copy-start(bf16[3072,256]{1,0:T(8,128)(2,1)} %w_ref.3) | copy-start | bytes 4718596
  118.6 17.4 %all-to-all-start.4 = ((bf16[6,48,256]{2,1,0:T(8,128)(2,1)}), bf16[6,48,256]{2,1,0:T(8,128)(2,1)S(1)}, u32[]{:S(2)}, u32[]{:S(2)}) async-start(bf16[6,48,256]{2,1,0:T(8,128)(2,1)} %middle.1), calls=%async_computation.4 | async-start | bytes 294912 | tf_op jit(solution)/shard_map/all_to_all | solution.py:323
  127.7 7.6 %collective-permute-start.4 = (f32[256,256]{1,0:T(8,128)S(1)}, f32[256,256]{1,0:T(8,128)S(1)}, u32[]{:S(2)}, u32[]{:S(2)}) collective-permute-start(f32[256,256]{1,0:T(8,128)S(1)} %get-tuple-element.62), channel_id=1, source_target_pairs={{0,16},{16,0},{1,17},{17,1},{2,18},{18,2},{3,19},{19,3},{4,20},{20... | collective-permute-start | bytes 786440 | tf_op jit(solution)/shard_map/ppermute | solution.py:337
  130.0 6.0 %collective-permute-start.10 = (f32[256,128]{1,0:T(8,128)S(1)}, f32[256,128]{1,0:T(8,128)S(1)}, u32[]{:S(2)}, u32[]{:S(2)}) collective-permute-start(f32[256,128]{1,0:T(8,128)S(1)} %get-tuple-element.79), channel_id=1, source_target_pairs={{0,16},{16,0},{1,17},{17,1},{2,18},{18,2},{3,19},{19,3},{4,20},{20... | collective-permute-start | bytes 393224 | tf_op jit(solution)/shard_map/ppermute | solution.py:337
  132.0 3.2 %collective-permute-start.9 = (bf16[96,256]{1,0:T(8,128)(2,1)S(1)}, bf16[96,256]{1,0:T(8,128)(2,1)S(1)}, u32[]{:S(2)}, u32[]{:S(2)}) collective-permute-start(bf16[96,256]{1,0:T(8,128)(2,1)S(1)} %get-tuple-element.71), channel_id=1, source_target_pairs={{0,16},{16,0},{1,17},{17,1},{2,18},{18,2},{3,19},{19,3},{4,20},{20... | collective-permute-start | bytes 147464 | tf_op jit(solution)/shard_map/ppermute | solution.py:337
  136.0 0.7 copy-start.9
  136.0 0.7 copy-start.10

commit v11 on v10

--- a/solution.py
+++ b/solution.py
@@ -170,20 +170,24 @@
             p_ref[q, :, at] = product
 
 
-def scan_backward_kernel(own_ref, other_ref, f_ref, got_ref, d_ref, c_ref, yo_ref, yx_ref, s_ref, go_ref, gx_ref, bt, y_ref):
+def scan_backward_kernel(own_ref, other_ref, f_ref, got_ref, d_ref, c_ref, yo_ref, x_ref, s_ref, go_ref, bt, y_ref):
     tok = got_ref.shape[2]
     half = own_ref.shape[0]
     core = lax.axis_index(CORE)
-    for h, ref, out in ((core, own_ref, go_ref), (1 - core, other_ref, gx_ref)):
+    for h, ref in ((core, own_ref), (1 - core, other_ref)):
         total = ref[...]
-        out[...] = (total * f_ref[h].astype(f32)).astype(bf16)
+        grad_outer = (total * f_ref[h].astype(f32)).astype(bf16)
+        if ref is own_ref:
+            go_ref[...] = grad_outer
+        else:
+            x_ref[:, LANES:] = to_columns(grad_outer.astype(f32))
         outer = got_ref[h, tok + half :].astype(f32)
         at = pl.ds(pl.multiple_of(h * tok, tok), tok)
         bt[at, :] = to_columns((total * outer).astype(bf16).astype(f32))
     state = scan(bt, y_ref, jnp.exp(-d_ref[...]), c_ref[...], True)
     put_state(s_ref, state)
     yo_ref[...] = y_ref[pl.ds(pl.multiple_of(core * tok, tok), tok), :]
-    yx_ref[...] = y_ref[pl.ds(pl.multiple_of((1 - core) * tok, tok), tok), :]
+    x_ref[:, :LANES] = y_ref[pl.ds(pl.multiple_of((1 - core) * tok, tok), tok), :]
 
 
 def put_state(ref, state):
@@ -257,21 +261,20 @@
     other_ref[...] = total[:, pl.ds(pl.multiple_of((1 - core) * tok, tok), tok)]
 
 
-def halves(core, own_ref, other_ref, count):
-    for h, ref in ((core, own_ref), (1 - core, other_ref)):
-        for b in range(count):
+def finish_kernel(m_ref, mr_ref, own_ref, x_ref, mixed_ref, go_ref):
+    mixed_ref[...] = (m_ref[...] + mr_ref[...]).T.astype(bf16)
+    half = own_ref.shape[0]
+    other = x_ref[:, LANES:].T[:half].astype(bf16)
+    core = lax.axis_index(CORE)
+    for h, part in ((core, own_ref[...]), (1 - core, other)):
+        for b in range(half // SUB):
             at = pl.ds(pl.multiple_of(2 * SUB * b + SUB * h, SUB), SUB)
-            yield at, ref, pl.ds(SUB * b, SUB)
-
-
-def finish_kernel(m_ref, mr_ref, own_ref, other_ref, mixed_ref, go_ref):
-    mixed_ref[...] = (m_ref[...] + mr_ref[...]).T.astype(bf16)
-    for at, ref, src in halves(lax.axis_index(CORE), own_ref, other_ref, own_ref.shape[0] // SUB):
-        go_ref[at, :] = ref[src, :]
-
-
-def last_kernel(scale, t_hbm, yo_hbm, yx_hbm, i_hbm, v_hbm, d_hbm, c_hbm, gi_ref, gv_ref, gw_ref, t_ref, yo_ref, yx_ref, i_ref, v_ref, d_ref, c_ref, bt, sems):
-    pairs = ((t_hbm, t_ref), (yo_hbm, yo_ref), (yx_hbm, yx_ref), (i_hbm, i_ref), (v_hbm, v_ref))
+            go_ref[at, :] = part[SUB * b : SUB * (b + 1)]
+
+
+def last_kernel(scale, t_hbm, yo_hbm, x_hbm, i_hbm, v_hbm, d_hbm, c_hbm, gi_ref, gv_ref, gw_ref, t_ref, yo_ref, yx_ref, i_ref, v_ref, d_ref, c_ref, bt, sems):
+    part = x_hbm.at[:, pl.ds(0, LANES)]
+    pairs = ((t_hbm, t_ref), (yo_hbm, yo_ref), (part, yx_ref), (i_hbm, i_ref), (v_hbm, v_ref))
     fetch(sems, *pairs, (d_hbm, d_ref), (c_hbm, c_ref))
     tok = yo_ref.shape[0]
     half = i_ref.shape[0] // 2
@@ -402,10 +405,10 @@
     )
     product = spread(jnp.broadcast_to(product[None], (nx,) + product.shape), "x")
     half_columns = ((tok, LANES), f32)
-    yb, yb_other, state, grad_outer, grad_outer_other = call(
+    yb, other, state, grad_outer = call(
         scan_backward_kernel,
         "scan_backward",
-        [half_columns] * 2 + [((modes, 2 * LANES), bf16)] + [((half, tok), bf16)] * 2,
+        [half_columns, ((tok, 2 * LANES), f32), ((modes, 2 * LANES), bf16), ((half, tok), bf16)],
         (own, other_core(other), filtered, got, decay, coef),
         scratch=[columns] * 2,
     )
@@ -420,6 +423,7 @@
     last = ((2 * nh, SUB + modes, cols), bf16)
     (partial,) = call(middle_kernel, "middle", [last], (partial, decay))
     partial = swap_back(partial, ("zh", "core"))
+    other = other_core(other)
     mixed, mixed_other = call(
         mixed_kernel,
         "mixed",
@@ -431,7 +435,7 @@
         finish_kernel,
         "finish",
         [((tok, cols), bf16), gate],
-        (mixed, other_core(mixed_other), grad_outer, other_core(grad_outer_other)),
+        (mixed, other_core(mixed_other), grad_outer, other),
     )
     mixed, grad_outer, partial = lax.optimization_barrier((mixed, grad_outer, partial))
     scale = 1.0 / math.sqrt(length * chips)
@@ -442,7 +446,7 @@
         (
             partial.reshape(last[0]),
             yb,
-            other_core(yb_other),
+            other,
             inner_gate,
             value_proj,
             decay_both,

time: 141 us -> 140 us (level)
  starting transfers between devices: 71 us -> 68.7 us
    ppermute x5 -> x4, starting transfers between devices: 23.8 us -> 21.4 us  [other_core(): return lax.ppermute(x, 'core', [(0, 1), (1, 0)])]
  transfers between devices with their start and end apart: 15 -> 14, of which waited for: 7 -> 7; matrix products, arithmetic and copies ran while one was open for 1% -> 1% of each run, Pallas kernels for 7% -> 7%
where the time goes in v11:
time: 140 us; the launch traced here: 138 us
  starting transfers between devices  68.7 us (49%)
  blocking collectives  27.1 us (19%)
  Pallas kernels  19.1 us (14%)
  waiting for transfers between devices  14.7 us (10%)
  local copies, waits for them, and re-layouts  7.24 us (5%)
    all_to_all x1, blocking collectives, swap_back(): return lax.all_to_all(x, axes, 0, 0, axis_index_groups=order, tiled=True)  27.1 us
    ppermute x4, starting transfers between devices, other_core(): return lax.ppermute(x, 'core', [(0, 1), (1, 0)])  21.4 us
    ppermute x6, starting transfers between devices, shift(): return lax.ppermute(x, axis, [(i, (i + k) % n) for i in range(n)])  19.5 us
    pallas_call x14, Pallas kernels, call(): pl.pallas_call(kernel, out_shape=tuple((jax.ShapeDtypeStruct(s, t) for s,...  19.1 us
    all_to_all x2, starting transfers between devices, swap_back(): return lax.all_to_all(x, axes, 0, 0, axis_index_groups=order, tiled=True)  18.7 us
    ppermute x6, waiting for transfers between devices, shift(): return lax.ppermute(x, axis, [(i, (i + k) % n) for i in range(n)])  9.23 us
    all_to_all x2, starting transfers between devices, swap(): return lax.all_to_all(x, axes, 0, 0, tiled=True)  9.01 us
    unnamed x22, local copies, waits for them, and re-layouts  5.92 us
  transfers between devices with their start and end apart: 14, of which 7 were waited for; matrix products, arithmetic and copies ran while one was open for 1% of the time, Pallas kernels for 7%

profile of v11, /device:TPU:1, one launch (start us, length us, event | category | flops | bytes accessed | tf_op | source)
XLA Modules:
  0.0 138.4 jit_solution(848853117196538794)
XLA Ops:
  0.6 1.9 %pack.1 = (bf16[448,256]{1,0:T(8,128)(2,1)}, bf16[448,256]{1,0:T(8,128)(2,1)}) custom-call(bf16[192,256]{1,0:T(8,128)(2,1)} %refs_3_.1, bf16[192,256]{1,0:T(8,128)(2,1)} %refs_4_.1, bf16[192,256]{1,0:T(8,128)(2,1)} %o_hbm.1, bf16[256,256]{1,0:T(8,128)(2,1)} %g_hbm.1), custom_call_target="tpu_custom_call" | custom-call | tf_op jit(solution)/shard_map/pack/pallas_call | solution.py:304
  2.5 12.4 %collective-permute-start.3 = (bf16[448,256]{1,0:T(8,128)(2,1)}, bf16[448,256]{1,0:T(8,128)(2,1)S(1)}, u32[]{:S(2)}, u32[]{:S(2)}) collective-permute-start(bf16[448,256]{1,0:T(8,128)(2,1)} %get-tuple-element.55), channel_id=1, source_target_pairs={{0,16},{16,0},{1,17},{17,1},{2,18},{18,2},{3,19},{19,3},{4,20},{20... | collective-permute-start | bytes 688136 | tf_op jit(solution)/shard_map/ppermute | solution.py:340
  15.0 0.8 multiply_bitcast_fusion.c_ref
  15.7 0.0 copy-start.7
  15.7 0.7 copy-done.7
  16.4 0.4 modes.1
  16.9 0.0 copy-start.8
  16.9 0.6 copy-done.8
  17.5 0.0 copy-start.9
  17.5 0.0 collective-permute-done.3.other_hbm
  17.5 0.0 copy-start.3
  17.5 0.9 copy-done.3
  18.4 0.0 copy-start.4
  18.4 2.8 %scan_forward.1 = (f32[512,128]{1,0:T(8,128)S(1)}, f32[24,16,128]{2,1,0:T(8,128)}) custom-call(f32[16,128]{1,0:T(8,128)S(1)} %get-tuple-element.52.d_ref, f32[16,128]{1,0:T(8,128)S(1)} %get-tuple-element.53.c_ref, bf16[448,256]{1,0:T(8,128)(2,1)S(1)} %copy-done.3, bf16[448,256]{1,0:T(8,128)(2,1)S(1)} %collective-permute-done.3.other_hbm), custom_call_target="tpu_custom_call" | custom-call | tf_op jit(solution)/shard_map/scan_forward/pallas_call | solution.py:304
  21.2 10.3 %all-to-all-start = ((f32[24,16,128]{2,1,0:T(8,128)}), f32[24,16,128]{2,1,0:T(8,128)S(1)}, u32[]{:S(2)}, u32[]{:S(2)}) async-start(f32[24,16,128]{2,1,0:T(8,128)} %get-tuple-element.56), calls=%async_computation | async-start | bytes 393216 | tf_op jit(solution)/shard_map/all_to_all | solution.py:326
  31.5 0.0 copy-start
  31.6 1.4 %copy-done = bf16[3072,256]{1,0:T(8,128)(2,1)S(1)} copy-done((bf16[3072,256]{1,0:T(8,128)(2,1)S(1)}, bf16[3072,256]{1,0:T(8,128)(2,1)}, u32[]{:S(2)}) %copy-start) | copy-done | bytes 1572888
  33.0 0.9 copy-done.5
  33.9 1.4 %back.1 = (bf16[768,256]{1,0:T(8,128)(2,1)S(1)}, bf16[768,256]{1,0:T(8,128)(2,1)}, bf16[768,256]{1,0:T(8,128)(2,1)}, bf16[768,256]{1,0:T(8,128)(2,1)S(1)}) custom-call(bf16[3072,256]{1,0:T(8,128)(2,1)S(1)} %copy-done, bf16[256,256]{1,0:T(8,128)(2,1)S(1)} %copy-done.5), custom_call_target="tpu_custom_call" | custom-call | tf_op jit(solution)/shard_map/back/pallas_call | solution.py:304
  35.3 3.1 %collective-permute-start = (bf16[768,256]{1,0:T(8,128)(2,1)}, bf16[768,256]{1,0:T(8,128)(2,1)S(1)}, u32[]{:S(2)}, u32[]{:S(2)}) collective-permute-start(bf16[768,256]{1,0:T(8,128)(2,1)} %get-tuple-element.45), channel_id=1, source_target_pairs={{0,4},{4,8},{8,12},{12,0},{1,5},{5,9},{9,13},{13,1},{2,6},{6,10},{... | collective-permute-start | bytes 1179656 | tf_op jit(solution)/shard_map/ppermute | solution.py:336
  38.4 4.4 %collective-permute-start.1 = (bf16[768,256]{1,0:T(8,128)(2,1)}, bf16[768,256]{1,0:T(8,128)(2,1)S(1)}, u32[]{:S(2)}, u32[]{:S(2)}) collective-permute-start(bf16[768,256]{1,0:T(8,128)(2,1)} %get-tuple-element.46), channel_id=1, source_target_pairs={{0,8},{4,12},{8,0},{12,4},{1,9},{5,13},{9,1},{13,5},{2,10},{6,14},... | collective-permute-start | bytes 1179656 | tf_op jit(solution)/shard_map/ppermute | solution.py:336
  42.8 3.1 %collective-permute-start.2 = (bf16[768,256]{1,0:T(8,128)(2,1)S(1)}, bf16[768,256]{1,0:T(8,128)(2,1)}, u32[]{:S(2)}, u32[]{:S(2)}) collective-permute-start(bf16[768,256]{1,0:T(8,128)(2,1)S(1)} %get-tuple-element.47), channel_id=1, source_target_pairs={{0,12},{4,0},{8,4},{12,8},{1,13},{5,1},{9,5},{13,9},{2,14},{6,2},{... | collective-permute-start | bytes 1179656 | tf_op jit(solution)/shard_map/ppermute | solution.py:336
  45.9 0.0 copy-done.4
  45.9 0.6 both.1.got_ref
  46.5 0.0 copy-done.9
  46.5 0.0 all-to-all-done.s_ref
  46.5 2.1 %heads_forward.1 = (bf16[4,96,512]{2,1,0:T(8,128)(2,1)}, bf16[2,96,256]{2,1,0:T(8,128)(2,1)S(1)}) custom-call(f32[24,16,128]{2,1,0:T(8,128)S(1)} %all-to-all-done.s_ref, f32[16,128]{1,0:T(8,128)S(1)} %get-tuple-element.52.d_ref, f32[16,128]{1,0:T(8,128)S(1)} %get-tuple-element.53.c_ref, f32[512,128]{1,0:T(8,128)S(1)} %get-tuple-element.57.y_ref, ...), custom_call_target="tpu_custom_call" | custom-call | tf_op jit(solution)/shard_map/heads_forward/pallas_call | solution.py:304
  48.7 5.4 %all-to-all-start.1 = ((bf16[4,96,512]{2,1,0:T(8,128)(2,1)}), bf16[4,96,512]{2,1,0:T(8,128)(2,1)S(1)}, u32[]{:S(2)}, u32[]{:S(2)}) async-start(bf16[4,96,512]{2,1,0:T(8,128)(2,1)} %get-tuple-element.58), calls=%async_computation.1 | async-start | bytes 786432 | tf_op jit(solution)/shard_map/all_to_all | solution.py:321
  54.1 0.0 collective-permute-done.p1
  54.1 4.0 %collective-permute-done.1.p2 = bf16[768,256]{1,0:T(8,128)(2,1)S(1)} collective-permute-done((bf16[768,256]{1,0:T(8,128)(2,1)}, bf16[768,256]{1,0:T(8,128)(2,1)S(1)}, u32[]{:S(2)}, u32[]{:S(2)}) %collective-permute-start.1) | collective-permute-done | bytes 393248 | tf_op jit(solution)/shard_map/ppermute | solution.py:336
  58.1 1.4 %collective-permute-done.2.p3 = bf16[768,256]{1,0:T(8,128)(2,1)} collective-permute-done((bf16[768,256]{1,0:T(8,128)(2,1)S(1)}, bf16[768,256]{1,0:T(8,128)(2,1)}, u32[]{:S(2)}, u32[]{:S(2)}) %collective-permute-start.2) | collective-permute-done | bytes 393248 | tf_op jit(solution)/shard_map/ppermute | solution.py:336
  59.6 1.2 split.1
  60.7 3.1 %all-to-all-done.1 = bf16[4,96,512]{2,1,0:T(8,128)(2,1)S(1)} async-done(((bf16[4,96,512]{2,1,0:T(8,128)(2,1)}), bf16[4,96,512]{2,1,0:T(8,128)(2,1)S(1)}, u32[]{:S(2)}, u32[]{:S(2)}) %all-to-all-start.1) | async-done | bytes 393248 | tf_op jit(solution)/shard_map/all_to_all | solution.py:321
  63.8 1.3 broadcast_in_dim.2
  65.2 3.6 %all-to-all-start.2 = ((bf16[4,384,512]{2,1,0:T(8,128)(2,1)}), bf16[4,384,512]{2,1,0:T(8,128)(2,1)S(1)}, u32[]{:S(2)}, u32[]{:S(2)}) async-start(bf16[4,384,512]{2,1,0:T(8,128)(2,1)} %broadcast_in_dim.2), calls=%async_computation.2 | async-start | bytes 3145728 | tf_op jit(solution)/shard_map/all_to_all | solution.py:321
  68.7 1.9 %collective-permute-start.5 = (bf16[192,256]{1,0:T(8,128)(2,1)S(1)}, bf16[192,256]{1,0:T(8,128)(2,1)S(1)}, u32[]{:S(2)}, u32[]{:S(2)}) collective-permute-start(bf16[192,256]{1,0:T(8,128)(2,1)S(1)} %get-tuple-element.63), channel_id=1, source_target_pairs={{0,1},{1,2},{2,3},{3,0},{4,5},{5,6},{6,7},{7,4},{8,9},{9,10},{10,1... | collective-permute-start | bytes 294920 | tf_op jit(solution)/shard_map/ppermute | solution.py:336
  70.7 4.5 %collective-permute-start.6 = (bf16[192,256]{1,0:T(8,128)(2,1)S(1)}, bf16[192,256]{1,0:T(8,128)(2,1)S(1)}, u32[]{:S(2)}, u32[]{:S(2)}) collective-permute-start(bf16[192,256]{1,0:T(8,128)(2,1)S(1)} %get-tuple-element.64), channel_id=1, source_target_pairs={{0,2},{1,3},{2,0},{3,1},{4,6},{5,7},{6,4},{7,5},{8,10},{9,11},{10,... | collective-permute-start | bytes 294920 | tf_op jit(solution)/shard_map/ppermute | solution.py:336
  75.2 2.6 %collective-permute-start.7 = (bf16[192,256]{1,0:T(8,128)(2,1)S(1)}, bf16[192,256]{1,0:T(8,128)(2,1)S(1)}, u32[]{:S(2)}, u32[]{:S(2)}) collective-permute-start(bf16[192,256]{1,0:T(8,128)(2,1)S(1)} %get-tuple-element.65), channel_id=1, source_target_pairs={{0,3},{1,0},{2,1},{3,2},{4,7},{5,4},{6,5},{7,6},{8,11},{9,8},{10,9... | collective-permute-start | bytes 294920 | tf_op jit(solution)/shard_map/ppermute | solution.py:336
  77.8 0.0 collective-permute-done.5.p1
  77.8 0.7 collective-permute-done.6.p2
  78.5 3.1 %collective-permute-done.7.p3 = bf16[192,256]{1,0:T(8,128)(2,1)S(1)} collective-permute-done((bf16[192,256]{1,0:T(8,128)(2,1)S(1)}, bf16[192,256]{1,0:T(8,128)(2,1)S(1)}, u32[]{:S(2)}, u32[]{:S(2)}) %collective-permute-start.7) | collective-permute-done | bytes 98336 | tf_op jit(solution)/shard_map/ppermute | solution.py:336
  81.6 4.7 %collective-permute-start.8 = (f32[96,256]{1,0:T(8,128)S(1)}, f32[96,256]{1,0:T(8,128)S(1)}, u32[]{:S(2)}, u32[]{:S(2)}) collective-permute-start(f32[96,256]{1,0:T(8,128)S(1)} %get-tuple-element.67), channel_id=1, source_target_pairs={{0,16},{16,0},{1,17},{17,1},{2,18},{18,2},{3,19},{19,3},{4,20},{20... | collective-permute-start | bytes 294920 | tf_op jit(solution)/shard_map/ppermute | solution.py:340
  86.3 0.9 collective-permute-done.8.other_ref
  87.2 2.2 %scan_backward.1 = (f32[256,128]{1,0:T(8,128)S(1)}, f32[256,256]{1,0:T(8,128)S(1)}, bf16[16,256]{1,0:T(8,128)(2,1)S(1)}, bf16[96,256]{1,0:T(8,128)(2,1)S(1)}) custom-call(f32[96,256]{1,0:T(8,128)S(1)} %get-tuple-element.66.own_ref, f32[96,256]{1,0:T(8,128)S(1)} %collective-permute-done.8.other_ref, bf16[2,96,256]{2,1,0:T(8,128)(2,1)S(1)} %get-tuple-element.68.f_ref, ...), custom_call_target="tpu_custom_call" | custom-call | tf_op jit(solution)/shard_map/scan_backward/pallas_call | solution.py:304
  89.4 0.0 copy-start.6
  89.4 0.6 copy-done.6
  90.1 0.7 copy-done.10
  90.8 0.0 all-to-all-done.2
  90.8 0.6 weight.1
  91.4 0.0 copy-start.1
  91.4 27.1 %all_to_all.32.t_ref = bf16[8,208,256]{2,1,0:T(8,128)(2,1)S(1)} all-to-all(bf16[8,208,256]{2,1,0:T(8,128)(2,1)S(1)} %weight.1), channel_id=1, replica_groups={{672,576,480,384,288,192,96,0},{673,577,481,385,289,193,97,1},{674,578,..., dimensions={0} | all-to-all | bytes 1703936 | tf_op jit(solution)/shard_map/all_to_all | solution.py:326
  118.5 0.8 middle.1
  119.3 8.4 %all-to-all-start.4 = ((bf16[6,48,256]{2,1,0:T(8,128)(2,1)}), bf16[6,48,256]{2,1,0:T(8,128)(2,1)}, u32[]{:S(2)}, u32[]{:S(2)}) async-start(bf16[6,48,256]{2,1,0:T(8,128)(2,1)} %middle.1), calls=%async_computation.4 | async-start | bytes 294912 | tf_op jit(solution)/shard_map/all_to_all | solution.py:326
  127.7 2.3 %collective-permute-start.9 = (f32[256,256]{1,0:T(8,128)}, f32[256,256]{1,0:T(8,128)S(1)}, u32[]{:S(2)}, u32[]{:S(2)}) collective-permute-start(f32[256,256]{1,0:T(8,128)} %copy-done.10), channel_id=1, source_target_pairs={{0,16},{16,0},{1,17},{17,1},{2,18},{18,2},{3,19},{19,3},{4,20},{20... | collective-permute-start | bytes 786440 | tf_op jit(solution)/shard_map/ppermute | solution.py:340
  130.0 0.0 copy-done.1
  130.0 0.7 mixed.1
  130.7 2.0 %collective-permute-start.4 = (f32[256,256]{1,0:T(8,128)S(1)}, f32[256,256]{1,0:T(8,128)S(1)}, u32[]{:S(2)}, u32[]{:S(2)}) collective-permute-start(f32[256,256]{1,0:T(8,128)S(1)} %get-tuple-element.61), channel_id=1, source_target_pairs={{0,16},{16,0},{1,17},{17,1},{2,18},{18,2},{3,19},{19,3},{4,20},{20... | collective-permute-start | bytes 786440 | tf_op jit(solution)/shard_map/ppermute | solution.py:340
  132.7 0.0 collective-permute-done.9.x_ref.refs_2_
  132.7 0.0 copy-start.2
  132.7 1.4 %collective-permute-done.4.mr_ref = f32[256,256]{1,0:T(8,128)S(1)} collective-permute-done((f32[256,256]{1,0:T(8,128)S(1)}, f32[256,256]{1,0:T(8,128)S(1)}, u32[]{:S(2)}, u32[]{:S(2)}) %collective-permute-start.4) | collective-permute-done | bytes 262176 | tf_op jit(solution)/shard_map/ppermute | solution.py:340
  134.1 0.8 finish.1
  134.9 0.0 all-to-all-done.4.refs_0_
  134.9 0.0 copy-done.2
  134.9 3.5 %last.1 = (bf16[192,256]{1,0:T(8,128)(2,1)}, bf16[192,256]{1,0:T(8,128)(2,1)}, f32[64,256]{1,0:T(8,128)}) custom-call(bf16[6,48,256]{2,1,0:T(8,128)(2,1)} %all-to-all-done.4.refs_0_, f32[256,128]{1,0:T(8,128)} %copy-done.6, f32[256,256]{1,0:T(8,128)} %copy-done.2, bf16[192,256]{1,0:T(8,128)(2,1)} %refs_3_.1, bf16[192,256]{1,0:T(8,128)(2,1)} %refs_4_.1, ...), custom_call_target="tpu_custom_call" | custom-call | tf_op jit(solution)/shard_map/last/pallas_call | solution.py:304
  (3 shorter events, 0.1 us)
Async XLA Ops:
  2.5 15.0 %collective-permute-start.3 = (bf16[448,256]{1,0:T(8,128)(2,1)}, bf16[448,256]{1,0:T(8,128)(2,1)S(1)}, u32[]{:S(2)}, u32[]{:S(2)}) collective-permute-start(bf16[448,256]{1,0:T(8,128)(2,1)} %get-tuple-element.55), channel_id=1, source_target_pairs={{0,16},{16,0},{1,17},{17,1},{2,18},{18,2},{3,19},{19,3},{4,20},{20... | collective-permute-start | bytes 688136 | tf_op jit(solution)/shard_map/ppermute | solution.py:340
  15.7 0.7 copy-start.7
  16.9 0.6 copy-start.8
  17.5 29.0 %copy-start.9 = (f32[2,16,128]{2,1,0:T(8,128)}, f32[2,16,128]{2,1,0:T(8,128)S(1)}, u32[]{:S(2)}) copy-start(f32[2,16,128]{2,1,0:T(8,128)S(1)} %get-tuple-element.79.refs_6_) | copy-start | bytes 49156
  17.5 0.9 copy-start.3
  18.4 27.4 %copy-start.4 = (bf16[448,256]{1,0:T(8,128)(2,1)S(1)}, bf16[448,256]{1,0:T(8,128)(2,1)}, u32[]{:S(2)}) copy-start(bf16[448,256]{1,0:T(8,128)(2,1)} %get-tuple-element.54.own_hbm) | copy-start | bytes 688132
  21.2 25.3 %all-to-all-start = ((f32[24,16,128]{2,1,0:T(8,128)}), f32[24,16,128]{2,1,0:T(8,128)S(1)}, u32[]{:S(2)}, u32[]{:S(2)}) async-start(f32[24,16,128]{2,1,0:T(8,128)} %get-tuple-element.56), calls=%async_computation | async-start | bytes 393216 | tf_op jit(solution)/shard_map/all_to_all | solution.py:326
  31.5 1.4 %copy-start = (bf16[3072,256]{1,0:T(8,128)(2,1)S(1)}, bf16[3072,256]{1,0:T(8,128)(2,1)}, u32[]{:S(2)}) copy-start(bf16[3072,256]{1,0:T(8,128)(2,1)} %w_ref.3) | copy-start | bytes 4718596
  33.0 0.9 copy-start.5
  35.3 18.8 %collective-permute-start = (bf16[768,256]{1,0:T(8,128)(2,1)}, bf16[768,256]{1,0:T(8,128)(2,1)S(1)}, u32[]{:S(2)}, u32[]{:S(2)}) collective-permute-start(bf16[768,256]{1,0:T(8,128)(2,1)} %get-tuple-element.45), channel_id=1, source_target_pairs={{0,4},{4,8},{8,12},{12,0},{1,5},{5,9},{9,13},{13,1},{2,6},{6,10},{... | collective-permute-start | bytes 1179656 | tf_op jit(solution)/shard_map/ppermute | solution.py:336
  38.4 19.7 %collective-permute-start.1 = (bf16[768,256]{1,0:T(8,128)(2,1)}, bf16[768,256]{1,0:T(8,128)(2,1)S(1)}, u32[]{:S(2)}, u32[]{:S(2)}) collective-permute-start(bf16[768,256]{1,0:T(8,128)(2,1)} %get-tuple-element.46), channel_id=1, source_target_pairs={{0,8},{4,12},{8,0},{12,4},{1,9},{5,13},{9,1},{13,5},{2,10},{6,14},... | collective-permute-start | bytes 1179656 | tf_op jit(solution)/shard_map/ppermute | solution.py:336
  42.8 16.8 %collective-permute-start.2 = (bf16[768,256]{1,0:T(8,128)(2,1)S(1)}, bf16[768,256]{1,0:T(8,128)(2,1)}, u32[]{:S(2)}, u32[]{:S(2)}) collective-permute-start(bf16[768,256]{1,0:T(8,128)(2,1)S(1)} %get-tuple-element.47), channel_id=1, source_target_pairs={{0,12},{4,0},{8,4},{12,8},{1,13},{5,1},{9,5},{13,9},{2,14},{6,2},{... | collective-permute-start | bytes 1179656 | tf_op jit(solution)/shard_map/ppermute | solution.py:336
  48.7 15.2 %all-to-all-start.1 = ((bf16[4,96,512]{2,1,0:T(8,128)(2,1)}), bf16[4,96,512]{2,1,0:T(8,128)(2,1)S(1)}, u32[]{:S(2)}, u32[]{:S(2)}) async-start(bf16[4,96,512]{2,1,0:T(8,128)(2,1)} %get-tuple-element.58), calls=%async_computation.1 | async-start | bytes 786432 | tf_op jit(solution)/shard_map/all_to_all | solution.py:321
  65.2 25.6 %all-to-all-start.2 = ((bf16[4,384,512]{2,1,0:T(8,128)(2,1)}), bf16[4,384,512]{2,1,0:T(8,128)(2,1)S(1)}, u32[]{:S(2)}, u32[]{:S(2)}) async-start(bf16[4,384,512]{2,1,0:T(8,128)(2,1)} %broadcast_in_dim.2), calls=%async_computation.2 | async-start | bytes 3145728 | tf_op jit(solution)/shard_map/all_to_all | solution.py:321
  68.7 9.0 %collective-permute-start.5 = (bf16[192,256]{1,0:T(8,128)(2,1)S(1)}, bf16[192,256]{1,0:T(8,128)(2,1)S(1)}, u32[]{:S(2)}, u32[]{:S(2)}) collective-permute-start(bf16[192,256]{1,0:T(8,128)(2,1)S(1)} %get-tuple-element.63), channel_id=1, source_target_pairs={{0,1},{1,2},{2,3},{3,0},{4,5},{5,6},{6,7},{7,4},{8,9},{9,10},{10,1... | collective-permute-start | bytes 294920 | tf_op jit(solution)/shard_map/ppermute | solution.py:336
  70.7 7.8 %collective-permute-start.6 = (bf16[192,256]{1,0:T(8,128)(2,1)S(1)}, bf16[192,256]{1,0:T(8,128)(2,1)S(1)}, u32[]{:S(2)}, u32[]{:S(2)}) collective-permute-start(bf16[192,256]{1,0:T(8,128)(2,1)S(1)} %get-tuple-element.64), channel_id=1, source_target_pairs={{0,2},{1,3},{2,0},{3,1},{4,6},{5,7},{6,4},{7,5},{8,10},{9,11},{10,... | collective-permute-start | bytes 294920 | tf_op jit(solution)/shard_map/ppermute | solution.py:336
  75.2 6.4 %collective-permute-start.7 = (bf16[192,256]{1,0:T(8,128)(2,1)S(1)}, bf16[192,256]{1,0:T(8,128)(2,1)S(1)}, u32[]{:S(2)}, u32[]{:S(2)}) collective-permute-start(bf16[192,256]{1,0:T(8,128)(2,1)S(1)} %get-tuple-element.65), channel_id=1, source_target_pairs={{0,3},{1,0},{2,1},{3,2},{4,7},{5,4},{6,5},{7,6},{8,11},{9,8},{10,9... | collective-permute-start | bytes 294920 | tf_op jit(solution)/shard_map/ppermute | solution.py:336
  81.6 5.6 %collective-permute-start.8 = (f32[96,256]{1,0:T(8,128)S(1)}, f32[96,256]{1,0:T(8,128)S(1)}, u32[]{:S(2)}, u32[]{:S(2)}) collective-permute-start(f32[96,256]{1,0:T(8,128)S(1)} %get-tuple-element.67), channel_id=1, source_target_pairs={{0,16},{16,0},{1,17},{17,1},{2,18},{18,2},{3,19},{19,3},{4,20},{20... | collective-permute-start | bytes 294920 | tf_op jit(solution)/shard_map/ppermute | solution.py:340
  89.4 0.7 copy-start.6
  90.1 0.7 copy-start.10
  91.4 38.6 %copy-start.1 = (bf16[3072,256]{1,0:T(8,128)(2,1)S(1)}, bf16[3072,256]{1,0:T(8,128)(2,1)}, u32[]{:S(2)}) copy-start(bf16[3072,256]{1,0:T(8,128)(2,1)} %w_ref.3) | copy-start | bytes 4718596
  119.3 15.7 %all-to-all-start.4 = ((bf16[6,48,256]{2,1,0:T(8,128)(2,1)}), bf16[6,48,256]{2,1,0:T(8,128)(2,1)}, u32[]{:S(2)}, u32[]{:S(2)}) async-start(bf16[6,48,256]{2,1,0:T(8,128)(2,1)} %middle.1), calls=%async_computation.4 | async-start | bytes 294912 | tf_op jit(solution)/shard_map/all_to_all | solution.py:326
  127.7 5.0 %collective-permute-start.9 = (f32[256,256]{1,0:T(8,128)}, f32[256,256]{1,0:T(8,128)S(1)}, u32[]{:S(2)}, u32[]{:S(2)}) collective-permute-start(f32[256,256]{1,0:T(8,128)} %copy-done.10), channel_id=1, source_target_pairs={{0,16},{16,0},{1,17},{17,1},{2,18},{18,2},{3,19},{19,3},{4,20},{20... | collective-permute-start | bytes 786440 | tf_op jit(solution)/shard_map/ppermute | solution.py:340
  130.7 3.4 %collective-permute-start.4 = (f32[256,256]{1,0:T(8,128)S(1)}, f32[256,256]{1,0:T(8,128)S(1)}, u32[]{:S(2)}, u32[]{:S(2)}) collective-permute-start(f32[256,256]{1,0:T(8,128)S(1)} %get-tuple-element.61), channel_id=1, source_target_pairs={{0,16},{16,0},{1,17},{17,1},{2,18},{18,2},{3,19},{19,3},{4,20},{20... | collective-permute-start | bytes 786440 | tf_op jit(solution)/shard_map/ppermute | solution.py:340
  132.7 2.2 %copy-start.2 = (f32[256,256]{1,0:T(8,128)}, f32[256,256]{1,0:T(8,128)S(1)}, u32[]{:S(2)}) copy-start(f32[256,256]{1,0:T(8,128)S(1)} %collective-permute-done.9.x_ref.refs_2_) | copy-start | bytes 786436
